TPU v7x, 32 devices: a whole 2x2x4 slice. The times are simulated.
32 devices in a mesh: seq: 16 (over z, y, x), head: 2 (over core).
Axes of the slice: x: 2, y: 2, z: 4, core: 2. Of those that a mesh axis runs over, the one named last changes fastest.
Arguments:
- activations: bfloat16 [16384, 1024], P('seq'), may hold values from -6 to 6
- log_decay: float32 [16384, 8], P('seq', 'head'), may hold values from -2 to 0, as said below
- doc_starts: int32 [3], replicated, may hold values from 0 to 16383, as said below
- query_weight: bfloat16 [1024, 1024], P('seq', 'head'), may hold values from -0.1875 to 0.1875
- key_weight: bfloat16 [1024, 2048], P('seq', 'head'), may hold values from -0.1875 to 0.1875
- value_weight: bfloat16 [1024, 2048], P('seq', 'head'), may hold values from -0.1875 to 0.1875
- beta_weight: bfloat16 [1024, 16], P('seq', 'head'), may hold values from -0.1875 to 0.1875
- gate_weight: bfloat16 [1024, 1024], P('seq', 'head'), may hold values from -0.1875 to 0.1875
- out_weight: bfloat16 [1024, 1024], P('head', 'seq'), may hold values from -0.375 to 0.375
- query_taps: bfloat16 [4, 1024], P(None, 'head'), may hold values from -3 to 3
- key_taps: bfloat16 [4, 2048], P(None, 'head'), may hold values from -3 to 3
- value_taps: bfloat16 [4, 2048], P(None, 'head'), may hold values from -3 to 3
- mixer_gain: bfloat16 [1024], P('seq'), may hold values from 0.5 to 1.5
- head_gain: bfloat16 [128], replicated, may hold values from 0.5 to 1.5
- feed_gain: bfloat16 [1024], P('seq'), may hold values from 0.5 to 1.5
- feed_gate: bfloat16 [1024, 2816], P('seq', 'head'), may hold values from -0.1875 to 0.1875
- feed_up: bfloat16 [1024, 2816], P('seq', 'head'), may hold values from -0.1875 to 0.1875
- feed_down: bfloat16 [2816, 1024], P('head', 'seq'), may hold values from -0.21875 to 0.21875
- cotangent: bfloat16 [16384, 1024], P('seq'), may hold values from -6 to 6
Outputs:
- output: bfloat16 [16384, 1024], P('seq', 'head')
- grad_input: float32 [16384, 1024], P('seq', 'head')
- grad_query: float32 [1024, 1024], P('seq', 'head')
- grad_key: float32 [1024, 2048], P('seq', 'head')
- grad_value: float32 [1024, 2048], P('seq', 'head')
- grad_beta: float32 [1024, 16], P('seq', 'head')
- grad_gate: float32 [1024, 1024], P('seq', 'head')
- grad_out: float32 [1024, 1024], P('head', 'seq')
- grad_query_taps: float32 [4, 1024], P(None, 'head')
- grad_key_taps: float32 [4, 2048], P(None, 'head')
- grad_value_taps: float32 [4, 2048], P(None, 'head')
- grad_mixer_gain: float32 [1024], P('seq')
- grad_head_gain: float32 [128], replicated
- grad_feed_gain: float32 [1024], P('seq')
- grad_feed_gate: float32 [1024, 2816], P('seq', 'head')
- grad_feed_up: float32 [1024, 2816], P('seq', 'head')
- grad_feed_down: float32 [2816, 1024], P('head', 'seq')
Inputs may be any that keep to these rules, and one draw needn't show every extreme that they name: `log_decay`: every entry is at most zero. doc_starts[0] is 0; doc_starts[1] lies in 1 to 1023 and doc_starts[2] in 15361 to 16383, so that the second sequence covers tokens of every index of seq.
All inputs are finite; a program needn't handle non-finite values.
Results may differ from a plain program's by a relative error of at most 0.014.
The roundings to bfloat16 on the way count: a program that leaves them out, or rounds other values in their place, can miss the bound.
Values may be sent and summed in bfloat16 or wider, within the bound.
No kernel may reach another device: no remote copies, remote signals or barrier semaphores. Data moves between devices by JAX's collectives and lax.ppermute only.
A program may use at most 384 MiB of HBM per device.

v0:
```python
import jax
import jax.numpy as jnp
from jax import lax
from jax.sharding import PartitionSpec as P

BLOCK = 64


TOP_PRECISION = lax.Precision.HIGHEST
NORM_EPS = 1e-05
UNIT_EPS = 1e-06


def from_behind(array, axis, by):
    count = lax.axis_size(axis)
    pairs = [(i, i + by) for i in range(count) if 0 <= i + by < count]
    return lax.ppermute(array, axis, pairs)


def entering(value, axis, join, neutral):
    count, mine = (lax.axis_size(axis), lax.axis_index(axis))
    pieces = jax.tree.map(lambda part: lax.all_gather(part, axis), value)
    total = jax.tree.map(
        lambda part, zero: jnp.full_like(part, 0) + jnp.asarray(zero, part.dtype), value, neutral
    )

    def entering_hop(position, total):
        longer = join(total, jax.tree.map(lambda part: part[position], pieces))
        return jax.tree.map(lambda new, old: jnp.where(position < mine, new, old), longer, total)

    return lax.fori_loop(0, count - 1, entering_hop, total)


def carried_in(array, axis, combine, identity):
    count, position = (lax.axis_size(axis), lax.axis_index(axis))
    everything = jax.tree.map(
        lambda part, kind: lax.all_gather(part.astype(kind), axis),
        array,
        jax.tree.map(lambda a: jnp.bfloat16 if a.dtype == jnp.float32 else a.dtype, array),
    )
    start = jax.tree.map(
        lambda part, zero: jnp.broadcast_to(jnp.asarray(zero, part.dtype), part.shape),
        array,
        identity,
    )

    def carried_hop(k, before):
        at = count - 1 - k
        reached = at > position
        new = combine(
            before, jax.tree.map(lambda part, own: part[at].astype(own.dtype), everything, array)
        )
        return jax.tree.map(lambda a, b: jnp.where(reached, a, b), new, before)

    return lax.fori_loop(0, count, carried_hop, start)


def product(former, latter):
    return jnp.dot(former, latter, preferred_element_type=jnp.float32)


def inner_rows(former, latter):
    return lax.dot_general(
        former, latter, (((0,), (0,)), ((), ())), preferred_element_type=jnp.float32
    )


def times_transposed(former, latter):
    return lax.dot_general(
        former, latter, (((1,), (1,)), ((), ())), preferred_element_type=jnp.float32
    )


def rounded(values):
    return lax.optimization_barrier(values.astype(jnp.bfloat16)).astype(jnp.float32)


def root_norm(values, gain_vector):
    return (
        values
        * lax.rsqrt(jnp.mean(values * values, axis=-1, keepdims=True) + NORM_EPS)
        * gain_vector
    )


def norm_back(values, gain_vector, gradient):
    row_scale = lax.rsqrt(jnp.mean(values * values, axis=-1, keepdims=True) + NORM_EPS)
    unit_value = values * row_scale
    scaled_grad = gradient * gain_vector
    back_value = row_scale * (
        scaled_grad - unit_value * jnp.mean(scaled_grad * unit_value, axis=-1, keepdims=True)
    )
    return (back_value, gradient * unit_value)


def silu_slope(values):
    sigma = jax.nn.sigmoid(values)
    return sigma * (1.0 + values * (1.0 - sigma))


def doc_number(token_position, doc_starts):
    return jnp.sum((token_position[:, None] >= doc_starts[None, :]).astype(jnp.int32), axis=1)


def short_conv(extended, conv_taps, same_doc, count):
    tap_count = conv_taps.shape[0]
    outcome = extended[tap_count - 1 : tap_count - 1 + count] * conv_taps[0]
    for offset in range(1, tap_count):
        window = extended[tap_count - 1 - offset : tap_count - 1 - offset + count]
        outcome = outcome + window * conv_taps[offset] * same_doc[offset][:, None]
    return outcome


def conv_back(extended, conv_taps, same_doc, gradient):
    tap_count = conv_taps.shape[0]
    count = gradient.shape[0]
    tap_grads = []
    spread = jnp.zeros(extended.shape, jnp.float32)
    for offset in range(tap_count):
        masked = gradient * same_doc[offset][:, None]
        window = extended[tap_count - 1 - offset : tap_count - 1 - offset + count]
        tap_grads.append(jnp.sum(masked * window, axis=0))
        spread = spread + jnp.pad(
            masked * conv_taps[offset], ((tap_count - 1 - offset, offset), (0, 0))
        )
    return (jnp.stack(tap_grads), spread)


def compose(earlier, latter):
    return (
        jnp.einsum("hij,hjk->hik", latter[0], earlier[0], precision=TOP_PRECISION),
        jnp.einsum("hij,hjk->hik", latter[0], earlier[1], precision=TOP_PRECISION) + latter[1],
    )


def to_pseudo(tensor, blocks, pseudo_rows):
    reordered = jnp.moveaxis(tensor, 1, 0)
    return reordered.reshape((reordered.shape[0], blocks, pseudo_rows) + reordered.shape[3:])


def block_terms(query_rows, key_rows, value_rows, beta_gate, log_gate, reset_flag):
    count, head_count, width = query_rows.shape
    substeps = key_rows.shape[2]
    blocks = count // BLOCK
    pseudo_rows = BLOCK * substeps
    query_blocks = jnp.transpose(query_rows.reshape(blocks, BLOCK, head_count, width), (2, 0, 1, 3))
    key_blocks = to_pseudo(key_rows, blocks, pseudo_rows)
    value_blocks = to_pseudo(value_rows, blocks, pseudo_rows)
    beta_blocks = to_pseudo(beta_gate, blocks, pseudo_rows)
    gate_steps = jnp.concatenate(
        [log_gate[:, :, None], jnp.zeros((count, head_count, substeps - 1), jnp.float32)], 2
    )
    gate_blocks = to_pseudo(gate_steps, blocks, pseudo_rows)
    reset_steps = jnp.concatenate(
        [reset_flag[:, None], jnp.zeros((count, substeps - 1), jnp.float32)], 1
    )
    reset_blocks = reset_steps.reshape(blocks, pseudo_rows)
    cumulative = jnp.cumsum(gate_blocks, axis=-1)
    segment = jnp.cumsum(reset_blocks, axis=-1)
    row_index = jnp.arange(pseudo_rows)
    causal_mask = row_index[:, None] >= row_index[None, :]
    strict_mask = row_index[:, None] > row_index[None, :]
    same_segment = segment[:, :, None] == segment[:, None, :]
    allowed = causal_mask & same_segment
    log_gap = cumulative[..., :, None] - cumulative[..., None, :]
    decay_ratio = jnp.where(allowed, jnp.exp(jnp.where(allowed, log_gap, 0.0)), 0.0)
    key_gram = jnp.einsum("hcik,hcjk->hcij", key_blocks, key_blocks, precision=TOP_PRECISION)
    lower_part = jnp.where(strict_mask, decay_ratio * key_gram * beta_blocks[..., :, None], 0.0)
    system = lower_part + jnp.eye(pseudo_rows, dtype=jnp.float32)
    alive_mask = (segment == 0).astype(jnp.float32)
    carry_gate = jnp.exp(cumulative) * alive_mask
    right_side = jnp.concatenate(
        [(beta_blocks * carry_gate)[..., None] * key_blocks, beta_blocks[..., None] * value_blocks],
        -1,
    )
    solved = jax.scipy.linalg.solve_triangular(system, right_side, lower=True, unit_diagonal=True)
    w_part = solved[..., :width]
    u_part = solved[..., width:]
    end_keys = decay_ratio[..., -1, :, None] * key_blocks
    end_gate = carry_gate[..., -1]
    query_ratio = decay_ratio[:, :, substeps - 1 :: substeps, :]
    query_mask = query_ratio * jnp.einsum(
        "hctk,hcjk->hctj", query_blocks, key_blocks, precision=TOP_PRECISION
    )
    query_gate = carry_gate[:, :, substeps - 1 :: substeps]
    return (w_part, u_part, end_keys, end_gate, query_mask, query_gate, query_blocks)


def device_map(terms):
    w_part, u_part, end_keys, end_gate = (terms[0], terms[1], terms[2], terms[3])
    width = w_part.shape[-1]
    square = jnp.eye(width, dtype=jnp.float32)
    maps_gain = end_gate[..., None, None] * square - jnp.einsum(
        "hcjk,hcjl->hckl", end_keys, w_part, precision=TOP_PRECISION
    )
    maps_shift = jnp.einsum("hcjk,hcjl->hckl", end_keys, u_part, precision=TOP_PRECISION)

    def absorb(composite, pieces):
        return (compose(composite, pieces), None)

    initial = (jnp.broadcast_to(square, maps_gain[:, 0].shape), jnp.zeros_like(maps_shift[:, 0]))
    composite, _ = lax.scan(
        absorb, initial, (jnp.moveaxis(maps_gain, 1, 0), jnp.moveaxis(maps_shift, 1, 0))
    )
    return composite


def run_blocks(current_state, terms):
    reordered = tuple((jnp.moveaxis(term, 1, 0) for term in terms))

    def advance(carried, pieces):
        w_part, u_part, end_keys, end_gate, query_mask, query_gate, query_blocks = pieces
        fresh_values = u_part - jnp.einsum("hjk,hkl->hjl", w_part, carried, precision=TOP_PRECISION)
        output = query_gate[..., None] * jnp.einsum(
            "htk,hkl->htl", query_blocks, carried, precision=TOP_PRECISION
        )
        output = output + jnp.einsum(
            "htj,hjl->htl", query_mask, fresh_values, precision=TOP_PRECISION
        )
        carried = end_gate[:, None, None] * carried + jnp.einsum(
            "hjk,hjl->hkl", end_keys, fresh_values, precision=TOP_PRECISION
        )
        return (carried, output)

    last_state, outputs = lax.scan(advance, current_state, reordered)
    blocks, head_count, block_len, width = outputs.shape
    return (
        jnp.transpose(outputs, (0, 2, 1, 3)).reshape(blocks * block_len, head_count, width),
        last_state,
    )


def per_device(
    activations,
    log_decay,
    doc_starts,
    query_weight,
    key_weight,
    value_weight,
    beta_weight,
    gate_weight,
    out_weight,
    query_taps,
    key_taps,
    value_taps,
    mixer_gain,
    head_gain,
    feed_gain,
    feed_gate,
    feed_up,
    feed_down,
    cotangent,
):
    gathered = (
        lax.all_gather(query_weight, "seq", axis=0, tiled=True),
        lax.all_gather(key_weight, "seq", axis=0, tiled=True),
        lax.all_gather(value_weight, "seq", axis=0, tiled=True),
        lax.all_gather(beta_weight, "seq", axis=0, tiled=True),
        lax.all_gather(gate_weight, "seq", axis=0, tiled=True),
        lax.all_gather(out_weight, "seq", axis=1, tiled=True),
        lax.all_gather(feed_gate, "seq", axis=0, tiled=True),
        lax.all_gather(feed_up, "seq", axis=0, tiled=True),
        lax.all_gather(feed_down, "seq", axis=1, tiled=True),
        lax.all_gather(mixer_gain, "seq", axis=0, tiled=True),
        lax.all_gather(feed_gain, "seq", axis=0, tiled=True),
    )
    (
        full_query,
        full_key,
        full_value,
        full_beta,
        full_gate,
        full_out,
        full_feed_gate,
        full_feed_up,
        full_feed_down,
        full_mixer_gain,
        full_feed_gain,
    ) = gathered
    count = activations.shape[0]
    tap_count = query_taps.shape[0]
    width = head_gain.shape[0]
    query_cols = full_query.shape[1]
    key_cols = full_key.shape[1]
    head_count = query_cols // width
    substeps = full_beta.shape[1] // head_count
    device_rank = lax.axis_index("seq")
    token_position = device_rank * count + jnp.arange(count, dtype=jnp.int32)
    own_doc = doc_number(token_position, doc_starts)
    same_doc = jnp.stack(
        [
            (
                (doc_number(token_position - offset, doc_starts) == own_doc)
                & (token_position >= offset)
            ).astype(jnp.float32)
            for offset in range(tap_count)
        ]
    )
    reset_flag = jnp.any(token_position[:, None] == doc_starts[None, :], axis=1).astype(jnp.float32)
    inputs = activations.astype(jnp.float32)
    gain_one = full_mixer_gain.astype(jnp.float32)
    normed = root_norm(inputs, gain_one).astype(jnp.bfloat16)
    raw_all = jnp.concatenate(
        [
            product(normed, full_query).astype(jnp.bfloat16),
            product(normed, full_key).astype(jnp.bfloat16),
            product(normed, full_value).astype(jnp.bfloat16),
        ],
        1,
    )
    beta_gate = jax.nn.sigmoid(product(normed, full_beta)).reshape(count, head_count, substeps)
    gate_view = product(normed, full_gate).reshape(count, head_count, width)
    taps_all = jnp.concatenate([query_taps, key_taps, value_taps], 1).astype(jnp.float32)
    previous = from_behind(raw_all[count - (tap_count - 1) :], "seq", 1)
    extended = jnp.concatenate([previous, raw_all], 0).astype(jnp.float32)
    conv_pre = short_conv(extended, taps_all, same_doc, count)
    conv_act = jax.nn.silu(conv_pre)
    query_act = conv_act[:, :query_cols].reshape(count, head_count, width)
    key_act = conv_act[:, query_cols : query_cols + key_cols].reshape(
        count, head_count, substeps, width
    )
    value_act = conv_act[:, query_cols + key_cols :].reshape(count, head_count, substeps, width)
    query_scale = lax.rsqrt(jnp.sum(query_act * query_act, axis=-1, keepdims=True) + UNIT_EPS)
    query_unit = query_act * query_scale
    query_rows = rounded(query_unit * width ** (-0.5))
    key_scale = lax.rsqrt(jnp.sum(key_act * key_act, axis=-1, keepdims=True) + UNIT_EPS)
    key_unit = key_act * key_scale
    key_rows = rounded(key_unit)
    value_rows = rounded(value_act)

    def make_terms(query_in, key_in, value_in, beta_in):
        return block_terms(query_in, key_in, value_in, beta_in, log_decay, reset_flag)

    terms, terms_pull = jax.vjp(make_terms, query_rows, key_rows, value_rows, beta_gate)
    state_map, state_offset = device_map(terms)
    eye_block = jnp.broadcast_to(jnp.eye(width, dtype=jnp.float32), state_map.shape)
    no_state = jnp.zeros_like(state_offset)
    _, state_in = entering((state_map, state_offset), "seq", compose, (eye_block, no_state))
    (mixer_out, _), run_pull = jax.vjp(run_blocks, state_in, terms)
    head_gain_f = head_gain.astype(jnp.float32)
    head_scale = lax.rsqrt(jnp.mean(mixer_out * mixer_out, axis=-1, keepdims=True) + NORM_EPS)
    head_unit = mixer_out * head_scale
    gate_act = jax.nn.silu(gate_view)
    heads_out = (head_unit * head_gain_f * gate_act).astype(jnp.bfloat16).reshape(count, query_cols)
    branch_one = lax.psum(product(heads_out, full_out), "head")
    hidden = inputs + branch_one
    gain_two = full_feed_gain.astype(jnp.float32)
    normed_ffn = root_norm(hidden, gain_two).astype(jnp.bfloat16)
    ffn_gate = product(normed_ffn, full_feed_gate)
    ffn_up = product(normed_ffn, full_feed_up)
    activation = (jax.nn.silu(ffn_gate) * ffn_up).astype(jnp.bfloat16)
    branch_two = lax.psum(product(activation, full_feed_down).astype(jnp.bfloat16), "head").astype(
        jnp.float32
    )
    result = hidden + branch_two
    half_width = result.shape[1] // lax.axis_size("head")
    head_rank = lax.axis_index("head")
    output = lax.dynamic_slice_in_dim(result, head_rank * half_width, half_width, 1).astype(
        jnp.bfloat16
    )
    weights_back = (
        lax.all_gather(query_weight, "seq", axis=0, tiled=True),
        lax.all_gather(key_weight, "seq", axis=0, tiled=True),
        lax.all_gather(value_weight, "seq", axis=0, tiled=True),
        lax.all_gather(beta_weight, "seq", axis=0, tiled=True),
        lax.all_gather(gate_weight, "seq", axis=0, tiled=True),
        lax.all_gather(out_weight, "seq", axis=1, tiled=True),
        lax.all_gather(feed_gate, "seq", axis=0, tiled=True),
        lax.all_gather(feed_up, "seq", axis=0, tiled=True),
        lax.all_gather(feed_down, "seq", axis=1, tiled=True),
        lax.all_gather(mixer_gain, "seq", axis=0, tiled=True),
        lax.all_gather(feed_gain, "seq", axis=0, tiled=True),
    )
    (
        back_query,
        back_key,
        back_value,
        back_beta,
        back_gate,
        back_out,
        back_feed_gate,
        back_feed_up,
        back_feed_down,
        back_mixer_gain,
        back_feed_gain,
    ) = weights_back
    gain_one = back_mixer_gain.astype(jnp.float32)
    gain_two = back_feed_gain.astype(jnp.float32)
    grad_result = cotangent.astype(jnp.float32)
    grad_feed_down = inner_rows(activation, cotangent)
    d_activation = times_transposed(cotangent, back_feed_down)
    d_up = (d_activation * jax.nn.silu(ffn_gate)).astype(jnp.bfloat16)
    d_gate = (d_activation * ffn_up * silu_slope(ffn_gate)).astype(jnp.bfloat16)
    grad_feed_gate = inner_rows(normed_ffn, d_gate)
    grad_feed_up = inner_rows(normed_ffn, d_up)
    d_normed_ffn = lax.psum(
        times_transposed(d_gate, back_feed_gate) + times_transposed(d_up, back_feed_up), "head"
    )
    d_hidden_norm, feed_terms = norm_back(hidden, gain_two, d_normed_ffn)
    grad_feed_gain = jnp.sum(feed_terms, axis=0)
    d_hidden = grad_result + d_hidden_norm
    grad_mixer = d_hidden.astype(jnp.bfloat16)
    grad_out = inner_rows(heads_out, grad_mixer)
    d_heads = times_transposed(grad_mixer, back_out).reshape(count, head_count, width)
    d_gate_logit = (
        (d_heads * head_unit * head_gain_f * silu_slope(gate_view))
        .astype(jnp.bfloat16)
        .reshape(count, query_cols)
    )
    d_mixer_out, head_terms = norm_back(mixer_out, head_gain_f, d_heads * gate_act)
    head_gain_part = jnp.sum(head_terms, axis=(0, 1))
    own_part = run_pull((d_mixer_out, no_state))[0]
    _, adjoint = carried_in(
        (jnp.swapaxes(state_map, 1, 2), own_part), "seq", compose, (eye_block, no_state)
    )
    _, d_terms = run_pull((d_mixer_out, adjoint))
    d_queries, d_key_rows, d_value_rows, d_beta = terms_pull(d_terms)
    d_query_act = (
        width ** (-0.5)
        * query_scale
        * (d_queries - query_unit * jnp.sum(d_queries * query_unit, axis=-1, keepdims=True))
    )
    d_key_act = key_scale * (
        d_key_rows - key_unit * jnp.sum(d_key_rows * key_unit, axis=-1, keepdims=True)
    )
    d_conv_act = jnp.concatenate(
        [
            d_query_act.reshape(count, query_cols),
            d_key_act.reshape(count, key_cols),
            d_value_rows.reshape(count, key_cols),
        ],
        1,
    )
    d_conv_pre = d_conv_act * silu_slope(conv_pre)
    tap_grads, d_extended = conv_back(extended, taps_all, same_doc, d_conv_pre)
    returned = from_behind(d_extended[: tap_count - 1], "seq", -1)
    d_raw = (
        d_extended[tap_count - 1 :] + jnp.pad(returned, ((count - (tap_count - 1), 0), (0, 0)))
    ).astype(jnp.bfloat16)
    d_raw_query = d_raw[:, :query_cols]
    d_raw_key = d_raw[:, query_cols : query_cols + key_cols]
    d_raw_value = d_raw[:, query_cols + key_cols :]
    d_beta_logit = (
        (d_beta * beta_gate * (1.0 - beta_gate))
        .reshape(count, head_count * substeps)
        .astype(jnp.bfloat16)
    )
    grad_query = inner_rows(normed, d_raw_query)
    grad_key = inner_rows(normed, d_raw_key)
    grad_value = inner_rows(normed, d_raw_value)
    grad_beta = inner_rows(normed, d_beta_logit)
    grad_gate = inner_rows(normed, d_gate_logit)
    d_normed_part = (
        times_transposed(d_raw_query, back_query)
        + times_transposed(d_raw_key, back_key)
        + times_transposed(d_raw_value, back_value)
    )
    d_normed_part = (
        d_normed_part
        + times_transposed(d_beta_logit, back_beta)
        + times_transposed(d_gate_logit, back_gate)
    )
    d_normed, head_gain_heads = (
        lax.psum(d_normed_part.astype(jnp.bfloat16), "head").astype(jnp.float32),
        lax.psum(head_gain_part.astype(jnp.bfloat16), "head").astype(jnp.float32),
    )
    d_input_norm, mixer_terms = norm_back(inputs, gain_one, d_normed)
    grad_mixer_gain = jnp.sum(mixer_terms, axis=0)
    d_input = d_hidden + d_input_norm
    grad_input = lax.dynamic_slice_in_dim(d_input, head_rank * half_width, half_width, 1)
    tap_total, grad_head_gain = lax.psum((tap_grads, head_gain_heads), "seq")
    every_grad = (
        lax.psum_scatter(grad_query, "seq", scatter_dimension=0, tiled=True),
        lax.psum_scatter(grad_key, "seq", scatter_dimension=0, tiled=True),
        lax.psum_scatter(grad_value, "seq", scatter_dimension=0, tiled=True),
        lax.psum_scatter(grad_beta, "seq", scatter_dimension=0, tiled=True),
        lax.psum_scatter(grad_gate, "seq", scatter_dimension=0, tiled=True),
        lax.psum_scatter(grad_out, "seq", scatter_dimension=1, tiled=True),
        lax.psum_scatter(grad_feed_gate, "seq", scatter_dimension=0, tiled=True),
        lax.psum_scatter(grad_feed_up, "seq", scatter_dimension=0, tiled=True),
        lax.psum_scatter(grad_feed_down, "seq", scatter_dimension=1, tiled=True),
        lax.psum_scatter(grad_mixer_gain, "seq", scatter_dimension=0, tiled=True),
        lax.psum_scatter(grad_feed_gain, "seq", scatter_dimension=0, tiled=True),
    )
    (
        sum_query,
        sum_key,
        sum_value,
        sum_beta,
        sum_gate,
        sum_out,
        sum_feed_gate,
        sum_feed_up,
        sum_feed_down,
        sum_mixer_gain,
        sum_feed_gain,
    ) = every_grad
    return (
        output,
        grad_input,
        sum_query,
        sum_key,
        sum_value,
        sum_beta,
        sum_gate,
        sum_out,
        tap_total[:, :query_cols],
        tap_total[:, query_cols : query_cols + key_cols],
        tap_total[:, query_cols + key_cols :],
        sum_mixer_gain,
        grad_head_gain,
        sum_feed_gain,
        sum_feed_gate,
        sum_feed_up,
        sum_feed_down,
    )


def solution(mesh):
    in_specs = (
        P("seq", None),
        P("seq", "head"),
        P(),
        P("seq", "head"),
        P("seq", "head"),
        P("seq", "head"),
        P("seq", "head"),
        P("seq", "head"),
        P("head", "seq"),
        P(None, "head"),
        P(None, "head"),
        P(None, "head"),
        P("seq"),
        P(),
        P("seq"),
        P("seq", "head"),
        P("seq", "head"),
        P("head", "seq"),
        P("seq", None),
    )
    out_specs = (
        P("seq", "head"),
        P("seq", "head"),
        P("seq", "head"),
        P("seq", "head"),
        P("seq", "head"),
        P("seq", "head"),
        P("seq", "head"),
        P("head", "seq"),
        P(None, "head"),
        P(None, "head"),
        P(None, "head"),
        P("seq"),
        P(),
        P("seq"),
        P("seq", "head"),
        P("seq", "head"),
        P("head", "seq"),
    )
    return jax.shard_map(
        per_device, mesh=mesh, in_specs=in_specs, out_specs=out_specs, check_vma=False
    )
```

profile of v0, /device:TPU:0, one launch (start us, length us, event | category | flops | bytes accessed | tf_op | source)
XLA Modules:
  0.0 3175.3 jit_solution(5908989879540584583)
XLA Ops:
  15.3 44.3 %all-reduce.14 = (bf16[1024]{0:T(1024)(128)(2,1)S(1)}, bf16[1024]{0:T(1024)(128)(2,1)}) all-reduce(bf16[1024]{0:T(1024)(128)(2,1)S(1)} %dynamic-update-slice, bf16[1024]{0:T(1024)(128)(2,1)S(1)} %dynamic-update-slice.1), channel_id=1, replica_groups=mesh['seq'=16,'head'=2] {'seq'}, use_global_device_ids=true, to_apply=%add.9 | all-reduce | flops 2048 | bytes 8192
  59.6 36.0 %all-gather.4 = bf16[16,64,8]{1,2,0:T(8,128)(2,1)S(1)} all-gather(bf16[1,64,8]{1,2,0:T(8,128)(2,1)} %bitcast.533), channel_id=1, replica_groups=mesh['seq'=16,'head'=2] {'seq'}, dimensions={0}, use_global_device_ids=true | all-gather | bytes 17408 | tf_op jit(solution)/shard_map/all_gather | solution.py:258
  109.9 21.4 all-gather.22.cloned.1.call-done
  136.9 56.7 %all-gather.20.cloned.1.call-done = bf16[1024,1024]{1,0:T(8,128)(2,1)} async-done(((bf16[64,1024]{1,0:T(8,128)(2,1)}), bf16[1024,1024]{1,0:T(8,128)(2,1)}) %all-gather.20.cloned.1.call-update) | async-done | bytes 2097168 | tf_op jit(solution)/shard_map/all_gather | solution.py:256
  216.9 22.8 fusion.107
  273.7 630.2 %custom-call.10 = f32[4,16,1,128,128]{3,4,2,1,0:T(8,128)} custom-call(f32[4,16,1,128,128]{4,3,2,1,0:T(8,128)} %get-tuple-element.1411), custom_call_target="InvertDiagBlocksLowerTriangular" | custom-call | tf_op jit(solution)/shard_map/jvp(jit(_solve_triangular))/vmap(vmap())/triangular_solve | solution.py:176
  939.8 45.9 %while.104 = (s32[]{:T(128)}, f32[4,128,128]{2,1,0:T(8,128)S(1)}, f32[4,128,128]{2,1,0:T(8,128)S(1)}, f32[16,4,128,128]{3,2,0,1:T(8,128)}, f32[16,4,128,128]{3,2,0,1:T(8,128)}, /*index=5*/s32[]{:T(128)}, s32[]{:T(128)}) while((s32[]{:T(128)}, f32[4,128,128]{2,1,0:T(8,128)S(1)}, f32[4,128,128]{2,1,0:T(8,128)S(1)}, ...), condition=%wide.region_10.11_spmd.clone, body=%wide.region_9.10_spmd.clone.sunk | while | flops 201457664 | bytes 2885207 | solution.py:202
  1021.9 41.3 %all-gather.34.cloned.1.call-done = f32[64,128,128]{2,1,0:T(8,128)} async-done(((f32[4,128,128]{2,1,0:T(8,128)}), f32[64,128,128]{2,1,0:T(8,128)}) %all-gather.34.cloned.1.call-update) | async-done | bytes 4194320 | tf_op jit(solution)/shard_map/all_gather | solution.py:22
  1063.3 77.9 %all-gather.36.cloned.1.call-done = f32[64,128,128]{2,1,0:T(8,128)} async-done(((f32[4,128,128]{2,1,0:T(8,128)}), f32[64,128,128]{2,1,0:T(8,128)}) %all-gather.36.cloned.1.call-update) | async-done | bytes 4194320 | tf_op jit(solution)/shard_map/all_gather | solution.py:22
  1141.2 22.2 while.105
  1168.5 115.4 %while.102 = (s32[]{:T(128)}, f32[4,128,128]{2,1,0:T(8,128)S(1)}, f32[16,4,64,128]{3,1,2,0:T(4,128)S(1)}, f32[16,4,128,128]{3,2,1,0:T(8,128)}, f32[16,4,64,1]{2,...) while((s32[]{:T(128)}, f32[4,128,128]{2,1,0:T(8,128)S(1)}, ...), condition=%wide.region_15.16_spmd, body=%wide.region_14.15_spmd.sunk | while | flops 302252032 | bytes 4336849 | solution.py:225
  1302.8 24.7 all-reduce.20.cloned.1.call-done
  1334.7 63.0 %all-gather.28.cloned.1.call-done = bf16[1024,1408]{1,0:T(8,128)(2,1)} async-done(((bf16[64,1408]{1,0:T(8,128)(2,1)}), bf16[1024,1408]{1,0:T(8,128)(2,1)}) %all-gather.28.cloned.1.call-update) | async-done | bytes 2883600 | tf_op jit(solution)/shard_map/all_gather | solution.py:261
  1406.1 59.5 %all-gather.30.cloned.1.call-done = bf16[1024,1408]{1,0:T(8,128)(2,1)} async-done(((bf16[64,1408]{1,0:T(8,128)(2,1)}), bf16[1024,1408]{1,0:T(8,128)(2,1)}) %all-gather.30.cloned.1.call-update) | async-done | bytes 2883600 | tf_op jit(solution)/shard_map/all_gather | solution.py:262
  1473.9 59.8 %all-gather.32.cloned.1.call-done = bf16[1408,1024]{0,1:T(8,128)(2,1)} async-done(((bf16[1408,64]{0,1:T(8,128)(2,1)}), bf16[1408,1024]{0,1:T(8,128)(2,1)}) %all-gather.32.cloned.1.call-update) | async-done | bytes 2883600 | tf_op jit(solution)/shard_map/all_gather | solution.py:263
  1612.1 93.6 %while.106 = (s32[]{:T(128)}, f32[4,128,128]{2,1,0:T(8,128)S(1)}, f32[16,4,1,1]{1,3,2,0:T(1,128)S(1)}, f32[16,4,64,128]{3,2,1,0:T(8,128)}, f32[16,4,64,1]{2,1,3,...) while((s32[]{:T(128)}, f32[4,128,128]{2,1,0:T(8,128)S(1)}, ...), condition=%wide.region_24.25_spmd.clone, body=%wide.region_23.24_spmd.clone.sunk | while | flops 302481408 | bytes 3415227 | solution.py:225
  1727.6 40.9 %all-gather.40.cloned.1.call-done = bf16[64,128,128]{2,1,0:T(8,128)(2,1)} async-done(((bf16[4,128,128]{2,1,0:T(8,128)(2,1)}), bf16[64,128,128]{2,1,0:T(8,128)(2,1)}) %all-gather.40.cloned.1.call-update) | async-done | bytes 2097168 | tf_op jit(solution)/shard_map/all_gather | solution.py:37
  1768.5 21.2 while.107
  1799.1 244.6 %while.103 = (s32[]{:T(128)}, f32[4,128,128]{2,1,0:T(8,128)S(1)}, f32[16,4,128,128]{3,2,1,0:T(8,128)}, f32[16,4,128,128]{3,2,1,0:T(8,128)}, f32[16,4,128,128]{3,...) while((s32[]{:T(128)}, f32[4,128,128]{2,1,0:T(8,128)S(1)}, ...), condition=%wide.region_28.29_spmd, body=%wide.region_27.28_spmd.sunk | while | flops 604438528 | bytes 6303473 | solution.py:225
  2045.1 16.3 fusion.112
  2160.6 28.1 multiply_reduce_fusion.3
  2188.7 14.7 multiply_multiply_fusion.3
  2206.3 19.2 pad_add_fusion
  2317.5 22.3 all-reduce.24.cloned.1.call-done
  2346.1 77.4 %all-reduce.13 = (f32[4,2560]{1,0:T(4,128)S(1)}, f32[1024]{0:T(1024)S(1)}, f32[128]{0:T(128)}, f32[1024]{0:T(1024)S(1)}) all-reduce(f32[4,2560]{1,0:T(4,128)S(1)} %pad_maximum_fusion.2, f32[1024]{0:T(1024)S(1)} %get-tuple-element.1257, bf16[128]{0:T(256)(128)(2,1)S(1)} %psum.54, ...), channel_id=1, replica_groups=mesh['seq'=16,'head'=2] {'seq'}, use_global_device_ids=true, to_apply=%region_46.47 | all-reduce | flops 12416 | bytes 99072 | tf_op jit(solution)/shard_map/psum | solution.py:471
  2433.1 72.0 %reduce-scatter.18.cloned.1.call-done = f32[64,512]{1,0:T(8,128)} async-done(((f32[1024,512]{1,0:T(8,128)}), f32[64,512]{1,0:T(8,128)}) %reduce-scatter.18.cloned.1.call-update) | async-done | bytes 131088 | tf_op jit(solution)/shard_map/reduce_scatter | solution.py:477
  2505.0 126.1 %reduce-scatter.22.cloned.1.call-done = f32[64,1408]{1,0:T(8,128)} async-done(((f32[1024,1408]{1,0:T(8,128)}), f32[64,1408]{1,0:T(8,128)}) %reduce-scatter.22.cloned.1.call-update) | async-done | bytes 360464 | tf_op jit(solution)/shard_map/reduce_scatter | solution.py:479
  2631.1 129.7 %reduce-scatter.24.cloned.1.call-done = f32[64,1408]{1,0:T(8,128)} async-done(((f32[1024,1408]{1,0:T(8,128)}), f32[64,1408]{1,0:T(8,128)}) %reduce-scatter.24.cloned.1.call-update) | async-done | bytes 360464 | tf_op jit(solution)/shard_map/reduce_scatter | solution.py:480
  2760.9 129.9 %reduce-scatter.26.cloned.1.call-done = f32[1408,64]{0,1:T(8,128)} async-done(((f32[1408,1024]{0,1:T(8,128)}), f32[1408,64]{0,1:T(8,128)}) %reduce-scatter.26.cloned.1.call-update) | async-done | bytes 360464 | tf_op jit(solution)/shard_map/reduce_scatter | solution.py:481
  2890.8 84.2 %reduce-scatter.12.cloned.1.call-done = f32[64,512]{1,0:T(8,128)} async-done(((f32[1024,512]{1,0:T(8,128)}), f32[64,512]{1,0:T(8,128)}) %reduce-scatter.12.cloned.1.call-update) | async-done | bytes 131088 | tf_op jit(solution)/shard_map/reduce_scatter | solution.py:473
  2975.0 95.6 %reduce-scatter.14.cloned.1.call-done = f32[64,1024]{1,0:T(8,128)} async-done(((f32[1024,1024]{1,0:T(8,128)}), f32[64,1024]{1,0:T(8,128)}) %reduce-scatter.14.cloned.1.call-update) | async-done | bytes 262160 | tf_op jit(solution)/shard_map/reduce_scatter | solution.py:474
  3070.6 97.4 %reduce-scatter.16.cloned.1.call-done = f32[64,1024]{1,0:T(8,128)} async-done(((f32[1024,1024]{1,0:T(8,128)}), f32[64,1024]{1,0:T(8,128)}) %reduce-scatter.16.cloned.1.call-update) | async-done | bytes 262160 | tf_op jit(solution)/shard_map/reduce_scatter | solution.py:475
  (1019 shorter events, 1061.1 us)
Async XLA Ops:
  7.2 100.1 %all-gather.18.cloned.1.call-start = ((), (), s32[]{:S(2)}) async-start(), calls=%async_computation.9 | async-start | bytes 1114112 | tf_op jit(solution)/shard_map/all_gather | solution.py:255
  7.9 123.4 %all-gather.22.cloned.1.call-start = ((), (), s32[]{:S(2)}) async-start(), calls=%async_computation.11 | async-start | bytes 2228224 | tf_op jit(solution)/shard_map/all_gather | solution.py:257
  8.7 184.9 %all-gather.20.cloned.1.call-start = ((), (), s32[]{:S(2)}) async-start(), calls=%async_computation.10 | async-start | bytes 2228224 | tf_op jit(solution)/shard_map/all_gather | solution.py:256
  9.4 1053.9 %all-gather.34.cloned.1.call-start = ((), (), s32[]{:S(2)}) async-start(), calls=%async_computation.27 | async-start | bytes 4456448 | tf_op jit(solution)/shard_map/all_gather | solution.py:22
  11.6 182.0 %copy-start.80 = (f32[1024]{0:T(1024)}, f32[1024]{0:T(1024)S(1)}, u32[]{:S(2)}) copy-start(f32[1024]{0:T(1024)S(1)} %add_rsqrt_fusion.4) | copy-start | bytes 12292
  105.5 158.3 %copy-start.65 = (pred[128,128]{1,0:T(8,128)(4,1)}, pred[128,128]{1,0:T(8,128)(4,1)S(1)}, u32[]{:S(2)}) copy-start(pred[128,128]{1,0:T(8,128)(4,1)S(1)} %get-tuple-element.1434) | copy-start | bytes 49156
  201.7 4.6 collective-permute-start
  205.0 724.4 %copy-start.95 = (f32[4,16]{1,0:T(4,128)}, f32[4,16]{1,0:T(4,128)S(1)}, u32[]{:S(2)}) copy-start(f32[4,16]{1,0:T(4,128)S(1)} %slice_reduce_fusion) | copy-start | bytes 772
  262.2 755.1 %copy-start = (bf16[4,1024,2,128]{3,2,1,0:T(2,128)(2,1)}, bf16[4,1024,2,128]{3,2,1,0:T(2,128)(2,1)S(1)}, u32[]{:S(2)}) copy-start(bf16[4,1024,2,128]{3,2,1,0:T(2,128)(2,1)S(1)} %copy.429) | copy-start | bytes 6291460
  266.4 637.5 %copy-start.58 = (f32[4,16,128]{2,1,0:T(8,128)S(1)}, f32[4,16,128]{2,1,0:T(8,128)}, u32[]{:S(2)}) copy-start(f32[4,16,128]{2,1,0:T(8,128)} %get-tuple-element.1386) | copy-start | bytes 98308
  273.7 655.8 %copy-start.51 = (f32[4,16,1,128]{3,2,1,0:T(1,128)}, f32[4,16,1,128]{3,2,1,0:T(1,128)S(1)}, u32[]{:S(2)}) copy-start(f32[4,16,1,128]{3,2,1,0:T(1,128)S(1)} %slice.132) | copy-start | bytes 98308
  986.4 154.7 %all-gather.36.cloned.1.call-start = ((), (), s32[]{:S(2)}) async-start(), calls=%async_computation.28 | async-start | bytes 4456448 | tf_op jit(solution)/shard_map/all_gather | solution.py:22
  987.0 302.7 %all-gather.24.cloned.1.call-start = ((), (), s32[]{:S(2)}) async-start(), calls=%async_computation.12 | async-start | bytes 1114112 | tf_op jit(solution)/shard_map/all_gather | solution.py:259
  987.6 307.7 %all-gather.26.cloned.1.call-start = ((), (), s32[]{:S(2)}) async-start(), calls=%async_computation.13 | async-start | bytes 1114112 | tf_op jit(solution)/shard_map/all_gather | solution.py:260
  988.4 339.1 %all-reduce.20.cloned.1.call-start = ((), (), s32[]{:S(2)}) async-start(), calls=%async_computation.14 | async-start | bytes 8388608 | tf_op jit(solution)/shard_map/psum | solution.py:345
  1300.2 97.5 %all-gather.28.cloned.1.call-start = ((), (), s32[]{:S(2)}) async-start(), calls=%async_computation.15 | async-start | bytes 3063808 | tf_op jit(solution)/shard_map/all_gather | solution.py:261
  1301.0 164.7 %all-gather.30.cloned.1.call-start = ((), (), s32[]{:S(2)}) async-start(), calls=%async_computation.16 | async-start | bytes 3063808 | tf_op jit(solution)/shard_map/all_gather | solution.py:262
  1301.6 232.2 %all-gather.32.cloned.1.call-start = ((), (), s32[]{:S(2)}) async-start(), calls=%async_computation.17 | async-start | bytes 3063808 | tf_op jit(solution)/shard_map/all_gather | solution.py:263
  1302.3 279.2 %all-reduce.22.cloned.1.call-start = ((), (), s32[]{:S(2)}) async-start(), calls=%async_computation.18 | async-start | bytes 8388608 | tf_op jit(solution)/shard_map/psum | solution.py:396
  1553.9 173.7 %all-gather.38.cloned.1.call-start = ((), (), s32[]{:S(2)}) async-start(), calls=%async_computation.29 | async-start | bytes 2228224 | tf_op jit(solution)/shard_map/all_gather | solution.py:37
  1564.9 203.6 %all-gather.40.cloned.1.call-start = ((), (), s32[]{:S(2)}) async-start(), calls=%async_computation.30 | async-start | bytes 2228224 | tf_op jit(solution)/shard_map/all_gather | solution.py:37
  1707.1 609.0 %reduce-scatter.28.cloned.1.call-start = ((), (), s32[]{:S(2)}) async-start(), calls=%async_computation.31 | async-start | bytes 557056
  2225.9 8.7 collective-permute-start.1
  2234.4 105.5 %all-reduce.24.cloned.1.call-start = ((), (), s32[]{:S(2)}) async-start(), calls=%async_computation.32 | async-start | bytes 8388608 | tf_op jit(solution)/shard_map/psum | solution.py:352
  2259.8 173.3 %reduce-scatter.20.cloned.1.call-start = ((), (), s32[]{:S(2)}) async-start(), calls=%async_computation.23 | async-start | bytes 2228224 | tf_op jit(solution)/shard_map/reduce_scatter | solution.py:478
  2265.8 239.2 %reduce-scatter.18.cloned.1.call-start = ((), (), s32[]{:S(2)}) async-start(), calls=%async_computation.22 | async-start | bytes 2228224 | tf_op jit(solution)/shard_map/reduce_scatter | solution.py:477
  2270.0 361.1 %reduce-scatter.22.cloned.1.call-start = ((), (), s32[]{:S(2)}) async-start(), calls=%async_computation.24 | async-start | bytes 6127616 | tf_op jit(solution)/shard_map/reduce_scatter | solution.py:479
  2278.8 482.1 %reduce-scatter.24.cloned.1.call-start = ((), (), s32[]{:S(2)}) async-start(), calls=%async_computation.25 | async-start | bytes 6127616 | tf_op jit(solution)/shard_map/reduce_scatter | solution.py:480
  2287.2 603.6 %reduce-scatter.26.cloned.1.call-start = ((), (), s32[]{:S(2)}) async-start(), calls=%async_computation.26 | async-start | bytes 6127616 | tf_op jit(solution)/shard_map/reduce_scatter | solution.py:481
  2295.7 679.3 %reduce-scatter.12.cloned.1.call-start = ((), (), s32[]{:S(2)}) async-start(), calls=%async_computation.19 | async-start | bytes 2228224 | tf_op jit(solution)/shard_map/reduce_scatter | solution.py:473
  2299.9 770.7 %reduce-scatter.14.cloned.1.call-start = ((), (), s32[]{:S(2)}) async-start(), calls=%async_computation.20 | async-start | bytes 4456448 | tf_op jit(solution)/shard_map/reduce_scatter | solution.py:474
  2306.4 861.7 %reduce-scatter.16.cloned.1.call-start = ((), (), s32[]{:S(2)}) async-start(), calls=%async_computation.21 | async-start | bytes 4456448 | tf_op jit(solution)/shard_map/reduce_scatter | solution.py:475
  (106 other events, 1529.4 us)
Sparse Core Ops, SparseCore 0:
  10.8 58.1 all-gather.17
  71.8 59.5 all-gather.21
  134.1 59.3 all-gather.19
  986.6 76.6 all-gather.33
  1066.5 74.6 all-gather.35
  1143.8 53.8 all-gather.23
  1200.5 54.1 all-gather.25
  1300.4 27.0 all-reduce.19
  1330.6 67.0 all-gather.27
  1400.7 64.9 all-gather.29
  1468.8 64.9 all-gather.31
  1554.0 27.4 all-reduce.21
  1584.8 61.9 all-gather.37
  1706.6 61.8 all-gather.39
  2234.5 77.2 reduce-scatter.27
  2314.9 24.8 all-reduce.23
  2342.5 81.6 reduce-scatter.19
  2426.9 78.0 reduce-scatter.17
  2507.9 123.1 reduce-scatter.21
  2633.9 126.9 reduce-scatter.23
  2763.8 126.9 reduce-scatter.25
  2893.6 81.3 reduce-scatter.11
  2977.9 92.6 reduce-scatter.13
  3073.3 94.6 reduce-scatter.15
where the time goes:
time: 3190 us; the launch traced here: 3180 us
  waiting for transfers between devices  1220 us (38%)
  other arithmetic  819 us (26%)
  matrix products  776 us (24%)
  local copies, waits for them, and re-layouts  175 us (5%)
  blocking collectives  160 us (5%)
    another operation x2, other arithmetic, block_terms(): jax.scipy.linalg.solve_triangular(system, right_side, lower=True, unit_di...  630 us
    reduce_scatter x1, waiting for transfers between devices, per_device(): lax.psum_scatter(grad_feed_down, 'seq', scatter_dimension=1, tiled=True)  130 us
    reduce_scatter x1, waiting for transfers between devices, per_device(): lax.psum_scatter(grad_feed_up, 'seq', scatter_dimension=0, tiled=True)  130 us
    reduce_scatter x1, waiting for transfers between devices, per_device(): lax.psum_scatter(grad_feed_gate, 'seq', scatter_dimension=0, tiled=True)  126 us
    all_gather x2, waiting for transfers between devices, entering(): pieces = jax.tree.map(lambda part: lax.all_gather(part, axis), value)  119 us
    dot_general x64, matrix products, advance(): jnp.einsum('hjk,hkl->hjl', w_part, carried, precision=TOP_PRECISION)  115 us
    dot_general x64, matrix products, advance(): jnp.einsum('htk,hkl->htl', query_blocks, carried, precision=TOP_PRECISION)  109 us
    dot_general x64, matrix products, advance(): jnp.einsum('htj,hjl->htl', query_mask, fresh_values, precision=TOP_PRECIS...  107 us
  transfers between devices with their start and end apart: 26, of which 19 were waited for; matrix products, arithmetic and copies ran while one was open for 16% of the time, Pallas kernels for 0%

commit v1 on v0

v1 whole, which is shorter than its diff:
```python
import functools

import jax
import jax.numpy as jnp
from jax import lax
from jax.experimental import pallas as pl
from jax.experimental.pallas import tpu as pltpu
from jax.sharding import PartitionSpec as P

BLOCK = 64
RESET = 256.0
HALO = 16
NORM_EPS = 1e-05
UNIT_EPS = 1e-06
F32 = jnp.float32
BF16 = jnp.bfloat16


def product(former, latter):
    return jnp.dot(former, latter, preferred_element_type=F32)


def inner_rows(former, latter):
    return lax.dot_general(former, latter, (((0,), (0,)), ((), ())), preferred_element_type=F32)


def times_transposed(former, latter):
    return lax.dot_general(former, latter, (((1,), (1,)), ((), ())), preferred_element_type=F32)


def low(values):
    return values.astype(BF16)


def split(values):
    high = values.astype(BF16)
    return high, (values - high.astype(F32)).astype(BF16)


def fine(form, former, latter):
    a_high, a_low = split(former)
    b_high, b_low = split(latter)
    return form(a_high, b_high) + (form(a_low, b_high) + form(a_high, b_low))


def silu_slope(values, sigma):
    return sigma * (1.0 + values * (1.0 - sigma))


def norm_back(values, gain_vector, gradient):
    row_scale = lax.rsqrt(jnp.mean(values * values, axis=-1, keepdims=True) + NORM_EPS)
    unit_value = values * row_scale
    scaled_grad = gradient * gain_vector
    back_value = row_scale * (
        scaled_grad - unit_value * jnp.mean(scaled_grad * unit_value, axis=-1, keepdims=True)
    )
    return (back_value, gradient * unit_value)


def row_maps(rows):
    row = lax.broadcasted_iota(jnp.int32, (rows, rows), 0)
    col = lax.broadcasted_iota(jnp.int32, (rows, rows), 1)
    return row % BLOCK, col % BLOCK, row // BLOCK, col // BLOCK


def lower_inverse(system, row_token, col_token, same_token):
    rows = system.shape[0]
    row = lax.broadcasted_iota(jnp.int32, (rows, rows), 0)
    col = lax.broadcasted_iota(jnp.int32, (rows, rows), 1)
    inverse = jnp.where(row == col, 1.0, 0.0) - jnp.where(same_token, system, 0.0)
    size = 1
    while size < BLOCK:
        joins = (
            (row_token // (2 * size) == col_token // (2 * size))
            & ((row_token // size) % 2 == 1)
            & ((col_token // size) % 2 == 0)
        )
        joint = jnp.where(joins, system, 0.0)
        low_inverse = low(inverse)
        inverse = inverse - product(low(product(low_inverse, low(joint))), low_inverse)
        size *= 2
    residual = jnp.where(row == col, 1.0, 0.0) - inverse - fine(product, system, inverse)
    return inverse + product(low(inverse), low(residual))


def conv_rows(tile, halo, taps, same, columns):
    count = tile.shape[0]
    extended = jnp.concatenate([halo, tile], 0)
    windows = [tile] + [
        pltpu.roll(extended, offset, 0)[8:] for offset in range(1, taps.shape[0])
    ]
    outcome = tile * taps[0:1]
    for offset in range(1, taps.shape[0]):
        outcome = outcome + windows[offset] * taps[offset : offset + 1] * same[:, offset : offset + 1]
    return outcome, windows


def unit_scale(values):
    return lax.rsqrt(jnp.sum(values * values, axis=-1, keepdims=True) + UNIT_EPS)


def pieces_of(head, head_count, substeps, width):
    query = [(head * width, width)]
    keys = [((head_count + head * substeps + n) * width, width) for n in range(substeps)]
    values = [
        ((head_count + (head_count + head) * substeps + n) * width, width) for n in range(substeps)
    ]
    return query + keys + values


def forward_kernel(
    head_count, substeps, width,
    raw, before, edge, taps, same, beta, cum_col, cum_row,
    t_out, p_out, s_out, qtil_out, local_out, map_out, shift_out,
    chain,
):
    chunk = pl.program_id(0)
    rows = BLOCK * substeps
    row_token, col_token, row_step, col_step = row_maps(rows)
    upto = col_token <= row_token
    earlier = (col_token < row_token) | ((col_token == row_token) & (col_step < row_step))
    same_token = (col_token == row_token) & (col_step < row_step)
    eye = jnp.where(
        lax.broadcasted_iota(jnp.int32, (width, width), 0)
        == lax.broadcasted_iota(jnp.int32, (width, width), 1),
        1.0,
        0.0,
    )
    same_rows = same[...]

    @pl.when(chunk == 0)
    def _():
        for head in range(head_count):
            chain[head, :, :width] = eye
            chain[head, :, width:] = jnp.zeros((width, width), F32)

    for head in range(head_count):
        acts = []
        for start, size in pieces_of(head, head_count, substeps, width):
            tile = raw[:, start : start + size].astype(F32)
            halo = jnp.where(
                chunk == 0, edge[:, start : start + size], before[:, start : start + size]
            ).astype(F32)[HALO - 8 :]
            pre, _ = conv_rows(tile, halo, taps[:, start : start + size], same_rows, None)
            acts.append(pre * jax.nn.sigmoid(pre))
        query = low(acts[0] * unit_scale(acts[0]) * width ** (-0.5))
        key = low(jnp.concatenate([a * unit_scale(a) for a in acts[1 : 1 + substeps]], 0))
        value = low(jnp.concatenate(acts[1 + substeps :], 0))
        beta_col = jnp.concatenate(
            [beta[:, head * substeps + n : head * substeps + n + 1] for n in range(substeps)], 0
        )
        cum_token = cum_col[:, head : head + 1]
        cum_rows = jnp.concatenate([cum_token] * substeps, 0)
        cum_cols = cum_row[0, head : head + 1, :]
        last = cum_cols[:, BLOCK - 1 : BLOCK]
        ratio = jnp.exp(jnp.where(upto, cum_rows - cum_cols, -1e4))
        gram = times_transposed(key, key)
        system = jnp.where(earlier, beta_col * ratio * gram, 0.0)
        inverse = low(lower_inverse(system, row_token, col_token, same_token))
        t_out[0, head] = inverse
        carry = jnp.exp(cum_rows)
        key_f = key.astype(F32)
        right = jnp.concatenate(
            [low(beta_col * carry * key_f), low(beta_col * value.astype(F32))], 1
        )
        solved = product(inverse, right)
        solved_low = low(solved)
        end_keys = low(jnp.exp(last - cum_rows) * key_f)
        moved = inner_rows(end_keys, solved_low)
        query_mask = low(ratio[:BLOCK] * times_transposed(query, key))
        seen = product(query_mask, solved_low)
        query_eff = jnp.exp(cum_token) * query.astype(F32) - seen[:, :width]
        chained = chain[head]
        chained_low = low(chained)
        p_out[0, head] = chained_low[:, :width]
        s_out[0, head] = chained_low[:, width:]
        reach = product(low(query_eff), chained_low)
        qtil_out[:, head * width : (head + 1) * width] = low(reach[:, :width])
        local_out[:, head * width : (head + 1) * width] = reach[:, width:] + seen[:, width:]
        step_map = jnp.exp(last) * eye - moved[:, :width]
        new = fine(product, step_map, chained)
        new = jnp.concatenate([new[:, :width], new[:, width:] + moved[:, width:]], 1)
        chain[head] = new
        map_out[head] = new[:, :width]
        shift_out[head] = new[:, width:]


def run_forward(raw, edge, taps, same, beta, cum_col, cum_row, head_count, substeps, width):
    count, columns = raw.shape
    chunks = count // BLOCK
    rows = BLOCK * substeps
    per_halo = BLOCK // HALO
    whole = lambda *shape: pl.BlockSpec(shape, lambda c: (0,) * len(shape))
    tokens = lambda cols: pl.BlockSpec((BLOCK, cols), lambda c: (c, 0))
    square = pl.BlockSpec((1, head_count, width, width), lambda c: (c, 0, 0, 0))
    return pl.pallas_call(
        functools.partial(forward_kernel, head_count, substeps, width),
        grid=(chunks,),
        in_specs=[
            tokens(columns),
            pl.BlockSpec((HALO, columns), lambda c: (jnp.maximum(c * per_halo - 1, 0), 0)),
            whole(HALO, columns),
            whole(*taps.shape),
            tokens(same.shape[1]),
            tokens(beta.shape[1]),
            tokens(head_count),
            pl.BlockSpec((1, head_count, rows), lambda c: (c, 0, 0)),
        ],
        out_specs=[
            pl.BlockSpec((1, head_count, rows, rows), lambda c: (c, 0, 0, 0)),
            square,
            square,
            tokens(head_count * width),
            tokens(head_count * width),
            whole(head_count, width, width),
            whole(head_count, width, width),
        ],
        out_shape=[
            jax.ShapeDtypeStruct((chunks, head_count, rows, rows), BF16),
            jax.ShapeDtypeStruct((chunks, head_count, width, width), BF16),
            jax.ShapeDtypeStruct((chunks, head_count, width, width), BF16),
            jax.ShapeDtypeStruct((count, head_count * width), BF16),
            jax.ShapeDtypeStruct((count, head_count * width), F32),
            jax.ShapeDtypeStruct((head_count, width, width), F32),
            jax.ShapeDtypeStruct((head_count, width, width), F32),
        ],
        scratch_shapes=[pltpu.VMEM((head_count, width, 2 * width), F32)],
        compiler_params=pltpu.CompilerParams(
            dimension_semantics=("arbitrary",), vmem_limit_bytes=48 * 1024 * 1024
        ),
        name="mixer_forward",
    )(raw, raw, edge, taps, same, beta, cum_col, cum_row)


def backward_kernel(
    head_count, substeps, width,
    raw, before, edge, taps, same, same_next, beta, cum_col, cum_row,
    t_in, p_in, s_in, state_in, adjoint_in, d_out,
    d_raw, d_logit, tail_out, first_out, tap_out,
    adjoint, carried,
):
    step = pl.program_id(0)
    chunks = pl.num_programs(0)
    chunk = chunks - 1 - step
    rows = BLOCK * substeps
    tap_count = 4
    row_token, col_token, row_step, col_step = row_maps(rows)
    upto = col_token <= row_token
    earlier = (col_token < row_token) | ((col_token == row_token) & (col_step < row_step))
    same_rows = same[...]
    same_long = jnp.concatenate([same_rows, same_next[...]], 0)

    @pl.when(step == 0)
    def _():
        adjoint[...] = adjoint_in[...]
        carried[...] = jnp.zeros(carried.shape, F32)
        tap_out[...] = jnp.zeros(tap_out.shape, F32)

    logit_cols = []
    for head in range(head_count):
        pieces = pieces_of(head, head_count, substeps, width)
        pres, windows, acts, sigmas = [], [], [], []
        for start, size in pieces:
            tile = raw[:, start : start + size].astype(F32)
            halo = jnp.where(
                chunk == 0, edge[:, start : start + size], before[:, start : start + size]
            ).astype(F32)[HALO - 8 :]
            pre, window = conv_rows(tile, halo, taps[:, start : start + size], same_rows, None)
            sigma = jax.nn.sigmoid(pre)
            pres.append(pre)
            windows.append(window)
            sigmas.append(sigma)
            acts.append(pre * sigma)
        scales = [unit_scale(a) for a in acts[: 1 + substeps]]
        units = [a * s for a, s in zip(acts[: 1 + substeps], scales)]
        query = low(units[0] * width ** (-0.5))
        key = low(jnp.concatenate(units[1:], 0))
        value = low(jnp.concatenate(acts[1 + substeps :], 0)).astype(F32)
        key_f = key.astype(F32)
        beta_col = jnp.concatenate(
            [beta[:, head * substeps + n : head * substeps + n + 1] for n in range(substeps)], 0
        )
        cum_token = cum_col[:, head : head + 1]
        cum_rows = jnp.concatenate([cum_token] * substeps, 0)
        cum_cols = cum_row[0, head : head + 1, :]
        last = cum_cols[:, BLOCK - 1 : BLOCK]
        ratio = jnp.exp(jnp.where(upto, cum_rows - cum_cols, -1e4))
        carry = jnp.exp(cum_rows)
        carry_token = jnp.exp(cum_token)
        end_ratio = jnp.exp(last - cum_rows)
        inverse = t_in[0, head]
        state = low(s_in[0, head].astype(F32) + product(p_in[0, head], state_in[head]))
        gram = times_transposed(key, key)
        fresh = value - carry * product(key, state)
        update = product(inverse, low(beta_col * fresh))
        update_low = low(update)
        d_mix = d_out[:, head * width : (head + 1) * width]
        later = adjoint[head]
        later_low = low(later)
        query_mask = low(ratio[:BLOCK] * times_transposed(query, key))
        d_update = inner_rows(query_mask, d_mix) + product(low(end_ratio * key_f), later_low)
        d_right = inner_rows(inverse, low(d_update))
        d_right_low = low(d_right)
        d_system = jnp.where(earlier, -times_transposed(d_right_low, update_low) * ratio, 0.0)
        d_beta = jnp.sum(d_right * fresh, axis=-1, keepdims=True) + jnp.sum(
            d_system * gram, axis=-1, keepdims=True
        )
        d_gram = low(beta_col * d_system)
        d_value = beta_col * d_right
        d_scores = low(times_transposed(d_mix, update_low) * ratio[:BLOCK])
        d_query = carry_token * times_transposed(d_mix, state) + product(d_scores, key)
        d_key = (
            inner_rows(d_scores, query)
            + end_ratio * times_transposed(update_low, later_low)
            - (beta_col * carry) * times_transposed(d_right_low, state)
            + product(d_gram, key)
            + inner_rows(d_gram, key)
        )
        adjoint[head] = (
            jnp.exp(last) * later
            + inner_rows(low(carry_token * query.astype(F32)), d_mix)
            - inner_rows(low((beta_col * carry) * key_f), d_right_low)
        )
        logits = d_beta * beta_col * (1.0 - beta_col)
        logit_cols += [logits[n * BLOCK : (n + 1) * BLOCK] for n in range(substeps)]
        grads = [width ** (-0.5) * d_query]
        grads += [d_key[n * BLOCK : (n + 1) * BLOCK] for n in range(substeps)]
        grads += [d_value[n * BLOCK : (n + 1) * BLOCK] for n in range(substeps)]
        for at, (start, size) in enumerate(pieces):
            grad = grads[at]
            if at <= substeps:
                grad = scales[at] * (
                    grad - units[at] * jnp.sum(grad * units[at], axis=-1, keepdims=True)
                )
            grad = grad * silu_slope(pres[at], sigmas[at])
            long = jnp.concatenate([grad, carried[:, start : start + size]], 0)
            tap = taps[:, start : start + size]
            spread = grad * tap[0:1]
            sums = [jnp.sum(grad * windows[at][0], axis=0, keepdims=True)]
            for offset in range(1, tap_count):
                masked = long * same_long[:, offset : offset + 1]
                spread = spread + (
                    pltpu.roll(masked, BLOCK + 8 - offset, 0)[:BLOCK] * tap[offset : offset + 1]
                )
                sums.append(
                    jnp.sum(masked[:BLOCK] * windows[at][offset], axis=0, keepdims=True)
                )
            carried[:, start : start + size] = grad[:8]
            tap_out[:, start : start + size] += jnp.concatenate(sums, 0)
            d_raw[:, start : start + size] = low(spread)

            @pl.when(step == 0)
            def _():
                tail_out[:, start : start + size] = spread[BLOCK - 8 :]

            @pl.when(step == chunks - 1)
            def _():
                first_out[:, start : start + size] = grad[:8]

    d_logit[...] = jnp.concatenate(logit_cols, 1)


def run_backward(
    raw, edge, taps, same, beta, cum_col, cum_row, t_part, p_part, s_part, state_in, adjoint_in,
    d_out, head_count, substeps, width,
):
    count, columns = raw.shape
    chunks = count // BLOCK
    rows = BLOCK * substeps
    per_halo = BLOCK // HALO
    per_eight = BLOCK // 8
    whole = lambda *shape: pl.BlockSpec(shape, lambda c: (0,) * len(shape))
    tokens = lambda cols: pl.BlockSpec((BLOCK, cols), lambda c: (chunks - 1 - c, 0))
    square = pl.BlockSpec((1, head_count, width, width), lambda c: (chunks - 1 - c, 0, 0, 0))
    return pl.pallas_call(
        functools.partial(backward_kernel, head_count, substeps, width),
        grid=(chunks,),
        in_specs=[
            tokens(columns),
            pl.BlockSpec(
                (HALO, columns), lambda c: (jnp.maximum((chunks - 1 - c) * per_halo - 1, 0), 0)
            ),
            whole(HALO, columns),
            whole(*taps.shape),
            tokens(same.shape[1]),
            pl.BlockSpec(
                (8, same.shape[1]),
                lambda c: (jnp.minimum((chunks - c) * per_eight, chunks * per_eight - 1), 0),
            ),
            tokens(beta.shape[1]),
            tokens(head_count),
            pl.BlockSpec((1, head_count, rows), lambda c: (chunks - 1 - c, 0, 0)),
            pl.BlockSpec((1, head_count, rows, rows), lambda c: (chunks - 1 - c, 0, 0, 0)),
            square,
            square,
            whole(head_count, width, width),
            whole(head_count, width, width),
            tokens(head_count * width),
        ],
        out_specs=[
            tokens(columns),
            tokens(head_count * substeps),
            whole(8, columns),
            whole(8, columns),
            whole(taps.shape[0], columns),
        ],
        out_shape=[
            jax.ShapeDtypeStruct((count, columns), BF16),
            jax.ShapeDtypeStruct((count, head_count * substeps), F32),
            jax.ShapeDtypeStruct((8, columns), F32),
            jax.ShapeDtypeStruct((8, columns), F32),
            jax.ShapeDtypeStruct((taps.shape[0], columns), F32),
        ],
        scratch_shapes=[
            pltpu.VMEM((head_count, width, width), F32),
            pltpu.VMEM((8, columns), F32),
        ],
        compiler_params=pltpu.CompilerParams(
            dimension_semantics=("arbitrary",), vmem_limit_bytes=48 * 1024 * 1024
        ),
        name="mixer_backward",
    )(
        raw, raw, edge, taps, same, same, beta, cum_col, cum_row, t_part, p_part, s_part,
        state_in, adjoint_in, d_out,
    )


def shift_seq(array, by):
    count = lax.axis_size("seq")
    return lax.ppermute(
        array, "seq", [(i, i + by) for i in range(count) if 0 <= i + by < count]
    )


def swap_seq(array, distance):
    return lax.ppermute(array, "seq", [(i, i ^ distance) for i in range(lax.axis_size("seq"))])


def swap_head(array):
    return lax.ppermute(array, "head", [(0, 1), (1, 0)])


def head_sum(array):
    return array + swap_head(array)


def state_dot(former, latter):
    return jnp.einsum("hij,hjk->hik", former, latter, precision=lax.Precision.HIGH)


def state_dot_t(former, latter):
    return jnp.einsum("hji,hjk->hik", former, latter, precision=lax.Precision.HIGH)


def states_before(state_map, state_shift):
    count, mine = lax.axis_size("seq"), lax.axis_index("seq")
    before = jnp.zeros_like(state_shift)
    before_map = jnp.broadcast_to(jnp.eye(state_map.shape[-1], dtype=F32), state_map.shape)
    maps, shifts = [], []
    distance = 1
    group_map, group_shift = state_map, state_shift
    while distance < count:
        other_map, other_shift = swap_seq(group_map, distance), swap_seq(group_shift, distance)
        upper = (mine & distance) != 0
        maps.append((group_map, other_map, upper))
        before = jnp.where(upper, state_dot(before_map, other_shift) + before, before)
        before_map = jnp.where(upper, state_dot(before_map, other_map), before_map)
        first_map = jnp.where(upper, other_map, group_map)
        first_shift = jnp.where(upper, other_shift, group_shift)
        second_map = jnp.where(upper, group_map, other_map)
        second_shift = jnp.where(upper, group_shift, other_shift)
        group_shift = state_dot(second_map, first_shift) + second_shift
        group_map = state_dot(second_map, first_map)
        distance *= 2
    return before, maps


def adjoints_after(own, maps):
    after = jnp.zeros_like(own)
    after_map = jnp.broadcast_to(jnp.eye(own.shape[-1], dtype=F32), own.shape)
    group = own
    distance = 1
    for group_map, other_map, upper in maps:
        other = swap_seq(group, distance)
        after = jnp.where(upper, after, after + state_dot_t(after_map, other))
        after_map = jnp.where(upper, after_map, state_dot(other_map, after_map))
        first_own = jnp.where(upper, other, group)
        second_own = jnp.where(upper, group, other)
        first_map = jnp.where(upper, other_map, group_map)
        group = first_own + state_dot_t(first_map, second_own)
        distance *= 2
    return after


def per_device(
    activations,
    log_decay,
    doc_starts,
    query_weight,
    key_weight,
    value_weight,
    beta_weight,
    gate_weight,
    out_weight,
    query_taps,
    key_taps,
    value_taps,
    mixer_gain,
    head_gain,
    feed_gain,
    feed_gate,
    feed_up,
    feed_down,
    cotangent,
):
    count, features = activations.shape
    tap_count = query_taps.shape[0]
    width = head_gain.shape[0]
    query_cols = query_weight.shape[1]
    key_cols = key_weight.shape[1]
    conv_cols = query_cols + 2 * key_cols
    hidden_cols = feed_gate.shape[1]
    head_count = query_cols // width
    beta_cols = beta_weight.shape[1]
    substeps = beta_cols // head_count
    device_rank = lax.axis_index("seq")
    head_rank = lax.axis_index("head")
    extra = 128
    shard_rows = query_weight.shape[0]
    pad = jnp.zeros((shard_rows, extra - beta_cols - 2), BF16)
    first_pack = jnp.concatenate(
        [
            query_weight,
            key_weight,
            value_weight,
            gate_weight,
            beta_weight,
            mixer_gain[:, None],
            feed_gain[:, None],
            pad,
        ],
        1,
    )
    second_pack = jnp.concatenate([out_weight.T, feed_gate, feed_up, feed_down.T], 1)
    first_full = lax.all_gather(first_pack, "seq", axis=0, tiled=True)
    first_full, second_pack = lax.optimization_barrier((first_full, second_pack))
    second_full = lax.all_gather(second_pack, "seq", axis=0, tiled=True)
    weight_conv = first_full[:, :conv_cols]
    weight_gate = first_full[:, conv_cols : conv_cols + query_cols]
    tail_cols = first_full[:, conv_cols + query_cols :]
    weight_beta = tail_cols[:, :beta_cols]
    gain_one = tail_cols[:, beta_cols].astype(F32)
    gain_two = tail_cols[:, beta_cols + 1].astype(F32)
    weight_out = second_full[:, :query_cols]
    weight_feed = second_full[:, query_cols : query_cols + 2 * hidden_cols]
    weight_down = second_full[:, query_cols + 2 * hidden_cols :]

    token_position = device_rank * count + jnp.arange(count, dtype=jnp.int32)
    is_start = jnp.any(token_position[:, None] == doc_starts[None, :], axis=1)

    def same_docs(position):
        doc = lambda p: jnp.sum((p[:, None] >= doc_starts[None, :]).astype(jnp.int32), axis=1)
        own = doc(position)
        return jnp.stack(
            [
                ((doc(position - offset) == own) & (position >= offset)).astype(F32)
                for offset in range(tap_count)
            ],
            1,
        )

    same = same_docs(token_position)
    log_gate = log_decay - RESET * is_start.astype(F32)[:, None]
    chunks = count // BLOCK
    cumulative = jnp.cumsum(log_gate.reshape(chunks, BLOCK, head_count), axis=1)
    cum_col = cumulative.reshape(count, head_count)
    cum_row = jnp.concatenate([jnp.swapaxes(cumulative, 1, 2)] * substeps, 2)
    taps_all = jnp.concatenate([query_taps, key_taps, value_taps], 1).astype(F32)

    inputs = activations.astype(F32)
    in_scale = lax.rsqrt(jnp.mean(inputs * inputs, axis=-1, keepdims=True) + NORM_EPS)
    normed = low(inputs * in_scale * gain_one)
    raw_all = low(product(normed, weight_conv))
    beta_gate = jax.nn.sigmoid(product(normed, weight_beta))
    gate_view = product(normed, weight_gate)
    edge = shift_seq(raw_all[count - HALO :], 1)
    t_part, p_part, s_part, q_reach, local_out, state_map, state_shift = run_forward(
        raw_all, edge, taps_all, same, beta_gate, cum_col, cum_row, head_count, substeps, width
    )
    state_in, maps = states_before(state_map, state_shift)
    state_low = low(state_in)

    by_head = lambda array: array.reshape(count, head_count, width)
    mixer_out = by_head(local_out) + jnp.einsum(
        "thk,hkv->thv", by_head(q_reach), state_low, preferred_element_type=F32
    )
    head_gain_f = head_gain.astype(F32)
    head_scale = lax.rsqrt(jnp.mean(mixer_out * mixer_out, axis=-1, keepdims=True) + NORM_EPS)
    head_unit = mixer_out * head_scale
    gate_view = by_head(gate_view)
    gate_sigma = jax.nn.sigmoid(gate_view)
    gate_act = gate_view * gate_sigma
    heads_out = low(head_unit * head_gain_f * gate_act).reshape(count, query_cols)
    hidden = inputs + head_sum(times_transposed(heads_out, weight_out))
    feed_scale = lax.rsqrt(jnp.mean(hidden * hidden, axis=-1, keepdims=True) + NORM_EPS)
    normed_ffn = low(hidden * feed_scale * gain_two)
    ffn = product(normed_ffn, weight_feed)
    ffn_gate, ffn_up = ffn[:, :hidden_cols], ffn[:, hidden_cols:]
    ffn_sigma = jax.nn.sigmoid(ffn_gate)
    activation = low(ffn_gate * ffn_sigma * ffn_up)
    branch_two = low(times_transposed(activation, weight_down))
    half = features // lax.axis_size("head")
    own_half = lambda array: lax.dynamic_slice_in_dim(array, head_rank * half, half, 1)
    other_half = lambda array: lax.dynamic_slice_in_dim(array, (1 - head_rank) * half, half, 1)
    output = low(
        own_half(hidden)
        + own_half(branch_two).astype(F32)
        + swap_head(other_half(branch_two)).astype(F32)
    )

    grad_result = cotangent.astype(F32)
    d_activation = product(cotangent, weight_down)
    d_up = low(d_activation * (ffn_gate * ffn_sigma))
    d_gate = low(d_activation * ffn_up * silu_slope(ffn_gate, ffn_sigma))
    d_ffn = jnp.concatenate([d_gate, d_up], 1)
    d_normed_ffn = head_sum(times_transposed(d_ffn, weight_feed))
    d_hidden_norm, feed_terms = norm_back(hidden, gain_two, d_normed_ffn)
    grad_feed_gain = jnp.sum(feed_terms, axis=0)
    d_hidden = grad_result + d_hidden_norm
    grad_mixer = low(d_hidden)
    d_heads = by_head(product(grad_mixer, weight_out))
    d_gate_logit = low(
        d_heads * head_unit * head_gain_f * silu_slope(gate_view, gate_sigma)
    ).reshape(count, query_cols)
    d_mixer_out, head_terms = norm_back(mixer_out, head_gain_f, d_heads * gate_act)
    head_gain_part = jnp.sum(head_terms, axis=(0, 1))
    d_mixer_low = low(d_mixer_out)
    own_part = jnp.einsum("thk,thv->hkv", by_head(q_reach), d_mixer_low, preferred_element_type=F32)
    adjoint = adjoints_after(own_part, maps)

    second_grads = jnp.concatenate(
        [
            low(inner_rows(grad_mixer, heads_out)),
            low(inner_rows(normed_ffn, d_ffn)),
            low(inner_rows(cotangent, activation)),
        ],
        1,
    )
    second_sum = lax.psum_scatter(second_grads, "seq", scatter_dimension=0, tiled=True).astype(F32)

    d_raw, d_beta_logit, tail, first_rows, tap_grads = run_backward(
        raw_all, edge, taps_all, same, beta_gate, cum_col, cum_row, t_part, p_part, s_part,
        state_low, adjoint, d_mixer_low.reshape(count, query_cols), head_count, substeps, width,
    )
    returned = shift_seq(first_rows, -1)
    same_after = same_docs(token_position[-1] + 1 + jnp.arange(8, dtype=jnp.int32))
    spread = jnp.zeros_like(tail)
    for offset in range(1, tap_count):
        masked = returned * same_after[:, offset : offset + 1] * taps_all[offset]
        spread = spread + jnp.pad(masked[:offset], ((8 - offset, 0), (0, 0)))
    d_raw = lax.dynamic_update_slice(d_raw, low(tail + spread), (count - 8, 0))
    d_beta_low = low(d_beta_logit)
    grad_conv = inner_rows(normed, d_raw)
    grad_gate = inner_rows(normed, d_gate_logit)
    grad_beta = inner_rows(normed, d_beta_low)
    d_normed_part = times_transposed(d_raw, weight_conv) + (
        times_transposed(d_beta_low, weight_beta) + times_transposed(d_gate_logit, weight_gate)
    )
    d_normed = head_sum(low(d_normed_part).astype(F32))
    d_input_norm, mixer_terms = norm_back(inputs, gain_one, d_normed)
    grad_mixer_gain = jnp.sum(mixer_terms, axis=0)
    grad_input = own_half(d_hidden + d_input_norm)
    first_grads = jnp.concatenate(
        [
            low(grad_conv),
            low(grad_gate),
            low(grad_beta),
            low(grad_mixer_gain)[:, None],
            low(grad_feed_gain)[:, None],
            jnp.zeros((features, extra - beta_cols - 2), BF16),
        ],
        1,
    )
    first_sum = lax.psum_scatter(first_grads, "seq", scatter_dimension=0, tiled=True).astype(F32)
    head_gain_sum = head_sum(head_gain_part)
    tap_total, grad_head_gain = lax.psum((tap_grads, head_gain_sum), "seq")
    cut = lambda array, start, size: array[:, start : start + size]
    base = conv_cols + query_cols
    return (
        output,
        grad_input,
        cut(first_sum, 0, query_cols),
        cut(first_sum, query_cols, key_cols),
        cut(first_sum, query_cols + key_cols, key_cols),
        cut(first_sum, base, beta_cols),
        cut(first_sum, conv_cols, query_cols),
        cut(second_sum, 0, query_cols).T,
        cut(tap_total, 0, query_cols),
        cut(tap_total, query_cols, key_cols),
        cut(tap_total, query_cols + key_cols, key_cols),
        first_sum[:, base + beta_cols],
        grad_head_gain,
        first_sum[:, base + beta_cols + 1],
        cut(second_sum, query_cols, hidden_cols),
        cut(second_sum, query_cols + hidden_cols, hidden_cols),
        cut(second_sum, query_cols + 2 * hidden_cols, hidden_cols).T,
    )


def solution(mesh):
    in_specs = (
        P("seq", None),
        P("seq", "head"),
        P(),
        P("seq", "head"),
        P("seq", "head"),
        P("seq", "head"),
        P("seq", "head"),
        P("seq", "head"),
        P("head", "seq"),
        P(None, "head"),
        P(None, "head"),
        P(None, "head"),
        P("seq"),
        P(),
        P("seq"),
        P("seq", "head"),
        P("seq", "head"),
        P("head", "seq"),
        P("seq", None),
    )
    out_specs = (
        P("seq", "head"),
        P("seq", "head"),
        P("seq", "head"),
        P("seq", "head"),
        P("seq", "head"),
        P("seq", "head"),
        P("seq", "head"),
        P("head", "seq"),
        P(None, "head"),
        P(None, "head"),
        P(None, "head"),
        P("seq"),
        P(),
        P("seq"),
        P("seq", "head"),
        P("seq", "head"),
        P("head", "seq"),
    )
    return jax.shard_map(
        per_device, mesh=mesh, in_specs=in_specs, out_specs=out_specs, check_vma=False
    )
```

time: 3190 us -> 971 us (0.30)
  waiting for transfers between devices: 1220 us -> 380 us
  other arithmetic: 819 us -> 54.1 us
  matrix products: 776 us -> 126 us
  Pallas kernels: 0 us -> 238 us
  local copies, waits for them, and re-layouts: 175 us -> 48.5 us
  blocking collectives: 160 us -> 75.6 us
    another operation x6 -> x3, other arithmetic: 632 us -> 6.4 us  [the longest x1 6.33 us: per_device(): cumulative = jnp.cumsum(log_gate.reshape(chunks, BLOCK, head_count), axis=1)]
    dot_general x337 -> x30, matrix products: 644 us -> 62.2 us  [the longest x6 42.8 us: product(): return jnp.dot(former, latter, preferred_element_type=F32)]
    reduce_scatter x8 -> x2, waiting for transfers between devices: 735 us -> 223 us  [the longest x1 202 us: per_device(): lax.psum_scatter(second_grads, 'seq', scatter_dimension=0, tiled=True)]
    all_gather x12 -> x2, waiting for transfers between devices: 421 us -> 97.5 us  [the longest x1 97.5 us: per_device(): first_full = lax.all_gather(first_pack, 'seq', axis=0, tiled=True)]
    pallas_call x0 -> x2, Pallas kernels: none -> 238 us  [the longest x1 149 us: run_forward(): pl.pallas_call(functools.partial(forward_kernel, head_count, substeps, wi...]
    ppermute x2 -> x18, waiting for transfers between devices: 1.29 us -> 59.1 us  [the longest x11 43.7 us: swap_seq(): lax.ppermute(array, 'seq', [(i, i ^ distance) for i in range(lax.axis_siz...]
    psum x3 -> x0, waiting for transfers between devices: 52.6 us -> none  [the longest x1 24.7 us: per_device(): branch_one = lax.psum(product(heads_out, full_out), 'head')]
    mul x6 -> x4, other arithmetic: 51.4 us -> 0.21 us  [the longest x3 0.2 us: per_device(): masked = returned * same_after[:, offset:offset + 1] * taps_all[offset]]
  transfers between devices with their start and end apart: 26 -> 22, of which waited for: 19 -> 17; matrix products, arithmetic and copies ran while one was open for 16% -> 13% of each run, Pallas kernels for 0% -> 15%
where the time goes in v1:
time: 971 us; the launch traced here: 962 us
  waiting for transfers between devices  380 us (39%)
  Pallas kernels  238 us (25%)
  matrix products  126 us (13%)
  blocking collectives  75.6 us (8%)
  other arithmetic  54.1 us (6%)
  local copies, waits for them, and re-layouts  48.5 us (5%)
  starting transfers between devices  24.7 us (3%)
  between operations  16 us (2%)
    reduce_scatter x1, waiting for transfers between devices, per_device(): lax.psum_scatter(second_grads, 'seq', scatter_dimension=0, tiled=True)  202 us
    pallas_call x1, Pallas kernels, run_forward(): pl.pallas_call(functools.partial(forward_kernel, head_count, substeps, wi...  149 us
    all_gather x1, waiting for transfers between devices, per_device(): first_full = lax.all_gather(first_pack, 'seq', axis=0, tiled=True)  97.5 us
    pallas_call x1, Pallas kernels, run_backward(): pl.pallas_call(functools.partial(backward_kernel, head_count, substeps, w...  89 us
    psum x1, blocking collectives, per_device(): tap_total, grad_head_gain = lax.psum((tap_grads, head_gain_sum), 'seq')  75.6 us
    ppermute x11, waiting for transfers between devices, swap_seq(): lax.ppermute(array, 'seq', [(i, i ^ distance) for i in range(lax.axis_siz...  43.7 us
    dot_general x6, matrix products, product(): return jnp.dot(former, latter, preferred_element_type=F32)  42.8 us
    dot_general x6, matrix products, times_transposed(): lax.dot_general(former, latter, (((1,), (1,)), ((), ())), preferred_eleme...  33.7 us
  transfers between devices with their start and end apart: 22, of which 17 were waited for; matrix products, arithmetic and copies ran while one was open for 13% of the time, Pallas kernels for 15%

profile of v1, /device:TPU:0, one launch (start us, length us, event | category | flops | bytes accessed | tf_op | source)
XLA Modules:
  0.0 962.5 jit_solution(3971848483335519584)
XLA Ops:
  13.4 97.5 %all-gather.3.cloned.1.call-done = bf16[1024,3200]{1,0:T(8,128)(2,1)} async-done(((bf16[64,3200]{1,0:T(8,128)(2,1)}), bf16[1024,3200]{1,0:T(8,128)(2,1)}) %all-gather.3.cloned.1.call-update) | async-done | bytes 6553616 | tf_op jit(solution)/shard_map/all_gather | solution.py:545
  113.0 6.3 fusion.98
  125.5 8.6 convolution_convert_fusion.2.raw.before
  140.1 148.9 %mixer_forward.1 = (bf16[16,4,128,128]{3,2,1,0:T(8,128)(2,1)S(1)}, bf16[16,4,128,128]{3,2,1,0:T(8,128)(2,1)}, bf16[16,4,128,128]{3,2,1,0:T(8,128)(2,1)}, bf16[10...) custom-call(bf16[1024,2560]{1,0:T(8,128)(2,1)} %copy-done.2, ...), custom_call_target="tpu_custom_call" | custom-call | tf_op jit(solution)/shard_map/mixer_forward/pallas_call | solution.py:196
  318.4 4.5 collective-permute-done.6
  326.0 5.2 collective-permute-start.7
  331.8 6.8 collective-permute-done.7
  340.8 4.5 multiply_convert_fusion.5
  348.4 7.1 collective-permute-done.8
  357.3 13.9 %fusion.6 = f32[1024,2816]{1,0:T(8,128)} fusion(bf16[1024,4736]{1,0:T(8,128)(2,1)} %all-gather.5.cloned.1.call-done, f32[1024,1024]{0,1:T(8,128)S(1)} %get-tuple-element.155, f32[1024]{0:T(1024)S(1)} %get-tuple-element.132, f32[1024]{0:T(1024)S(1)} %add_rsqrt_fusion.1), kind=kOutput, calls=%fused_computation.18 | convolution fusion | flops 5908725760 | bytes 21504000 | tf_op jit(solution)/shard_map/dot_general | solution.py:20
  371.2 9.6 fusion.1
  380.8 10.1 %fusion.4 = f32[1024,1024]{0,1:T(8,128)} fusion(bf16[1024,4736]{1,0:T(8,128)(2,1)S(1)} %bitcast.110, bf16[1024,1408]{1,0:T(8,128)(2,1)} %get-tuple-element.159, bf16[1024,1408]{1,0:T(8,128)(2,1)S(1)} %get-tuple-element.158), kind=kOutput, calls=%fused_computation.16 | convolution fusion | flops 5917114368 | bytes 15728640 | tf_op jit(solution)/shard_map/dot_general | solution.py:28
  391.1 4.0 copy.204
  398.4 6.9 multiply_reduce_fusion
  405.3 4.8 multiply_add_fusion
  421.6 5.5 collective-permute-done.11
  430.2 5.2 collective-permute-done.12
  437.1 4.5 fusion.41
  452.6 7.6 collective-permute-done.14
  461.6 89.0 %mixer_backward.1 = (bf16[1024,2560]{1,0:T(8,128)(2,1)}, f32[1024,8]{1,0:T(8,128)S(1)}, f32[8,2560]{1,0:T(8,128)S(1)}, f32[8,2560]{1,0:T(8,128)S(1)}, f32[4,2560]{1,0:T(4,128)S(1)}) custom-call(bf16[1024,2560]{1,0:T(8,128)(2,1)} %copy-done.2, bf16[1024,2560]{1,0:T(8,128)(2,1)} %copy-done.2, bf16[16,2560]{1,0:T(8,128)(2,1)S(1)} %collective-permute-done.edge, ...), custom_call_target="tpu_custom_call" | custom-call | tf_op jit(solution)/shard_map/mixer_backward/pallas_call | solution.py:375
  552.8 4.5 collective-permute-done.15
  558.2 9.3 fusion.17
  570.0 10.6 %convolution_convert_fusion.1 = bf16[1024,2560]{1,0:T(8,128)(2,1)} fusion(bf16[1024,2560]{1,0:T(8,128)(2,1)} %fusion.83, bf16[1024,1024]{0,1:T(8,128)(2,1)} %copy-done.3, f32[1024]{0:T(1024)S(1)} %get-tuple-element.133, f32[1024]{0:T(1024)S(1)} %add_rsqrt_fusion.2), kind=kOutput, calls=%fused_computation.14 | convolution fusion | flops 5375524864 | bytes 12591104 | tf_op jit(solution)/shard_map/dot_general | solution.py:24
  580.6 6.4 multiply_reduce_fusion.1
  587.2 10.8 %concatenate.26 = bf16[1024,3200]{1,0:T(8,128)(2,1)} concatenate(bf16[1024,2560]{1,0:T(8,128)(2,1)} %convolution_convert_fusion.1, bf16[1024,512]{1,0:T(8,128)(2,1)S(1)} %convolution_convert_fusion.5, bf16[1024,8]{1,0:T(8,128)(2,1)S(1)} %copy.222, bf16[1024,1]{1,0:T(8,128)(2,1)S(1)} %convert_element_type.296, bf16[1024,1]{1,0:T(8,128)(2,1)S(1)} %convert_element_type.297, ...), dimensions={1} | concatenate | bytes 13107200 | tf_op jit(solution)/shard_map/concatenate | solution.py:673
  598.1 7.6 fusion.12
  605.8 8.4 convolution_convert_fusion
  616.0 8.8 pad_maximum_fusion
  624.9 6.2 fusion.20
  639.1 75.6 %all-reduce.3 = (f32[4,2560]{1,0:T(4,128)S(1)}, f32[128]{0:T(128)}) all-reduce(f32[4,2560]{1,0:T(4,128)S(1)} %get-tuple-element.44, f32[128]{0:T(128)S(1)} %add.294), channel_id=1, replica_groups=mesh['seq'=16,'head'=2] {'seq'}, use_global_device_ids=true, to_apply=%region_20.21 | all-reduce | flops 10368 | bytes 82944 | tf_op jit(solution)/shard_map/psum | solution.py:686
  721.3 21.5 %reduce-scatter.3.cloned.1.call-done = bf16[64,3200]{1,0:T(8,128)(2,1)} async-done(((bf16[1024,3200]{1,0:T(8,128)(2,1)}), bf16[64,3200]{1,0:T(8,128)(2,1)}) %reduce-scatter.3.cloned.1.call-update) | async-done | bytes 409616 | tf_op jit(solution)/shard_map/reduce_scatter | solution.py:684
  749.3 201.7 %reduce-scatter.5.cloned.1.call-done = bf16[64,4736]{1,0:T(8,128)(2,1)} async-done(((bf16[1024,4736]{1,0:T(8,128)(2,1)}), bf16[64,4736]{1,0:T(8,128)(2,1)}) %reduce-scatter.5.cloned.1.call-update) | async-done | bytes 606224 | tf_op jit(solution)/shard_map/reduce_scatter | solution.py:649
  (257 shorter events, 124.6 us)
Async XLA Ops:
  7.2 103.8 %all-gather.3.cloned.1.call-start = ((), (), s32[]{:S(2)}) async-start(), calls=%async_computation.2 | async-start | bytes 6963200 | tf_op jit(solution)/shard_map/all_gather | solution.py:545
  11.4 333.9 %all-gather.5.cloned.1.call-start = ((), (), s32[]{:S(2)}) async-start(), calls=%async_computation.3 | async-start | bytes 10305536 | tf_op jit(solution)/shard_map/all_gather | solution.py:547
  13.4 109.4 %copy-start.39 = (s32[3]{0:T(128)S(1)}, s32[3]{0:T(128)}, u32[]{:S(2)}) copy-start(s32[3]{0:T(128)} %param.21) | copy-start | bytes 40
  111.0 631.8 %reduce-scatter.3.cloned.1.call-start = ((), (), s32[]{:S(2)}) async-start(), calls=%async_computation.4 | async-start | bytes 6963200 | tf_op jit(solution)/shard_map/reduce_scatter | solution.py:684
  134.2 5.9 collective-permute-start
  140.1 152.3 %copy-start.45 = (bf16[128]{0:T(256)(128)(2,1)S(1)}, bf16[128]{0:T(256)(128)(2,1)}, u32[]{:S(2)}) copy-start(bf16[128]{0:T(256)(128)(2,1)} %param.32) | copy-start | bytes 772
  290.4 9.3 collective-permute-start.4
  292.2 10.4 %collective-permute-start.1 = (f32[4,128,128]{2,1,0:T(8,128)S(1)}, f32[4,128,128]{2,1,0:T(8,128)}, u32[]{:S(2)}, u32[]{:S(2)}) collective-permute-start(f32[4,128,128]{2,1,0:T(8,128)S(1)} %get-tuple-element.33), channel_id=1, source_target_pairs={{0,2},{2,0},{4,6},{6,4},{8,10},{10,8},{12,14},{14,12},{16,18},{18,... | collective-permute-start | bytes 786440 | tf_op jit(solution)/shard_map/ppermute | solution.py:436
  303.9 8.4 collective-permute-start.5
  307.0 24.7 %copy-start.20 = (f32[4,128,128]{2,1,0:T(8,128)}, f32[4,128,128]{2,1,0:T(8,128)S(1)}, u32[]{:S(2)}) copy-start(f32[4,128,128]{2,1,0:T(8,128)S(1)} %fusion.81) | copy-start | bytes 786436
  307.0 8.1 collective-permute-start.2
  309.7 29.1 %copy-start.16 = (bf16[1024,512]{0,1:T(8,128)(2,1)S(1)}, bf16[1024,512]{0,1:T(8,128)(2,1)}, u32[]{:S(2)}) copy-start(bf16[1024,512]{0,1:T(8,128)(2,1)} %copy.250) | copy-start | bytes 3145732
  309.7 29.1 %copy-start.19 = (f32[1024,512]{0,1:T(8,128)S(1)}, f32[1024,512]{0,1:T(8,128)}, u32[]{:S(2)}) copy-start(f32[1024,512]{0,1:T(8,128)} %copy.248) | copy-start | bytes 6291460
  315.4 7.5 collective-permute-start.6
  317.3 21.6 %copy-start.25 = (f32[4,128,128]{2,1,0:T(8,128)}, f32[4,128,128]{2,1,0:T(8,128)S(1)}, u32[]{:S(2)}) copy-start(f32[4,128,128]{2,1,0:T(8,128)S(1)} %fusion.80) | copy-start | bytes 786436
  317.3 8.4 collective-permute-start.3
  326.0 12.5 %collective-permute-start.7 = (f32[4,128,128]{2,1,0:T(8,128)S(1)}, f32[4,128,128]{2,1,0:T(8,128)S(1)}, u32[]{:S(2)}, u32[]{:S(2)}) collective-permute-start(f32[4,128,128]{2,1,0:T(8,128)S(1)} %convolution_add_fusion.6), channel_id=1, source_target_pairs={{0,16},{2,18},{4,20},{6,22},{8,24},{10,26},{12,28},{14,30},{16,0},... | collective-permute-start | bytes 786440 | tf_op jit(solution)/shard_map/ppermute | solution.py:436
  348.3 7.2 collective-permute-start.8
  390.9 7.5 collective-permute-start.10
  416.9 20.1 %copy-start.32 = (bf16[1024,4,128]{0,2,1:T(8,128)(2,1)}, bf16[1024,4,128]{0,2,1:T(8,128)(2,1)S(1)}, u32[]{:S(2)}) copy-start(bf16[1024,4,128]{0,2,1:T(8,128)(2,1)S(1)} %get-tuple-element.161) | copy-start | bytes 3145732
  417.8 23.7 %copy-start.17 = (bf16[1024,4,128]{0,2,1:T(8,128)(2,1)}, bf16[1024,4,128]{0,2,1:T(8,128)(2,1)S(1)}, u32[]{:S(2)}) copy-start(bf16[1024,4,128]{0,2,1:T(8,128)(2,1)S(1)} %multiply_convert_fusion.4) | copy-start | bytes 3145732
  418.3 8.8 collective-permute-start.11
  427.5 7.9 collective-permute-start.12
  436.6 8.0 collective-permute-start.13
  444.6 107.5 %slice-start = ((s8[6553600]{0:T(1024)(128)(4,1)}), s8[2359296]{0:T(1024)(128)(4,1)S(1)}, s32[]{:S(2)}) async-start(s8[6553600]{0:T(1024)(128)(4,1)} %bitcast.99), calls=%async_computation.6 | async-start | bytes 4718592
  446.3 13.9 %collective-permute-start.14 = (f32[4,128,128]{2,1,0:T(8,128)S(1)}, f32[4,128,128]{2,1,0:T(8,128)S(1)}, u32[]{:S(2)}, u32[]{:S(2)}) collective-permute-start(f32[4,128,128]{2,1,0:T(8,128)S(1)} %select_add_fusion), channel_id=1, source_target_pairs={{0,16},{2,18},{4,20},{6,22},{8,24},{10,26},{12,28},{14,30},{16,0},... | collective-permute-start | bytes 786440 | tf_op jit(solution)/shard_map/ppermute | solution.py:436
  461.6 90.6 %slice-start.1 = ((s8[6553600]{0:T(1024)(128)(4,1)}), s8[4194304]{0:T(1024)(128)(4,1)S(1)}, s32[]{:S(2)}) async-start(s8[6553600]{0:T(1024)(128)(4,1)} %bitcast.99), calls=%async_computation.7 | async-start | bytes 8388608
  550.5 6.8 collective-permute-start.15
  567.5 13.1 %collective-permute-start.16 = (f32[1024,1024]{0,1:T(8,128)}, f32[1024,1024]{0,1:T(8,128)}, u32[]{:S(2)}, u32[]{:S(2)}) collective-permute-start(f32[1024,1024]{0,1:T(8,128)} %fusion.17), channel_id=1, source_target_pairs={{0,1},{1,0},{2,3},{3,2},{4,5},{5,4},{6,7},{7,6},{8,9},{9,8},{10,11... | collective-permute-start | bytes 12582920 | tf_op jit(solution)/shard_map/ppermute | solution.py:440
  598.0 353.0 %reduce-scatter.5.cloned.1.call-start = ((), (), s32[]{:S(2)}) async-start(), calls=%async_computation.5 | async-start | bytes 10305536 | tf_op jit(solution)/shard_map/reduce_scatter | solution.py:649
  632.5 2.8 collective-permute-start.9
  633.1 6.0 collective-permute-start.17
  (45 other events, 411.1 us)
Sparse Core Ops, SparseCore 0:
  11.5 99.3 all-gather.2
  113.7 123.4 all-gather.4
  598.1 144.5 reduce-scatter.2
  745.0 205.9 reduce-scatter.4

commit v2 on v1

v2 whole, which is shorter than its diff:
```python
import functools

import jax
import jax.numpy as jnp
from jax import lax
from jax.experimental import pallas as pl
from jax.experimental.pallas import tpu as pltpu
from jax.sharding import PartitionSpec as P

BLOCK = 64
RESET = 256.0
HALO = 16
BACK_CALLS = 3
NORM_EPS = 1e-05
UNIT_EPS = 1e-06
F32 = jnp.float32
BF16 = jnp.bfloat16


def product(former, latter):
    return jnp.dot(former, latter, preferred_element_type=F32)


def inner_rows(former, latter):
    return lax.dot_general(former, latter, (((0,), (0,)), ((), ())), preferred_element_type=F32)


def times_transposed(former, latter):
    return lax.dot_general(former, latter, (((1,), (1,)), ((), ())), preferred_element_type=F32)


def low(values):
    return values.astype(BF16)


def split(values):
    high = values.astype(BF16)
    return high, (values - high.astype(F32)).astype(BF16)


def fine(form, former, latter):
    a_high, a_low = split(former)
    b_high, b_low = split(latter)
    return form(a_high, b_high) + (form(a_low, b_high) + form(a_high, b_low))


def silu_slope(values, sigma):
    return sigma * (1.0 + values * (1.0 - sigma))


def norm_back(values, gain_vector, gradient):
    row_scale = lax.rsqrt(jnp.mean(values * values, axis=-1, keepdims=True) + NORM_EPS)
    unit_value = values * row_scale
    scaled_grad = gradient * gain_vector
    back_value = row_scale * (
        scaled_grad - unit_value * jnp.mean(scaled_grad * unit_value, axis=-1, keepdims=True)
    )
    return (back_value, gradient * unit_value)


def row_maps(rows):
    row = lax.broadcasted_iota(jnp.int32, (rows, rows), 0)
    col = lax.broadcasted_iota(jnp.int32, (rows, rows), 1)
    return row % BLOCK, col % BLOCK, row // BLOCK, col // BLOCK


def lower_inverses(systems, apart):
    rows = systems[0].shape[0]
    row = lax.broadcasted_iota(jnp.int32, (rows, rows), 0)
    col = lax.broadcasted_iota(jnp.int32, (rows, rows), 1)
    eye = jnp.where(row == col, 1.0, 0.0)
    inverses = [eye - jnp.where(apart == 0, system, 0.0) for system in systems]
    level = 0
    while (1 << level) < BLOCK:
        joins = (apart >> level) == 1
        joints = [low(jnp.where(joins, system, 0.0)) for system in systems]
        lows = [low(inverse) for inverse in inverses]
        halves = [low(product(a, b)) for a, b in zip(lows, joints)]
        inverses = [c - product(a, b) for a, b, c in zip(halves, lows, inverses)]
        level += 1
    return inverses


def conv_rows(tile, halo, taps, same, columns):
    count = tile.shape[0]
    extended = jnp.concatenate([halo, tile], 0)
    windows = [tile] + [
        pltpu.roll(extended, offset, 0)[8:] for offset in range(1, taps.shape[0])
    ]
    outcome = tile * taps[0:1]
    for offset in range(1, taps.shape[0]):
        outcome = outcome + windows[offset] * taps[offset : offset + 1] * same[:, offset : offset + 1]
    return outcome, windows


def unit_scale(values):
    return lax.rsqrt(jnp.sum(values * values, axis=-1, keepdims=True) + UNIT_EPS)


def pieces_of(head, head_count, substeps, width):
    query = [(head * width, width)]
    keys = [((head_count + head * substeps + n) * width, width) for n in range(substeps)]
    values = [
        ((head_count + (head_count + head) * substeps + n) * width, width) for n in range(substeps)
    ]
    return query + keys + values


def forward_kernel(
    head_count, substeps, width,
    raw, before, edge, taps, same, beta, cum_col, cum_row,
    t_out, p_out, s_out, qtil_out, local_out, group_out,
    chain,
):
    chunk = pl.program_id(0)
    rows = BLOCK * substeps
    row_token, col_token, row_step, col_step = row_maps(rows)
    upto = col_token <= row_token
    earlier = (col_token < row_token) | ((col_token == row_token) & (col_step < row_step))
    apart = row_token ^ col_token
    eye = jnp.where(
        lax.broadcasted_iota(jnp.int32, (width, width), 0)
        == lax.broadcasted_iota(jnp.int32, (width, width), 1),
        1.0,
        0.0,
    )
    same_rows = same[...]

    @pl.when(chunk == 0)
    def _():
        for head in range(head_count):
            chain[head, :, :width] = eye
            chain[head, :, width:] = jnp.zeros((width, width), F32)

    heads = range(head_count)
    queries, keys, values, betas, ratios, systems = [], [], [], [], [], []
    for head in heads:
        acts = []
        for start, size in pieces_of(head, head_count, substeps, width):
            tile = raw[:, start : start + size].astype(F32)
            halo = jnp.where(
                chunk == 0, edge[:, start : start + size], before[:, start : start + size]
            ).astype(F32)[HALO - 8 :]
            pre, _ = conv_rows(tile, halo, taps[:, start : start + size], same_rows, None)
            acts.append(pre * jax.nn.sigmoid(pre))
        queries.append(low(acts[0] * unit_scale(acts[0]) * width ** (-0.5)))
        keys.append(low(jnp.concatenate([a * unit_scale(a) for a in acts[1 : 1 + substeps]], 0)))
        values.append(low(jnp.concatenate(acts[1 + substeps :], 0)))
        betas.append(
            jnp.concatenate(
                [beta[:, head * substeps + n : head * substeps + n + 1] for n in range(substeps)], 0
            )
        )
    cum_rows = [jnp.concatenate([cum_col[:, h : h + 1]] * substeps, 0) for h in heads]
    cum_cols = [cum_row[0, h : h + 1, :] for h in heads]
    lasts = [c[:, BLOCK - 1 : BLOCK] for c in cum_cols]
    ratios = [jnp.exp(jnp.where(upto, a - b, -1e4)) for a, b in zip(cum_rows, cum_cols)]
    grams = [times_transposed(key, key) for key in keys]
    scores = [times_transposed(query, key) for query, key in zip(queries, keys)]
    systems = [
        jnp.where(earlier, beta_col * ratio * gram, 0.0)
        for beta_col, ratio, gram in zip(betas, ratios, grams)
    ]
    inverses = [low(inverse) for inverse in lower_inverses(systems, apart)]
    rights = [
        jnp.concatenate(
            [
                low(beta_col * jnp.exp(cum) * key.astype(F32)),
                low(beta_col * value.astype(F32)),
            ],
            1,
        )
        for beta_col, cum, key, value in zip(betas, cum_rows, keys, values)
    ]
    solved = [low(product(inverse, right)) for inverse, right in zip(inverses, rights)]
    ends = [
        low(jnp.exp(last - cum) * key.astype(F32))
        for last, cum, key in zip(lasts, cum_rows, keys)
    ]
    moved = [inner_rows(end, both) for end, both in zip(ends, solved)]
    seen = [
        product(low(ratio[:BLOCK] * score), both)
        for ratio, score, both in zip(ratios, scores, solved)
    ]
    chains = [chain[head] for head in heads]
    chains_low = [low(chained) for chained in chains]
    reached = [
        product(
            low(jnp.exp(cum[:BLOCK]) * query.astype(F32) - see[:, :width]), chained
        )
        for cum, query, see, chained in zip(cum_rows, queries, seen, chains_low)
    ]
    grown = [
        fine(product, jnp.exp(last) * eye - move[:, :width], chained)
        for last, move, chained in zip(lasts, moved, chains)
    ]
    for head in heads:
        at = slice(head * width, (head + 1) * width)
        t_out[0, head] = inverses[head]
        p_out[0, head] = chains_low[head][:, :width]
        s_out[0, head] = chains_low[head][:, width:]
        qtil_out[:, at] = low(reached[head][:, :width])
        local_out[:, at] = reached[head][:, width:] + seen[head][:, width:]
        new_map = grown[head][:, :width]
        new_shift = grown[head][:, width:] + moved[head][:, width:]
        chain[head, :, :width] = new_map
        chain[head, :, width:] = new_shift
        group_out[head, :, :width] = new_map
        group_out[head, :, width:] = new_shift


def run_forward(raw, edge, taps, same, beta, cum_col, cum_row, head_count, substeps, width):
    count, columns = raw.shape
    chunks = count // BLOCK
    rows = BLOCK * substeps
    per_halo = BLOCK // HALO
    whole = lambda *shape: pl.BlockSpec(shape, lambda c: (0,) * len(shape))
    tokens = lambda cols: pl.BlockSpec((BLOCK, cols), lambda c: (c, 0))
    square = pl.BlockSpec((1, head_count, width, width), lambda c: (c, 0, 0, 0))
    return pl.pallas_call(
        functools.partial(forward_kernel, head_count, substeps, width),
        grid=(chunks,),
        in_specs=[
            tokens(columns),
            pl.BlockSpec((HALO, columns), lambda c: (jnp.maximum(c * per_halo - 1, 0), 0)),
            whole(HALO, columns),
            whole(*taps.shape),
            tokens(same.shape[1]),
            tokens(beta.shape[1]),
            tokens(head_count),
            pl.BlockSpec((1, head_count, rows), lambda c: (c, 0, 0)),
        ],
        out_specs=[
            pl.BlockSpec((1, head_count, rows, rows), lambda c: (c, 0, 0, 0)),
            square,
            square,
            tokens(head_count * width),
            tokens(head_count * width),
            whole(head_count, width, 2 * width),
        ],
        out_shape=[
            jax.ShapeDtypeStruct((chunks, head_count, rows, rows), BF16),
            jax.ShapeDtypeStruct((chunks, head_count, width, width), BF16),
            jax.ShapeDtypeStruct((chunks, head_count, width, width), BF16),
            jax.ShapeDtypeStruct((count, head_count * width), BF16),
            jax.ShapeDtypeStruct((count, head_count * width), F32),
            jax.ShapeDtypeStruct((head_count, width, 2 * width), F32),
        ],
        scratch_shapes=[pltpu.VMEM((head_count, width, 2 * width), F32)],
        compiler_params=pltpu.CompilerParams(
            dimension_semantics=("arbitrary",), vmem_limit_bytes=48 * 1024 * 1024
        ),
        name="mixer_forward",
    )(raw, raw, edge, taps, same, beta, cum_col, cum_row)


def backward_kernel(
    head_count, substeps, width, end,
    raw, before, edge, taps, same, same_next, beta, cum_col, cum_row,
    t_in, p_in, s_in, state_in, d_out, adjoint_in, carried_in, tap_in, raw_in, logit_in,
    d_raw, d_logit, tail_out, adjoint, carried, tap_out,
    tail_next,
):
    step = pl.program_id(0)
    chunk = end - 1 - step
    rows = BLOCK * substeps
    tap_count = taps.shape[0]
    row_token, col_token, row_step, col_step = row_maps(rows)
    upto = col_token <= row_token
    earlier = (col_token < row_token) | ((col_token == row_token) & (col_step < row_step))
    same_rows = same[...]
    same_long = jnp.concatenate([same_rows, same_next[...]], 0)

    @pl.when(step == 0)
    def _():
        adjoint[...] = adjoint_in[...]
        carried[...] = carried_in[...]
        tap_out[...] = tap_in[...]

    heads = range(head_count)
    pieces = [pieces_of(head, head_count, substeps, width) for head in heads]
    pres, sigmas, scales, units = [], [], [], []
    queries, keys, values, betas = [], [], [], []

    def windows_of(start, size):
        tile = raw[:, start : start + size].astype(F32)
        halo = jnp.where(
            chunk == 0, edge[:, start : start + size], before[:, start : start + size]
        ).astype(F32)[HALO - 8 :]
        return conv_rows(tile, halo, taps[:, start : start + size], same_rows, None)

    for head in heads:
        pre = [windows_of(start, size)[0] for start, size in pieces[head]]
        sigma = [jax.nn.sigmoid(p) for p in pre]
        acts = [p * s for p, s in zip(pre, sigma)]
        pres.append(pre)
        sigmas.append(sigma)
        scales.append([unit_scale(a) for a in acts[: 1 + substeps]])
        units.append([a * s for a, s in zip(acts[: 1 + substeps], scales[head])])
        queries.append(low(units[head][0] * width ** (-0.5)))
        keys.append(low(jnp.concatenate(units[head][1:], 0)))
        values.append(low(jnp.concatenate(acts[1 + substeps :], 0)))
        betas.append(
            jnp.concatenate(
                [beta[:, head * substeps + n : head * substeps + n + 1] for n in range(substeps)], 0
            )
        )
    cum_rows = [jnp.concatenate([cum_col[:, h : h + 1]] * substeps, 0) for h in heads]
    cum_cols = [cum_row[0, h : h + 1, :] for h in heads]
    lasts = [c[:, BLOCK - 1 : BLOCK] for c in cum_cols]
    ratios = [jnp.exp(jnp.where(upto, a - b, -1e4)) for a, b in zip(cum_rows, cum_cols)]
    carries = [jnp.exp(c) for c in cum_rows]
    end_ratios = [jnp.exp(last - c) for last, c in zip(lasts, cum_rows)]
    inverses = [t_in[0, h] for h in heads]
    laters = [adjoint[h] for h in heads]
    laters_low = [low(later) for later in laters]
    d_mixes = [d_out[:, h * width : (h + 1) * width] for h in heads]
    states = [low(s_in[0, h].astype(F32) + product(p_in[0, h], state_in[h])) for h in heads]
    scores = [times_transposed(query, key) for query, key in zip(queries, keys)]
    masks = [low(ratio[:BLOCK] * score) for ratio, score in zip(ratios, scores)]
    d_updates = [
        low(inner_rows(mask, d_mix) + product(low(end * key.astype(F32)), later))
        for mask, d_mix, end, key, later in zip(masks, d_mixes, end_ratios, keys, laters_low)
    ]
    d_rights = [inner_rows(inverse, d_update) for inverse, d_update in zip(inverses, d_updates)]
    d_rights_low = [low(d_right) for d_right in d_rights]
    d_states = [
        inner_rows(low(carry[:BLOCK] * query.astype(F32)), d_mix)
        - inner_rows(low((beta_col * carry) * key.astype(F32)), d_right)
        for carry, query, d_mix, beta_col, key, d_right in zip(
            carries, queries, d_mixes, betas, keys, d_rights_low
        )
    ]
    for h in heads:
        adjoint[h] = jnp.exp(lasts[h]) * laters[h] + d_states[h]
    grams = [times_transposed(key, key) for key in keys]
    freshes = [
        value.astype(F32) - carry * product(key, state)
        for value, carry, key, state in zip(values, carries, keys, states)
    ]
    updates = [
        low(product(inverse, low(beta_col * fresh)))
        for inverse, beta_col, fresh in zip(inverses, betas, freshes)
    ]
    d_systems = [
        jnp.where(earlier, -times_transposed(d_right, update) * ratio, 0.0)
        for d_right, update, ratio in zip(d_rights_low, updates, ratios)
    ]
    d_scores = [
        low(times_transposed(d_mix, update) * ratio[:BLOCK])
        for d_mix, update, ratio in zip(d_mixes, updates, ratios)
    ]
    d_grams = [low(beta_col * d_system) for beta_col, d_system in zip(betas, d_systems)]
    d_betas = [
        jnp.sum(d_right * fresh, axis=-1, keepdims=True)
        + jnp.sum(d_system * gram, axis=-1, keepdims=True)
        for d_right, fresh, d_system, gram in zip(d_rights, freshes, d_systems, grams)
    ]
    d_queries = [
        carry[:BLOCK] * times_transposed(d_mix, state) + product(d_score, key)
        for carry, d_mix, state, d_score, key in zip(carries, d_mixes, states, d_scores, keys)
    ]
    d_keys = [
        inner_rows(d_scores[h], queries[h])
        + end_ratios[h] * times_transposed(updates[h], laters_low[h])
        - (betas[h] * carries[h]) * times_transposed(d_rights_low[h], states[h])
        + product(d_grams[h], keys[h])
        + inner_rows(d_grams[h], keys[h])
        for h in heads
    ]
    logit_cols = []
    for h in heads:
        logits = d_betas[h] * betas[h] * (1.0 - betas[h])
        logit_cols += [logits[n * BLOCK : (n + 1) * BLOCK] for n in range(substeps)]
    d_logit[...] = jnp.concatenate(logit_cols, 1)

    for head in heads:
        d_value = betas[head] * d_rights[head]
        grads = [width ** (-0.5) * d_queries[head]]
        grads += [d_keys[head][n * BLOCK : (n + 1) * BLOCK] for n in range(substeps)]
        grads += [d_value[n * BLOCK : (n + 1) * BLOCK] for n in range(substeps)]
        for at, (start, size) in enumerate(pieces[head]):
            grad = grads[at]
            if at <= substeps:
                unit = units[head][at]
                grad = scales[head][at] * (
                    grad - unit * jnp.sum(grad * unit, axis=-1, keepdims=True)
                )
            grad = grad * silu_slope(pres[head][at], sigmas[head][at])
            windows = windows_of(start, size)[1]
            long = jnp.concatenate([grad, carried[:, start : start + size]], 0)
            tap = taps[:, start : start + size]
            spread = grad * tap[0:1]
            sums = [jnp.sum(grad * windows[0], axis=0, keepdims=True)]
            for offset in range(1, tap_count):
                masked = long * same_long[:, offset : offset + 1]
                spread = spread + (
                    pltpu.roll(masked, BLOCK + 8 - offset, 0)[:BLOCK] * tap[offset : offset + 1]
                )
                sums.append(jnp.sum(masked[:BLOCK] * windows[offset], axis=0, keepdims=True))
            carried[:, start : start + size] = grad[:8]
            tap_out[:, start : start + size] += jnp.concatenate(sums, 0)
            d_raw[:, start : start + size] = low(spread)
            tail_next[:, start : start + size] = spread[BLOCK - 8 :]

    @pl.when(step == 0)
    def _():
        tail_out[...] = tail_next[...]


def run_backward(
    begin, end, raw, edge, taps, same, beta, cum_col, cum_row, t_part, p_part, s_part, state_in,
    d_out, passed, head_count, substeps, width,
):
    count, columns = raw.shape
    chunks = count // BLOCK
    rows = BLOCK * substeps
    per_halo = BLOCK // HALO
    per_eight = BLOCK // 8
    whole = lambda *shape: pl.BlockSpec(shape, lambda c: (0,) * len(shape))
    tokens = lambda cols: pl.BlockSpec((BLOCK, cols), lambda c: (end - 1 - c, 0))
    square = pl.BlockSpec((1, head_count, width, width), lambda c: (end - 1 - c, 0, 0, 0))
    anywhere = pl.BlockSpec(memory_space=pl.ANY)
    state = (head_count, width, width)
    return pl.pallas_call(
        functools.partial(backward_kernel, head_count, substeps, width, end),
        grid=(end - begin,),
        in_specs=[
            tokens(columns),
            pl.BlockSpec(
                (HALO, columns), lambda c: (jnp.maximum((end - 1 - c) * per_halo - 1, 0), 0)
            ),
            whole(HALO, columns),
            whole(*taps.shape),
            tokens(same.shape[1]),
            pl.BlockSpec(
                (8, same.shape[1]),
                lambda c: (jnp.minimum((end - c) * per_eight, chunks * per_eight - 1), 0),
            ),
            tokens(beta.shape[1]),
            tokens(head_count),
            pl.BlockSpec((1, head_count, rows), lambda c: (end - 1 - c, 0, 0)),
            pl.BlockSpec((1, head_count, rows, rows), lambda c: (end - 1 - c, 0, 0, 0)),
            square,
            square,
            whole(*state),
            tokens(head_count * width),
            whole(*state),
            whole(8, columns),
            whole(*taps.shape),
            anywhere,
            anywhere,
        ],
        out_specs=[
            tokens(columns),
            tokens(head_count * substeps),
            whole(8, columns),
            whole(*state),
            whole(8, columns),
            whole(*taps.shape),
        ],
        out_shape=[
            jax.ShapeDtypeStruct((count, columns), BF16),
            jax.ShapeDtypeStruct((count, head_count * substeps), F32),
            jax.ShapeDtypeStruct((8, columns), F32),
            jax.ShapeDtypeStruct(state, F32),
            jax.ShapeDtypeStruct((8, columns), F32),
            jax.ShapeDtypeStruct(taps.shape, F32),
        ],
        scratch_shapes=[pltpu.VMEM((8, columns), F32)],
        input_output_aliases={17: 0, 18: 1},
        compiler_params=pltpu.CompilerParams(
            dimension_semantics=("arbitrary",), vmem_limit_bytes=48 * 1024 * 1024
        ),
        name="mixer_backward",
    )(
        raw, raw, edge, taps, same, same, beta, cum_col, cum_row, t_part, p_part, s_part,
        state_in, d_out, *passed,
    )


def shift_seq(array, by):
    count = lax.axis_size("seq")
    return lax.ppermute(
        array, "seq", [(i, i + by) for i in range(count) if 0 <= i + by < count]
    )


def swap_seq(array, distance):
    return lax.ppermute(array, "seq", [(i, i ^ distance) for i in range(lax.axis_size("seq"))])


def swap_head(array):
    return lax.ppermute(array, "head", [(0, 1), (1, 0)])


def head_sum(array):
    return array + swap_head(array)


def fine_low(form, former, latter):
    high, rest = split(former)
    return form(high, latter) + form(rest, latter)


def fine_first(form, former, latter):
    high, rest = split(latter)
    return form(former, high) + form(former, rest)


def join_kernel(final, upper, group, other, before, group_out, low_out, before_out):
    heads, width, _ = group.shape

    @pl.when(upper[0] == 1)
    def _():
        for head in range(heads):
            theirs = other[head]
            reach = fine_low(product, before[head, :, :width], theirs)
            before_out[head, :, :width] = reach[:, :width]
            before_out[head, :, width:] = reach[:, width:] + before[head, :, width:]
            if not final:
                mine = fine_low(product, group[head, :, :width], theirs)
                group_out[head, :, :width] = mine[:, :width]
                group_out[head, :, width:] = mine[:, width:] + group[head, :, width:]

    @pl.when(upper[0] == 0)
    def _():
        before_out[...] = before[...]
        if not final:
            for head in range(heads):
                theirs = other[head]
                mine = fine_first(product, theirs[:, :width], group[head])
                group_out[head, :, :width] = mine[:, :width]
                group_out[head, :, width:] = mine[:, width:] + theirs[:, width:].astype(F32)

    low_out[...] = low(group_out[...]) if not final else low(before_out[...])


def join_groups(final, upper, group, other, before):
    whole = pl.BlockSpec(memory_space=pltpu.VMEM)
    full = jax.ShapeDtypeStruct(group.shape, F32)
    return pl.pallas_call(
        functools.partial(join_kernel, final),
        in_specs=[pl.BlockSpec(memory_space=pltpu.SMEM), whole, whole, whole],
        out_specs=[whole, whole, whole],
        out_shape=[full, jax.ShapeDtypeStruct(group.shape, BF16), full],
        name="join_groups",
    )(upper, group, other, before)


def back_kernel(final, upper, group, other, after, group_map, other_map, after_map, *outs):
    group_out, low_out, after_out, after_map_out = outs
    heads, width, _ = group.shape
    after_out[...] = after[...]
    after_map_out[...] = after_map[...]
    if final:
        group_out[...] = group[...]

    @pl.when(upper[0] == 1)
    def _():
        if not final:
            for head in range(heads):
                theirs = other_map[head, :, :width]
                group_out[head] = other[head].astype(F32) + fine_first(
                    inner_rows, theirs, group[head]
                )

    @pl.when(upper[0] == 0)
    def _():
        for head in range(heads):
            theirs = other[head]
            after_out[head] += fine_low(inner_rows, after_map[head], theirs)
            if not final:
                group_out[head] = group[head] + fine_low(
                    inner_rows, group_map[head, :, :width], theirs
                )
                after_map_out[head] = fine_first(
                    product, other_map[head, :, :width], after_map[head]
                )

    low_out[...] = low(group_out[...])


def join_back(final, upper, group, other, after, group_map, other_map, after_map):
    whole = pl.BlockSpec(memory_space=pltpu.VMEM)
    full = jax.ShapeDtypeStruct(group.shape, F32)
    return pl.pallas_call(
        functools.partial(back_kernel, final),
        in_specs=[pl.BlockSpec(memory_space=pltpu.SMEM)] + [whole] * 6,
        out_specs=[whole] * 4,
        out_shape=[full, jax.ShapeDtypeStruct(group.shape, BF16), full, full],
        name="join_back",
    )(upper, group, other, after, group_map, other_map, after_map)


def states_before(group, eye):
    count, mine = lax.axis_size("seq"), lax.axis_index("seq")
    before = jnp.concatenate([eye, jnp.zeros_like(eye)], 2)
    group_low = low(group)
    kept = []
    distance = 1
    while distance < count:
        other = swap_seq(group_low, distance)
        upper = ((mine // distance) % 2).astype(jnp.int32).reshape(1)
        kept.append((group, other, upper))
        final = 2 * distance >= count
        group, group_low, before = join_groups(final, upper, group, other, before)
        distance *= 2
    return group_low[:, :, group.shape[1] :], kept


def adjoints_after(own, kept, eye):
    group, group_low = own, low(own)
    after, after_map = jnp.zeros_like(own), eye
    distance = 1
    for group_map, other_map, upper in kept:
        other = swap_seq(group_low, distance)
        final = 2 * distance >= lax.axis_size("seq")
        group, group_low, after, after_map = join_back(
            final, upper, group, other, after, group_map, other_map, after_map
        )
        distance *= 2
    return after


def bit_orders(count):
    distances = [1 << k for k in range(count.bit_length() - 1)]
    near, far = distances[:3], distances[3:]
    return [near[k:] + near[:k] for k in range(len(near))], far


def scatter_view(array):
    count = lax.axis_size("seq")
    bits = count.bit_length() - 1
    return array.reshape((2,) * bits + (array.shape[0] // count, array.shape[1]))


def scatter_halves(view, distance):
    axis = view.ndim - 2 - distance.bit_length()
    own = (lax.axis_index("seq") // distance) % 2
    keep = lax.dynamic_slice_in_dim(view, own, 1, axis)
    send = lax.dynamic_slice_in_dim(view, 1 - own, 1, axis)
    return keep, low(send)


def swap_all(arrays, distances):
    return [swap_seq(array, distance) for array, distance in zip(arrays, distances)]


def halve_all(views, distances):
    halves = [scatter_halves(view, distance) for view, distance in zip(views, distances)]
    return [half[0] for half in halves], [half[1] for half in halves]


def join_all(keeps, others):
    return [keep.astype(F32) + other.astype(F32) for keep, other in zip(keeps, others)]


def far_steps(views, distances):
    for distance in distances:
        keeps, sends = halve_all(views, [distance] * len(views))
        widths = [send.shape[-1] for send in sends]
        merged = swap_seq(jnp.concatenate(sends, -1), distance)
        others, start = [], 0
        for wide in widths:
            others.append(lax.slice_in_dim(merged, start, start + wide, axis=merged.ndim - 1))
            start += wide
        views = join_all(keeps, others)
    return [view.reshape(view.shape[-2:]) for view in views]


def per_device(
    activations,
    log_decay,
    doc_starts,
    query_weight,
    key_weight,
    value_weight,
    beta_weight,
    gate_weight,
    out_weight,
    query_taps,
    key_taps,
    value_taps,
    mixer_gain,
    head_gain,
    feed_gain,
    feed_gate,
    feed_up,
    feed_down,
    cotangent,
):
    count, features = activations.shape
    tap_count = query_taps.shape[0]
    width = head_gain.shape[0]
    query_cols = query_weight.shape[1]
    key_cols = key_weight.shape[1]
    conv_cols = query_cols + 2 * key_cols
    hidden_cols = feed_gate.shape[1]
    head_count = query_cols // width
    beta_cols = beta_weight.shape[1]
    substeps = beta_cols // head_count
    device_rank = lax.axis_index("seq")
    head_rank = lax.axis_index("head")
    extra = 128
    shard_rows = query_weight.shape[0]
    pad = jnp.zeros((shard_rows, extra - beta_cols - 2), BF16)
    first_pack = jnp.concatenate(
        [
            query_weight,
            key_weight,
            value_weight,
            gate_weight,
            beta_weight,
            mixer_gain[:, None],
            feed_gain[:, None],
            pad,
        ],
        1,
    )
    second_pack = jnp.concatenate([out_weight.T, feed_gate, feed_up, feed_down.T], 1)
    first_full = lax.all_gather(first_pack, "seq", axis=0, tiled=True)
    first_full, second_pack = lax.optimization_barrier((first_full, second_pack))
    second_full = lax.all_gather(second_pack, "seq", axis=0, tiled=True)
    weight_conv = first_full[:, :conv_cols]
    weight_gate = first_full[:, conv_cols : conv_cols + query_cols]
    tail_cols = first_full[:, conv_cols + query_cols :]
    weight_beta = tail_cols[:, :beta_cols]
    gain_one = tail_cols[:, beta_cols].astype(F32)
    gain_two = tail_cols[:, beta_cols + 1].astype(F32)
    weight_out = second_full[:, :query_cols]
    weight_feed = second_full[:, query_cols : query_cols + 2 * hidden_cols]
    weight_down = second_full[:, query_cols + 2 * hidden_cols :]

    token_position = device_rank * count + jnp.arange(count, dtype=jnp.int32)
    is_start = jnp.any(token_position[:, None] == doc_starts[None, :], axis=1)

    def same_docs(position):
        doc = lambda p: jnp.sum((p[:, None] >= doc_starts[None, :]).astype(jnp.int32), axis=1)
        own = doc(position)
        return jnp.stack(
            [
                ((doc(position - offset) == own) & (position >= offset)).astype(F32)
                for offset in range(tap_count)
            ],
            1,
        )

    same = same_docs(token_position)
    log_gate = log_decay - RESET * is_start.astype(F32)[:, None]
    chunks = count // BLOCK
    cumulative = jnp.cumsum(log_gate.reshape(chunks, BLOCK, head_count), axis=1)
    cum_col = cumulative.reshape(count, head_count)
    cum_row = jnp.concatenate([jnp.swapaxes(cumulative, 1, 2)] * substeps, 2)
    taps_all = jnp.concatenate([query_taps, key_taps, value_taps], 1).astype(F32)

    inputs = activations.astype(F32)
    in_scale = lax.rsqrt(jnp.mean(inputs * inputs, axis=-1, keepdims=True) + NORM_EPS)
    normed = low(inputs * in_scale * gain_one)
    raw_all = low(product(normed, weight_conv))
    beta_gate = jax.nn.sigmoid(product(normed, weight_beta))
    gate_view = product(normed, weight_gate)
    edge = shift_seq(raw_all[count - HALO :], 1)
    t_part, p_part, s_part, q_reach, local_out, group = run_forward(
        raw_all, edge, taps_all, same, beta_gate, cum_col, cum_row, head_count, substeps, width
    )
    eye = jnp.broadcast_to(jnp.eye(width, dtype=F32), (head_count, width, width))
    state_low, kept = states_before(group, eye)

    by_head = lambda array: array.reshape(count, head_count, width)
    mixer_out = by_head(local_out) + jnp.einsum(
        "thk,hkv->thv", by_head(q_reach), state_low, preferred_element_type=F32
    )
    head_gain_f = head_gain.astype(F32)
    head_scale = lax.rsqrt(jnp.mean(mixer_out * mixer_out, axis=-1, keepdims=True) + NORM_EPS)
    head_unit = mixer_out * head_scale
    gate_view = by_head(gate_view)
    gate_sigma = jax.nn.sigmoid(gate_view)
    gate_act = gate_view * gate_sigma
    heads_out = low(head_unit * head_gain_f * gate_act).reshape(count, query_cols)
    hidden = inputs + head_sum(times_transposed(heads_out, weight_out))
    feed_scale = lax.rsqrt(jnp.mean(hidden * hidden, axis=-1, keepdims=True) + NORM_EPS)
    normed_ffn = low(hidden * feed_scale * gain_two)
    ffn = product(normed_ffn, weight_feed)
    ffn_gate, ffn_up = ffn[:, :hidden_cols], ffn[:, hidden_cols:]
    ffn_sigma = jax.nn.sigmoid(ffn_gate)
    activation = low(ffn_gate * ffn_sigma * ffn_up)
    branch_two = low(times_transposed(activation, weight_down))
    half = features // lax.axis_size("head")
    own_half = lambda array: lax.dynamic_slice_in_dim(array, head_rank * half, half, 1)
    other_half = lambda array: lax.dynamic_slice_in_dim(array, (1 - head_rank) * half, half, 1)
    output = low(
        own_half(hidden)
        + own_half(branch_two).astype(F32)
        + swap_head(other_half(branch_two)).astype(F32)
    )

    grad_result = cotangent.astype(F32)
    d_activation = product(cotangent, weight_down)
    d_up = low(d_activation * (ffn_gate * ffn_sigma))
    d_gate = low(d_activation * ffn_up * silu_slope(ffn_gate, ffn_sigma))
    orders, far = bit_orders(lax.axis_size("seq"))
    at_step = lambda k: [order[k] for order in orders]
    feed_keeps, feed_sends = halve_all(
        [
            scatter_view(inner_rows(normed_ffn, d_gate)),
            scatter_view(inner_rows(normed_ffn, d_up)),
            scatter_view(inner_rows(cotangent, activation)),
        ],
        at_step(0),
    )
    d_gate, d_up, feed_sends = lax.optimization_barrier((d_gate, d_up, feed_sends))
    feed_others = swap_all(feed_sends, at_step(0))
    d_ffn = jnp.concatenate([d_gate, d_up], 1)
    d_normed_ffn = head_sum(times_transposed(d_ffn, weight_feed))
    d_hidden_norm, feed_terms = norm_back(hidden, gain_two, d_normed_ffn)
    grad_feed_gain = jnp.sum(feed_terms, axis=0)
    d_hidden = grad_result + d_hidden_norm
    grad_mixer = low(d_hidden)
    d_heads = by_head(product(grad_mixer, weight_out))
    d_gate_logit = low(
        d_heads * head_unit * head_gain_f * silu_slope(gate_view, gate_sigma)
    ).reshape(count, query_cols)
    d_mixer_out, head_terms = norm_back(mixer_out, head_gain_f, d_heads * gate_act)
    head_gain_part = jnp.sum(head_terms, axis=(0, 1))
    d_mixer_low = low(d_mixer_out)
    own_part = jnp.einsum("thk,thv->hkv", by_head(q_reach), d_mixer_low, preferred_element_type=F32)
    adjoint = adjoints_after(own_part, kept, eye)

    side_views = [
        scatter_view(inner_rows(grad_mixer, heads_out)),
        scatter_view(inner_rows(normed, d_gate_logit)),
    ]
    chunks_at = [chunks - (chunks * k) // BACK_CALLS for k in range(BACK_CALLS + 1)]
    adjoint, feed_others = lax.optimization_barrier((adjoint, feed_others))
    feed_views = join_all(feed_keeps, feed_others)
    passed = (
        adjoint,
        jnp.zeros((8, conv_cols), F32),
        jnp.zeros((tap_count, conv_cols), F32),
        jnp.zeros((count, conv_cols), BF16),
        jnp.zeros((count, beta_cols), F32),
    )
    for call in range(BACK_CALLS):
        distances = (at_step(call + 1) if call < 2 else []) + at_step(call)[:2]
        last = call == BACK_CALLS - 1
        views = side_views if last else feed_views + side_views
        keeps, sends = halve_all(views, distances)
        first_passed, sends = lax.optimization_barrier((passed[0], sends))
        others = swap_all(sends, distances)
        if last:
            feed_sums = far_steps(feed_views, far)
        d_raw, d_beta_logit, new_tail, *carried = run_backward(
            chunks_at[call + 1], chunks_at[call],
            raw_all, edge, taps_all, same, beta_gate, cum_col, cum_row, t_part, p_part, s_part,
            state_low, d_mixer_low.reshape(count, query_cols), (first_passed,) + passed[1:],
            head_count, substeps, width,
        )
        if call == 0:
            tail = new_tail
        carried[0], others = lax.optimization_barrier((carried[0], others))
        passed = (*carried, d_raw, d_beta_logit)
        joined = join_all(keeps, others)
        if not last:
            feed_views = joined[:3]
        side_views = joined[-2:]
    first_rows, tap_grads = carried[1], carried[2]
    returned = shift_seq(first_rows, -1)
    same_after = same_docs(token_position[-1] + 1 + jnp.arange(8, dtype=jnp.int32))
    spread = jnp.zeros_like(tail)
    for offset in range(1, tap_count):
        masked = returned * same_after[:, offset : offset + 1] * taps_all[offset]
        spread = spread + jnp.pad(masked[:offset], ((8 - offset, 0), (0, 0)))
    d_raw = lax.dynamic_update_slice(d_raw, low(tail + spread), (count - 8, 0))
    d_beta_low = low(d_beta_logit)
    each = -(-conv_cols // (len(orders) * width)) * width
    keeps, sends = halve_all(
        [
            scatter_view(inner_rows(normed, d_raw[:, k * each : (k + 1) * each]))
            for k in range(len(orders))
        ],
        at_step(0),
    )
    d_raw, d_beta_low, sends = lax.optimization_barrier((d_raw, d_beta_low, sends))
    others = swap_all(sends, at_step(0))
    grad_beta = inner_rows(normed, d_beta_low)
    d_normed_part = times_transposed(d_raw, weight_conv) + (
        times_transposed(d_beta_low, weight_beta) + times_transposed(d_gate_logit, weight_gate)
    )
    d_normed = head_sum(low(d_normed_part).astype(F32))
    d_input_norm, mixer_terms = norm_back(inputs, gain_one, d_normed)
    grad_mixer_gain = jnp.sum(mixer_terms, axis=0)
    small = jnp.concatenate(
        [
            grad_beta.T.reshape(-1),
            grad_mixer_gain,
            grad_feed_gain,
            tap_grads.reshape(-1),
            head_gain_part + swap_head(head_gain_part),
        ]
    )
    small = jnp.pad(small, (0, -small.shape[0] % 1024)).reshape(-1, 128)
    small, d_input_norm, others = lax.optimization_barrier((small, d_input_norm, others))
    grad_input = own_half(d_hidden + d_input_norm)
    near = orders[0]
    for at in (1, 2):
        keeps, sends = halve_all(join_all(keeps, others), at_step(at))
        small, sends = lax.optimization_barrier((small, sends))
        others = swap_all(sends, at_step(at))
        small = small + swap_seq(small, near[at - 1])
        small, others = lax.optimization_barrier((small, others))
    conv_views = join_all(keeps, others)
    *conv_sums, side_out, side_gate = far_steps(conv_views + side_views, far)
    conv_sum = jnp.concatenate(conv_sums, 1)
    for distance in near[2:] + far:
        small = small + swap_seq(small, distance)
    small = small.reshape(-1)
    ends, at = [], 0
    for size in (beta_cols * features, features, features, tap_count * conv_cols, width):
        ends.append(small[at : at + size])
        at += size
    own_rows = lambda vector: lax.dynamic_slice_in_dim(
        vector, device_rank * shard_rows, shard_rows, vector.ndim - 1
    )
    tap_total = ends[3].reshape(tap_count, conv_cols)
    cut = lambda array, start, size: array[:, start : start + size]
    return (
        output,
        grad_input,
        cut(conv_sum, 0, query_cols),
        cut(conv_sum, query_cols, key_cols),
        cut(conv_sum, query_cols + key_cols, key_cols),
        own_rows(ends[0].reshape(beta_cols, features)).T,
        side_gate,
        side_out.T,
        cut(tap_total, 0, query_cols),
        cut(tap_total, query_cols, key_cols),
        cut(tap_total, query_cols + key_cols, key_cols),
        own_rows(ends[1]),
        ends[4],
        own_rows(ends[2]),
        feed_sums[0],
        feed_sums[1],
        feed_sums[2].T,
    )


def solution(mesh):
    in_specs = (
        P("seq", None),
        P("seq", "head"),
        P(),
        P("seq", "head"),
        P("seq", "head"),
        P("seq", "head"),
        P("seq", "head"),
        P("seq", "head"),
        P("head", "seq"),
        P(None, "head"),
        P(None, "head"),
        P(None, "head"),
        P("seq"),
        P(),
        P("seq"),
        P("seq", "head"),
        P("seq", "head"),
        P("head", "seq"),
        P("seq", None),
    )
    out_specs = (
        P("seq", "head"),
        P("seq", "head"),
        P("seq", "head"),
        P("seq", "head"),
        P("seq", "head"),
        P("seq", "head"),
        P("seq", "head"),
        P("head", "seq"),
        P(None, "head"),
        P(None, "head"),
        P(None, "head"),
        P("seq"),
        P(),
        P("seq"),
        P("seq", "head"),
        P("seq", "head"),
        P("head", "seq"),
    )
    return jax.shard_map(
        per_device, mesh=mesh, in_specs=in_specs, out_specs=out_specs, check_vma=False
    )
```

time: 971 us -> 666 us (0.69)
  waiting for transfers between devices: 380 us -> 217 us
  Pallas kernels: 238 us -> 125 us
  blocking collectives: 75.6 us -> 0 us
  matrix products: 126 us -> 100 us
  other arithmetic: 54.1 us -> 78.7 us
  starting transfers between devices: 24.7 us -> 49 us
  local copies, waits for them, and re-layouts: 48.5 us -> 70.1 us
    reduce_scatter x2 -> x0, waiting for transfers between devices: 223 us -> none  [the longest x1 202 us: per_device(): lax.psum_scatter(second_grads, 'seq', scatter_dimension=0, tiled=True)]
    pallas_call x1, Pallas kernels: 149 us -> 49.1 us  [run_forward(): pl.pallas_call(functools.partial(forward_kernel, head_count, substeps, wi...]
    psum x1 -> x0, blocking collectives: 75.6 us -> none  [per_device(): tap_total, grad_head_gain = lax.psum((tap_grads, head_gain_sum), 'seq')]
    ppermute x11 -> x38, waiting for transfers between devices: 43.7 us -> 105 us  [swap_seq(): lax.ppermute(array, 'seq', [(i, i ^ distance) for i in range(lax.axis_siz...]
    pallas_call x1 -> x3, Pallas kernels: 89 us -> 54.4 us  [run_backward(): pl.pallas_call(functools.partial(backward_kernel, head_count, substeps, w...]
    ppermute x11 -> x38, starting transfers between devices: 18.8 us -> 43.2 us  [swap_seq(): lax.ppermute(array, 'seq', [(i, i ^ distance) for i in range(lax.axis_siz...]
    pallas_call x0 -> x8, Pallas kernels: none -> 21.8 us  [the longest x4 11 us: join_back(): pl.pallas_call(functools.partial(back_kernel, final), in_specs=[pl.BlockS...]
    add x2 -> x28, other arithmetic: 4.83 us -> 23.5 us  [the longest x24 23.5 us: join_all(): keep.astype(F32) + other.astype(F32)]
  transfers between devices with their start and end apart: 22 -> 47, of which waited for: 17 -> 18; matrix products, arithmetic and copies ran while one was open for 13% -> 23% of each run, Pallas kernels for 15% -> 16%
where the time goes in v2:
time: 666 us; the launch traced here: 657 us
  waiting for transfers between devices  217 us (33%)
  Pallas kernels  125 us (19%)
  matrix products  100 us (15%)
  other arithmetic  78.7 us (12%)
  local copies, waits for them, and re-layouts  70.1 us (11%)
  starting transfers between devices  49 us (7%)
  between operations  16.8 us (3%)
    ppermute x38, waiting for transfers between devices, swap_seq(): lax.ppermute(array, 'seq', [(i, i ^ distance) for i in range(lax.axis_siz...  105 us
    all_gather x1, waiting for transfers between devices, per_device(): first_full = lax.all_gather(first_pack, 'seq', axis=0, tiled=True)  97.6 us
    pallas_call x3, Pallas kernels, run_backward(): pl.pallas_call(functools.partial(backward_kernel, head_count, substeps, w...  54.4 us
    pallas_call x1, Pallas kernels, run_forward(): pl.pallas_call(functools.partial(forward_kernel, head_count, substeps, wi...  49.1 us
    ppermute x38, starting transfers between devices, swap_seq(): lax.ppermute(array, 'seq', [(i, i ^ distance) for i in range(lax.axis_siz...  43.2 us
    dot_general x6, matrix products, product(): return jnp.dot(former, latter, preferred_element_type=F32)  36.7 us
    unnamed x195, local copies, waits for them, and re-layouts  32.4 us
    dot_general x9, matrix products, inner_rows(): lax.dot_general(former, latter, (((0,), (0,)), ((), ())), preferred_eleme...  32.1 us
  transfers between devices with their start and end apart: 47, of which 18 were waited for; matrix products, arithmetic and copies ran while one was open for 23% of the time, Pallas kernels for 16%

profile of v2, /device:TPU:0, one launch (start us, length us, event | category | flops | bytes accessed | tf_op | source)
XLA Modules:
  0.0 656.7 jit_solution(18356942971274799575)
XLA Ops:
  13.4 97.6 %all-gather.3.cloned.1.call-done = bf16[1024,3200]{1,0:T(8,128)(2,1)} async-done(((bf16[64,3200]{1,0:T(8,128)(2,1)}), bf16[1024,3200]{1,0:T(8,128)(2,1)}) %all-gather.3.cloned.1.call-update) | async-done | bytes 6553616 | tf_op jit(solution)/shard_map/all_gather | solution.py:722
  111.6 6.3 fusion.75
  127.3 9.2 %convolution_convert_fusion.raw.before = bf16[1024,2560]{1,0:T(8,128)(2,1)S(1)} fusion(bf16[1024,1024]{0,1:T(8,128)(2,1)S(1)} %fusion.18, bf16[1024,3200]{1,0:T(8,128)(2,1)} %all-gather.3.cloned.1.call-done), kind=kOutput, calls=%fused_computation.19 | convolution fusion | flops 5371330560 | bytes 12582912 | tf_op jit(solution)/shard_map/dot_general | solution.py:21
  142.0 49.1 %mixer_forward.1 = (bf16[16,4,128,128]{3,2,1,0:T(8,128)(2,1)S(1)}, bf16[16,4,128,128]{3,2,1,0:T(8,128)(2,1)}, bf16[16,4,128,128]{3,2,1,0:T(8,128)(2,1)}, bf16[10...) custom-call(bf16[1024,2560]{1,0:T(8,128)(2,1)} %copy-done.5, ...), custom_call_target="tpu_custom_call" | custom-call | tf_op jit(solution)/shard_map/mixer_forward/pallas_call | solution.py:220
  196.7 10.7 %collective-permute-done.1.other.other_map = bf16[4,128,256]{2,1,0:T(8,128)(2,1)S(1)} collective-permute-done((bf16[4,128,256]{2,1,0:T(8,128)(2,1)S(1)}, bf16[4,128,256]{2,1,0:T(8,128)(2,1)S(1)}, u32[]{:S(2)}, u32[]{:S(2)}) %collective-permute-start.1) | collective-permute-done | bytes 262176 | tf_op jit(solution)/shard_map/ppermute | solution.py:490
  213.7 7.0 %collective-permute-done.2.other.other_map = bf16[4,128,256]{2,1,0:T(8,128)(2,1)S(1)} collective-permute-done((bf16[4,128,256]{2,1,0:T(8,128)(2,1)}, bf16[4,128,256]{2,1,0:T(8,128)(2,1)S(1)}, u32[]{:S(2)}, u32[]{:S(2)}) %collective-permute-start.2) | collective-permute-done | bytes 262176 | tf_op jit(solution)/shard_map/ppermute | solution.py:490
  225.7 20.1 %collective-permute-done.3.other.other_map = bf16[4,128,256]{2,1,0:T(8,128)(2,1)S(1)} collective-permute-done((bf16[4,128,256]{2,1,0:T(8,128)(2,1)}, bf16[4,128,256]{2,1,0:T(8,128)(2,1)S(1)}, u32[]{:S(2)}, u32[]{:S(2)}) %collective-permute-start.3) | collective-permute-done | bytes 262176 | tf_op jit(solution)/shard_map/ppermute | solution.py:490
  254.2 8.7 %collective-permute-done.4.other.other_map = bf16[4,128,256]{2,1,0:T(8,128)(2,1)S(1)} collective-permute-done((bf16[4,128,256]{2,1,0:T(8,128)(2,1)}, bf16[4,128,256]{2,1,0:T(8,128)(2,1)S(1)}, u32[]{:S(2)}, u32[]{:S(2)}) %collective-permute-start.4) | collective-permute-done | bytes 262176 | tf_op jit(solution)/shard_map/ppermute | solution.py:490
  274.1 4.8 fusion.44
  278.9 7.5 %collective-permute-done.5 = f32[1024,1024]{0,1:T(8,128)} collective-permute-done((f32[1024,1024]{0,1:T(8,128)}, f32[1024,1024]{0,1:T(8,128)}, u32[]{:S(2)}, u32[]{:S(2)}) %collective-permute-start.5) | collective-permute-done | bytes 4194336 | tf_op jit(solution)/shard_map/ppermute | solution.py:494
  286.4 5.9 multiply_reduce_fusion.2
  294.3 9.1 %fusion.13 = f32[1024,2816]{1,0:T(8,128)} fusion(bf16[1024,1024]{0,1:T(8,128)(2,1)S(1)} %multiply_convert_fusion.1, bf16[1024,4736]{1,0:T(8,128)(2,1)S(1)} %copy-done.84), kind=kOutput, calls=%fused_computation.21 | convolution fusion | flops 5905580032 | bytes 19398656 | tf_op jit(solution)/shard_map/dot_general | solution.py:21
  303.4 9.3 %fusion.10 = (bf16[1024,1408]{1,0:T(8,128)(2,1)S(1)}, bf16[1024,1408]{1,0:T(8,128)(2,1)S(1)}, bf16[1024,1408]{1,0:T(8,128)(2,1)}) fusion(f32[1024,2816]{1,0:T(8,128)} %fusion.13, bf16[1024,1024]{1,0:T(8,128)(2,1)S(1)} %copy-done.38, bf16[1024,4736]{1,0:T(8,128)(2,1)S(1)} %copy-done.84), kind=kOutput, calls=%fused_computation.15 | convolution fusion | flops 2974416896 | bytes 25165824 | tf_op jit(solution)/shard_map/dot_general | solution.py:21
  319.5 7.6 %fusion.78 = f32[1408,1024]{0,1:T(8,128)S(1)} fusion(bf16[1024,1408]{1,0:T(8,128)(2,1)} %get-tuple-element.349, bf16[1024,1024]{1,0:T(8,128)(2,1)S(1)} %copy-done.38), kind=kOutput, calls=%fused_computation.223 | convolution fusion | flops 2952790016 | bytes 10747904 | tf_op jit(solution)/shard_map/dot_general | solution.py:25
  331.8 7.7 %fusion.4 = f32[1024,1024]{0,1:T(8,128)} fusion(bf16[1024,1408]{1,0:T(8,128)(2,1)S(1)} %get-tuple-element.143, bf16[1024,1408]{1,0:T(8,128)(2,1)S(1)} %get-tuple-element.142, bf16[1024,4736]{1,0:T(8,128)(2,1)S(1)} %copy-done.84), kind=kOutput, calls=%fused_computation.7 | convolution fusion | flops 5917114368 | bytes 15728640 | tf_op jit(solution)/shard_map/dot_general | solution.py:29
  347.0 6.1 multiply_reduce_fusion
  353.1 6.1 fusion.71
  370.2 10.2 %collective-permute-done.8.other = bf16[4,128,128]{2,1,0:T(8,128)(2,1)S(1)} collective-permute-done((bf16[4,128,128]{2,1,0:T(8,128)(2,1)S(1)}, bf16[4,128,128]{2,1,0:T(8,128)(2,1)S(1)}, u32[]{:S(2)}, u32[]{:S(2)}) %collective-permute-start.8) | collective-permute-done | bytes 131104 | tf_op jit(solution)/shard_map/ppermute | solution.py:490
  384.7 4.5 fusion.79
  393.2 4.5 fusion.80
  435.5 16.9 %mixer_backward.3 = (bf16[1024,2560]{1,0:T(8,128)(2,1)}, f32[1024,8]{1,0:T(8,128)S(1)}, f32[8,2560]{1,0:T(8,128)S(1)}, f32[4,128,128]{2,1,0:T(8,128)S(1)}, f32[8,2560]{1,0:T(8,128)S(1)}, /*index=5*/f32[4,2560]{1,0:T(4,128)S(1)}) custom-call(bf16[1024,2560]{1,0:T(8,128)(2,1)} %copy-done.5, ...), custom_call_target="tpu_custom_call", output_to_operand_aliasing={{0}: (17, {}), {1}: (18, {})} | custom-call | tf_op jit(solution)/shard_map/mixer_backward/pallas_call | solution.py:425
  467.5 5.5 fusion.29
  473.0 17.4 %mixer_backward.4 = (bf16[1024,2560]{1,0:T(8,128)(2,1)}, f32[1024,8]{1,0:T(8,128)S(1)}, f32[8,2560]{1,0:T(8,128)}, f32[4,128,128]{2,1,0:T(8,128)S(1)}, f32[8,2560]{1,0:T(8,128)S(1)}, /*index=5*/f32[4,2560]{1,0:T(4,128)S(1)}) custom-call(bf16[1024,2560]{1,0:T(8,128)(2,1)} %copy-done.5, ...), custom_call_target="tpu_custom_call", output_to_operand_aliasing={{0}: (17, {}), {1}: (18, {})} | custom-call | tf_op jit(solution)/shard_map/mixer_backward/pallas_call | solution.py:425
  491.5 20.0 %mixer_backward.5 = (bf16[1024,2560]{1,0:T(8,128)(2,1)}, f32[1024,8]{1,0:T(8,128)S(1)}, f32[8,2560]{1,0:T(8,128)}, f32[4,128,128]{2,1,0:T(8,128)}, f32[8,2560]{1,0:T(8,128)S(1)}, /*index=5*/f32[4,2560]{1,0:T(4,128)S(1)}) custom-call(bf16[1024,2560]{1,0:T(8,128)(2,1)} %copy-done.5, ...), custom_call_target="tpu_custom_call", output_to_operand_aliasing={{0}: (17, {}), {1}: (18, {})} | custom-call | tf_op jit(solution)/shard_map/mixer_backward/pallas_call | solution.py:425
  513.4 4.6 collective-permute-done.25
  530.3 5.6 fusion.15
  560.0 5.0 fusion.20
  565.1 4.7 fusion.22
  569.8 19.8 %collective-permute-done.30 = bf16[2,1,2,2,64,768]{5,4,3,2,1,0:T(8,128)(2,1)S(1)} collective-permute-done((bf16[2,1,2,2,64,768]{5,4,3,2,1,0:T(8,128)(2,1)S(1)}, bf16[2,1,2,2,64,768]{5,4,3,2,1,0:T(8,128)(2,1)S(1)}, u32[]{:S(2)}, u32[]{:S(2)}) %collective-permute-start.30) | collective-permute-done | bytes 786464 | tf_op jit(solution)/shard_map/ppermute | solution.py:490
  595.5 8.2 %collective-permute-done.31 = f32[168,128]{1,0:T(8,128)S(1)} collective-permute-done((f32[168,128]{1,0:T(8,128)S(1)}, f32[168,128]{1,0:T(8,128)S(1)}, u32[]{:S(2)}, u32[]{:S(2)}) %collective-permute-start.31) | collective-permute-done | bytes 86048 | tf_op jit(solution)/shard_map/ppermute | solution.py:490
  631.5 7.7 %collective-permute-done.43 = f32[168,128]{1,0:T(8,128)S(1)} collective-permute-done((f32[168,128]{1,0:T(8,128)S(1)}, f32[168,128]{1,0:T(8,128)S(1)}, u32[]{:S(2)}, u32[]{:S(2)}) %collective-permute-start.43) | collective-permute-done | bytes 86048 | tf_op jit(solution)/shard_map/ppermute | solution.py:490
  642.8 4.3 collective-permute-done.41
  (445 shorter events, 228.2 us)
Async XLA Ops:
  7.2 103.8 %all-gather.3.cloned.1.call-start = ((), (), s32[]{:S(2)}) async-start(), calls=%async_computation | async-start | bytes 6963200 | tf_op jit(solution)/shard_map/all_gather | solution.py:722
  11.4 262.6 %all-gather.5.cloned.1.call-start = ((), (), s32[]{:S(2)}) async-start(), calls=%async_computation.1 | async-start | bytes 10305536 | tf_op jit(solution)/shard_map/all_gather | solution.py:724
  193.4 14.1 %collective-permute-start.1 = (bf16[4,128,256]{2,1,0:T(8,128)(2,1)S(1)}, bf16[4,128,256]{2,1,0:T(8,128)(2,1)S(1)}, u32[]{:S(2)}, u32[]{:S(2)}) collective-permute-start(bf16[4,128,256]{2,1,0:T(8,128)(2,1)S(1)} %convert_element_type.387), channel_id=1, source_target_pairs={{0,2},{2,0},{4,6},{6,4},{8,10},{10,8},{12,14},{14,12},{16,18},{18,... | collective-permute-start | bytes 786440 | tf_op jit(solution)/shard_map/ppermute | solution.py:490
  224.2 21.6 %collective-permute-start.3 = (bf16[4,128,256]{2,1,0:T(8,128)(2,1)}, bf16[4,128,256]{2,1,0:T(8,128)(2,1)S(1)}, u32[]{:S(2)}, u32[]{:S(2)}) collective-permute-start(bf16[4,128,256]{2,1,0:T(8,128)(2,1)} %get-tuple-element.134), channel_id=1, source_target_pairs={{0,8},{2,10},{4,12},{6,14},{8,0},{10,2},{12,4},{14,6},{16,24},{18,... | collective-permute-start | bytes 786440 | tf_op jit(solution)/shard_map/ppermute | solution.py:490
  249.3 13.6 %collective-permute-start.4 = (bf16[4,128,256]{2,1,0:T(8,128)(2,1)}, bf16[4,128,256]{2,1,0:T(8,128)(2,1)S(1)}, u32[]{:S(2)}, u32[]{:S(2)}) collective-permute-start(bf16[4,128,256]{2,1,0:T(8,128)(2,1)} %get-tuple-element.137), channel_id=1, source_target_pairs={{0,16},{2,18},{4,20},{6,22},{8,24},{10,26},{12,28},{14,30},{16,0},... | collective-permute-start | bytes 786440 | tf_op jit(solution)/shard_map/ppermute | solution.py:490
  343.5 70.1 %collective-permute-start.12 = (bf16[2,2,2,1,64,1408]{5,4,3,2,1,0:T(8,128)(2,1)}, bf16[2,2,2,1,64,1408]{5,4,3,2,1,0:T(8,128)(2,1)}, u32[]{:S(2)}, u32[]{:S(2)}) collective-permute-start(bf16[2,2,2,1,64,1408]{5,4,3,2,1,0:T(8,128)(2,1)} %dynamic-slice_convert_fusion.2), channel_id=1, source_target_pairs={{0,2},{2,0},{4,6},{6,4},{8,10},{10,8},{12,14},{14,12},{16,18},{18,... | collective-permute-start | bytes 4325384 | tf_op jit(solution)/shard_map/ppermute | solution.py:490
  345.2 68.4 %collective-permute-start.13 = (bf16[2,2,1,2,64,1408]{5,4,3,2,1,0:T(8,128)(2,1)}, bf16[2,2,1,2,64,1408]{5,4,3,2,1,0:T(8,128)(2,1)}, u32[]{:S(2)}, u32[]{:S(2)}) collective-permute-start(bf16[2,2,1,2,64,1408]{5,4,3,2,1,0:T(8,128)(2,1)} %dynamic-slice_convert_fusion.1), channel_id=1, source_target_pairs={{0,4},{2,6},{4,0},{6,2},{8,12},{10,14},{12,8},{14,10},{16,20},{18,... | collective-permute-start | bytes 4325384 | tf_op jit(solution)/shard_map/ppermute | solution.py:490
  345.7 68.0 %collective-permute-start.14 = (bf16[2,1,2,2,64,1408]{5,4,3,2,1,0:T(8,128)(2,1)}, bf16[2,1,2,2,64,1408]{5,4,3,2,1,0:T(8,128)(2,1)}, u32[]{:S(2)}, u32[]{:S(2)}) collective-permute-start(bf16[2,1,2,2,64,1408]{5,4,3,2,1,0:T(8,128)(2,1)} %dynamic-slice_convert_fusion), channel_id=1, source_target_pairs={{0,8},{2,10},{4,12},{6,14},{8,0},{10,2},{12,4},{14,6},{16,24},{18,... | collective-permute-start | bytes 4325384 | tf_op jit(solution)/shard_map/ppermute | solution.py:490
  368.5 11.9 %collective-permute-start.8 = (bf16[4,128,128]{2,1,0:T(8,128)(2,1)S(1)}, bf16[4,128,128]{2,1,0:T(8,128)(2,1)S(1)}, u32[]{:S(2)}, u32[]{:S(2)}) collective-permute-start(bf16[4,128,128]{2,1,0:T(8,128)(2,1)S(1)} %get-tuple-element.372), channel_id=1, source_target_pairs={{0,2},{2,0},{4,6},{6,4},{8,10},{10,8},{12,14},{14,12},{16,18},{18,... | collective-permute-start | bytes 393224 | tf_op jit(solution)/shard_map/ppermute | solution.py:490
  424.9 29.4 %collective-permute-start.15 = (bf16[2,2,1,1,64,1408]{5,4,3,2,1,0:T(8,128)(2,1)}, bf16[2,2,1,1,64,1408]{5,4,3,2,1,0:T(8,128)(2,1)}, u32[]{:S(2)}, u32[]{:S(2)}) collective-permute-start(bf16[2,2,1,1,64,1408]{5,4,3,2,1,0:T(8,128)(2,1)} %dynamic-slice_convert_fusion.8), channel_id=1, source_target_pairs={{0,4},{2,6},{4,0},{6,2},{8,12},{10,14},{12,8},{14,10},{16,20},{18,... | collective-permute-start | bytes 2162696 | tf_op jit(solution)/shard_map/ppermute | solution.py:490
  425.3 29.0 %collective-permute-start.16 = (bf16[2,1,1,2,64,1408]{5,4,3,2,1,0:T(8,128)(2,1)}, bf16[2,1,1,2,64,1408]{5,4,3,2,1,0:T(8,128)(2,1)}, u32[]{:S(2)}, u32[]{:S(2)}) collective-permute-start(bf16[2,1,1,2,64,1408]{5,4,3,2,1,0:T(8,128)(2,1)} %dynamic-slice_convert_fusion.7), channel_id=1, source_target_pairs={{0,8},{2,10},{4,12},{6,14},{8,0},{10,2},{12,4},{14,6},{16,24},{18,... | collective-permute-start | bytes 2162696 | tf_op jit(solution)/shard_map/ppermute | solution.py:490
  425.3 29.0 %collective-permute-start.17 = (bf16[2,1,2,1,64,1408]{5,4,3,2,1,0:T(8,128)(2,1)}, bf16[2,1,2,1,64,1408]{5,4,3,2,1,0:T(8,128)(2,1)}, u32[]{:S(2)}, u32[]{:S(2)}) collective-permute-start(bf16[2,1,2,1,64,1408]{5,4,3,2,1,0:T(8,128)(2,1)} %dynamic-slice_convert_fusion.6), channel_id=1, source_target_pairs={{0,2},{2,0},{4,6},{6,4},{8,10},{10,8},{12,14},{14,12},{16,18},{18,... | collective-permute-start | bytes 2162696 | tf_op jit(solution)/shard_map/ppermute | solution.py:490
  427.6 26.7 %collective-permute-start.18 = (bf16[2,2,2,1,64,512]{5,4,3,2,1,0:T(8,128)(2,1)}, bf16[2,2,2,1,64,512]{5,4,3,2,1,0:T(8,128)(2,1)}, u32[]{:S(2)}, u32[]{:S(2)}) collective-permute-start(bf16[2,2,2,1,64,512]{5,4,3,2,1,0:T(8,128)(2,1)} %dynamic-slice_convert_fusion.10), channel_id=1, source_target_pairs={{0,2},{2,0},{4,6},{6,4},{8,10},{10,8},{12,14},{14,12},{16,18},{18,... | collective-permute-start | bytes 1572872 | tf_op jit(solution)/shard_map/ppermute | solution.py:490
  428.7 25.6 %collective-permute-start.19 = (bf16[2,2,1,2,64,512]{5,4,3,2,1,0:T(8,128)(2,1)S(1)}, bf16[2,2,1,2,64,512]{5,4,3,2,1,0:T(8,128)(2,1)}, u32[]{:S(2)}, u32[]{:S(2)}) collective-permute-start(bf16[2,2,1,2,64,512]{5,4,3,2,1,0:T(8,128)(2,1)S(1)} %dynamic-slice_convert_fusion.9), channel_id=1, source_target_pairs={{0,4},{2,6},{4,0},{6,2},{8,12},{10,14},{12,8},{14,10},{16,20},{18,... | collective-permute-start | bytes 1572872 | tf_op jit(solution)/shard_map/ppermute | solution.py:490
  463.1 27.3 %collective-permute-start.20 = (bf16[2,1,1,1,64,1408]{5,4,3,2,1,0:T(8,128)(2,1)S(1)}, bf16[2,1,1,1,64,1408]{5,4,3,2,1,0:T(8,128)(2,1)S(1)}, u32[]{:S(2)}, u32[]{:S(2)}) collective-permute-start(bf16[2,1,1,1,64,1408]{5,4,3,2,1,0:T(8,128)(2,1)S(1)} %dynamic-slice_convert_fusion.16), channel_id=1, source_target_pairs={{0,8},{2,10},{4,12},{6,14},{8,0},{10,2},{12,4},{14,6},{16,24},{18,... | collective-permute-start | bytes 1081352 | tf_op jit(solution)/shard_map/ppermute | solution.py:490
  464.9 25.5 %collective-permute-start.21 = (bf16[2,1,1,1,64,1408]{5,4,3,2,1,0:T(8,128)(2,1)S(1)}, bf16[2,1,1,1,64,1408]{5,4,3,2,1,0:T(8,128)(2,1)S(1)}, u32[]{:S(2)}, u32[]{:S(2)}) collective-permute-start(bf16[2,1,1,1,64,1408]{5,4,3,2,1,0:T(8,128)(2,1)S(1)} %dynamic-slice_convert_fusion.15), channel_id=1, source_target_pairs={{0,2},{2,0},{4,6},{6,4},{8,10},{10,8},{12,14},{14,12},{16,18},{18,... | collective-permute-start | bytes 1081352 | tf_op jit(solution)/shard_map/ppermute | solution.py:490
  465.2 25.3 %collective-permute-start.22 = (bf16[2,1,1,1,64,1408]{5,4,3,2,1,0:T(8,128)(2,1)S(1)}, bf16[2,1,1,1,64,1408]{5,4,3,2,1,0:T(8,128)(2,1)S(1)}, u32[]{:S(2)}, u32[]{:S(2)}) collective-permute-start(bf16[2,1,1,1,64,1408]{5,4,3,2,1,0:T(8,128)(2,1)S(1)} %dynamic-slice_convert_fusion.14), channel_id=1, source_target_pairs={{0,4},{2,6},{4,0},{6,2},{8,12},{10,14},{12,8},{14,10},{16,20},{18,... | collective-permute-start | bytes 1081352 | tf_op jit(solution)/shard_map/ppermute | solution.py:490
  467.0 23.5 %collective-permute-start.23 = (bf16[2,2,1,1,64,512]{5,4,3,2,1,0:T(8,128)(2,1)S(1)}, bf16[2,2,1,1,64,512]{5,4,3,2,1,0:T(8,128)(2,1)S(1)}, u32[]{:S(2)}, u32[]{:S(2)}) collective-permute-start(bf16[2,2,1,1,64,512]{5,4,3,2,1,0:T(8,128)(2,1)S(1)} %dynamic-slice_convert_fusion.18), channel_id=1, source_target_pairs={{0,4},{2,6},{4,0},{6,2},{8,12},{10,14},{12,8},{14,10},{16,20},{18,... | collective-permute-start | bytes 786440 | tf_op jit(solution)/shard_map/ppermute | solution.py:490
  467.2 23.2 %collective-permute-start.24 = (bf16[2,1,1,2,64,512]{5,4,3,2,1,0:T(8,128)(2,1)S(1)}, bf16[2,1,1,2,64,512]{5,4,3,2,1,0:T(8,128)(2,1)S(1)}, u32[]{:S(2)}, u32[]{:S(2)}) collective-permute-start(bf16[2,1,1,2,64,512]{5,4,3,2,1,0:T(8,128)(2,1)S(1)} %dynamic-slice_convert_fusion.17), channel_id=1, source_target_pairs={{0,8},{2,10},{4,12},{6,14},{8,0},{10,2},{12,4},{14,6},{16,24},{18,... | collective-permute-start | bytes 786440 | tf_op jit(solution)/shard_map/ppermute | solution.py:490
  513.3 27.3 %collective-permute-start.6 = (bf16[1024,512]{0,1:T(8,128)(2,1)S(1)}, bf16[1024,512]{0,1:T(8,128)(2,1)}, u32[]{:S(2)}, u32[]{:S(2)}) collective-permute-start(bf16[1024,512]{0,1:T(8,128)(2,1)S(1)} %constant_dynamic-slice_fusion.1), channel_id=1, source_target_pairs={{0,1},{1,0},{2,3},{3,2},{4,5},{5,4},{6,7},{7,6},{8,9},{9,8},{10,11... | collective-permute-start | bytes 3145736 | tf_op jit(solution)/shard_map/ppermute | solution.py:494
  540.6 18.9 %collective-permute-start.26 = (f32[1024,1024]{0,1:T(8,128)}, f32[1024,1024]{0,1:T(8,128)}, u32[]{:S(2)}, u32[]{:S(2)}) collective-permute-start(f32[1024,1024]{0,1:T(8,128)} %fusion.32), channel_id=1, source_target_pairs={{0,1},{1,0},{2,3},{3,2},{4,5},{5,4},{6,7},{7,6},{8,9},{9,8},{10,11... | collective-permute-start | bytes 12582920 | tf_op jit(solution)/shard_map/ppermute | solution.py:494
  547.0 18.0 %collective-permute-start.27 = (f32[128]{0:T(128)S(1)}, f32[128]{0:T(128)S(1)}, u32[]{:S(2)}, u32[]{:S(2)}) collective-permute-start(f32[128]{0:T(128)S(1)} %copy-done.83), channel_id=1, source_target_pairs={{0,1},{1,0},{2,3},{3,2},{4,5},{5,4},{6,7},{7,6},{8,9},{9,8},{10,11... | collective-permute-start | bytes 1544 | tf_op jit(solution)/shard_map/ppermute | solution.py:494
  555.9 54.1 %collective-permute-start.44 = (bf16[1,1,1,1,64,4224]{5,4,3,2,1,0:T(8,128)(2,1)S(1)}, bf16[1,1,1,1,64,4224]{5,4,3,2,1,0:T(8,128)(2,1)S(1)}, u32[]{:S(2)}, u32[]{:S(2)}) collective-permute-start(bf16[1,1,1,1,64,4224]{5,4,3,2,1,0:T(8,128)(2,1)S(1)} %pad_maximum_fusion.1), channel_id=1, source_target_pairs={{0,16},{2,18},{4,20},{6,22},{8,24},{10,26},{12,28},{14,30},{16,0},... | collective-permute-start | bytes 1622024 | tf_op jit(solution)/shard_map/ppermute | solution.py:490
  556.7 32.9 %collective-permute-start.28 = (bf16[2,2,2,1,64,896]{5,4,3,2,1,0:T(8,128)(2,1)S(1)}, bf16[2,2,2,1,64,896]{5,4,3,2,1,0:T(8,128)(2,1)S(1)}, u32[]{:S(2)}, u32[]{:S(2)}) collective-permute-start(bf16[2,2,2,1,64,896]{5,4,3,2,1,0:T(8,128)(2,1)S(1)} %copy-done.59), channel_id=1, source_target_pairs={{0,2},{2,0},{4,6},{6,4},{8,10},{10,8},{12,14},{14,12},{16,18},{18,... | collective-permute-start | bytes 2752520 | tf_op jit(solution)/shard_map/ppermute | solution.py:490
  557.6 32.0 %collective-permute-start.29 = (bf16[2,2,1,2,64,896]{5,4,3,2,1,0:T(8,128)(2,1)S(1)}, bf16[2,2,1,2,64,896]{5,4,3,2,1,0:T(8,128)(2,1)S(1)}, u32[]{:S(2)}, u32[]{:S(2)}) collective-permute-start(bf16[2,2,1,2,64,896]{5,4,3,2,1,0:T(8,128)(2,1)S(1)} %copy-done.58), channel_id=1, source_target_pairs={{0,4},{2,6},{4,0},{6,2},{8,12},{10,14},{12,8},{14,10},{16,20},{18,... | collective-permute-start | bytes 2752520 | tf_op jit(solution)/shard_map/ppermute | solution.py:490
  559.5 30.1 %collective-permute-start.30 = (bf16[2,1,2,2,64,768]{5,4,3,2,1,0:T(8,128)(2,1)S(1)}, bf16[2,1,2,2,64,768]{5,4,3,2,1,0:T(8,128)(2,1)S(1)}, u32[]{:S(2)}, u32[]{:S(2)}) collective-permute-start(bf16[2,1,2,2,64,768]{5,4,3,2,1,0:T(8,128)(2,1)S(1)} %copy-done.61), channel_id=1, source_target_pairs={{0,8},{2,10},{4,12},{6,14},{8,0},{10,2},{12,4},{14,6},{16,24},{18,... | collective-permute-start | bytes 2359304 | tf_op jit(solution)/shard_map/ppermute | solution.py:490
  592.1 11.7 %collective-permute-start.32 = (bf16[2,2,1,1,64,896]{5,4,3,2,1,0:T(8,128)(2,1)S(1)}, bf16[2,2,1,1,64,896]{5,4,3,2,1,0:T(8,128)(2,1)S(1)}, u32[]{:S(2)}, u32[]{:S(2)}) collective-permute-start(bf16[2,2,1,1,64,896]{5,4,3,2,1,0:T(8,128)(2,1)S(1)} %dynamic-slice_convert_fusion.12), channel_id=1, source_target_pairs={{0,4},{2,6},{4,0},{6,2},{8,12},{10,14},{12,8},{14,10},{16,20},{18,... | collective-permute-start | bytes 1376264 | tf_op jit(solution)/shard_map/ppermute | solution.py:490
  592.6 11.2 %collective-permute-start.33 = (bf16[2,1,1,2,64,896]{5,4,3,2,1,0:T(8,128)(2,1)S(1)}, bf16[2,1,1,2,64,896]{5,4,3,2,1,0:T(8,128)(2,1)S(1)}, u32[]{:S(2)}, u32[]{:S(2)}) collective-permute-start(bf16[2,1,1,2,64,896]{5,4,3,2,1,0:T(8,128)(2,1)S(1)} %dynamic-slice_convert_fusion.11), channel_id=1, source_target_pairs={{0,8},{2,10},{4,12},{6,14},{8,0},{10,2},{12,4},{14,6},{16,24},{18,... | collective-permute-start | bytes 1376264 | tf_op jit(solution)/shard_map/ppermute | solution.py:490
  592.6 11.1 %collective-permute-start.34 = (bf16[2,1,2,1,64,768]{5,4,3,2,1,0:T(8,128)(2,1)S(1)}, bf16[2,1,2,1,64,768]{5,4,3,2,1,0:T(8,128)(2,1)S(1)}, u32[]{:S(2)}, u32[]{:S(2)}) collective-permute-start(bf16[2,1,2,1,64,768]{5,4,3,2,1,0:T(8,128)(2,1)S(1)} %dynamic-slice_convert_fusion.13), channel_id=1, source_target_pairs={{0,2},{2,0},{4,6},{6,4},{8,10},{10,8},{12,14},{14,12},{16,18},{18,... | collective-permute-start | bytes 1179656 | tf_op jit(solution)/shard_map/ppermute | solution.py:490
  605.5 10.7 %collective-permute-start.36 = (bf16[2,1,1,1,64,896]{5,4,3,2,1,0:T(8,128)(2,1)}, bf16[2,1,1,1,64,896]{5,4,3,2,1,0:T(8,128)(2,1)S(1)}, u32[]{:S(2)}, u32[]{:S(2)}) collective-permute-start(bf16[2,1,1,1,64,896]{5,4,3,2,1,0:T(8,128)(2,1)} %dynamic-slice_convert_fusion.20), channel_id=1, source_target_pairs={{0,8},{2,10},{4,12},{6,14},{8,0},{10,2},{12,4},{14,6},{16,24},{18,... | collective-permute-start | bytes 688136 | tf_op jit(solution)/shard_map/ppermute | solution.py:490
  626.9 12.2 %collective-permute-start.43 = (f32[168,128]{1,0:T(8,128)S(1)}, f32[168,128]{1,0:T(8,128)S(1)}, u32[]{:S(2)}, u32[]{:S(2)}) collective-permute-start(f32[168,128]{1,0:T(8,128)S(1)} %add.527), channel_id=1, source_target_pairs={{0,16},{2,18},{4,20},{6,22},{8,24},{10,26},{12,28},{14,30},{16,0},... | collective-permute-start | bytes 258056 | tf_op jit(solution)/shard_map/ppermute | solution.py:490
  628.6 18.5 %collective-permute-start.41 = (bf16[1,1,1,1,64,3584]{5,4,3,2,1,0:T(8,128)(2,1)}, bf16[1,1,1,1,64,3584]{5,4,3,2,1,0:T(8,128)(2,1)S(1)}, u32[]{:S(2)}, u32[]{:S(2)}) collective-permute-start(bf16[1,1,1,1,64,3584]{5,4,3,2,1,0:T(8,128)(2,1)} %fusion.57), channel_id=1, source_target_pairs={{0,16},{2,18},{4,20},{6,22},{8,24},{10,26},{12,28},{14,30},{16,0},... | collective-permute-start | bytes 1376264 | tf_op jit(solution)/shard_map/ppermute | solution.py:490
  (106 other events, 1032.9 us)
Sparse Core Ops, SparseCore 0:
  11.6 99.3 all-gather.2
  113.7 133.3 all-gather.4

commit v3 on v2

v3 whole, which is shorter than its diff:
```python
import functools

import jax
import jax.numpy as jnp
from jax import lax
from jax.experimental import pallas as pl
from jax.experimental.pallas import tpu as pltpu
from jax.sharding import PartitionSpec as P

BLOCK = 64
RESET = 256.0
HALO = 16
VMEM_BYTES = 63 * 1024 * 1024
PAIR = 2
QUERY_CHUNKS = 2
TILE = 256
AHEAD_CALLS = 3
NORM_EPS = 1e-05
UNIT_EPS = 1e-06
F32 = jnp.float32
BF16 = jnp.bfloat16


def product(former, latter):
    return jnp.dot(former, latter, preferred_element_type=F32)


def inner_rows(former, latter):
    return lax.dot_general(former, latter, (((0,), (0,)), ((), ())), preferred_element_type=F32)


def times_transposed(former, latter):
    return lax.dot_general(former, latter, (((1,), (1,)), ((), ())), preferred_element_type=F32)


def low(values):
    return values.astype(BF16)


def split(values):
    high = values.astype(BF16)
    return high, (values - high.astype(F32)).astype(BF16)


def fine(form, former, latter):
    a_high, a_low = split(former)
    b_high, b_low = split(latter)
    return form(a_high, b_high) + (form(a_low, b_high) + form(a_high, b_low))


def silu_slope(values, sigma):
    return sigma * (1.0 + values * (1.0 - sigma))


def norm_back(values, gain_vector, gradient):
    row_scale = lax.rsqrt(jnp.mean(values * values, axis=-1, keepdims=True) + NORM_EPS)
    unit_value = values * row_scale
    scaled_grad = gradient * gain_vector
    back_value = row_scale * (
        scaled_grad - unit_value * jnp.mean(scaled_grad * unit_value, axis=-1, keepdims=True)
    )
    return (back_value, gradient * unit_value)


def row_maps(rows):
    row = lax.broadcasted_iota(jnp.int32, (rows, rows), 0)
    col = lax.broadcasted_iota(jnp.int32, (rows, rows), 1)
    return row % BLOCK, col % BLOCK, row // BLOCK, col // BLOCK


def lower_inverses(systems, apart):
    rows = systems[0].shape[0]
    row = lax.broadcasted_iota(jnp.int32, (rows, rows), 0)
    col = lax.broadcasted_iota(jnp.int32, (rows, rows), 1)
    eye = jnp.where(row == col, 1.0, 0.0)
    inverses = [eye - jnp.where(apart == 0, system, 0.0) for system in systems]
    level = 0
    while (1 << level) < BLOCK:
        joins = (apart >> level) == 1
        joints = [low(jnp.where(joins, system, 0.0)) for system in systems]
        lows = [low(inverse) for inverse in inverses]
        halves = [low(product(a, b)) for a, b in zip(lows, joints)]
        inverses = [c - product(a, b) for a, b, c in zip(halves, lows, inverses)]
        level += 1
    return inverses


def conv_rows(tile, halo, taps, same):
    count = tile.shape[0]
    extended = jnp.concatenate([halo, tile], 0)
    windows = [tile] + [
        pltpu.roll(extended, offset, 0)[8:] for offset in range(1, taps.shape[0])
    ]
    outcome = tile * taps[0:1]
    for offset in range(1, taps.shape[0]):
        outcome = outcome + windows[offset] * taps[offset : offset + 1] * same[:, offset : offset + 1]
    return outcome, windows


def unit_scale(values):
    return lax.rsqrt(jnp.sum(values * values, axis=-1, keepdims=True) + UNIT_EPS)


def pieces_of(head, head_count, substeps, width):
    query = [(head * width, width)]
    keys = [((head_count + head * substeps + n) * width, width) for n in range(substeps)]
    values = [
        ((head_count + (head_count + head) * substeps + n) * width, width) for n in range(substeps)
    ]
    return query + keys + values


def conv_of(source, first, start, size, taps, same_rows):
    tile_ref, before, edge, offset = source
    columns = slice(start - offset, start - offset + size)
    halo = jnp.where(first, edge[:, columns], before[:, columns]).astype(F32)[HALO - 8 :]
    return conv_rows(
        tile_ref[:, columns].astype(F32), halo, taps[:, start : start + size], same_rows
    )


def beta_rows(beta, head, substeps):
    columns = [beta[:, head * substeps + n : head * substeps + n + 1] for n in range(substeps)]
    return jnp.concatenate(columns, 0)


def forward_kernel(
    head_count, substeps, width, begin,
    raw, before, edge, taps, same, beta, cum_col, cum_row, chain_in, *refs,
):
    t_out, p_out, s_out, key_out, solved_out, chain = refs[-6:]
    step = pl.program_id(0)
    first = step + begin == 0
    rows = BLOCK * substeps
    row_token, col_token, row_step, col_step = row_maps(rows)
    upto = col_token <= row_token
    earlier = (col_token < row_token) | ((col_token == row_token) & (col_step < row_step))
    apart = row_token ^ col_token
    eye = jnp.where(
        lax.broadcasted_iota(jnp.int32, (width, width), 0)
        == lax.broadcasted_iota(jnp.int32, (width, width), 1),
        1.0,
        0.0,
    )
    same_rows = same[...]

    @pl.when(step == 0)
    def _():
        chain[...] = chain_in[...]

    heads = range(head_count)
    offset = head_count * width
    source = (raw, before, edge, offset)
    units = [(j, h) for j in range(PAIR) for h in heads]
    rows_at = [slice(j * BLOCK, (j + 1) * BLOCK) for j in range(PAIR)]
    keys, values, betas = {}, {}, {}
    for head in heads:
        acts = []
        for start, size in pieces_of(head, head_count, substeps, width)[1:]:
            pre, _ = conv_of(source, first, start, size, taps, same_rows)
            acts.append(pre * jax.nn.sigmoid(pre))
        acts = [a * unit_scale(a) for a in acts[:substeps]] + acts[substeps:]
        acts = [low(a) for a in acts]
        for j, at in enumerate(rows_at):
            keys[j, head] = jnp.concatenate([a[at] for a in acts[:substeps]], 0)
            values[j, head] = jnp.concatenate([a[at] for a in acts[substeps:]], 0)
            betas[j, head] = beta_rows(beta[at], head, substeps)
    keys, values, betas = ([held[u] for u in units] for held in (keys, values, betas))
    cum_rows = [jnp.concatenate([cum_col[rows_at[j], h : h + 1]] * substeps, 0) for j, h in units]
    cum_cols = [cum_row[j, h : h + 1, :] for j, h in units]
    lasts = [c[:, BLOCK - 1 : BLOCK] for c in cum_cols]
    ratios = [jnp.exp(jnp.where(upto, a - b, -1e4)) for a, b in zip(cum_rows, cum_cols)]
    grams = [times_transposed(key, key) for key in keys]
    systems = [
        jnp.where(earlier, beta_col * ratio * gram, 0.0)
        for beta_col, ratio, gram in zip(betas, ratios, grams)
    ]
    inverses = [low(inverse) for inverse in lower_inverses(systems, apart)]
    rights = [
        jnp.concatenate(
            [
                low(beta_col * jnp.exp(cum) * key.astype(F32)),
                low(beta_col * value.astype(F32)),
            ],
            1,
        )
        for beta_col, cum, key, value in zip(betas, cum_rows, keys, values)
    ]
    solved = [low(product(inverse, right)) for inverse, right in zip(inverses, rights)]
    ends = [
        low(jnp.exp(last - cum) * key.astype(F32))
        for last, cum, key in zip(lasts, cum_rows, keys)
    ]
    moved = [inner_rows(end, both) for end, both in zip(ends, solved)]
    step_maps = [split(jnp.exp(last) * eye - move[:, :width]) for last, move in zip(lasts, moved)]
    chains = [chain[head] for head in heads]
    for at, (j, head) in enumerate(units):
        t_out[j, head] = inverses[at]
        key_out[j, head] = keys[at]
        solved_out[j, head] = solved[at]
    for j in range(PAIR):
        at = j * head_count
        splits = [split(chained) for chained in chains]
        for head in heads:
            p_out[j, head] = splits[head][0][:, :width]
            s_out[j, head] = splits[head][0][:, width:]
        chains = [
            product(step_maps[at + h][0], splits[h][0])
            + (product(step_maps[at + h][1], splits[h][0]) + product(step_maps[at + h][0], splits[h][1]))
            for h in heads
        ]
        chains = [
            jnp.concatenate([c[:, :width], c[:, width:] + moved[at + h][:, width:]], 1)
            for h, c in enumerate(chains)
        ]
    for head in heads:
        chain[head] = chains[head]


def whole_spec(*shape):
    return pl.BlockSpec(shape, lambda *c: (0,) * len(shape))


def run_forward(
    begin, end, raw, edge, taps, same, beta, cum_col, cum_row, chain, passed,
    head_count, substeps, width,
):
    count, columns = raw.shape
    chunks = count // BLOCK
    rows = BLOCK * substeps
    begin, end = begin // PAIR, end // PAIR
    per_halo = PAIR * BLOCK // HALO
    tokens = lambda cols: pl.BlockSpec((PAIR * BLOCK, cols), lambda c: (c + begin, 0))
    tiles = lambda *shape: pl.BlockSpec((PAIR, head_count) + shape, lambda c: (c + begin, 0, 0, 0))
    shapes = [(rows, rows), (width, width), (width, width), (rows, width), (rows, 2 * width)]
    anywhere = pl.BlockSpec(memory_space=pl.ANY)
    return pl.pallas_call(
        functools.partial(forward_kernel, head_count, substeps, width, begin),
        grid=(end - begin,),
        in_specs=[
            tokens(columns),
            pl.BlockSpec(
                (HALO, columns), lambda c: (jnp.maximum((c + begin) * per_halo - 1, 0), 0)
            ),
            whole_spec(HALO, columns),
            whole_spec(*taps.shape),
            tokens(same.shape[1]),
            tokens(beta.shape[1]),
            tokens(head_count),
            pl.BlockSpec((PAIR, head_count, rows), lambda c: (c + begin, 0, 0)),
            whole_spec(*chain.shape),
        ]
        + [anywhere] * len(passed),
        out_specs=[tiles(*shape) for shape in shapes] + [whole_spec(*chain.shape)],
        out_shape=[
            jax.ShapeDtypeStruct((chunks, head_count) + shape, BF16) for shape in shapes
        ]
        + [jax.ShapeDtypeStruct(chain.shape, F32)],
        input_output_aliases={9 + k: k for k in range(len(passed))},
        compiler_params=pltpu.CompilerParams(
            dimension_semantics=("arbitrary",), vmem_limit_bytes=VMEM_BYTES
        ),
        name="mixer_forward",
    )(raw, raw, edge, taps, same, beta, cum_col, cum_row, chain, *passed)


def query_kernel(
    head_count, substeps, width,
    raw, before, edge, taps, same, cum_col, cum_row, key_in, solved_in, p_in, s_in,
    qtil_out, local_out,
):
    first = pl.program_id(0) == 0
    rows = BLOCK * substeps
    row_token, col_token, _, _ = row_maps(rows)
    upto = (col_token <= row_token)[:BLOCK]
    same_rows = same[...]
    heads = range(head_count)
    units = [(j, h) for j in range(QUERY_CHUNKS) for h in heads]
    rows_at = [slice(j * BLOCK, (j + 1) * BLOCK) for j in range(QUERY_CHUNKS)]
    queries = []
    for head in heads:
        start, size = pieces_of(head, head_count, substeps, width)[0]
        pre, _ = conv_of((raw, before, edge, 0), first, start, size, taps, same_rows)
        act = pre * jax.nn.sigmoid(pre)
        queries.append(low(act * unit_scale(act) * width ** (-0.5)))
    queries = [queries[h][rows_at[j]] for j, h in units]
    cum_rows = [cum_col[rows_at[j], h : h + 1] for j, h in units]
    ratios = [
        jnp.exp(jnp.where(upto, cum - cum_row[j, h : h + 1, :], -1e4))
        for cum, (j, h) in zip(cum_rows, units)
    ]
    scores = [times_transposed(query, key_in[j, h]) for query, (j, h) in zip(queries, units)]
    seen = [
        product(low(ratio * score), solved_in[j, h])
        for ratio, score, (j, h) in zip(ratios, scores, units)
    ]
    effective = [
        low(jnp.exp(cum) * query.astype(F32) - see[:, :width])
        for cum, query, see in zip(cum_rows, queries, seen)
    ]
    reached = [
        (product(eff, p_in[j, h]), product(eff, s_in[j, h]))
        for eff, (j, h) in zip(effective, units)
    ]
    for k, (j, h) in enumerate(units):
        at = slice(h * width, (h + 1) * width)
        qtil_out[rows_at[j], at] = low(reached[k][0])
        local_out[rows_at[j], at] = reached[k][1] + seen[k][:, width:]


def run_query(
    raw, edge, taps, same, cum_col, cum_row, key_rows, solved, p_part, s_part,
    head_count, substeps, width,
):
    count, columns = raw.shape
    chunks = count // BLOCK
    rows = BLOCK * substeps
    per_halo = QUERY_CHUNKS * BLOCK // HALO
    tokens = lambda cols: pl.BlockSpec((QUERY_CHUNKS * BLOCK, cols), lambda c: (c, 0))
    tiles = lambda *shape: pl.BlockSpec((QUERY_CHUNKS, head_count) + shape, lambda c: (c, 0, 0, 0))
    return pl.pallas_call(
        functools.partial(query_kernel, head_count, substeps, width),
        grid=(chunks // QUERY_CHUNKS,),
        in_specs=[
            tokens(columns),
            pl.BlockSpec((HALO, columns), lambda c: (jnp.maximum(c * per_halo - 1, 0), 0)),
            whole_spec(HALO, columns),
            whole_spec(*taps.shape),
            tokens(same.shape[1]),
            tokens(head_count),
            pl.BlockSpec((QUERY_CHUNKS, head_count, rows), lambda c: (c, 0, 0)),
            tiles(rows, width),
            tiles(rows, 2 * width),
            tiles(width, width),
            tiles(width, width),
        ],
        out_specs=[tokens(columns), tokens(columns)],
        out_shape=[
            jax.ShapeDtypeStruct((count, columns), BF16),
            jax.ShapeDtypeStruct((count, columns), F32),
        ],
        compiler_params=pltpu.CompilerParams(
            dimension_semantics=("arbitrary",), vmem_limit_bytes=VMEM_BYTES
        ),
        name="mixer_query",
    )(raw, raw, edge, taps, same, cum_col, cum_row, key_rows, solved, p_part, s_part)


def backward_kernel(
    head_count, substeps, width, end,
    raw_q, before_q, edge_q, raw, before, edge, taps, same, same_next, beta, cum_col, cum_row,
    t_in, p_in, s_in, state_in, d_out, adjoint_in, carried_in, tap_in, *refs,
):
    d_raw, d_logit, tail_out, adjoint, carried, tap_out, tail_next = refs[-7:]
    step = pl.program_id(0)
    pair = end - 1 - step
    rows = BLOCK * substeps
    tap_count = taps.shape[0]
    count = PAIR * BLOCK
    row_token, col_token, row_step, col_step = row_maps(rows)
    upto = col_token <= row_token
    earlier = (col_token < row_token) | ((col_token == row_token) & (col_step < row_step))
    same_rows = same[...]
    same_long = jnp.concatenate([same_rows, same_next[...]], 0)

    @pl.when(step == 0)
    def _():
        adjoint[...] = adjoint_in[...]
        carried[...] = carried_in[...]
        tap_out[...] = tap_in[...]

    heads = range(head_count)
    units_at = [(j, h) for j in range(PAIR) for h in heads]
    rows_at = [slice(j * BLOCK, (j + 1) * BLOCK) for j in range(PAIR)]
    pieces = [pieces_of(head, head_count, substeps, width) for head in heads]
    pres, sigmas, scales, units = [], [], [], []
    queries, keys, values, betas = {}, {}, {}, {}
    key_start = head_count * width
    sources = [(raw_q, before_q, edge_q, 0), (raw, before, edge, key_start)]

    def windows_of(start, size):
        return conv_of(sources[int(start >= key_start)], pair == 0, start, size, taps, same_rows)

    for head in heads:
        pre = [windows_of(start, size)[0] for start, size in pieces[head]]
        sigma = [jax.nn.sigmoid(p) for p in pre]
        acts = [p * s for p, s in zip(pre, sigma)]
        pres.append(pre)
        sigmas.append(sigma)
        scales.append([unit_scale(a) for a in acts[: 1 + substeps]])
        units.append([a * s for a, s in zip(acts[: 1 + substeps], scales[head])])
        query = low(units[head][0] * width ** (-0.5))
        key = [low(unit) for unit in units[head][1:]]
        value = [low(act) for act in acts[1 + substeps :]]
        for j, at in enumerate(rows_at):
            queries[j, head] = query[at]
            keys[j, head] = jnp.concatenate([k[at] for k in key], 0)
            values[j, head] = jnp.concatenate([v[at] for v in value], 0)
            betas[j, head] = beta_rows(beta[at], head, substeps)
    queries, keys, values, betas = (
        [held[u] for u in units_at] for held in (queries, keys, values, betas)
    )
    cum_rows = [
        jnp.concatenate([cum_col[rows_at[j], h : h + 1]] * substeps, 0) for j, h in units_at
    ]
    cum_cols = [cum_row[j, h : h + 1, :] for j, h in units_at]
    lasts = [c[:, BLOCK - 1 : BLOCK] for c in cum_cols]
    ratios = [jnp.exp(jnp.where(upto, a - b, -1e4)) for a, b in zip(cum_rows, cum_cols)]
    carries = [jnp.exp(c) for c in cum_rows]
    end_ratios = [jnp.exp(last - c) for last, c in zip(lasts, cum_rows)]
    inverses = [t_in[j, h] for j, h in units_at]
    d_mixes = [d_out[rows_at[j], h * width : (h + 1) * width] for j, h in units_at]
    states = [
        low(s_in[j, h].astype(F32) + product(p_in[j, h], state_in[h])) for j, h in units_at
    ]
    stacks = [jnp.concatenate([query, key], 0) for query, key in zip(queries, keys)]
    both_grams = [times_transposed(stack, key) for stack, key in zip(stacks, keys)]
    grams = [both[BLOCK:] for both in both_grams]
    masks = [low(ratio[:BLOCK] * both[:BLOCK]) for ratio, both in zip(ratios, both_grams)]
    d_both = [
        inner_rows(
            jnp.concatenate([mask, low(carry[:BLOCK] * query.astype(F32))], 1), d_mix
        )
        for mask, carry, query, d_mix in zip(masks, carries, queries, d_mixes)
    ]
    d_seen = [both[:rows] for both in d_both]
    d_reach = [both[rows:] for both in d_both]
    end_keys = [low(end * key.astype(F32)) for end, key in zip(end_ratios, keys)]
    start_keys = [
        low((beta_col * carry) * key.astype(F32))
        for beta_col, carry, key in zip(betas, carries, keys)
    ]
    freshes = [
        value.astype(F32) - carry * product(key, state)
        for value, carry, key, state in zip(values, carries, keys, states)
    ]
    updates = [
        low(product(inverse, low(beta_col * fresh)))
        for inverse, beta_col, fresh in zip(inverses, betas, freshes)
    ]
    laters_low, d_rights, d_rights_low = {}, {}, {}
    for j in range(PAIR - 1, -1, -1):
        ids = [j * head_count + h for h in heads]
        laters = [adjoint[h] for h in heads]
        for h, at in enumerate(ids):
            laters_low[at] = low(laters[h])
        d_updates = [low(d_seen[at] + product(end_keys[at], laters_low[at])) for at in ids]
        for h, at in enumerate(ids):
            d_rights[at] = inner_rows(inverses[at], d_updates[h])
            d_rights_low[at] = low(d_rights[at])
        for h, at in enumerate(ids):
            adjoint[h] = (
                jnp.exp(lasts[at]) * laters[h]
                + d_reach[at]
                - inner_rows(start_keys[at], d_rights_low[at])
            )
    ids = range(len(units_at))
    outer = [jnp.concatenate([d_mixes[at], d_rights_low[at]], 0) for at in ids]
    by_update = [times_transposed(outer[at], updates[at]) for at in ids]
    by_state = [times_transposed(outer[at], states[at]) for at in ids]
    d_systems = [
        jnp.where(earlier, -by_update[at][BLOCK:] * ratios[at], 0.0) for at in ids
    ]
    d_scores = [by_update[at][:BLOCK] * ratios[at][:BLOCK] for at in ids]
    d_grams = [betas[at] * d_systems[at] for at in ids]
    d_scores = [low(d_score) for d_score in d_scores]
    d_grams = [low(d_gram + jnp.transpose(d_gram)) for d_gram in d_grams]
    d_betas = [
        jnp.sum(d_rights[at] * freshes[at], axis=-1, keepdims=True)
        + jnp.sum(d_systems[at] * grams[at], axis=-1, keepdims=True)
        for at in ids
    ]
    d_queries = [
        carries[at][:BLOCK] * by_state[at][:BLOCK] + product(d_scores[at], keys[at])
        for at in ids
    ]
    d_keys = [
        inner_rows(jnp.concatenate([d_scores[at], d_grams[at]], 0), stacks[at])
        + end_ratios[at] * times_transposed(updates[at], laters_low[at])
        - (betas[at] * carries[at]) * by_state[at][BLOCK:]
        for at in ids
    ]
    for j in range(PAIR):
        logit_cols = []
        for h in heads:
            at = j * head_count + h
            logits = d_betas[at] * betas[at] * (1.0 - betas[at])
            logit_cols += [logits[n * BLOCK : (n + 1) * BLOCK] for n in range(substeps)]
        d_logit[rows_at[j], :] = jnp.concatenate(logit_cols, 1)

    for head in heads:
        mine = [j * head_count + head for j in range(PAIR)]
        step_rows = lambda arrays, n: jnp.concatenate(
            [array[n * BLOCK : (n + 1) * BLOCK] for array in arrays], 0
        )
        d_value = [betas[at] * d_rights[at] for at in mine]
        grads = [width ** (-0.5) * jnp.concatenate([d_queries[at] for at in mine], 0)]
        grads += [step_rows([d_keys[at] for at in mine], n) for n in range(substeps)]
        grads += [step_rows(d_value, n) for n in range(substeps)]
        for at, (start, size) in enumerate(pieces[head]):
            grad = grads[at]
            if at <= substeps:
                unit = units[head][at]
                grad = scales[head][at] * (
                    grad - unit * jnp.sum(grad * unit, axis=-1, keepdims=True)
                )
            grad = grad * silu_slope(pres[head][at], sigmas[head][at])
            windows = windows_of(start, size)[1]
            long = jnp.concatenate([grad, carried[:, start : start + size]], 0)
            tap = taps[:, start : start + size]
            spread = grad * tap[0:1]
            sums = [jnp.sum(grad * windows[0], axis=0, keepdims=True)]
            for offset in range(1, tap_count):
                masked = long * same_long[:, offset : offset + 1]
                spread = spread + (
                    pltpu.roll(masked, count + 8 - offset, 0)[:count] * tap[offset : offset + 1]
                )
                sums.append(jnp.sum(masked[:count] * windows[offset], axis=0, keepdims=True))
            carried[:, start : start + size] = grad[:8]
            tap_out[:, start : start + size] += jnp.concatenate(sums, 0)
            d_raw[:, start : start + size] = low(spread)
            tail_next[:, start : start + size] = spread[count - 8 :]

    @pl.when(step == 0)
    def _():
        tail_out[...] = tail_next[...]


def run_backward(
    begin, end, raw_q, edge_q, raw, edge, taps, same, beta, cum_col, cum_row, t_part, p_part,
    s_part, state_in, d_out, adjoint, carried, tap_grads, passed, head_count, substeps, width,
):
    count = raw.shape[0]
    columns = taps.shape[1]
    chunks = count // BLOCK
    rows = BLOCK * substeps
    begin, end, chunks = begin // PAIR, end // PAIR, chunks // PAIR
    per_halo = PAIR * BLOCK // HALO
    per_eight = PAIR * BLOCK // 8
    tokens = lambda cols: pl.BlockSpec((PAIR * BLOCK, cols), lambda c: (end - 1 - c, 0))
    halo = lambda cols: pl.BlockSpec(
        (HALO, cols), lambda c: (jnp.maximum((end - 1 - c) * per_halo - 1, 0), 0)
    )
    tiles = lambda *shape: pl.BlockSpec((PAIR, head_count) + shape, lambda c: (end - 1 - c, 0, 0, 0))
    anywhere = pl.BlockSpec(memory_space=pl.ANY)
    state = (head_count, width, width)
    sources = []
    for array in (raw_q, raw):
        cols = array.shape[1]
        sources += [tokens(cols), halo(cols), whole_spec(HALO, cols)]
    return pl.pallas_call(
        functools.partial(backward_kernel, head_count, substeps, width, end),
        grid=(end - begin,),
        in_specs=sources
        + [
            whole_spec(*taps.shape),
            tokens(same.shape[1]),
            pl.BlockSpec(
                (8, same.shape[1]),
                lambda c: (jnp.minimum((end - c) * per_eight, chunks * per_eight - 1), 0),
            ),
            tokens(beta.shape[1]),
            tokens(head_count),
            pl.BlockSpec((PAIR, head_count, rows), lambda c: (end - 1 - c, 0, 0)),
            tiles(rows, rows),
            tiles(width, width),
            tiles(width, width),
            whole_spec(*state),
            tokens(head_count * width),
            whole_spec(*state),
            whole_spec(8, columns),
            whole_spec(*taps.shape),
        ]
        + [anywhere] * len(passed),
        out_specs=[
            tokens(columns),
            tokens(head_count * substeps),
            whole_spec(8, columns),
            whole_spec(*state),
            whole_spec(8, columns),
            whole_spec(*taps.shape),
        ],
        out_shape=[
            jax.ShapeDtypeStruct((count, columns), BF16),
            jax.ShapeDtypeStruct((count, head_count * substeps), F32),
            jax.ShapeDtypeStruct((8, columns), F32),
            jax.ShapeDtypeStruct(state, F32),
            jax.ShapeDtypeStruct((8, columns), F32),
            jax.ShapeDtypeStruct(taps.shape, F32),
        ],
        scratch_shapes=[pltpu.VMEM((8, columns), F32)],
        input_output_aliases={20 + k: k for k in range(len(passed))},
        compiler_params=pltpu.CompilerParams(
            dimension_semantics=("arbitrary",), vmem_limit_bytes=VMEM_BYTES
        ),
        name="mixer_backward",
    )(
        raw_q, raw_q, edge_q, raw, raw, edge, taps, same, same, beta, cum_col, cum_row,
        t_part, p_part, s_part, state_in, d_out, adjoint, carried, tap_grads, *passed,
    )


def row_scale_of(values):
    return lax.rsqrt(jnp.mean(values * values, axis=-1, keepdims=True) + NORM_EPS)


def project_kernel(parts, raw_cols, inputs, edge, gain, *refs):
    weights, outs = refs[:parts], refs[parts:]
    normed_out, edge_normed, raw_out, edge_out, extra_out = outs
    gain_row = gain[...]

    def rows_of(values):
        values = values.astype(F32)
        return low(values * row_scale_of(values) * gain_row)

    def fill(normed, raw_ref, extra_ref):
        at = 0
        for weight in weights:
            cols = weight.shape[1]
            both = product(normed, weight[...])
            raw_part = min(cols, raw_cols - at)
            raw_ref[:, at : at + raw_part] = low(both[:, :raw_part])
            if extra_ref is not None and raw_part < cols:
                extra_ref[...] = jax.nn.sigmoid(both[:, raw_part:])
            at += cols

    normed = rows_of(inputs[...])
    normed_out[...] = normed
    fill(normed, raw_out, extra_out)

    @pl.when(pl.program_id(0) == 0)
    def _():
        normed_edge = rows_of(edge[...])
        edge_normed[...] = normed_edge
        fill(normed_edge, edge_out, None)


def once(shape):
    return pl.BlockSpec(shape, lambda *c: (0,) * len(shape), pipeline_mode=pl.Buffered(1))


def run_project(inputs, edge, gain, weights, raw_cols, extra):
    count, features = inputs.shape
    tile = min(TILE, count)
    tokens = lambda cols: pl.BlockSpec((tile, cols), lambda c: (c, 0))
    return pl.pallas_call(
        functools.partial(project_kernel, len(weights), raw_cols),
        grid=(count // tile,),
        in_specs=[tokens(features), whole_spec(HALO, features), whole_spec(1, features)]
        + [once(weight.shape) for weight in weights],
        out_specs=[
            tokens(features), whole_spec(HALO, features), tokens(raw_cols),
            whole_spec(HALO, raw_cols), tokens(extra),
        ],
        out_shape=[
            jax.ShapeDtypeStruct((count, features), BF16),
            jax.ShapeDtypeStruct((HALO, features), BF16),
            jax.ShapeDtypeStruct((count, raw_cols), BF16),
            jax.ShapeDtypeStruct((HALO, raw_cols), BF16),
            jax.ShapeDtypeStruct((count, extra), F32),
        ],
        compiler_params=pltpu.CompilerParams(
            dimension_semantics=("arbitrary",), vmem_limit_bytes=VMEM_BYTES
        ),
        name="project",
    )(inputs, edge, gain, *weights)


def project_side_kernel(normed, edge, query_w, gate_w, raw_out, edge_out, gate_out):
    raw_out[...] = low(product(normed[...], query_w[...]))
    gate_out[...] = product(normed[...], gate_w[...])

    @pl.when(pl.program_id(0) == 0)
    def _():
        edge_out[...] = low(product(edge[...], query_w[...]))


def run_project_side(normed, edge, query_w, gate_w):
    count, features = normed.shape
    cols = query_w.shape[1]
    tile = min(TILE, count)
    tokens = lambda cols: pl.BlockSpec((tile, cols), lambda c: (c, 0))
    return pl.pallas_call(
        project_side_kernel,
        grid=(count // tile,),
        in_specs=[
            tokens(features), whole_spec(HALO, features), once(query_w.shape), once(gate_w.shape)
        ],
        out_specs=[tokens(cols), whole_spec(HALO, cols), tokens(cols)],
        out_shape=[
            jax.ShapeDtypeStruct((count, cols), BF16),
            jax.ShapeDtypeStruct((HALO, cols), BF16),
            jax.ShapeDtypeStruct((count, cols), F32),
        ],
        compiler_params=pltpu.CompilerParams(
            dimension_semantics=("arbitrary",), vmem_limit_bytes=VMEM_BYTES
        ),
        name="project_side",
    )(normed, edge, query_w, gate_w)


def heads_kernel(
    head_count, width,
    local, reach, state, gate, gain, weight,
    mixer_out, heads_out, own_out, low_out,
):
    gain_row = gain[...]
    for h in range(head_count):
        at = slice(h * width, (h + 1) * width)
        mixer = local[:, at] + product(reach[:, at], state[h])
        logit = gate[:, at]
        mixer_out[:, at] = mixer
        heads_out[:, at] = low(
            mixer * row_scale_of(mixer) * gain_row * (logit * jax.nn.sigmoid(logit))
        )
    branch = times_transposed(heads_out[...], weight[...])
    own_out[...] = branch
    low_out[...] = low(branch)


def run_heads(local, reach, state, gate, gain, weight, head_count, width):
    count, cols = local.shape
    features = weight.shape[0]
    tile = min(TILE, count)
    tokens = lambda cols: pl.BlockSpec((tile, cols), lambda c: (c, 0))
    return pl.pallas_call(
        functools.partial(heads_kernel, head_count, width),
        grid=(count // tile,),
        in_specs=[
            tokens(cols), tokens(cols), whole_spec(*state.shape), tokens(cols),
            whole_spec(*gain.shape), once(weight.shape),
        ],
        out_specs=[tokens(cols), tokens(cols), tokens(features), tokens(features)],
        out_shape=[
            jax.ShapeDtypeStruct((count, cols), F32),
            jax.ShapeDtypeStruct((count, cols), BF16),
            jax.ShapeDtypeStruct((count, features), F32),
            jax.ShapeDtypeStruct((count, features), BF16),
        ],
        compiler_params=pltpu.CompilerParams(
            dimension_semantics=("arbitrary",), vmem_limit_bytes=VMEM_BYTES
        ),
        name="heads",
    )(local, reach, state, gate, gain, weight)


def feed_kernel(
    inputs, own, other, gain, cotangent, gate_w, up_w, down_w,
    hidden_out, normed_out, act_out, d_gate_out, d_up_out, branch_out, own_out, low_out,
):
    hidden = inputs[...].astype(F32) + own[...] + other[...].astype(F32)
    hidden_out[...] = hidden
    normed = low(hidden * row_scale_of(hidden) * gain[...])
    normed_out[...] = normed
    gate = product(normed, gate_w[...])
    up = product(normed, up_w[...])
    d_act = product(cotangent[...], down_w[...])
    sigma = jax.nn.sigmoid(gate)
    act = gate * sigma
    activation = low(act * up)
    d_up = low(d_act * act)
    d_gate = low(d_act * up * silu_slope(gate, sigma))
    act_out[...] = activation
    d_gate_out[...] = d_gate
    d_up_out[...] = d_up
    branch_out[...] = low(times_transposed(activation, down_w[...]))
    d_normed = times_transposed(d_gate, gate_w[...]) + times_transposed(d_up, up_w[...])
    own_out[...] = d_normed
    low_out[...] = low(d_normed)


def run_feed(inputs, own, other, gain, cotangent, gate_w, up_w, down_w):
    count, features = inputs.shape
    cols = gate_w.shape[1]
    tile = min(TILE, count)
    tokens = lambda cols: pl.BlockSpec((tile, cols), lambda c: (c, 0))
    shape = lambda cols, kind: jax.ShapeDtypeStruct((count, cols), kind)
    return pl.pallas_call(
        feed_kernel,
        grid=(count // tile,),
        in_specs=[tokens(features)] * 3
        + [whole_spec(1, features), tokens(features)]
        + [once(weight.shape) for weight in (gate_w, up_w, down_w)],
        out_specs=[tokens(features)] * 2 + [tokens(cols)] * 3 + [tokens(features)] * 3,
        out_shape=[shape(features, F32), shape(features, BF16)]
        + [shape(cols, BF16)] * 3
        + [shape(features, BF16), shape(features, F32), shape(features, BF16)],
        compiler_params=pltpu.CompilerParams(
            dimension_semantics=("arbitrary",), vmem_limit_bytes=VMEM_BYTES
        ),
        name="feed",
    )(inputs, own, other, gain, cotangent, gate_w, up_w, down_w)


def turn_kernel(
    head_count, width,
    hidden, own, other, gain, cotangent, weight, mixer_in, gate, head_gain, reach,
    d_hidden_out, d_low_out, d_gate_out, d_mixer_out, state_out, feed_gain_out, head_gain_out,
):
    @pl.when(pl.program_id(0) == 0)
    def _():
        state_out[...] = jnp.zeros(state_out.shape, F32)
        feed_gain_out[...] = jnp.zeros(feed_gain_out.shape, F32)
        head_gain_out[...] = jnp.zeros(head_gain_out.shape, F32)

    d_normed = own[...] + other[...].astype(F32)
    back, terms = norm_back(hidden[...], gain[...], d_normed)
    feed_gain_out[...] += jnp.sum(terms, axis=0, keepdims=True)
    d_hidden = cotangent[...].astype(F32) + back
    d_hidden_out[...] = d_hidden
    d_low = low(d_hidden)
    d_low_out[...] = d_low
    d_heads = product(d_low, weight[...])
    gain_row = head_gain[...]
    for h in range(head_count):
        at = slice(h * width, (h + 1) * width)
        mixer = mixer_in[:, at]
        unit = mixer * row_scale_of(mixer)
        logit = gate[:, at]
        sigma = jax.nn.sigmoid(logit)
        d_head = d_heads[:, at]
        d_gate_out[:, at] = low(d_head * (unit * gain_row) * silu_slope(logit, sigma))
        d_mixer, head_terms = norm_back(mixer, gain_row, d_head * (logit * sigma))
        head_gain_out[...] += jnp.sum(head_terms, axis=0, keepdims=True)
        d_mixer_low = low(d_mixer)
        d_mixer_out[:, at] = d_mixer_low
        state_out[h] += inner_rows(reach[:, at], d_mixer_low)


def run_turn(
    hidden, own, other, gain, cotangent, weight, mixer, gate, head_gain, reach, head_count, width
):
    count, features = hidden.shape
    cols = mixer.shape[1]
    tile = min(TILE, count)
    tokens = lambda cols: pl.BlockSpec((tile, cols), lambda c: (c, 0))
    shape = lambda cols, kind: jax.ShapeDtypeStruct((count, cols), kind)
    state = (head_count, width, width)
    return pl.pallas_call(
        functools.partial(turn_kernel, head_count, width),
        grid=(count // tile,),
        in_specs=[tokens(features)] * 3
        + [whole_spec(1, features), tokens(features), once(weight.shape)]
        + [tokens(cols), tokens(cols), whole_spec(1, width), tokens(cols)],
        out_specs=[tokens(features)] * 2
        + [tokens(cols)] * 2
        + [whole_spec(*state), whole_spec(1, features), whole_spec(1, width)],
        out_shape=[shape(features, F32), shape(features, BF16)]
        + [shape(cols, BF16)] * 2
        + [
            jax.ShapeDtypeStruct(state, F32),
            jax.ShapeDtypeStruct((1, features), F32),
            jax.ShapeDtypeStruct((1, width), F32),
        ],
        compiler_params=pltpu.CompilerParams(
            dimension_semantics=("arbitrary",), vmem_limit_bytes=VMEM_BYTES
        ),
        name="turn",
    )(hidden, own, other, gain, cotangent, weight, mixer, gate, head_gain, reach)


def back_project_kernel(extra, inputs, d_raw, d_extra, d_gate, query_w, gate_w, *refs):
    weights, (out, gain_out) = refs[:-2], refs[-2:]
    at = query_w.shape[1]
    total = times_transposed(d_raw[:, :at], query_w[...])
    for k, weight in enumerate(weights):
        size = weight.shape[1] - (extra if k == len(weights) - 1 else 0)
        total += times_transposed(d_raw[:, at : at + size], weight[:, :size])
        at += size
    total += times_transposed(d_extra[...], weights[-1][:, -extra:])
    total += times_transposed(d_gate[...], gate_w[...])
    total = low(total)
    out[...] = total

    @pl.when(pl.program_id(0) == 0)
    def _():
        gain_out[...] = jnp.zeros(gain_out.shape, F32)

    values = inputs[...].astype(F32)
    gain_out[...] += jnp.sum(
        total.astype(F32) * (values * row_scale_of(values)), axis=0, keepdims=True
    )


def run_back_project(inputs, d_raw, d_extra, d_gate, weights):
    count, features = inputs.shape
    tile = min(TILE, count)
    tokens = lambda cols: pl.BlockSpec((tile, cols), lambda c: (c, 0))
    return pl.pallas_call(
        functools.partial(back_project_kernel, d_extra.shape[1]),
        grid=(count // tile,),
        in_specs=[tokens(array.shape[1]) for array in (inputs, d_raw, d_extra, d_gate)]
        + [once(weight.shape) for weight in weights],
        out_specs=[tokens(features), whole_spec(1, features)],
        out_shape=[
            jax.ShapeDtypeStruct((count, features), BF16),
            jax.ShapeDtypeStruct((1, features), F32),
        ],
        compiler_params=pltpu.CompilerParams(
            dimension_semantics=("arbitrary",), vmem_limit_bytes=VMEM_BYTES
        ),
        name="back_project",
    )(inputs, d_raw, d_extra, d_gate, *weights)


def shift_seq(array, by):
    count = lax.axis_size("seq")
    return lax.ppermute(
        array, "seq", [(i, i + by) for i in range(count) if 0 <= i + by < count]
    )


def swap_seq(array, distance):
    return lax.ppermute(array, "seq", [(i, i ^ distance) for i in range(lax.axis_size("seq"))])


def swap_head(array):
    return lax.ppermute(array, "head", [(0, 1), (1, 0)])


def head_sum(array):
    return array + swap_head(array)


def fine_low(form, former, latter):
    high, rest = split(former)
    return form(high, latter) + form(rest, latter)


def fine_first(form, former, latter):
    high, rest = split(latter)
    return form(former, high) + form(former, rest)


def join_kernel(final, upper, group, other, before, group_out, low_out, before_out):
    heads, width, _ = group.shape

    @pl.when(upper[0] == 1)
    def _():
        for head in range(heads):
            theirs = other[head]
            reach = fine_low(product, before[head, :, :width], theirs)
            before_out[head, :, :width] = reach[:, :width]
            before_out[head, :, width:] = reach[:, width:] + before[head, :, width:]
            if not final:
                mine = fine_low(product, group[head, :, :width], theirs)
                group_out[head, :, :width] = mine[:, :width]
                group_out[head, :, width:] = mine[:, width:] + group[head, :, width:]

    @pl.when(upper[0] == 0)
    def _():
        before_out[...] = before[...]
        if not final:
            for head in range(heads):
                theirs = other[head]
                mine = fine_first(product, theirs[:, :width], group[head])
                group_out[head, :, :width] = mine[:, :width]
                group_out[head, :, width:] = mine[:, width:] + theirs[:, width:].astype(F32)

    low_out[...] = low(group_out[...]) if not final else low(before_out[...])


def join_groups(final, upper, group, other, before):
    whole = pl.BlockSpec(memory_space=pltpu.VMEM)
    full = jax.ShapeDtypeStruct(group.shape, F32)
    return pl.pallas_call(
        functools.partial(join_kernel, final),
        in_specs=[pl.BlockSpec(memory_space=pltpu.SMEM), whole, whole, whole],
        out_specs=[whole, whole, whole],
        out_shape=[full, jax.ShapeDtypeStruct(group.shape, BF16), full],
        compiler_params=pltpu.CompilerParams(vmem_limit_bytes=VMEM_BYTES),
        name="join_groups",
    )(upper, group, other, before)


def back_kernel(final, upper, group, other, after, group_map, other_map, after_map, *outs):
    group_out, low_out, after_out, after_map_out = outs
    heads, width, _ = group.shape
    after_out[...] = after[...]
    after_map_out[...] = after_map[...]
    if final:
        group_out[...] = group[...]

    @pl.when(upper[0] == 1)
    def _():
        if not final:
            for head in range(heads):
                theirs = other_map[head, :, :width]
                group_out[head] = other[head].astype(F32) + fine_first(
                    inner_rows, theirs, group[head]
                )

    @pl.when(upper[0] == 0)
    def _():
        for head in range(heads):
            theirs = other[head]
            after_out[head] += fine_low(inner_rows, after_map[head], theirs)
            if not final:
                group_out[head] = group[head] + fine_low(
                    inner_rows, group_map[head, :, :width], theirs
                )
                after_map_out[head] = fine_first(
                    product, other_map[head, :, :width], after_map[head]
                )

    low_out[...] = low(group_out[...])


def join_back(final, upper, group, other, after, group_map, other_map, after_map):
    whole = pl.BlockSpec(memory_space=pltpu.VMEM)
    full = jax.ShapeDtypeStruct(group.shape, F32)
    return pl.pallas_call(
        functools.partial(back_kernel, final),
        in_specs=[pl.BlockSpec(memory_space=pltpu.SMEM)] + [whole] * 6,
        out_specs=[whole] * 4,
        out_shape=[full, jax.ShapeDtypeStruct(group.shape, BF16), full, full],
        compiler_params=pltpu.CompilerParams(vmem_limit_bytes=VMEM_BYTES),
        name="join_back",
    )(upper, group, other, after, group_map, other_map, after_map)


def states_before(group, eye):
    count, mine = lax.axis_size("seq"), lax.axis_index("seq")
    before = jnp.concatenate([eye, jnp.zeros_like(eye)], 2)
    group_low = low(group)
    kept = []
    distance = 1
    while distance < count:
        other = swap_seq(group_low, distance)
        upper = ((mine // distance) % 2).astype(jnp.int32).reshape(1)
        kept.append((group, other, upper))
        final = 2 * distance >= count
        group, group_low, before = join_groups(final, upper, group, other, before)
        distance *= 2
    return group_low[:, :, group.shape[1] :], kept


def adjoints_after(own, kept, eye):
    group, group_low = own, low(own)
    after, after_map = jnp.zeros_like(own), eye
    distance = 1
    for group_map, other_map, upper in kept:
        other = swap_seq(group_low, distance)
        final = 2 * distance >= lax.axis_size("seq")
        group, group_low, after, after_map = join_back(
            final, upper, group, other, after, group_map, other_map, after_map
        )
        distance *= 2
    return after


def bit_orders(count):
    distances = [1 << k for k in range(count.bit_length() - 1)]
    near, far = distances[:3], distances[3:]
    return [near[k:] + near[:k] for k in range(len(near))], far


def scatter_view(array):
    count = lax.axis_size("seq")
    bits = count.bit_length() - 1
    return array.reshape((2,) * bits + (array.shape[0] // count, array.shape[1]))


def swap_all(arrays, distances):
    return [swap_seq(array, distance) for array, distance in zip(arrays, distances)]


def halve_all(terms, distances):
    keeps, sends = [], []
    for arrays, distance in zip(terms, distances):
        axis = arrays[0].ndim - 2 - distance.bit_length()
        own = (lax.axis_index("seq") // distance) % 2
        cut = lambda array, at: lax.dynamic_slice_in_dim(array, at, 1, axis).astype(F32)
        keeps.append(low(functools.reduce(jnp.add, [cut(array, own) for array in arrays])))
        sends.append(low(functools.reduce(jnp.add, [cut(array, 1 - own) for array in arrays])))
    return keeps, sends


def block_at(me, q, have, free, flipped):
    index, left = 0, len(free)
    for distance in have:
        if distance in free:
            left -= 1
            digit = (q // (1 << left)) % 2
        else:
            digit = (me // distance) % 2
            digit = 1 - digit if distance == flipped else digit
        index = index * 2 + digit
    return index


def halve_kernel(counts, me, *refs):
    ins, outs = refs[: 2 * sum(counts)], refs[2 * sum(counts) :]
    for part, count in enumerate(counts):
        for side in range(2):
            total = ins[0][...].astype(F32)
            for ref in ins[1:count]:
                total = total + ref[...].astype(F32)
            outs[2 * part + side][...] = low(total)
            ins = ins[count:]


def halve_parts(terms, haves, distances):
    rows = terms[0][0].shape[-2]
    arrays, specs, out_specs, shapes = [], [], [], []
    blocks = 1 << (min(len(have) for have in haves[0]) - 1)
    for part, part_haves, distance in zip(terms, haves, distances):
        free = [d for d in min(part_haves, key=len) if d != distance]
        columns = part[0].shape[-1]
        for flipped in (None, distance):
            for array, have in zip(part, part_haves):
                arrays.append(array.reshape(-1, columns))
                specs.append(
                    pl.BlockSpec(
                        (rows, columns),
                        lambda q, me, have=have, free=free, flipped=flipped: (
                            block_at(me[0], q, have, free, flipped), 0
                        ),
                    )
                )
            out_specs.append(pl.BlockSpec((rows, columns), lambda q, me: (q, 0)))
            shapes.append(jax.ShapeDtypeStruct((blocks * rows, columns), BF16))
    outs = pl.pallas_call(
        functools.partial(halve_kernel, [len(part) for part in terms]),
        grid_spec=pltpu.PrefetchScalarGridSpec(
            num_scalar_prefetch=1, grid=(blocks,), in_specs=specs, out_specs=out_specs
        ),
        out_shape=shapes,
        compiler_params=pltpu.CompilerParams(
            dimension_semantics=("arbitrary",), vmem_limit_bytes=VMEM_BYTES
        ),
        name="halve",
    )(lax.axis_index("seq").astype(jnp.int32).reshape(1), *arrays)
    return outs[0::2], outs[1::2]


def far_steps(terms, distances):
    for distance in distances:
        keeps, sends = halve_all(terms, [distance] * len(terms))
        merged = swap_seq(jnp.concatenate(sends, -1), distance)
        others, start = [], 0
        for send in sends:
            wide = send.shape[-1]
            others.append(lax.slice_in_dim(merged, start, start + wide, axis=merged.ndim - 1))
            start += wide
        terms = list(zip(keeps, others))
    return [
        functools.reduce(jnp.add, [a.astype(F32) for a in arrays]).reshape(arrays[0].shape[-2:])
        for arrays in terms
    ]


def gather_join(view, other, distance):
    axis = view.ndim - 2 - distance.bit_length()
    upper = (lax.axis_index("seq") // distance) % 2 == 1
    return jnp.concatenate(
        [jnp.where(upper, other, view), jnp.where(upper, view, other)], axis
    )


def gather_far(pack, distances):
    bits = lax.axis_size("seq").bit_length() - 1
    view = pack.reshape((1,) * bits + pack.shape)
    for distance in distances[::-1]:
        view = gather_join(view, swap_seq(view, distance), distance)
    return view


def gather_cut(view, widths):
    parts, at = [], 0
    for wide in widths:
        parts.append(lax.slice_in_dim(view, at, at + wide, axis=view.ndim - 1))
        at += wide
    return parts


def gather_end(views):
    return [view.reshape(-1, view.shape[-1]) for view in views]


def tied(*values):
    return lax.optimization_barrier(values)


def per_device(
    activations,
    log_decay,
    doc_starts,
    query_weight,
    key_weight,
    value_weight,
    beta_weight,
    gate_weight,
    out_weight,
    query_taps,
    key_taps,
    value_taps,
    mixer_gain,
    head_gain,
    feed_gain,
    feed_gate,
    feed_up,
    feed_down,
    cotangent,
):
    count, features = activations.shape
    tap_count = query_taps.shape[0]
    width = head_gain.shape[0]
    query_cols = query_weight.shape[1]
    key_cols = key_weight.shape[1]
    conv_cols = query_cols + 2 * key_cols
    hidden_cols = feed_gate.shape[1]
    head_count = query_cols // width
    beta_cols = beta_weight.shape[1]
    substeps = beta_cols // head_count
    device_rank = lax.axis_index("seq")
    head_rank = lax.axis_index("head")
    extra = 128
    shard_rows = query_weight.shape[0]
    orders, far = bit_orders(lax.axis_size("seq"))
    at_step = lambda k: [order[k] for order in orders]
    gather_at = lambda k: [order[2 - k] for order in orders]
    pad = jnp.zeros((shard_rows, extra - beta_cols - 2), BF16)
    kv_pack = jnp.concatenate(
        [key_weight, value_weight, beta_weight, mixer_gain[:, None], feed_gain[:, None], pad], 1
    )
    side_pack = jnp.concatenate([query_weight, gate_weight, out_weight.T], 1)
    feed_pack = jnp.concatenate([feed_gate, feed_up, feed_down.T], 1)
    third = -(-kv_pack.shape[1] // (3 * width)) * width
    input_edge = shift_seq(activations[count - HALO :], 1)
    kv_view = gather_far(kv_pack, far)
    kv_view, side_pack = tied(kv_view, side_pack)
    kv_parts = gather_cut(kv_view, [third, third, kv_pack.shape[1] - 2 * third])
    side_view = gather_far(side_pack, far)
    for k in range(3):
        others = swap_all(kv_parts, gather_at(k))
        kv_parts = [gather_join(v, o, d) for v, o, d in zip(kv_parts, others, gather_at(k))]
    side_parts = gather_cut(side_view, [query_cols] * 3)
    weights_kv = gather_end(kv_parts)
    weights_kv, side_parts, feed_pack, input_edge = tied(
        weights_kv, side_parts, feed_pack, input_edge
    )
    gains = weights_kv[2][:, -extra + beta_cols : -extra + beta_cols + 2].T.astype(F32)
    gain_one, gain_two = gains[0:1], gains[1:2]

    token_position = device_rank * count + jnp.arange(count, dtype=jnp.int32)
    is_start = jnp.any(token_position[:, None] == doc_starts[None, :], axis=1)

    def same_docs(position):
        doc = lambda p: jnp.sum((p[:, None] >= doc_starts[None, :]).astype(jnp.int32), axis=1)
        own = doc(position)
        return jnp.stack(
            [
                ((doc(position - offset) == own) & (position >= offset)).astype(F32)
                for offset in range(tap_count)
            ],
            1,
        )

    same = same_docs(token_position)
    log_gate = log_decay - RESET * is_start.astype(F32)[:, None]
    chunks = count // BLOCK
    cumulative = jnp.cumsum(log_gate.reshape(chunks, BLOCK, head_count), axis=1)
    cum_col = cumulative.reshape(count, head_count)
    cum_row = jnp.concatenate([jnp.swapaxes(cumulative, 1, 2)] * substeps, 2)
    taps_all = jnp.concatenate([query_taps, key_taps, value_taps], 1).astype(F32)

    side_others = swap_all(side_parts, gather_at(0))
    feed_view = gather_far(feed_pack, far)
    normed, edge_normed, raw_kv, edge_kv, sigmas = run_project(
        activations, input_edge, gain_one, weights_kv, 2 * key_cols, extra
    )
    beta_gate = sigmas[:, :beta_cols]
    eye = jnp.broadcast_to(jnp.eye(width, dtype=F32), (head_count, width, width))
    chain = jnp.concatenate([eye, jnp.zeros_like(eye)], 2)
    passed = ()
    feed_parts = None
    side_at, feed_at = 1, 0
    sides = [gather_join(v, o, d) for v, o, d in zip(side_parts, side_others, gather_at(0))]
    marks = [(chunks * k) // (AHEAD_CALLS * PAIR) * PAIR for k in range(AHEAD_CALLS + 1)]
    sends, distances = sides, gather_at(1)
    for call in range(AHEAD_CALLS):
        chain, sends = tied(chain, sends)
        others = swap_all(sends, distances)
        *passed, chain = run_forward(
            marks[call], marks[call + 1], raw_kv, edge_kv, taps_all, same, beta_gate, cum_col,
            cum_row, chain, tuple(passed), head_count, substeps, width,
        )
        if call == 0:
            chain, others, feed_view = tied(chain, others, feed_view)
        else:
            chain, others = tied(chain, others)
        joined = [gather_join(v, o, d) for v, o, d in zip(sends, others, distances)]
        if call == 0:
            feed_parts = gather_cut(feed_view, [hidden_cols] * 3)
            sends, distances = joined + feed_parts, gather_at(2) + gather_at(0)
        elif call == 1:
            sides, sends, distances = joined[:3], joined[3:], gather_at(1)
        else:
            feed_parts = joined
    t_part, p_part, s_part, key_rows, solved = passed
    weight_query, weight_gate, weight_out = gather_end(sides)

    state_low, kept = states_before(chain, eye)
    state_low, feed_parts = tied(state_low, feed_parts)
    others = swap_all(feed_parts, gather_at(2))
    feed_gate_w, feed_up_w, feed_down_w = gather_end(
        [gather_join(v, o, d) for v, o, d in zip(feed_parts, others, gather_at(2))]
    )
    raw_query, edge_query, gate_view = run_project_side(
        normed, edge_normed, weight_query, weight_gate
    )
    q_reach, local_out = run_query(
        raw_query, edge_query, taps_all[:, :query_cols], same, cum_col, cum_row, key_rows, solved,
        p_part, s_part, head_count, substeps, width,
    )
    head_gain_row = head_gain.astype(F32)[None]
    mixer_out, heads_out, branch_own, branch_low = run_heads(
        local_out, q_reach, state_low, gate_view, head_gain_row, weight_out, head_count, width
    )
    (
        hidden, normed_ffn, activation, d_gate, d_up, branch_two, d_normed_own, d_normed_low,
    ) = run_feed(
        activations, branch_own, swap_head(branch_low), gain_two, cotangent,
        feed_gate_w, feed_up_w, feed_down_w,
    )
    half = features // lax.axis_size("head")
    own_half = lambda array: lax.dynamic_slice_in_dim(array, head_rank * half, half, 1)
    other_half = lambda array: lax.dynamic_slice_in_dim(array, (1 - head_rank) * half, half, 1)
    output = low(
        own_half(hidden)
        + own_half(branch_two).astype(F32)
        + swap_head(other_half(branch_two)).astype(F32)
    )

    near = orders[0]
    grad_orders = [
        [near[2], near[1], near[0]],
        [near[0], near[2], near[1]],
        [near[1], near[0], near[2]],
        [near[1], near[0], near[2]],
        [near[1], near[2], near[0]],
    ]
    down_grad = scatter_view(low(inner_rows(cotangent, activation)))
    _, down_send = halve_all([(down_grad,)], [grad_orders[2][0]])
    d_normed_other, down_send = tied(swap_head(d_normed_low), down_send)
    down_other = swap_all(down_send, [grad_orders[2][0]])[0]
    (
        d_hidden, grad_mixer, d_gate_logit, d_mixer_low, own_part, grad_feed_gain, head_gain_part,
    ) = run_turn(
        hidden, d_normed_own, d_normed_other, gain_two, cotangent, weight_out,
        mixer_out, gate_view, head_gain_row, q_reach, head_count, width,
    )
    grad_feed_gain, head_gain_part = grad_feed_gain[0], head_gain_part[0]
    adjoint = adjoints_after(own_part, kept, eye)
    terms = [
        (scatter_view(low(inner_rows(normed_ffn, d_gate))),),
        (scatter_view(low(inner_rows(normed_ffn, d_up))),),
        (scatter_view(low(inner_rows(grad_mixer, heads_out))),),
        (scatter_view(low(inner_rows(normed, d_gate_logit))),),
    ]
    down_other, adjoint = tied(down_other, adjoint)
    marks = [chunks, (3 * chunks // 8) // PAIR * PAIR, (chunks // 8) // PAIR * PAIR, 0]
    carried = jnp.zeros((8, conv_cols), F32)
    tap_grads = jnp.zeros((tap_count, conv_cols), F32)
    passed = ()
    every = [1 << k for k in range(lax.axis_size("seq").bit_length() - 1)][::-1]
    left = [every] * 5
    haves = [[every]] * 5
    down_terms = (down_grad, down_other)
    bits = len(every)
    for call in range(3):
        distances = [order[call] for order in grad_orders]
        if call == 0:
            kinds = [0, 1, 3, 4]
            sends = halve_all(terms, [distances[k] for k in kinds])[1]
            keeps = [part[0] for part in terms]
            distances = [distances[k] for k in kinds]
        elif shard_rows < HALO:
            views = [
                (
                    [array.reshape((2,) * len(have) + array.shape[-2:]) for array, have in zip(*p)],
                    p[1],
                )
                for p in zip(terms, haves)
            ]
            sums = []
            for part, part_haves in views:
                small_have = min(part_haves, key=len)
                total = None
                for array, have in zip(part, part_haves):
                    for axis, d in reversed(list(enumerate(have))):
                        if d not in small_have:
                            array = lax.dynamic_index_in_dim(
                                array, (lax.axis_index("seq") // d) % 2, axis, keepdims=False
                            )
                    array = array.astype(F32)
                    total = array if total is None else total + array
                sums.append((total, small_have))
            keeps, sends = [], []
            for (total, have), d in zip(sums, distances):
                own = (lax.axis_index("seq") // d) % 2
                columns = total.shape[-1]
                pick = lambda at: low(
                    lax.dynamic_index_in_dim(total, at, have.index(d), keepdims=False)
                ).reshape(-1, columns)
                keeps.append(pick(own))
                sends.append(pick(1 - own))
        else:
            keeps, sends = halve_parts(terms, haves, distances)
        adjoint, sends, keeps = tied(adjoint, sends, keeps)
        others = swap_all(sends, distances)
        d_raw, d_beta_logit, new_tail, adjoint, carried, tap_grads = run_backward(
            marks[call + 1], marks[call],
            raw_query, edge_query, raw_kv, edge_kv, taps_all, same, beta_gate, cum_col, cum_row,
            t_part, p_part, s_part, state_low, d_mixer_low, adjoint, carried, tap_grads, passed,
            head_count, substeps, width,
        )
        if call == 0:
            tail = new_tail
        adjoint, carried, others = tied(adjoint, carried, others)
        passed = (d_raw, d_beta_logit)
        terms = [
            (k.reshape(-1, k.shape[-1]), o.reshape(-1, o.shape[-1])) for k, o in zip(keeps, others)
        ]
        if call == 0:
            down = tuple(array.reshape(-1, array.shape[-1]) for array in down_terms)
            terms = terms[:2] + [down] + terms[2:]
        left = [[d for d in l if d != order[call]] for l, order in zip(left, grad_orders)]
        haves = [[every if call == 0 else l, l] for l in left]
        cube = lambda a: a.reshape(-1, shard_rows, a.shape[-1])
        terms = [tuple(cube(a) for a in part) for part in terms]
    ones = (1,) * (bits - len(far))
    terms = [
        tuple(a.reshape((2,) * len(far) + ones + (shard_rows, a.shape[-1])) for a in part)
        for part in terms
    ]
    first_rows = carried
    returned = shift_seq(first_rows, -1)
    same_after = same_docs(token_position[-1] + 1 + jnp.arange(8, dtype=jnp.int32))
    spread = jnp.zeros_like(tail)
    for offset in range(1, tap_count):
        masked = returned * same_after[:, offset : offset + 1] * taps_all[offset]
        spread = spread + jnp.pad(masked[:offset], ((8 - offset, 0), (0, 0)))
    d_raw = lax.dynamic_update_slice(d_raw, low(tail + spread), (count - 8, 0))
    d_beta_low = low(d_beta_logit)
    fifth = -(-conv_cols // (5 * width)) * width
    conv_marks = [0, 2 * fifth, 4 * fifth, conv_cols]
    keeps, sends = halve_all(
        [
            (scatter_view(low(inner_rows(normed, d_raw[:, a:b]))),)
            for a, b in zip(conv_marks[:-1], conv_marks[1:])
        ],
        at_step(0),
    )
    d_raw, d_beta_low, sends, keeps = tied(d_raw, d_beta_low, sends, keeps)
    others = swap_all(sends, at_step(0))
    feed_sums = far_steps(terms, far)
    d_extra = jnp.pad(d_beta_low, ((0, 0), (0, extra - beta_cols)))
    d_low, gain_part = run_back_project(
        activations, d_raw, d_extra, d_gate_logit, [weight_query, weight_gate, *weights_kv]
    )
    d_low, gain_part, others = tied(d_low, gain_part, others)
    both_heads = jnp.concatenate([gain_part[0], head_gain_part])
    both_heads = both_heads + swap_head(both_heads)
    d_other = swap_head(d_low)
    small = jnp.concatenate(
        [
            inner_rows(d_beta_low, normed).reshape(-1),
            both_heads[:features],
            grad_feed_gain,
            tap_grads.reshape(-1),
            both_heads[features:],
        ]
    )
    small = jnp.pad(small, (0, -small.shape[0] % 1024)).reshape(-1, 128)
    for at in (1, 2):
        keeps, sends = halve_all(list(zip(keeps, others)), at_step(at))
        small, sends, keeps = tied(small, sends, keeps)
        others = swap_all(sends, at_step(at))
        small = small + swap_seq(small, near[at - 1])
        if at == 1:
            d_normed = d_low.astype(F32) + d_other.astype(F32)
            d_input_norm, _ = norm_back(activations.astype(F32), gain_one, d_normed)
            grad_input = own_half(d_hidden + d_input_norm)
            grad_input, small, others = tied(grad_input, small, others)
        else:
            small, others = tied(small, others)
    conv_sum = jnp.concatenate(far_steps(list(zip(keeps, others)), far), 1)
    for distance in near[2:] + far:
        small = small + swap_seq(small, distance)
    small = small.reshape(-1)
    ends, at = [], 0
    for size in (beta_cols * features, features, features, tap_count * conv_cols, width):
        ends.append(small[at : at + size])
        at += size
    own_rows = lambda vector: lax.dynamic_slice_in_dim(
        vector, device_rank * shard_rows, shard_rows, vector.ndim - 1
    )
    tap_total = ends[3].reshape(tap_count, conv_cols)
    cut = lambda array, start, size: array[:, start : start + size]
    return (
        output,
        grad_input,
        cut(conv_sum, 0, query_cols),
        cut(conv_sum, query_cols, key_cols),
        cut(conv_sum, query_cols + key_cols, key_cols),
        own_rows(ends[0].reshape(beta_cols, features)).T,
        feed_sums[4],
        feed_sums[3].T,
        cut(tap_total, 0, query_cols),
        cut(tap_total, query_cols, key_cols),
        cut(tap_total, query_cols + key_cols, key_cols),
        own_rows(ends[1]),
        ends[4],
        own_rows(ends[2]),
        feed_sums[0],
        feed_sums[1],
        feed_sums[2].T,
    )


def solution(mesh):
    in_specs = (
        P("seq", None),
        P("seq", "head"),
        P(),
        P("seq", "head"),
        P("seq", "head"),
        P("seq", "head"),
        P("seq", "head"),
        P("seq", "head"),
        P("head", "seq"),
        P(None, "head"),
        P(None, "head"),
        P(None, "head"),
        P("seq"),
        P(),
        P("seq"),
        P("seq", "head"),
        P("seq", "head"),
        P("head", "seq"),
        P("seq", None),
    )
    out_specs = (
        P("seq", "head"),
        P("seq", "head"),
        P("seq", "head"),
        P("seq", "head"),
        P("seq", "head"),
        P("seq", "head"),
        P("seq", "head"),
        P("head", "seq"),
        P(None, "head"),
        P(None, "head"),
        P(None, "head"),
        P("seq"),
        P(),
        P("seq"),
        P("seq", "head"),
        P("seq", "head"),
        P("head", "seq"),
    )
    return jax.shard_map(
        per_device, mesh=mesh, in_specs=in_specs, out_specs=out_specs, check_vma=False
    )
```

time: 666 us -> 587 us (0.88)
  waiting for transfers between devices: 217 us -> 106 us
  Pallas kernels: 125 us -> 211 us
  matrix products: 100 us -> 32.8 us
  starting transfers between devices: 49 us -> 85.5 us
  local copies, waits for them, and re-layouts: 70.1 us -> 49.6 us
  between operations: 16.8 us -> 3.34 us
  other arithmetic: 78.7 us -> 87.6 us
    pallas_call x0 -> x9, Pallas kernels: none -> 101 us  [the longest x1 28.1 us: run_feed(): pl.pallas_call(feed_kernel, grid=(count // tile,), in_specs=[tokens(featu...]
    all_gather x2 -> x0, waiting for transfers between devices: 97.6 us -> none  [the longest x1 97.6 us: per_device(): first_full = lax.all_gather(first_pack, 'seq', axis=0, tiled=True)]
    dot_general x14 -> x0, matrix products: 68.2 us -> none  [the longest x6 36.7 us: product(): return jnp.dot(former, latter, preferred_element_type=F32)]
    ppermute x38 -> x68, starting transfers between devices: 43.2 us -> 79.7 us  [swap_seq(): lax.ppermute(array, 'seq', [(i, i ^ distance) for i in range(lax.axis_siz...]
    select_n x0 -> x29, other arithmetic: none -> 27.4 us  [the longest x28 27.4 us: gather_join(): jnp.where(upper, other, view)]
    add x24 -> x1, other arithmetic: 23.5 us -> 0.01 us  [per_device(): both_heads = both_heads + swap_head(both_heads)]
    concatenate x3 -> x34, other arithmetic: 2.8 us -> 25.8 us  [the longest x30 24.9 us: gather_join(): jnp.concatenate([jnp.where(upper, other, view), jnp.where(upper, view, ot...]
    unnamed x195 -> x161, local copies, waits for them, and re-layouts: 32.4 us -> 12.2 us
  transfers between devices with their start and end apart: 47 -> 75, of which waited for: 18 -> 30; matrix products, arithmetic and copies ran while one was open for 23% -> 24% of each run, Pallas kernels for 16% -> 28%
where the time goes in v3:
time: 587 us; the launch traced here: 576 us
  Pallas kernels  211 us (36%)
  waiting for transfers between devices  106 us (18%)
  other arithmetic  87.6 us (15%)
  starting transfers between devices  85.5 us (15%)
  local copies, waits for them, and re-layouts  49.6 us (8%)
  matrix products  32.8 us (6%)
    ppermute x68, waiting for transfers between devices, swap_seq(): lax.ppermute(array, 'seq', [(i, i ^ distance) for i in range(lax.axis_siz...  103 us
    ppermute x68, starting transfers between devices, swap_seq(): lax.ppermute(array, 'seq', [(i, i ^ distance) for i in range(lax.axis_siz...  79.7 us
    pallas_call x3, Pallas kernels, run_backward(): pl.pallas_call(functools.partial(backward_kernel, head_count, substeps, w...  51.5 us
    pallas_call x3, Pallas kernels, run_forward(): pl.pallas_call(functools.partial(forward_kernel, head_count, substeps, wi...  36.9 us
    dot_general x9, matrix products, inner_rows(): lax.dot_general(former, latter, (((0,), (0,)), ((), ())), preferred_eleme...  32.8 us
    pallas_call x1, Pallas kernels, run_feed(): pl.pallas_call(feed_kernel, grid=(count // tile,), in_specs=[tokens(featu...  28.1 us
    select_n x28, other arithmetic, gather_join(): jnp.where(upper, other, view)  27.4 us
    concatenate x30, other arithmetic, gather_join(): jnp.concatenate([jnp.where(upper, other, view), jnp.where(upper, view, ot...  24.9 us
  transfers between devices with their start and end apart: 75, of which 30 were waited for; matrix products, arithmetic and copies ran while one was open for 24% of the time, Pallas kernels for 28%

profile of v3, /device:TPU:0, one launch (start us, length us, event | category | flops | bytes accessed | tf_op | source)
XLA Modules:
  0.0 576.0 jit_solution(4731402378159614208)
XLA Ops:
  4.2 4.1 collective-permute-start
  15.8 6.3 %fusion.35 = f32[16,64,4]{2,0,1:T(8,128)S(1)} fusion(f32[16,64,4]{2,0,1:T(8,128)S(1)} %copy.161), kind=kOutput, calls=%fused_computation.243 | output fusion | flops 258048 | bytes 32768 | tf_op jit(solution)/shard_map/jit(cumsum)/reduce_window_sum | solution.py:1263
  44.0 6.7 %collective-permute-done.5 = bf16[2,1,1,2,64,768]{5,4,3,2,1,0:T(8,128)(2,1)S(1)} collective-permute-done((bf16[2,1,1,2,64,768]{5,4,3,2,1,0:T(8,128)(2,1)S(1)}, bf16[2,1,1,2,64,768]{5,4,3,2,1,0:T(8,128)(2,1)S(1)}, u32[]{:S(2)}, u32[]{:S(2)}) %collective-permute-start.5) | collective-permute-done | bytes 393248 | tf_op jit(solution)/shard_map/ppermute | solution.py:914
  52.7 9.1 %collective-permute-done.9 = bf16[2,1,2,2,64,640]{5,4,3,2,1,0:T(8,128)(2,1)S(1)} collective-permute-done((bf16[2,1,2,2,64,640]{5,4,3,2,1,0:T(8,128)(2,1)S(1)}, bf16[2,1,2,2,64,640]{5,4,3,2,1,0:T(8,128)(2,1)S(1)}, u32[]{:S(2)}, u32[]{:S(2)}) %collective-permute-start.9) | collective-permute-done | bytes 655392 | tf_op jit(solution)/shard_map/ppermute | solution.py:914
  74.3 10.5 %project.1 = (bf16[1024,1024]{1,0:T(8,128)(2,1)}, bf16[16,1024]{1,0:T(8,128)(2,1)}, bf16[1024,2048]{1,0:T(8,128)(2,1)}, bf16[16,2048]{1,0:T(8,128)(2,1)}, f32[1024,128]{1,0:T(8,128)}) custom-call(bf16[1024,1024]{1,0:T(8,128)(2,1)} %inputs.5, bf16[16,1024]{1,0:T(8,128)(2,1)} %copy-done.62, f32[1,1024]{1,0:T(1,128)} %copy.159.gain, ...), custom_call_target="tpu_custom_call" | custom-call | tf_op jit(solution)/shard_map/project/pallas_call | solution.py:646
  93.4 9.7 %mixer_forward.3 = (bf16[16,4,128,128]{3,2,1,0:T(8,128)(2,1)}, bf16[16,4,128,128]{3,2,1,0:T(8,128)(2,1)}, bf16[16,4,128,128]{3,2,1,0:T(8,128)(2,1)}, bf16[16,4,1...) custom-call(bf16[1024,2048]{1,0:T(8,128)(2,1)} %get-tuple-element.267.raw.before, ...), custom_call_target="tpu_custom_call" | custom-call | tf_op jit(solution)/shard_map/mixer_forward/pallas_call | solution.py:237
  114.9 4.0 collective-permute-done.22
  120.1 13.7 %mixer_forward.4 = (bf16[16,4,128,128]{3,2,1,0:T(8,128)(2,1)}, bf16[16,4,128,128]{3,2,1,0:T(8,128)(2,1)}, bf16[16,4,128,128]{3,2,1,0:T(8,128)(2,1)}, bf16[16,4,1...) custom-call(bf16[1024,2048]{1,0:T(8,128)(2,1)} %get-tuple-element.26, ...), custom_call_target="tpu_custom_call", output_to_operand_aliasing={{0}: (9, {}), {1}: (10, {}), {2}: (11, {}), {3}: (12, {}), ... | custom-call | tf_op jit(solution)/shard_map/mixer_forward/pallas_call | solution.py:237
  142.0 13.4 %mixer_forward.5 = (bf16[16,4,128,128]{3,2,1,0:T(8,128)(2,1)}, bf16[16,4,128,128]{3,2,1,0:T(8,128)(2,1)}, bf16[16,4,128,128]{3,2,1,0:T(8,128)(2,1)}, bf16[16,4,1...) custom-call(bf16[1024,2048]{1,0:T(8,128)(2,1)} %get-tuple-element.26, ...), custom_call_target="tpu_custom_call", output_to_operand_aliasing={{0}: (9, {}), {1}: (10, {}), {2}: (11, {}), {3}: (12, {}), ... | custom-call | tf_op jit(solution)/shard_map/mixer_forward/pallas_call | solution.py:237
  184.7 3.8 collective-permute-done.30.other.other_map
  195.5 6.5 %collective-permute-done.31.other.other_map = bf16[4,128,256]{2,1,0:T(8,128)(2,1)S(1)} collective-permute-done((bf16[4,128,256]{2,1,0:T(8,128)(2,1)}, bf16[4,128,256]{2,1,0:T(8,128)(2,1)S(1)}, u32[]{:S(2)}, u32[]{:S(2)}) %collective-permute-start.31) | collective-permute-done | bytes 262176 | tf_op jit(solution)/shard_map/ppermute | solution.py:914
  216.6 6.8 %project_side.1 = (bf16[1024,512]{1,0:T(8,128)(2,1)}, bf16[16,512]{1,0:T(8,128)(2,1)}, f32[1024,512]{1,0:T(8,128)}) custom-call(bf16[1024,1024]{1,0:T(8,128)(2,1)} %get-tuple-element.265.normed, bf16[16,1024]{1,0:T(8,128)(2,1)} %get-tuple-element.266.edge, bf16[1024,512]{1,0:T(8,128)(2,1)} %bitcast.195, bf16[1024,512]{1,0:T(8,128)(2,1)} %bitcast.193), custom_call_target="tpu_custom_call" | custom-call | tf_op jit(solution)/shard_map/project_side/pallas_call | solution.py:683
  223.4 11.0 %mixer_query.1 = (bf16[1024,512]{1,0:T(8,128)(2,1)}, f32[1024,512]{1,0:T(8,128)}) custom-call(bf16[1024,512]{1,0:T(8,128)(2,1)} %get-tuple-element.299.raw.before.raw_q.before_q, bf16[1024,512]{1,0:T(8,128)(2,1)} %get-tuple-element.299.raw.before.raw_q.before_q, bf16[16,512]{1,0:T(8,128)(2,1)} %get-tuple-element.300.edge.edge_q, f32[4,512]{1,0:T(4,128)} %slice.209.taps, ...), custom_call_target="tpu_custom_call" | custom-call | tf_op jit(solution)/shard_map/mixer_query/pallas_call | solution.py:321
  238.2 7.6 %heads.1 = (f32[1024,512]{1,0:T(8,128)}, bf16[1024,512]{1,0:T(8,128)(2,1)}, f32[1024,1024]{1,0:T(8,128)}, bf16[1024,1024]{1,0:T(8,128)(2,1)}) custom-call(f32[1024,512]{1,0:T(8,128)} %get-tuple-element.315.local, bf16[1024,512]{1,0:T(8,128)(2,1)} %get-tuple-element.316.reach, bf16[4,128,128]{2,1,0:T(8,128)(2,1)} %slice.168.state.state_in, ...), custom_call_target="tpu_custom_call" | custom-call | tf_op jit(solution)/shard_map/heads/pallas_call | solution.py:726
  259.8 28.1 %feed.1 = (f32[1024,1024]{1,0:T(8,128)}, bf16[1024,1024]{1,0:T(8,128)(2,1)}, bf16[1024,1408]{1,0:T(8,128)(2,1)}, bf16[1024,1408]{1,0:T(8,128)(2,1)}, bf16[1024,1...) custom-call(bf16[1024,1024]{1,0:T(8,128)(2,1)} %inputs.5, ...), custom_call_target="tpu_custom_call" | custom-call | tf_op jit(solution)/shard_map/feed/pallas_call | solution.py:778
  288.0 6.1 %convolution_convert_fusion.2 = bf16[1408,1024]{0,1:T(8,128)(2,1)S(1)} fusion(bf16[1024,1408]{1,0:T(8,128)(2,1)} %get-tuple-element.347, bf16[1024,1024]{1,0:T(8,128)(2,1)} %cotangent.3), kind=kOutput, calls=%fused_computation.7 | convolution fusion | flops 2954231808 | bytes 7864320 | tf_op jit(solution)/shard_map/dot_general | solution.py:29
  297.5 3.7 convolution_convert_fusion
  301.2 4.8 convolution_convert_fusion.1
  308.1 11.9 %turn.1 = (f32[1024,1024]{1,0:T(8,128)}, bf16[1024,1024]{1,0:T(8,128)(2,1)}, bf16[1024,512]{1,0:T(8,128)(2,1)}, bf16[1024,512]{1,0:T(8,128)(2,1)}, f32[4,128,128...) custom-call(f32[1024,1024]{1,0:T(8,128)} %get-tuple-element.343.hidden, f32[1024,1024]{1,0:T(8,128)} %get-tuple-element.345.own, ...), custom_call_target="tpu_custom_call" | custom-call | tf_op jit(solution)/shard_map/turn/pallas_call | solution.py:839
  331.4 4.1 convolution_convert_fusion.4
  335.5 7.6 %collective-permute-done.40.other = bf16[4,128,128]{2,1,0:T(8,128)(2,1)S(1)} collective-permute-done((bf16[4,128,128]{2,1,0:T(8,128)(2,1)}, bf16[4,128,128]{2,1,0:T(8,128)(2,1)S(1)}, u32[]{:S(2)}, u32[]{:S(2)}) %collective-permute-start.40) | collective-permute-done | bytes 131104 | tf_op jit(solution)/shard_map/ppermute | solution.py:914
  348.3 4.2 convolution_convert_fusion.5
  372.8 29.9 %mixer_backward.3 = (bf16[1024,2560]{1,0:T(8,128)(2,1)}, f32[1024,8]{1,0:T(8,128)}, f32[8,2560]{1,0:T(8,128)}, f32[4,128,128]{2,1,0:T(8,128)}, f32[8,2560]{1,0:T(8,128)}, /*index=5*/f32[4,2560]{1,0:T(4,128)}) custom-call(bf16[1024,512]{1,0:T(8,128)(2,1)} %get-tuple-element.299.raw.before.raw_q.before_q, ...), custom_call_target="tpu_custom_call" | custom-call | tf_op jit(solution)/shard_map/mixer_backward/pallas_call | solution.py:551
  403.5 7.0 %halve.2 = (bf16[256,1408]{1,0:T(8,128)(2,1)}, bf16[256,1408]{1,0:T(8,128)(2,1)}, bf16[256,1408]{1,0:T(8,128)(2,1)}, bf16[256,1408]{1,0:T(8,128)(2,1)}, bf16[256...) custom-call(s32[1]{0:T(128)} %bitcast.31.me, ...), custom_call_target="tpu_custom_call" | custom-call | tf_op jit(solution)/shard_map/halve/pallas_call | solution.py:1123
  421.1 13.8 %mixer_backward.4 = (bf16[1024,2560]{1,0:T(8,128)(2,1)}, f32[1024,8]{1,0:T(8,128)}, f32[8,2560]{1,0:T(8,128)}, f32[4,128,128]{2,1,0:T(8,128)}, f32[8,2560]{1,0:T(8,128)}, /*index=5*/f32[4,2560]{1,0:T(4,128)}) custom-call(bf16[1024,512]{1,0:T(8,128)(2,1)} %get-tuple-element.299.raw.before.raw_q.before_q, ...), custom_call_target="tpu_custom_call", output_to_operand_aliasing={{0}: (20, {}), {1}: (21, {})} | custom-call | tf_op jit(solution)/shard_map/mixer_backward/pallas_call | solution.py:551
  436.3 4.6 halve.3
  446.2 7.8 %mixer_backward.5 = (bf16[1024,2560]{1,0:T(8,128)(2,1)}, f32[1024,8]{1,0:T(8,128)}, f32[8,2560]{1,0:T(8,128)}, f32[4,128,128]{2,1,0:T(8,128)}, f32[8,2560]{1,0:T(8,128)}, /*index=5*/f32[4,2560]{1,0:T(4,128)}) custom-call(bf16[1024,512]{1,0:T(8,128)(2,1)} %get-tuple-element.299.raw.before.raw_q.before_q, ...), custom_call_target="tpu_custom_call", output_to_operand_aliasing={{0}: (20, {}), {1}: (21, {})} | custom-call | tf_op jit(solution)/shard_map/mixer_backward/pallas_call | solution.py:551
  461.8 4.2 fusion.9
  483.0 14.1 %back_project.1 = (bf16[1024,1024]{1,0:T(8,128)(2,1)}, f32[1,1024]{1,0:T(1,128)}) custom-call(bf16[1024,1024]{1,0:T(8,128)(2,1)} %inputs.5, bf16[1024,2560]{1,0:T(8,128)(2,1)} %fusion.21.d_raw, bf16[1024,128]{1,0:T(8,128)(2,1)} %pad.24.d_extra, bf16[1024,512]{1,0:T(8,128)(2,1)} %get-tuple-element.374.d_gate, bf16[1024,512]{1,0:T(8,128)(2,1)} %bitcast.196, ...), custom_call_target="tpu_custom_call" | custom-call | tf_op jit(solution)/shard_map/back_project/pallas_call | solution.py:889
  520.7 3.9 collective-permute-done.64
  524.7 12.2 %collective-permute-done.65 = bf16[2,1,1,2,64,1024]{5,4,3,2,1,0:T(8,128)(2,1)S(1)} collective-permute-done((bf16[2,1,1,2,64,1024]{5,4,3,2,1,0:T(8,128)(2,1)S(1)}, bf16[2,1,1,2,64,1024]{5,4,3,2,1,0:T(8,128)(2,1)S(1)}, u32[]{:S(2)}, u32[]{:S(2)}) %collective-permute-start.65) | collective-permute-done | bytes 524320 | tf_op jit(solution)/shard_map/ppermute | solution.py:914
  557.5 11.2 %collective-permute-done.73 = f32[168,128]{1,0:T(8,128)S(1)} collective-permute-done((f32[168,128]{1,0:T(8,128)S(1)}, f32[168,128]{1,0:T(8,128)S(1)}, u32[]{:S(2)}, u32[]{:S(2)}) %collective-permute-start.73) | collective-permute-done | bytes 86048 | tf_op jit(solution)/shard_map/ppermute | solution.py:914
  (484 shorter events, 280.3 us)
Async XLA Ops:
  4.2 23.0 %collective-permute-start = (bf16[1,1,1,1,64,2176]{5,4,3,2,1,0:T(8,128)(2,1)S(1)}, bf16[1,1,1,1,64,2176]{5,4,3,2,1,0:T(8,128)(2,1)S(1)}, u32[]{:S(2)}, u32[]{:S(2)}) collective-permute-start(bf16[1,1,1,1,64,2176]{5,4,3,2,1,0:T(8,128)(2,1)S(1)} %bitcast.204), channel_id=1, source_target_pairs={{0,16},{2,18},{4,20},{6,22},{8,24},{10,26},{12,28},{14,30},{16,0},... | collective-permute-start | bytes 835592 | tf_op jit(solution)/shard_map/ppermute | solution.py:914
  9.6 58.6 %collective-permute-start.11 = (bf16[16,1024]{1,0:T(8,128)(2,1)}, bf16[16,1024]{1,0:T(8,128)(2,1)S(1)}, u32[]{:S(2)}, u32[]{:S(2)}) collective-permute-start(bf16[16,1024]{1,0:T(8,128)(2,1)} %slice.160), channel_id=1, source_target_pairs={{0,2},{2,4},{4,6},{6,8},{8,10},{10,12},{12,14},{14,16},{16,18},{18... | collective-permute-start | bytes 98312 | tf_op jit(solution)/shard_map/ppermute | solution.py:908
  43.3 18.4 %collective-permute-start.9 = (bf16[2,1,2,2,64,640]{5,4,3,2,1,0:T(8,128)(2,1)S(1)}, bf16[2,1,2,2,64,640]{5,4,3,2,1,0:T(8,128)(2,1)S(1)}, u32[]{:S(2)}, u32[]{:S(2)}) collective-permute-start(bf16[2,1,2,2,64,640]{5,4,3,2,1,0:T(8,128)(2,1)S(1)} %pad_maximum_fusion.18), channel_id=1, source_target_pairs={{0,8},{2,10},{4,12},{6,14},{8,0},{10,2},{12,4},{14,6},{16,24},{18,... | collective-permute-start | bytes 1966088 | tf_op jit(solution)/shard_map/ppermute | solution.py:914
  68.2 34.9 %collective-permute-start.18 = (bf16[1,1,1,1,64,4224]{5,4,3,2,1,0:T(8,128)(2,1)S(1)}, bf16[1,1,1,1,64,4224]{5,4,3,2,1,0:T(8,128)(2,1)}, u32[]{:S(2)}, u32[]{:S(2)}) collective-permute-start(bf16[1,1,1,1,64,4224]{5,4,3,2,1,0:T(8,128)(2,1)S(1)} %bitcast.199), channel_id=1, source_target_pairs={{0,16},{2,18},{4,20},{6,22},{8,24},{10,26},{12,28},{14,30},{16,0},... | collective-permute-start | bytes 1622024 | tf_op jit(solution)/shard_map/ppermute | solution.py:914
  71.5 16.0 %collective-permute-start.12 = (bf16[2,1,1,1,64,512]{5,4,3,2,1,0:T(8,128)(2,1)S(1)}, bf16[2,1,1,1,64,512]{5,4,3,2,1,0:T(8,128)(2,1)}, u32[]{:S(2)}, u32[]{:S(2)}) collective-permute-start(bf16[2,1,1,1,64,512]{5,4,3,2,1,0:T(8,128)(2,1)S(1)} %get-tuple-element.270), channel_id=1, source_target_pairs={{0,8},{2,10},{4,12},{6,14},{8,0},{10,2},{12,4},{14,6},{16,24},{18,... | collective-permute-start | bytes 393224 | tf_op jit(solution)/shard_map/ppermute | solution.py:914
  110.4 23.5 %collective-permute-start.19 = (bf16[2,2,2,1,64,512]{5,4,3,2,1,0:T(8,128)(2,1)}, bf16[2,2,2,1,64,512]{5,4,3,2,1,0:T(8,128)(2,1)}, u32[]{:S(2)}, u32[]{:S(2)}) collective-permute-start(bf16[2,2,2,1,64,512]{5,4,3,2,1,0:T(8,128)(2,1)} %pad_maximum_fusion.21), channel_id=1, source_target_pairs={{0,2},{2,0},{4,6},{6,4},{8,10},{10,8},{12,14},{14,12},{16,18},{18,... | collective-permute-start | bytes 1572872 | tf_op jit(solution)/shard_map/ppermute | solution.py:914
  110.5 23.3 %collective-permute-start.20 = (bf16[2,2,1,2,64,512]{5,4,3,2,1,0:T(8,128)(2,1)}, bf16[2,2,1,2,64,512]{5,4,3,2,1,0:T(8,128)(2,1)}, u32[]{:S(2)}, u32[]{:S(2)}) collective-permute-start(bf16[2,2,1,2,64,512]{5,4,3,2,1,0:T(8,128)(2,1)} %pad_maximum_fusion.22), channel_id=1, source_target_pairs={{0,4},{2,6},{4,0},{6,2},{8,12},{10,14},{12,8},{14,10},{16,20},{18,... | collective-permute-start | bytes 1572872 | tf_op jit(solution)/shard_map/ppermute | solution.py:914
  112.2 21.7 %collective-permute-start.21 = (bf16[2,1,2,2,64,512]{5,4,3,2,1,0:T(8,128)(2,1)S(1)}, bf16[2,1,2,2,64,512]{5,4,3,2,1,0:T(8,128)(2,1)}, u32[]{:S(2)}, u32[]{:S(2)}) collective-permute-start(bf16[2,1,2,2,64,512]{5,4,3,2,1,0:T(8,128)(2,1)S(1)} %pad_maximum_fusion.23), channel_id=1, source_target_pairs={{0,8},{2,10},{4,12},{6,14},{8,0},{10,2},{12,4},{14,6},{16,24},{18,... | collective-permute-start | bytes 1572872 | tf_op jit(solution)/shard_map/ppermute | solution.py:914
  113.9 19.9 %collective-permute-start.23 = (bf16[2,1,1,1,64,1408]{5,4,3,2,1,0:T(8,128)(2,1)}, bf16[2,1,1,1,64,1408]{5,4,3,2,1,0:T(8,128)(2,1)}, u32[]{:S(2)}, u32[]{:S(2)}) collective-permute-start(bf16[2,1,1,1,64,1408]{5,4,3,2,1,0:T(8,128)(2,1)} %get-tuple-element.295), channel_id=1, source_target_pairs={{0,2},{2,0},{4,6},{6,4},{8,10},{10,8},{12,14},{14,12},{16,18},{18,... | collective-permute-start | bytes 1081352 | tf_op jit(solution)/shard_map/ppermute | solution.py:914
  138.3 17.2 %collective-permute-start.25 = (bf16[2,2,1,1,64,1408]{5,4,3,2,1,0:T(8,128)(2,1)S(1)}, bf16[2,2,1,1,64,1408]{5,4,3,2,1,0:T(8,128)(2,1)}, u32[]{:S(2)}, u32[]{:S(2)}) collective-permute-start(bf16[2,2,1,1,64,1408]{5,4,3,2,1,0:T(8,128)(2,1)S(1)} %pad_maximum_fusion.15), channel_id=1, source_target_pairs={{0,4},{2,6},{4,0},{6,2},{8,12},{10,14},{12,8},{14,10},{16,20},{18,... | collective-permute-start | bytes 2162696 | tf_op jit(solution)/shard_map/ppermute | solution.py:914
  139.9 15.6 %collective-permute-start.26 = (bf16[2,1,1,2,64,1408]{5,4,3,2,1,0:T(8,128)(2,1)}, bf16[2,1,1,2,64,1408]{5,4,3,2,1,0:T(8,128)(2,1)}, u32[]{:S(2)}, u32[]{:S(2)}) collective-permute-start(bf16[2,1,1,2,64,1408]{5,4,3,2,1,0:T(8,128)(2,1)} %pad_maximum_fusion.16), channel_id=1, source_target_pairs={{0,8},{2,10},{4,12},{6,14},{8,0},{10,2},{12,4},{14,6},{16,24},{18,... | collective-permute-start | bytes 2162696 | tf_op jit(solution)/shard_map/ppermute | solution.py:914
  206.7 39.1 %collective-permute-start.35 = (bf16[2,1,2,2,64,1408]{5,4,3,2,1,0:T(8,128)(2,1)}, bf16[2,1,2,2,64,1408]{5,4,3,2,1,0:T(8,128)(2,1)}, u32[]{:S(2)}, u32[]{:S(2)}) collective-permute-start(bf16[2,1,2,2,64,1408]{5,4,3,2,1,0:T(8,128)(2,1)} %pad_maximum_fusion.7), channel_id=1, source_target_pairs={{0,8},{2,10},{4,12},{6,14},{8,0},{10,2},{12,4},{14,6},{16,24},{18,... | collective-permute-start | bytes 4325384 | tf_op jit(solution)/shard_map/ppermute | solution.py:914
  214.2 35.6 %collective-permute-start.34 = (bf16[2,2,1,2,64,1408]{5,4,3,2,1,0:T(8,128)(2,1)}, bf16[2,2,1,2,64,1408]{5,4,3,2,1,0:T(8,128)(2,1)}, u32[]{:S(2)}, u32[]{:S(2)}) collective-permute-start(bf16[2,2,1,2,64,1408]{5,4,3,2,1,0:T(8,128)(2,1)} %pad_maximum_fusion.6), channel_id=1, source_target_pairs={{0,4},{2,6},{4,0},{6,2},{8,12},{10,14},{12,8},{14,10},{16,20},{18,... | collective-permute-start | bytes 4325384 | tf_op jit(solution)/shard_map/ppermute | solution.py:914
  236.6 19.3 %collective-permute-start.33 = (bf16[2,2,2,1,64,1408]{5,4,3,2,1,0:T(8,128)(2,1)}, bf16[2,2,2,1,64,1408]{5,4,3,2,1,0:T(8,128)(2,1)}, u32[]{:S(2)}, u32[]{:S(2)}) collective-permute-start(bf16[2,2,2,1,64,1408]{5,4,3,2,1,0:T(8,128)(2,1)} %pad_maximum_fusion.5), channel_id=1, source_target_pairs={{0,2},{2,0},{4,6},{6,4},{8,10},{10,8},{12,14},{14,12},{16,18},{18,... | collective-permute-start | bytes 4325384 | tf_op jit(solution)/shard_map/ppermute | solution.py:914
  287.9 18.2 %collective-permute-start.37 = (bf16[1024,1024]{1,0:T(8,128)(2,1)}, bf16[1024,1024]{1,0:T(8,128)(2,1)S(1)}, u32[]{:S(2)}, u32[]{:S(2)}) collective-permute-start(bf16[1024,1024]{1,0:T(8,128)(2,1)} %get-tuple-element.346), channel_id=1, source_target_pairs={{0,1},{1,0},{2,3},{3,2},{4,5},{5,4},{6,7},{7,6},{8,9},{9,8},{10,11... | collective-permute-start | bytes 6291464 | tf_op jit(solution)/shard_map/ppermute | solution.py:918
  306.1 62.1 %collective-permute-start.38 = (bf16[2,2,1,2,64,1408]{5,4,3,1,0,2:T(8,128)(2,1)}, bf16[2,2,1,2,64,1408]{5,4,3,1,0,2:T(8,128)(2,1)}, u32[]{:S(2)}, u32[]{:S(2)}) collective-permute-start(bf16[2,2,1,2,64,1408]{5,4,3,1,0,2:T(8,128)(2,1)} %dynamic-slice_bitcast_fusion.2), channel_id=1, source_target_pairs={{0,4},{2,6},{4,0},{6,2},{8,12},{10,14},{12,8},{14,10},{16,20},{18,... | collective-permute-start | bytes 4325384 | tf_op jit(solution)/shard_map/ppermute | solution.py:914
  368.2 34.6 %collective-permute-start.43 = (bf16[2,1,2,2,64,1408]{5,4,3,2,0,1:T(8,128)(2,1)}, bf16[2,1,2,2,64,1408]{5,4,3,2,0,1:T(8,128)(2,1)}, u32[]{:S(2)}, u32[]{:S(2)}) collective-permute-start(bf16[2,1,2,2,64,1408]{5,4,3,2,0,1:T(8,128)(2,1)} %dynamic-slice_bitcast_fusion.1), channel_id=1, source_target_pairs={{0,8},{2,10},{4,12},{6,14},{8,0},{10,2},{12,4},{14,6},{16,24},{18,... | collective-permute-start | bytes 4325384 | tf_op jit(solution)/shard_map/ppermute | solution.py:914
  368.2 34.5 %collective-permute-start.44 = (bf16[2,2,2,1,64,1408]{5,4,2,1,0,3:T(8,128)(2,1)}, bf16[2,2,2,1,64,1408]{5,4,2,1,0,3:T(8,128)(2,1)}, u32[]{:S(2)}, u32[]{:S(2)}) collective-permute-start(bf16[2,2,2,1,64,1408]{5,4,2,1,0,3:T(8,128)(2,1)} %dynamic-slice_bitcast_fusion), channel_id=1, source_target_pairs={{0,2},{2,0},{4,6},{6,4},{8,10},{10,8},{12,14},{14,12},{16,18},{18,... | collective-permute-start | bytes 4325384 | tf_op jit(solution)/shard_map/ppermute | solution.py:914
  369.5 33.2 %collective-permute-start.45 = (bf16[2,2,1,2,64,512]{5,4,3,1,0,2:T(8,128)(2,1)}, bf16[2,2,1,2,64,512]{5,4,3,1,0,2:T(8,128)(2,1)S(1)}, u32[]{:S(2)}, u32[]{:S(2)}) collective-permute-start(bf16[2,2,1,2,64,512]{5,4,3,1,0,2:T(8,128)(2,1)} %dynamic-slice_bitcast_fusion.4), channel_id=1, source_target_pairs={{0,4},{2,6},{4,0},{6,2},{8,12},{10,14},{12,8},{14,10},{16,20},{18,... | collective-permute-start | bytes 1572872 | tf_op jit(solution)/shard_map/ppermute | solution.py:914
  370.2 32.5 %collective-permute-start.46 = (bf16[2,2,1,2,64,512]{5,4,3,1,0,2:T(8,128)(2,1)}, bf16[2,2,1,2,64,512]{5,4,3,1,0,2:T(8,128)(2,1)}, u32[]{:S(2)}, u32[]{:S(2)}) collective-permute-start(bf16[2,2,1,2,64,512]{5,4,3,1,0,2:T(8,128)(2,1)} %dynamic-slice_bitcast_fusion.3), channel_id=1, source_target_pairs={{0,4},{2,6},{4,0},{6,2},{8,12},{10,14},{12,8},{14,10},{16,20},{18,... | collective-permute-start | bytes 1572872 | tf_op jit(solution)/shard_map/ppermute | solution.py:914
  410.5 24.8 %collective-permute-start.47 = (bf16[256,1408]{1,0:T(8,128)(2,1)}, bf16[256,1408]{1,0:T(8,128)(2,1)S(1)}, u32[]{:S(2)}, u32[]{:S(2)}) collective-permute-start(bf16[256,1408]{1,0:T(8,128)(2,1)} %get-tuple-element.409), channel_id=1, source_target_pairs={{0,4},{2,6},{4,0},{6,2},{8,12},{10,14},{12,8},{14,10},{16,20},{18,... | collective-permute-start | bytes 2162696 | tf_op jit(solution)/shard_map/ppermute | solution.py:914
  411.3 24.1 %collective-permute-start.48 = (bf16[256,1408]{1,0:T(8,128)(2,1)}, bf16[256,1408]{1,0:T(8,128)(2,1)}, u32[]{:S(2)}, u32[]{:S(2)}) collective-permute-start(bf16[256,1408]{1,0:T(8,128)(2,1)} %get-tuple-element.410), channel_id=1, source_target_pairs={{0,8},{2,10},{4,12},{6,14},{8,0},{10,2},{12,4},{14,6},{16,24},{18,... | collective-permute-start | bytes 2162696 | tf_op jit(solution)/shard_map/ppermute | solution.py:914
  413.2 22.2 %collective-permute-start.49 = (bf16[256,1408]{1,0:T(8,128)(2,1)}, bf16[256,1408]{1,0:T(8,128)(2,1)}, u32[]{:S(2)}, u32[]{:S(2)}) collective-permute-start(bf16[256,1408]{1,0:T(8,128)(2,1)} %get-tuple-element.411), channel_id=1, source_target_pairs={{0,2},{2,0},{4,6},{6,4},{8,10},{10,8},{12,14},{14,12},{16,18},{18,... | collective-permute-start | bytes 2162696 | tf_op jit(solution)/shard_map/ppermute | solution.py:914
  418.1 17.2 %collective-permute-start.50 = (bf16[256,512]{1,0:T(8,128)(2,1)}, bf16[256,512]{1,0:T(8,128)(2,1)S(1)}, u32[]{:S(2)}, u32[]{:S(2)}) collective-permute-start(bf16[256,512]{1,0:T(8,128)(2,1)} %get-tuple-element.412), channel_id=1, source_target_pairs={{0,2},{2,0},{4,6},{6,4},{8,10},{10,8},{12,14},{14,12},{16,18},{18,... | collective-permute-start | bytes 786440 | tf_op jit(solution)/shard_map/ppermute | solution.py:914
  419.9 15.5 %collective-permute-start.51 = (bf16[256,512]{1,0:T(8,128)(2,1)}, bf16[256,512]{1,0:T(8,128)(2,1)}, u32[]{:S(2)}, u32[]{:S(2)}) collective-permute-start(bf16[256,512]{1,0:T(8,128)(2,1)} %get-tuple-element.413), channel_id=1, source_target_pairs={{0,8},{2,10},{4,12},{6,14},{8,0},{10,2},{12,4},{14,6},{16,24},{18,... | collective-permute-start | bytes 786440 | tf_op jit(solution)/shard_map/ppermute | solution.py:914
  457.1 20.2 %collective-permute-start.36 = (bf16[1024,512]{1,0:T(8,128)(2,1)S(1)}, bf16[1024,512]{1,0:T(8,128)(2,1)S(1)}, u32[]{:S(2)}, u32[]{:S(2)}) collective-permute-start(bf16[1024,512]{1,0:T(8,128)(2,1)S(1)} %constant_dynamic-slice_fusion.7), channel_id=1, source_target_pairs={{0,1},{1,0},{2,3},{3,2},{4,5},{5,4},{6,7},{7,6},{8,9},{9,8},{10,11... | collective-permute-start | bytes 3145736 | tf_op jit(solution)/shard_map/ppermute | solution.py:918
  473.8 24.2 %collective-permute-start.58 = (bf16[2,2,2,1,64,1024]{5,4,3,2,1,0:T(8,128)(2,1)}, bf16[2,2,2,1,64,1024]{5,4,3,2,1,0:T(8,128)(2,1)}, u32[]{:S(2)}, u32[]{:S(2)}) collective-permute-start(bf16[2,2,2,1,64,1024]{5,4,3,2,1,0:T(8,128)(2,1)} %get-tuple-element.454), channel_id=1, source_target_pairs={{0,2},{2,0},{4,6},{6,4},{8,10},{10,8},{12,14},{14,12},{16,18},{18,... | collective-permute-start | bytes 3145736 | tf_op jit(solution)/shard_map/ppermute | solution.py:914
  476.0 23.4 %collective-permute-start.59 = (bf16[2,2,1,2,64,1024]{5,4,3,2,1,0:T(8,128)(2,1)}, bf16[2,2,1,2,64,1024]{5,4,3,2,1,0:T(8,128)(2,1)}, u32[]{:S(2)}, u32[]{:S(2)}) collective-permute-start(bf16[2,2,1,2,64,1024]{5,4,3,2,1,0:T(8,128)(2,1)} %get-tuple-element.455), channel_id=1, source_target_pairs={{0,4},{2,6},{4,0},{6,2},{8,12},{10,14},{12,8},{14,10},{16,20},{18,... | collective-permute-start | bytes 3145736 | tf_op jit(solution)/shard_map/ppermute | solution.py:914
  478.9 18.2 %collective-permute-start.60 = (bf16[2,1,2,2,64,512]{5,4,3,2,1,0:T(8,128)(2,1)}, bf16[2,1,2,2,64,512]{5,4,3,2,1,0:T(8,128)(2,1)}, u32[]{:S(2)}, u32[]{:S(2)}) collective-permute-start(bf16[2,1,2,2,64,512]{5,4,3,2,1,0:T(8,128)(2,1)} %get-tuple-element.456), channel_id=1, source_target_pairs={{0,8},{2,10},{4,12},{6,14},{8,0},{10,2},{12,4},{14,6},{16,24},{18,... | collective-permute-start | bytes 1572872 | tf_op jit(solution)/shard_map/ppermute | solution.py:914
  508.8 32.7 %collective-permute-start.74 = (bf16[1,1,1,1,64,5248]{5,4,3,2,1,0:T(8,128)(2,1)S(1)}, bf16[1,1,1,1,64,5248]{5,4,3,2,1,0:T(8,128)(2,1)S(1)}, u32[]{:S(2)}, u32[]{:S(2)}) collective-permute-start(bf16[1,1,1,1,64,5248]{5,4,3,2,1,0:T(8,128)(2,1)S(1)} %fusion.19), channel_id=1, source_target_pairs={{0,16},{2,18},{4,20},{6,22},{8,24},{10,26},{12,28},{14,30},{16,0},... | collective-permute-start | bytes 2015240 | tf_op jit(solution)/shard_map/ppermute | solution.py:914
  513.0 23.9 %collective-permute-start.65 = (bf16[2,1,1,2,64,1024]{5,4,3,2,1,0:T(8,128)(2,1)S(1)}, bf16[2,1,1,2,64,1024]{5,4,3,2,1,0:T(8,128)(2,1)S(1)}, u32[]{:S(2)}, u32[]{:S(2)}) collective-permute-start(bf16[2,1,1,2,64,1024]{5,4,3,2,1,0:T(8,128)(2,1)S(1)} %get-tuple-element.470), channel_id=1, source_target_pairs={{0,8},{2,10},{4,12},{6,14},{8,0},{10,2},{12,4},{14,6},{16,24},{18,... | collective-permute-start | bytes 1572872 | tf_op jit(solution)/shard_map/ppermute | solution.py:914
  556.7 17.4 %collective-permute-start.71 = (bf16[1,1,1,1,64,2560]{5,4,3,2,1,0:T(8,128)(2,1)S(1)}, bf16[1,1,1,1,64,2560]{5,4,3,2,1,0:T(8,128)(2,1)S(1)}, u32[]{:S(2)}, u32[]{:S(2)}) collective-permute-start(bf16[1,1,1,1,64,2560]{5,4,3,2,1,0:T(8,128)(2,1)S(1)} %pad_maximum_fusion.27), channel_id=1, source_target_pairs={{0,16},{2,18},{4,20},{6,22},{8,24},{10,26},{12,28},{14,30},{16,0},... | collective-permute-start | bytes 983048 | tf_op jit(solution)/shard_map/ppermute | solution.py:914
  (121 other events, 1066.9 us)

commit v4 on v3

--- a/solution.py
+++ b/solution.py
@@ -744,10 +744,40 @@
     )(local, reach, state, gate, gain, weight)
 
 
-def feed_kernel(
-    inputs, own, other, gain, cotangent, gate_w, up_w, down_w,
-    hidden_out, normed_out, act_out, d_gate_out, d_up_out, branch_out, own_out, low_out,
-):
+def lay_copies(view, other, own, short, rows, scratch, semaphores):
+    run = short * rows
+    copies = []
+    for block in range(view.shape[0] // run):
+        for side, at in ((view, own), (other, 1 - own)):
+            row = pl.multiple_of((2 * block + at) * run, run)
+            copies.append(
+                pltpu.make_async_copy(
+                    side.at[pl.ds(block * run, run)],
+                    scratch.at[pl.ds(row, run)],
+                    semaphores.at[len(copies)],
+                )
+            )
+    return copies
+
+
+def feed_kernel(runs, rows, me, inputs, own, other, gain, cotangent, *refs):
+    halves, outs, rest = refs[:6], refs[6:14], refs[14:]
+    hidden_out, normed_out, act_out, d_gate_out, d_up_out, branch_out, own_out, low_out = outs
+    gate_w, up_w, down_w = rest[:3]
+
+    @pl.when(pl.program_id(0) == 0)
+    def _():
+        copies = []
+        for k, short in enumerate(runs):
+            copies += lay_copies(
+                halves[2 * k], halves[2 * k + 1], (me[0] // short) % 2, short, rows, rest[k],
+                rest[3 + k],
+            )
+        for copy in copies:
+            copy.start()
+        for copy in copies:
+            copy.wait()
+
     hidden = inputs[...].astype(F32) + own[...] + other[...].astype(F32)
     hidden_out[...] = hidden
     normed = low(hidden * row_scale_of(hidden) * gain[...])
@@ -769,18 +799,34 @@
     low_out[...] = low(d_normed)
 
 
-def run_feed(inputs, own, other, gain, cotangent, gate_w, up_w, down_w):
+def run_feed(inputs, own, other, gain, cotangent, views, others, distances):
+    rows = views[0].shape[-2]
+    if rows < HALO:
+        full = gather_end([gather_join(*part) for part in zip(views, others, distances)])
+        half = full[0].shape[0] // 2
+        views, others = [w[:half] for w in full], [w[half:] for w in full]
+        distances, rows, me = [1] * 3, half, jnp.zeros((1,), jnp.int32)
+    else:
+        views, others = gather_end(views), gather_end(others)
+        me = lax.axis_index("seq").astype(jnp.int32).reshape(1)
+    halves = [half for pair in zip(views, others) for half in pair]
     count, features = inputs.shape
-    cols = gate_w.shape[1]
+    cols = views[0].shape[1]
     tile = min(TILE, count)
     tokens = lambda cols: pl.BlockSpec((tile, cols), lambda c: (c, 0))
     shape = lambda cols, kind: jax.ShapeDtypeStruct((count, cols), kind)
     return pl.pallas_call(
-        feed_kernel,
+        functools.partial(feed_kernel, distances, rows),
         grid=(count // tile,),
-        in_specs=[tokens(features)] * 3
+        in_specs=[pl.BlockSpec(memory_space=pltpu.SMEM)]
+        + [tokens(features)] * 3
         + [whole_spec(1, features), tokens(features)]
-        + [once(weight.shape) for weight in (gate_w, up_w, down_w)],
+        + [pl.BlockSpec(memory_space=pl.ANY)] * 6,
+        scratch_shapes=[pltpu.VMEM((2 * view.shape[0], cols), BF16) for view in views]
+        + [
+            pltpu.SemaphoreType.DMA((2 * (view.shape[0] // (short * rows)),))
+            for view, short in zip(views, distances)
+        ],
         out_specs=[tokens(features)] * 2 + [tokens(cols)] * 3 + [tokens(features)] * 3,
         out_shape=[shape(features, F32), shape(features, BF16)]
         + [shape(cols, BF16)] * 3
@@ -789,7 +835,7 @@
             dimension_semantics=("arbitrary",), vmem_limit_bytes=VMEM_BYTES
         ),
         name="feed",
-    )(inputs, own, other, gain, cotangent, gate_w, up_w, down_w)
+    )(me, inputs, own, other, gain, cotangent, *halves)
 
 
 def turn_kernel(
@@ -1019,7 +1065,7 @@
     )(upper, group, other, after, group_map, other_map, after_map)
 
 
-def states_before(group, eye):
+def states_before(group, eye, beside):
     count, mine = lax.axis_size("seq"), lax.axis_index("seq")
     before = jnp.concatenate([eye, jnp.zeros_like(eye)], 2)
     group_low = low(group)
@@ -1027,6 +1073,8 @@
     distance = 1
     while distance < count:
         other = swap_seq(group_low, distance)
+        if distance in beside:
+            other, _ = tied(other, beside[distance]())
         upper = ((mine // distance) % 2).astype(jnp.int32).reshape(1)
         kept.append((group, other, upper))
         final = 2 * distance >= count
@@ -1156,6 +1204,55 @@
     return jnp.concatenate(
         [jnp.where(upper, other, view), jnp.where(upper, view, other)], axis
     )
+
+
+def lay_kernel(distances, me, *refs):
+    parts = len(distances)
+    for k, distance in enumerate(distances):
+        upper = (me[0] // distance) % 2 == 1
+        view, other, out = refs[2 * k], refs[2 * k + 1], refs[2 * parts + k]
+        out[:, 0] = jnp.where(upper, other[...], view[...])
+        out[:, 1] = jnp.where(upper, view[...], other[...])
+
+
+def gather_lay(views, others, distances):
+    rows = views[0].shape[-2]
+    if rows < HALO:
+        return [gather_join(*part) for part in zip(views, others, distances)]
+    arrays, specs, out_specs, shapes, full = [], [], [], [], []
+    for view, other, distance in zip(views, others, distances):
+        axis = view.ndim - 2 - distance.bit_length()
+        before, after = view.shape[:axis], view.shape[axis + 1 :]
+        high = functools.reduce(lambda a, b: a * b, before, 1)
+        short = functools.reduce(lambda a, b: a * b, after[:-2], 1)
+        columns = view.shape[-1]
+        group = max(1, high * short // 4)
+        near_rows, far_rows = min(short, group), max(1, group // short)
+        steps = short // near_rows
+        place = lambda q, me, steps=steps: (q // steps, q % steps, 0, 0)
+        specs += [pl.BlockSpec((far_rows, near_rows, rows, columns), place)] * 2
+        out_specs.append(
+            pl.BlockSpec(
+                (far_rows, 2, near_rows, rows, columns),
+                lambda q, me, steps=steps: (q // steps, 0, q % steps, 0, 0),
+            )
+        )
+        arrays += [array.reshape(high, short, rows, columns) for array in (view, other)]
+        shapes.append(jax.ShapeDtypeStruct((high, 2, short, rows, columns), BF16))
+        full.append(before + (2,) + after)
+        blocks = high * short // group
+    outs = pl.pallas_call(
+        functools.partial(lay_kernel, distances),
+        grid_spec=pltpu.PrefetchScalarGridSpec(
+            num_scalar_prefetch=1, grid=(blocks,), in_specs=specs, out_specs=out_specs
+        ),
+        out_shape=shapes,
+        compiler_params=pltpu.CompilerParams(
+            dimension_semantics=("arbitrary",), vmem_limit_bytes=VMEM_BYTES
+        ),
+        name="lay",
+    )(lax.axis_index("seq").astype(jnp.int32).reshape(1), *arrays)
+    return [out.reshape(shape) for out, shape in zip(outs, full)]
 
 
 def gather_far(pack, distances):
@@ -1290,7 +1387,13 @@
             chain, others, feed_view = tied(chain, others, feed_view)
         else:
             chain, others = tied(chain, others)
-        joined = [gather_join(v, o, d) for v, o, d in zip(sends, others, distances)]
+        sided = 3 if call < 2 else 0
+        joined = [
+            gather_join(v, o, d)
+            for v, o, d in zip(sends[:sided], others[:sided], distances[:sided])
+        ]
+        if call > 0:
+            joined += gather_lay(sends[sided:], others[sided:], distances[sided:])
         if call == 0:
             feed_parts = gather_cut(feed_view, [hidden_cols] * 3)
             sends, distances = joined + feed_parts, gather_at(2) + gather_at(0)
@@ -1301,15 +1404,16 @@
     t_part, p_part, s_part, key_rows, solved = passed
     weight_query, weight_gate, weight_out = gather_end(sides)
 
-    state_low, kept = states_before(chain, eye)
+    held = {}
+
+    def first():
+        held["side"] = run_project_side(normed, edge_normed, weight_query, weight_gate)
+        return held["side"]
+
+    state_low, kept = states_before(chain, eye, {2: first})
+    raw_query, edge_query, gate_view = held["side"]
     state_low, feed_parts = tied(state_low, feed_parts)
     others = swap_all(feed_parts, gather_at(2))
-    feed_gate_w, feed_up_w, feed_down_w = gather_end(
-        [gather_join(v, o, d) for v, o, d in zip(feed_parts, others, gather_at(2))]
-    )
-    raw_query, edge_query, gate_view = run_project_side(
-        normed, edge_normed, weight_query, weight_gate
-    )
     q_reach, local_out = run_query(
         raw_query, edge_query, taps_all[:, :query_cols], same, cum_col, cum_row, key_rows, solved,
         p_part, s_part, head_count, substeps, width,
@@ -1318,11 +1422,12 @@
     mixer_out, heads_out, branch_own, branch_low = run_heads(
         local_out, q_reach, state_low, gate_view, head_gain_row, weight_out, head_count, width
     )
+    branch_low, others = tied(branch_low, others)
     (
         hidden, normed_ffn, activation, d_gate, d_up, branch_two, d_normed_own, d_normed_low,
     ) = run_feed(
         activations, branch_own, swap_head(branch_low), gain_two, cotangent,
-        feed_gate_w, feed_up_w, feed_down_w,
+        feed_parts, others, gather_at(2),
     )
     half = features // lax.axis_size("head")
     own_half = lambda array: lax.dynamic_slice_in_dim(array, head_rank * half, half, 1)
@@ -1335,11 +1440,11 @@
 
     near = orders[0]
     grad_orders = [
+        [near[1], near[2], near[0]],
+        [near[0], near[1], near[2]],
+        [near[2], near[0], near[1]],
+        [near[2], near[0], near[1]],
         [near[2], near[1], near[0]],
-        [near[0], near[2], near[1]],
-        [near[1], near[0], near[2]],
-        [near[1], near[0], near[2]],
-        [near[1], near[2], near[0]],
     ]
     down_grad = scatter_view(low(inner_rows(cotangent, activation)))
     _, down_send = halve_all([(down_grad,)], [grad_orders[2][0]])
@@ -1436,6 +1541,8 @@
         for part in terms
     ]
     first_rows = carried
+    zh_keeps, zh_sends = halve_all(terms, [far[0]] * len(terms))
+    zh_other = swap_seq(jnp.concatenate(zh_sends, -1), far[0])
     returned = shift_seq(first_rows, -1)
     same_after = same_docs(token_position[-1] + 1 + jnp.arange(8, dtype=jnp.int32))
     spread = jnp.zeros_like(tail)
@@ -1455,12 +1562,18 @@
     )
     d_raw, d_beta_low, sends, keeps = tied(d_raw, d_beta_low, sends, keeps)
     others = swap_all(sends, at_step(0))
-    feed_sums = far_steps(terms, far)
     d_extra = jnp.pad(d_beta_low, ((0, 0), (0, extra - beta_cols)))
     d_low, gain_part = run_back_project(
         activations, d_raw, d_extra, d_gate_logit, [weight_query, weight_gate, *weights_kv]
     )
-    d_low, gain_part, others = tied(d_low, gain_part, others)
+    d_low, gain_part, others, zh_other = tied(d_low, gain_part, others, zh_other)
+    start, feed_sums = 0, []
+    for keep in zh_keeps:
+        wide = keep.shape[-1]
+        other = lax.slice_in_dim(zh_other, start, start + wide, axis=zh_other.ndim - 1)
+        feed_sums.append((keep, other))
+        start += wide
+    feed_sums = far_steps(feed_sums, far[1:])
     both_heads = jnp.concatenate([gain_part[0], head_gain_part])
     both_heads = both_heads + swap_head(both_heads)
     d_other = swap_head(d_low)

time: 587 us -> 544 us (0.927)
  other arithmetic: 87.6 us -> 62.2 us
  waiting for transfers between devices: 106 us -> 92.2 us
  starting transfers between devices: 85.5 us -> 76.3 us
  Pallas kernels: 211 us -> 220 us
    select_n x28 -> x19, other arithmetic: 27.4 us -> 10.9 us  [gather_join(): jnp.where(upper, other, view)]
    concatenate x30 -> x21, other arithmetic: 24.9 us -> 9.41 us  [gather_join(): jnp.concatenate([jnp.where(upper, other, view), jnp.where(upper, view, ot...]
    ppermute x68, waiting for transfers between devices: 103 us -> 88.5 us  [swap_seq(): lax.ppermute(array, 'seq', [(i, i ^ distance) for i in range(lax.axis_siz...]
    ppermute x68, starting transfers between devices: 79.7 us -> 70.5 us  [swap_seq(): lax.ppermute(array, 'seq', [(i, i ^ distance) for i in range(lax.axis_siz...]
    pallas_call x1 -> x3, Pallas kernels: 28.1 us -> 36.8 us  [the longest x1 29.1 us: run_feed(): pl.pallas_call(functools.partial(feed_kernel, distances, rows), grid=(cou...]
    unnamed x161 -> x165, local copies, waits for them, and re-layouts: 12.2 us -> 10.7 us
  transfers between devices with their start and end apart: 75 -> 75, of which waited for: 30 -> 28; matrix products, arithmetic and copies ran while one was open for 24% -> 20% of each run, Pallas kernels for 28% -> 31%
where the time goes in v4:
time: 544 us; the launch traced here: 534 us
  Pallas kernels  220 us (40%)
  waiting for transfers between devices  92.2 us (17%)
  starting transfers between devices  76.3 us (14%)
  other arithmetic  62.2 us (11%)
  local copies, waits for them, and re-layouts  46.8 us (9%)
  matrix products  32.9 us (6%)
    ppermute x68, waiting for transfers between devices, swap_seq(): lax.ppermute(array, 'seq', [(i, i ^ distance) for i in range(lax.axis_siz...  88.5 us
    ppermute x68, starting transfers between devices, swap_seq(): lax.ppermute(array, 'seq', [(i, i ^ distance) for i in range(lax.axis_siz...  70.5 us
    pallas_call x3, Pallas kernels, run_backward(): pl.pallas_call(functools.partial(backward_kernel, head_count, substeps, w...  51.6 us
    pallas_call x3, Pallas kernels, run_forward(): pl.pallas_call(functools.partial(forward_kernel, head_count, substeps, wi...  36.7 us
    dot_general x9, matrix products, inner_rows(): lax.dot_general(former, latter, (((0,), (0,)), ((), ())), preferred_eleme...  32.9 us
    pallas_call x1, Pallas kernels, run_feed(): pl.pallas_call(functools.partial(feed_kernel, distances, rows), grid=(cou...  29.1 us
    pallas_call x1, Pallas kernels, run_back_project(): pl.pallas_call(functools.partial(back_project_kernel, d_extra.shape[1]),...  14.2 us
    pallas_call x1, Pallas kernels, run_turn(): pl.pallas_call(functools.partial(turn_kernel, head_count, width), grid=(c...  11.9 us
  transfers between devices with their start and end apart: 75, of which 28 were waited for; matrix products, arithmetic and copies ran while one was open for 20% of the time, Pallas kernels for 31%

profile of v4, /device:TPU:0, one launch (start us, length us, event | category | flops | bytes accessed | tf_op | source)
XLA Modules:
  0.0 533.5 jit_solution(2583003003204968682)
XLA Ops:
  4.2 4.1 collective-permute-start
  15.2 6.3 %fusion.35 = f32[16,64,4]{2,0,1:T(8,128)S(1)} fusion(f32[16,64,4]{2,0,1:T(8,128)S(1)} %copy.176), kind=kOutput, calls=%fused_computation.216 | output fusion | flops 258048 | bytes 32768 | tf_op jit(solution)/shard_map/jit(cumsum)/reduce_window_sum | solution.py:1360
  44.1 6.7 %collective-permute-done.5 = bf16[2,1,1,2,64,768]{5,4,3,2,1,0:T(8,128)(2,1)S(1)} collective-permute-done((bf16[2,1,1,2,64,768]{5,4,3,2,1,0:T(8,128)(2,1)S(1)}, bf16[2,1,1,2,64,768]{5,4,3,2,1,0:T(8,128)(2,1)S(1)}, u32[]{:S(2)}, u32[]{:S(2)}) %collective-permute-start.5) | collective-permute-done | bytes 393248 | tf_op jit(solution)/shard_map/ppermute | solution.py:960
  52.8 9.1 %collective-permute-done.9 = bf16[2,1,2,2,64,640]{5,4,3,2,1,0:T(8,128)(2,1)S(1)} collective-permute-done((bf16[2,1,2,2,64,640]{5,4,3,2,1,0:T(8,128)(2,1)S(1)}, bf16[2,1,2,2,64,640]{5,4,3,2,1,0:T(8,128)(2,1)S(1)}, u32[]{:S(2)}, u32[]{:S(2)}) %collective-permute-start.9) | collective-permute-done | bytes 655392 | tf_op jit(solution)/shard_map/ppermute | solution.py:960
  74.4 10.6 %project.1 = (bf16[1024,1024]{1,0:T(8,128)(2,1)}, bf16[16,1024]{1,0:T(8,128)(2,1)}, bf16[1024,2048]{1,0:T(8,128)(2,1)}, bf16[16,2048]{1,0:T(8,128)(2,1)}, f32[1024,128]{1,0:T(8,128)}) custom-call(bf16[1024,1024]{1,0:T(8,128)(2,1)} %inputs.5, bf16[16,1024]{1,0:T(8,128)(2,1)} %copy-done.60, f32[1,1024]{1,0:T(1,128)} %copy.174.gain, ...), custom_call_target="tpu_custom_call" | custom-call | tf_op jit(solution)/shard_map/project/pallas_call | solution.py:646
  89.5 9.7 %mixer_forward.3 = (bf16[16,4,128,128]{3,2,1,0:T(8,128)(2,1)}, bf16[16,4,128,128]{3,2,1,0:T(8,128)(2,1)}, bf16[16,4,128,128]{3,2,1,0:T(8,128)(2,1)}, bf16[16,4,1...) custom-call(bf16[1024,2048]{1,0:T(8,128)(2,1)} %get-tuple-element.279.raw.before, ...), custom_call_target="tpu_custom_call" | custom-call | tf_op jit(solution)/shard_map/mixer_forward/pallas_call | solution.py:237
  111.1 6.2 %collective-permute-done.22 = bf16[2,1,1,1,64,1408]{5,4,0,3,2,1:T(8,128)(2,1)S(1)} collective-permute-done((bf16[2,1,1,1,64,1408]{5,4,0,3,2,1:T(8,128)(2,1)S(1)}, bf16[2,1,1,1,64,1408]{5,4,0,3,2,1:T(8,128)(2,1)S(1)}, u32[]{:S(2)}, u32[]{:S(2)}) %collective-permute-start.22) | collective-permute-done | bytes 360480 | tf_op jit(solution)/shard_map/ppermute | solution.py:960
  118.4 13.6 %mixer_forward.4 = (bf16[16,4,128,128]{3,2,1,0:T(8,128)(2,1)}, bf16[16,4,128,128]{3,2,1,0:T(8,128)(2,1)}, bf16[16,4,128,128]{3,2,1,0:T(8,128)(2,1)}, bf16[16,4,1...) custom-call(bf16[1024,2048]{1,0:T(8,128)(2,1)} %get-tuple-element.27, ...), custom_call_target="tpu_custom_call", output_to_operand_aliasing={{0}: (9, {}), {1}: (10, {}), {2}: (11, {}), {3}: (12, {}), ... | custom-call | tf_op jit(solution)/shard_map/mixer_forward/pallas_call | solution.py:237
  136.8 13.4 %mixer_forward.5 = (bf16[16,4,128,128]{3,2,1,0:T(8,128)(2,1)}, bf16[16,4,128,128]{3,2,1,0:T(8,128)(2,1)}, bf16[16,4,128,128]{3,2,1,0:T(8,128)(2,1)}, bf16[16,4,1...) custom-call(bf16[1024,2048]{1,0:T(8,128)(2,1)} %get-tuple-element.27, ...), custom_call_target="tpu_custom_call", output_to_operand_aliasing={{0}: (9, {}), {1}: (10, {}), {2}: (11, {}), {3}: (12, {}), ... | custom-call | tf_op jit(solution)/shard_map/mixer_forward/pallas_call | solution.py:237
  166.9 6.3 %project_side.1 = (bf16[1024,512]{1,0:T(8,128)(2,1)}, bf16[16,512]{1,0:T(8,128)(2,1)}, f32[1024,512]{1,0:T(8,128)}) custom-call(bf16[1024,1024]{1,0:T(8,128)(2,1)} %get-tuple-element.277.normed, bf16[16,1024]{1,0:T(8,128)(2,1)} %get-tuple-element.278.edge, bf16[1024,512]{1,0:T(8,128)(2,1)} %bitcast.223, bf16[1024,512]{1,0:T(8,128)(2,1)} %bitcast.221), custom_call_target="tpu_custom_call" | custom-call | tf_op jit(solution)/shard_map/project_side/pallas_call | solution.py:683
  178.3 7.4 %collective-permute-done.30.other.other_map = bf16[4,128,256]{2,1,0:T(8,128)(2,1)S(1)} collective-permute-done((bf16[4,128,256]{2,1,0:T(8,128)(2,1)}, bf16[4,128,256]{2,1,0:T(8,128)(2,1)S(1)}, u32[]{:S(2)}, u32[]{:S(2)}) %collective-permute-start.30) | collective-permute-done | bytes 262176 | tf_op jit(solution)/shard_map/ppermute | solution.py:960
  189.2 4.9 lay.3
  194.1 4.6 collective-permute-done.31.other.other_map
  207.0 11.2 %mixer_query.1 = (bf16[1024,512]{1,0:T(8,128)(2,1)}, f32[1024,512]{1,0:T(8,128)}) custom-call(bf16[1024,512]{1,0:T(8,128)(2,1)} %get-tuple-element.311.raw.before.raw_q.before_q, bf16[1024,512]{1,0:T(8,128)(2,1)} %get-tuple-element.311.raw.before.raw_q.before_q, bf16[16,512]{1,0:T(8,128)(2,1)} %get-tuple-element.312.edge.edge_q, f32[4,512]{1,0:T(4,128)} %slice.209.taps, ...), custom_call_target="tpu_custom_call" | custom-call | tf_op jit(solution)/shard_map/mixer_query/pallas_call | solution.py:321
  220.4 7.5 %heads.1 = (f32[1024,512]{1,0:T(8,128)}, bf16[1024,512]{1,0:T(8,128)(2,1)}, f32[1024,1024]{1,0:T(8,128)}, bf16[1024,1024]{1,0:T(8,128)(2,1)}) custom-call(f32[1024,512]{1,0:T(8,128)} %get-tuple-element.330.local, bf16[1024,512]{1,0:T(8,128)(2,1)} %get-tuple-element.331.reach, bf16[4,128,128]{2,1,0:T(8,128)(2,1)} %slice.168.state.state_in, ...), custom_call_target="tpu_custom_call" | custom-call | tf_op jit(solution)/shard_map/heads/pallas_call | solution.py:726
  228.8 3.7 collective-permute-done.35.other
  232.5 29.1 %feed.1 = (f32[1024,1024]{1,0:T(8,128)}, bf16[1024,1024]{1,0:T(8,128)(2,1)}, bf16[1024,1408]{1,0:T(8,128)(2,1)}, bf16[1024,1408]{1,0:T(8,128)(2,1)}, bf16[1024,1...) custom-call(s32[1]{0:T(128)} %bitcast.me, ...), custom_call_target="tpu_custom_call" | custom-call | tf_op jit(solution)/shard_map/feed/pallas_call | solution.py:818
  261.8 6.1 %convolution_convert_fusion.2 = bf16[1408,1024]{0,1:T(8,128)(2,1)S(1)} fusion(bf16[1024,1408]{1,0:T(8,128)(2,1)} %get-tuple-element.370, bf16[1024,1024]{1,0:T(8,128)(2,1)} %cotangent.3), kind=kOutput, calls=%fused_computation.7 | convolution fusion | flops 2954231808 | bytes 7864320 | tf_op jit(solution)/shard_map/dot_general | solution.py:29
  271.3 3.7 convolution_convert_fusion
  275.0 5.2 convolution_convert_fusion.1
  283.6 11.9 %turn.1 = (f32[1024,1024]{1,0:T(8,128)}, bf16[1024,1024]{1,0:T(8,128)(2,1)}, bf16[1024,512]{1,0:T(8,128)(2,1)}, bf16[1024,512]{1,0:T(8,128)(2,1)}, f32[4,128,128...) custom-call(f32[1024,1024]{1,0:T(8,128)} %get-tuple-element.366.hidden, f32[1024,1024]{1,0:T(8,128)} %get-tuple-element.368.own, ...), custom_call_target="tpu_custom_call" | custom-call | tf_op jit(solution)/shard_map/turn/pallas_call | solution.py:885
  306.6 4.1 convolution_convert_fusion.4
  315.0 4.2 convolution_convert_fusion.5
  339.7 30.1 %mixer_backward.3 = (bf16[1024,2560]{1,0:T(8,128)(2,1)}, f32[1024,8]{1,0:T(8,128)}, f32[8,2560]{1,0:T(8,128)}, f32[4,128,128]{2,1,0:T(8,128)}, f32[8,2560]{1,0:T(8,128)}, /*index=5*/f32[4,2560]{1,0:T(4,128)}) custom-call(bf16[1024,512]{1,0:T(8,128)(2,1)} %get-tuple-element.311.raw.before.raw_q.before_q, ...), custom_call_target="tpu_custom_call" | custom-call | tf_op jit(solution)/shard_map/mixer_backward/pallas_call | solution.py:551
  370.6 7.0 %halve.2 = (bf16[256,1408]{1,0:T(8,128)(2,1)}, bf16[256,1408]{1,0:T(8,128)(2,1)}, bf16[256,1408]{1,0:T(8,128)(2,1)}, bf16[256,1408]{1,0:T(8,128)(2,1)}, bf16[256...) custom-call(s32[1]{0:T(128)} %bitcast.me, ...), custom_call_target="tpu_custom_call" | custom-call | tf_op jit(solution)/shard_map/halve/pallas_call | solution.py:1171
  384.9 13.7 %mixer_backward.4 = (bf16[1024,2560]{1,0:T(8,128)(2,1)}, f32[1024,8]{1,0:T(8,128)}, f32[8,2560]{1,0:T(8,128)}, f32[4,128,128]{2,1,0:T(8,128)}, f32[8,2560]{1,0:T(8,128)}, /*index=5*/f32[4,2560]{1,0:T(4,128)}) custom-call(bf16[1024,512]{1,0:T(8,128)(2,1)} %get-tuple-element.311.raw.before.raw_q.before_q, ...), custom_call_target="tpu_custom_call", output_to_operand_aliasing={{0}: (20, {}), {1}: (21, {})} | custom-call | tf_op jit(solution)/shard_map/mixer_backward/pallas_call | solution.py:551
  401.0 4.4 halve.3
  412.6 7.8 %mixer_backward.5 = (bf16[1024,2560]{1,0:T(8,128)(2,1)}, f32[1024,8]{1,0:T(8,128)}, f32[8,2560]{1,0:T(8,128)}, f32[4,128,128]{2,1,0:T(8,128)}, f32[8,2560]{1,0:T(8,128)}, /*index=5*/f32[4,2560]{1,0:T(4,128)}) custom-call(bf16[1024,512]{1,0:T(8,128)(2,1)} %get-tuple-element.311.raw.before.raw_q.before_q, ...), custom_call_target="tpu_custom_call", output_to_operand_aliasing={{0}: (20, {}), {1}: (21, {})} | custom-call | tf_op jit(solution)/shard_map/mixer_backward/pallas_call | solution.py:551
  451.4 14.2 %back_project.1 = (bf16[1024,1024]{1,0:T(8,128)(2,1)}, f32[1,1024]{1,0:T(1,128)}) custom-call(bf16[1024,1024]{1,0:T(8,128)(2,1)} %inputs.5, bf16[1024,2560]{1,0:T(8,128)(2,1)} %fusion.21.d_raw, bf16[1024,128]{1,0:T(8,128)(2,1)} %pad.24.d_extra, bf16[1024,512]{1,0:T(8,128)(2,1)} %get-tuple-element.397.d_gate, bf16[1024,512]{1,0:T(8,128)(2,1)} %bitcast.224, ...), custom_call_target="tpu_custom_call" | custom-call | tf_op jit(solution)/shard_map/back_project/pallas_call | solution.py:935
  469.3 6.2 %collective-permute-done.61 = bf16[1,1,1,1,64,5248]{5,4,3,2,1,0:T(8,128)(2,1)} collective-permute-done((bf16[1,1,1,1,64,5248]{5,4,3,2,1,0:T(8,128)(2,1)}, bf16[1,1,1,1,64,5248]{5,4,3,2,1,0:T(8,128)(2,1)}, u32[]{:S(2)}, u32[]{:S(2)}) %collective-permute-start.61) | collective-permute-done | bytes 671776 | tf_op jit(solution)/shard_map/ppermute | solution.py:960
  493.4 5.4 %collective-permute-done.65 = bf16[2,2,1,1,64,1024]{5,4,3,2,1,0:T(8,128)(2,1)S(1)} collective-permute-done((bf16[2,2,1,1,64,1024]{5,4,3,2,1,0:T(8,128)(2,1)S(1)}, bf16[2,2,1,1,64,1024]{5,4,3,2,1,0:T(8,128)(2,1)S(1)}, u32[]{:S(2)}, u32[]{:S(2)}) %collective-permute-start.65) | collective-permute-done | bytes 524320 | tf_op jit(solution)/shard_map/ppermute | solution.py:960
  518.1 7.8 %collective-permute-done.74 = f32[168,128]{1,0:T(8,128)S(1)} collective-permute-done((f32[168,128]{1,0:T(8,128)S(1)}, f32[168,128]{1,0:T(8,128)S(1)}, u32[]{:S(2)}, u32[]{:S(2)}) %collective-permute-start.74) | collective-permute-done | bytes 86048 | tf_op jit(solution)/shard_map/ppermute | solution.py:960
  (472 shorter events, 243.8 us)
Async XLA Ops:
  4.2 23.1 %collective-permute-start = (bf16[1,1,1,1,64,2176]{5,4,3,2,1,0:T(8,128)(2,1)S(1)}, bf16[1,1,1,1,64,2176]{5,4,3,2,1,0:T(8,128)(2,1)S(1)}, u32[]{:S(2)}, u32[]{:S(2)}) collective-permute-start(bf16[1,1,1,1,64,2176]{5,4,3,2,1,0:T(8,128)(2,1)S(1)} %bitcast.239), channel_id=1, source_target_pairs={{0,16},{2,18},{4,20},{6,22},{8,24},{10,26},{12,28},{14,30},{16,0},... | collective-permute-start | bytes 835592 | tf_op jit(solution)/shard_map/ppermute | solution.py:960
  9.0 59.3 %collective-permute-start.11 = (bf16[16,1024]{1,0:T(8,128)(2,1)S(1)}, bf16[16,1024]{1,0:T(8,128)(2,1)S(1)}, u32[]{:S(2)}, u32[]{:S(2)}) collective-permute-start(bf16[16,1024]{1,0:T(8,128)(2,1)S(1)} %slice.160), channel_id=1, source_target_pairs={{0,2},{2,4},{4,6},{6,8},{8,10},{10,12},{12,14},{14,16},{16,18},{18... | collective-permute-start | bytes 98312 | tf_op jit(solution)/shard_map/ppermute | solution.py:954
  43.4 18.4 %collective-permute-start.9 = (bf16[2,1,2,2,64,640]{5,4,3,2,1,0:T(8,128)(2,1)S(1)}, bf16[2,1,2,2,64,640]{5,4,3,2,1,0:T(8,128)(2,1)S(1)}, u32[]{:S(2)}, u32[]{:S(2)}) collective-permute-start(bf16[2,1,2,2,64,640]{5,4,3,2,1,0:T(8,128)(2,1)S(1)} %pad_maximum_fusion.9), channel_id=1, source_target_pairs={{0,8},{2,10},{4,12},{6,14},{8,0},{10,2},{12,4},{14,6},{16,24},{18,... | collective-permute-start | bytes 1966088 | tf_op jit(solution)/shard_map/ppermute | solution.py:960
  68.4 30.9 %collective-permute-start.18 = (bf16[1,1,1,1,64,4224]{5,4,0,3,2,1:T(8,128)(2,1)}, bf16[1,1,1,1,64,4224]{5,4,0,3,2,1:T(8,128)(2,1)}, u32[]{:S(2)}, u32[]{:S(2)}) collective-permute-start(bf16[1,1,1,1,64,4224]{5,4,0,3,2,1:T(8,128)(2,1)} %bitcast.13), channel_id=1, source_target_pairs={{0,16},{2,18},{4,20},{6,22},{8,24},{10,26},{12,28},{14,30},{16,0},... | collective-permute-start | bytes 1622024 | tf_op jit(solution)/shard_map/ppermute | solution.py:960
  106.6 25.4 %collective-permute-start.19 = (bf16[2,2,2,1,64,512]{5,4,3,2,1,0:T(8,128)(2,1)}, bf16[2,2,2,1,64,512]{5,4,3,2,1,0:T(8,128)(2,1)}, u32[]{:S(2)}, u32[]{:S(2)}) collective-permute-start(bf16[2,2,2,1,64,512]{5,4,3,2,1,0:T(8,128)(2,1)} %pad_maximum_fusion.12), channel_id=1, source_target_pairs={{0,2},{2,0},{4,6},{6,4},{8,10},{10,8},{12,14},{14,12},{16,18},{18,... | collective-permute-start | bytes 1572872 | tf_op jit(solution)/shard_map/ppermute | solution.py:960
  106.8 25.2 %collective-permute-start.20 = (bf16[2,2,1,2,64,512]{5,4,3,2,1,0:T(8,128)(2,1)}, bf16[2,2,1,2,64,512]{5,4,3,2,1,0:T(8,128)(2,1)}, u32[]{:S(2)}, u32[]{:S(2)}) collective-permute-start(bf16[2,2,1,2,64,512]{5,4,3,2,1,0:T(8,128)(2,1)} %pad_maximum_fusion.13), channel_id=1, source_target_pairs={{0,4},{2,6},{4,0},{6,2},{8,12},{10,14},{12,8},{14,10},{16,20},{18,... | collective-permute-start | bytes 1572872 | tf_op jit(solution)/shard_map/ppermute | solution.py:960
  108.4 23.7 %collective-permute-start.21 = (bf16[2,1,2,2,64,512]{5,4,3,2,1,0:T(8,128)(2,1)S(1)}, bf16[2,1,2,2,64,512]{5,4,3,2,1,0:T(8,128)(2,1)}, u32[]{:S(2)}, u32[]{:S(2)}) collective-permute-start(bf16[2,1,2,2,64,512]{5,4,3,2,1,0:T(8,128)(2,1)S(1)} %pad_maximum_fusion.14), channel_id=1, source_target_pairs={{0,8},{2,10},{4,12},{6,14},{8,0},{10,2},{12,4},{14,6},{16,24},{18,... | collective-permute-start | bytes 1572872 | tf_op jit(solution)/shard_map/ppermute | solution.py:960
  110.1 21.9 %collective-permute-start.23 = (bf16[2,1,1,1,64,1408]{5,4,0,3,2,1:T(8,128)(2,1)}, bf16[2,1,1,1,64,1408]{5,4,0,3,2,1:T(8,128)(2,1)}, u32[]{:S(2)}, u32[]{:S(2)}) collective-permute-start(bf16[2,1,1,1,64,1408]{5,4,0,3,2,1:T(8,128)(2,1)} %get-tuple-element.307), channel_id=1, source_target_pairs={{0,2},{2,0},{4,6},{6,4},{8,10},{10,8},{12,14},{14,12},{16,18},{18,... | collective-permute-start | bytes 1081352 | tf_op jit(solution)/shard_map/ppermute | solution.py:960
  134.9 17.7 %collective-permute-start.25 = (bf16[2,2,1,1,64,1408]{5,4,1,0,3,2:T(8,128)(2,1)}, bf16[2,2,1,1,64,1408]{5,4,1,0,3,2:T(8,128)(2,1)}, u32[]{:S(2)}, u32[]{:S(2)}) collective-permute-start(bf16[2,2,1,1,64,1408]{5,4,1,0,3,2:T(8,128)(2,1)} %bitcast.242), channel_id=1, source_target_pairs={{0,4},{2,6},{4,0},{6,2},{8,12},{10,14},{12,8},{14,10},{16,20},{18,... | collective-permute-start | bytes 2162696 | tf_op jit(solution)/shard_map/ppermute | solution.py:960
  135.8 16.7 %collective-permute-start.26 = (bf16[2,1,1,2,64,1408]{5,4,3,0,2,1:T(8,128)(2,1)}, bf16[2,1,1,2,64,1408]{5,4,3,0,2,1:T(8,128)(2,1)}, u32[]{:S(2)}, u32[]{:S(2)}) collective-permute-start(bf16[2,1,1,2,64,1408]{5,4,3,0,2,1:T(8,128)(2,1)} %bitcast.244), channel_id=1, source_target_pairs={{0,8},{2,10},{4,12},{6,14},{8,0},{10,2},{12,4},{14,6},{16,24},{18,... | collective-permute-start | bytes 2162696 | tf_op jit(solution)/shard_map/ppermute | solution.py:960
  136.1 16.4 %collective-permute-start.27 = (bf16[2,1,2,1,64,1408]{5,4,2,0,3,1:T(8,128)(2,1)}, bf16[2,1,2,1,64,1408]{5,4,2,0,3,1:T(8,128)(2,1)}, u32[]{:S(2)}, u32[]{:S(2)}) collective-permute-start(bf16[2,1,2,1,64,1408]{5,4,2,0,3,1:T(8,128)(2,1)} %bitcast.246), channel_id=1, source_target_pairs={{0,2},{2,0},{4,6},{6,4},{8,10},{10,8},{12,14},{14,12},{16,18},{18,... | collective-permute-start | bytes 2162696 | tf_op jit(solution)/shard_map/ppermute | solution.py:960
  203.4 24.5 %collective-permute-start.32 = (bf16[2,2,2,1,64,1408]{5,4,2,1,0,3:T(8,128)(2,1)}, bf16[2,2,2,1,64,1408]{5,4,2,1,0,3:T(8,128)(2,1)}, u32[]{:S(2)}, u32[]{:S(2)}) collective-permute-start(bf16[2,2,2,1,64,1408]{5,4,2,1,0,3:T(8,128)(2,1)} %bitcast.233), channel_id=1, source_target_pairs={{0,2},{2,0},{4,6},{6,4},{8,10},{10,8},{12,14},{14,12},{16,18},{18,... | collective-permute-start | bytes 4325384 | tf_op jit(solution)/shard_map/ppermute | solution.py:960
  204.3 23.6 %collective-permute-start.33 = (bf16[2,2,1,2,64,1408]{5,4,3,1,0,2:T(8,128)(2,1)}, bf16[2,2,1,2,64,1408]{5,4,3,1,0,2:T(8,128)(2,1)}, u32[]{:S(2)}, u32[]{:S(2)}) collective-permute-start(bf16[2,2,1,2,64,1408]{5,4,3,1,0,2:T(8,128)(2,1)} %bitcast.235), channel_id=1, source_target_pairs={{0,4},{2,6},{4,0},{6,2},{8,12},{10,14},{12,8},{14,10},{16,20},{18,... | collective-permute-start | bytes 4325384 | tf_op jit(solution)/shard_map/ppermute | solution.py:960
  205.2 22.8 %collective-permute-start.34 = (bf16[2,1,2,2,64,1408]{5,4,3,2,0,1:T(8,128)(2,1)}, bf16[2,1,2,2,64,1408]{5,4,3,2,0,1:T(8,128)(2,1)}, u32[]{:S(2)}, u32[]{:S(2)}) collective-permute-start(bf16[2,1,2,2,64,1408]{5,4,3,2,0,1:T(8,128)(2,1)} %bitcast.237), channel_id=1, source_target_pairs={{0,8},{2,10},{4,12},{6,14},{8,0},{10,2},{12,4},{14,6},{16,24},{18,... | collective-permute-start | bytes 4325384 | tf_op jit(solution)/shard_map/ppermute | solution.py:960
  261.6 18.7 %collective-permute-start.37 = (bf16[1024,1024]{1,0:T(8,128)(2,1)}, bf16[1024,1024]{1,0:T(8,128)(2,1)S(1)}, u32[]{:S(2)}, u32[]{:S(2)}) collective-permute-start(bf16[1024,1024]{1,0:T(8,128)(2,1)} %get-tuple-element.369), channel_id=1, source_target_pairs={{0,1},{1,0},{2,3},{3,2},{4,5},{5,4},{6,7},{7,6},{8,9},{9,8},{10,11... | collective-permute-start | bytes 6291464 | tf_op jit(solution)/shard_map/ppermute | solution.py:964
  280.3 54.0 %collective-permute-start.38 = (bf16[2,1,2,2,64,1408]{5,4,3,2,0,1:T(8,128)(2,1)}, bf16[2,1,2,2,64,1408]{5,4,3,2,0,1:T(8,128)(2,1)}, u32[]{:S(2)}, u32[]{:S(2)}) collective-permute-start(bf16[2,1,2,2,64,1408]{5,4,3,2,0,1:T(8,128)(2,1)} %dynamic-slice_bitcast_fusion.2), channel_id=1, source_target_pairs={{0,8},{2,10},{4,12},{6,14},{8,0},{10,2},{12,4},{14,6},{16,24},{18,... | collective-permute-start | bytes 4325384 | tf_op jit(solution)/shard_map/ppermute | solution.py:960
  334.3 35.5 %collective-permute-start.43 = (bf16[2,2,1,2,64,1408]{5,4,3,1,0,2:T(8,128)(2,1)}, bf16[2,2,1,2,64,1408]{5,4,3,1,0,2:T(8,128)(2,1)}, u32[]{:S(2)}, u32[]{:S(2)}) collective-permute-start(bf16[2,2,1,2,64,1408]{5,4,3,1,0,2:T(8,128)(2,1)} %dynamic-slice_bitcast_fusion.1), channel_id=1, source_target_pairs={{0,4},{2,6},{4,0},{6,2},{8,12},{10,14},{12,8},{14,10},{16,20},{18,... | collective-permute-start | bytes 4325384 | tf_op jit(solution)/shard_map/ppermute | solution.py:960
  335.0 34.8 %collective-permute-start.44 = (bf16[2,2,2,1,64,1408]{5,4,2,1,0,3:T(8,128)(2,1)}, bf16[2,2,2,1,64,1408]{5,4,2,1,0,3:T(8,128)(2,1)}, u32[]{:S(2)}, u32[]{:S(2)}) collective-permute-start(bf16[2,2,2,1,64,1408]{5,4,2,1,0,3:T(8,128)(2,1)} %dynamic-slice_bitcast_fusion), channel_id=1, source_target_pairs={{0,2},{2,0},{4,6},{6,4},{8,10},{10,8},{12,14},{14,12},{16,18},{18,... | collective-permute-start | bytes 4325384 | tf_op jit(solution)/shard_map/ppermute | solution.py:960
  336.4 33.4 %collective-permute-start.45 = (bf16[2,1,2,2,64,512]{5,4,3,2,0,1:T(8,128)(2,1)}, bf16[2,1,2,2,64,512]{5,4,3,2,0,1:T(8,128)(2,1)S(1)}, u32[]{:S(2)}, u32[]{:S(2)}) collective-permute-start(bf16[2,1,2,2,64,512]{5,4,3,2,0,1:T(8,128)(2,1)} %dynamic-slice_bitcast_fusion.4), channel_id=1, source_target_pairs={{0,8},{2,10},{4,12},{6,14},{8,0},{10,2},{12,4},{14,6},{16,24},{18,... | collective-permute-start | bytes 1572872 | tf_op jit(solution)/shard_map/ppermute | solution.py:960
  336.4 33.4 %collective-permute-start.46 = (bf16[2,1,2,2,64,512]{5,4,3,2,0,1:T(8,128)(2,1)}, bf16[2,1,2,2,64,512]{5,4,3,2,0,1:T(8,128)(2,1)}, u32[]{:S(2)}, u32[]{:S(2)}) collective-permute-start(bf16[2,1,2,2,64,512]{5,4,3,2,0,1:T(8,128)(2,1)} %dynamic-slice_bitcast_fusion.3), channel_id=1, source_target_pairs={{0,8},{2,10},{4,12},{6,14},{8,0},{10,2},{12,4},{14,6},{16,24},{18,... | collective-permute-start | bytes 1572872 | tf_op jit(solution)/shard_map/ppermute | solution.py:960
  377.6 22.5 %collective-permute-start.47 = (bf16[256,1408]{1,0:T(8,128)(2,1)}, bf16[256,1408]{1,0:T(8,128)(2,1)S(1)}, u32[]{:S(2)}, u32[]{:S(2)}) collective-permute-start(bf16[256,1408]{1,0:T(8,128)(2,1)} %get-tuple-element.432), channel_id=1, source_target_pairs={{0,8},{2,10},{4,12},{6,14},{8,0},{10,2},{12,4},{14,6},{16,24},{18,... | collective-permute-start | bytes 2162696 | tf_op jit(solution)/shard_map/ppermute | solution.py:960
  377.7 22.4 %collective-permute-start.48 = (bf16[256,1408]{1,0:T(8,128)(2,1)}, bf16[256,1408]{1,0:T(8,128)(2,1)}, u32[]{:S(2)}, u32[]{:S(2)}) collective-permute-start(bf16[256,1408]{1,0:T(8,128)(2,1)} %get-tuple-element.433), channel_id=1, source_target_pairs={{0,4},{2,6},{4,0},{6,2},{8,12},{10,14},{12,8},{14,10},{16,20},{18,... | collective-permute-start | bytes 2162696 | tf_op jit(solution)/shard_map/ppermute | solution.py:960
  378.6 21.5 %collective-permute-start.49 = (bf16[256,1408]{1,0:T(8,128)(2,1)}, bf16[256,1408]{1,0:T(8,128)(2,1)}, u32[]{:S(2)}, u32[]{:S(2)}) collective-permute-start(bf16[256,1408]{1,0:T(8,128)(2,1)} %get-tuple-element.434), channel_id=1, source_target_pairs={{0,2},{2,0},{4,6},{6,4},{8,10},{10,8},{12,14},{14,12},{16,18},{18,... | collective-permute-start | bytes 2162696 | tf_op jit(solution)/shard_map/ppermute | solution.py:960
  379.7 20.4 %collective-permute-start.50 = (bf16[256,512]{1,0:T(8,128)(2,1)}, bf16[256,512]{1,0:T(8,128)(2,1)S(1)}, u32[]{:S(2)}, u32[]{:S(2)}) collective-permute-start(bf16[256,512]{1,0:T(8,128)(2,1)} %get-tuple-element.435), channel_id=1, source_target_pairs={{0,2},{2,0},{4,6},{6,4},{8,10},{10,8},{12,14},{14,12},{16,18},{18,... | collective-permute-start | bytes 786440 | tf_op jit(solution)/shard_map/ppermute | solution.py:960
  380.6 19.4 %collective-permute-start.51 = (bf16[256,512]{1,0:T(8,128)(2,1)}, bf16[256,512]{1,0:T(8,128)(2,1)}, u32[]{:S(2)}, u32[]{:S(2)}) collective-permute-start(bf16[256,512]{1,0:T(8,128)(2,1)} %get-tuple-element.436), channel_id=1, source_target_pairs={{0,4},{2,6},{4,0},{6,2},{8,12},{10,14},{12,8},{14,10},{16,20},{18,... | collective-permute-start | bytes 786440 | tf_op jit(solution)/shard_map/ppermute | solution.py:960
  405.4 16.4 %collective-permute-start.52 = (bf16[128,1408]{1,0:T(8,128)(2,1)}, bf16[128,1408]{1,0:T(8,128)(2,1)}, u32[]{:S(2)}, u32[]{:S(2)}) collective-permute-start(bf16[128,1408]{1,0:T(8,128)(2,1)} %get-tuple-element.466), channel_id=1, source_target_pairs={{0,2},{2,0},{4,6},{6,4},{8,10},{10,8},{12,14},{14,12},{16,18},{18,... | collective-permute-start | bytes 1081352 | tf_op jit(solution)/shard_map/ppermute | solution.py:960
  441.1 34.3 %collective-permute-start.58 = (bf16[2,2,2,1,64,1024]{5,4,3,2,1,0:T(8,128)(2,1)}, bf16[2,2,2,1,64,1024]{5,4,3,2,1,0:T(8,128)(2,1)}, u32[]{:S(2)}, u32[]{:S(2)}) collective-permute-start(bf16[2,2,2,1,64,1024]{5,4,3,2,1,0:T(8,128)(2,1)} %get-tuple-element.477), channel_id=1, source_target_pairs={{0,2},{2,0},{4,6},{6,4},{8,10},{10,8},{12,14},{14,12},{16,18},{18,... | collective-permute-start | bytes 3145736 | tf_op jit(solution)/shard_map/ppermute | solution.py:960
  443.8 31.7 %collective-permute-start.59 = (bf16[2,2,1,2,64,1024]{5,4,3,2,1,0:T(8,128)(2,1)}, bf16[2,2,1,2,64,1024]{5,4,3,2,1,0:T(8,128)(2,1)}, u32[]{:S(2)}, u32[]{:S(2)}) collective-permute-start(bf16[2,2,1,2,64,1024]{5,4,3,2,1,0:T(8,128)(2,1)} %get-tuple-element.478), channel_id=1, source_target_pairs={{0,4},{2,6},{4,0},{6,2},{8,12},{10,14},{12,8},{14,10},{16,20},{18,... | collective-permute-start | bytes 3145736 | tf_op jit(solution)/shard_map/ppermute | solution.py:960
  448.3 27.2 %collective-permute-start.61 = (bf16[1,1,1,1,64,5248]{5,4,3,2,1,0:T(8,128)(2,1)}, bf16[1,1,1,1,64,5248]{5,4,3,2,1,0:T(8,128)(2,1)}, u32[]{:S(2)}, u32[]{:S(2)}) collective-permute-start(bf16[1,1,1,1,64,5248]{5,4,3,2,1,0:T(8,128)(2,1)} %fusion.19), channel_id=1, source_target_pairs={{0,16},{2,18},{4,20},{6,22},{8,24},{10,26},{12,28},{14,30},{16,0},... | collective-permute-start | bytes 2015240 | tf_op jit(solution)/shard_map/ppermute | solution.py:960
  448.8 20.5 %collective-permute-start.60 = (bf16[2,1,2,2,64,512]{5,4,3,2,1,0:T(8,128)(2,1)}, bf16[2,1,2,2,64,512]{5,4,3,2,1,0:T(8,128)(2,1)}, u32[]{:S(2)}, u32[]{:S(2)}) collective-permute-start(bf16[2,1,2,2,64,512]{5,4,3,2,1,0:T(8,128)(2,1)} %get-tuple-element.479), channel_id=1, source_target_pairs={{0,8},{2,10},{4,12},{6,14},{8,0},{10,2},{12,4},{14,6},{16,24},{18,... | collective-permute-start | bytes 1572872 | tf_op jit(solution)/shard_map/ppermute | solution.py:960
  450.6 31.8 %collective-permute-start.36 = (bf16[1024,512]{1,0:T(8,128)(2,1)}, bf16[1024,512]{1,0:T(8,128)(2,1)}, u32[]{:S(2)}, u32[]{:S(2)}) collective-permute-start(bf16[1024,512]{1,0:T(8,128)(2,1)} %constant_dynamic-slice_fusion.7), channel_id=1, source_target_pairs={{0,1},{1,0},{2,3},{3,2},{4,5},{5,4},{6,7},{7,6},{8,9},{9,8},{10,11... | collective-permute-start | bytes 3145736 | tf_op jit(solution)/shard_map/ppermute | solution.py:964
  515.1 16.2 %collective-permute-start.72 = (bf16[1,1,1,1,64,2560]{5,4,3,2,1,0:T(8,128)(2,1)S(1)}, bf16[1,1,1,1,64,2560]{5,4,3,2,1,0:T(8,128)(2,1)S(1)}, u32[]{:S(2)}, u32[]{:S(2)}) collective-permute-start(bf16[1,1,1,1,64,2560]{5,4,3,2,1,0:T(8,128)(2,1)S(1)} %pad_maximum_fusion.18), channel_id=1, source_target_pairs={{0,16},{2,18},{4,20},{6,22},{8,24},{10,26},{12,28},{14,30},{16,0},... | collective-permute-start | bytes 983048 | tf_op jit(solution)/shard_map/ppermute | solution.py:960
  (123 other events, 1040.0 us)

commit v5 on v4

--- a/solution.py
+++ b/solution.py
@@ -949,6 +949,33 @@
     )(inputs, d_raw, d_extra, d_gate, *weights)
 
 
+def mend_kernel(d_raw_in, tail, returned, same_after, taps, d_raw):
+    row = lax.broadcasted_iota(jnp.int32, (8, 1), 0)
+    spread = tail[...]
+    for offset in range(1, taps.shape[0]):
+        masked = returned[...] * same_after[:, offset : offset + 1] * taps[offset : offset + 1]
+        moved = pltpu.roll(masked, 8 - offset, 0)
+        spread = spread + jnp.where(row >= 8 - offset, moved, 0.0)
+    d_raw[...] = low(jnp.concatenate([d_raw_in[...].astype(F32)[: HALO - 8], spread], 0))
+
+
+def mend(d_raw, tail, returned, same_after, taps):
+    count, columns = d_raw.shape
+    last = count // HALO - 1
+    rows = pl.BlockSpec((HALO, columns), lambda c: (last, 0))
+    return pl.pallas_call(
+        mend_kernel,
+        grid=(1,),
+        in_specs=[rows, whole_spec(8, columns), whole_spec(8, columns)]
+        + [whole_spec(*same_after.shape), whole_spec(*taps.shape)],
+        out_specs=rows,
+        out_shape=jax.ShapeDtypeStruct(d_raw.shape, BF16),
+        input_output_aliases={0: 0},
+        compiler_params=pltpu.CompilerParams(dimension_semantics=("arbitrary",)),
+        name="mend",
+    )(d_raw, tail, returned, same_after, taps)
+
+
 def shift_seq(array, by):
     count = lax.axis_size("seq")
     return lax.ppermute(
@@ -978,20 +1005,31 @@
     return form(former, high) + form(former, rest)
 
 
-def join_kernel(final, upper, group, other, before, group_out, low_out, before_out):
+def join_kernel(final, shift_next, upper, group, other, before, group_out, low_out, before_out):
     heads, width, _ = group.shape
 
     @pl.when(upper[0] == 1)
     def _():
+        lefts = [before] if final else [before, group]
+        stacked = []
         for head in range(heads):
-            theirs = other[head]
-            reach = fine_low(product, before[head, :, :width], theirs)
-            before_out[head, :, :width] = reach[:, :width]
-            before_out[head, :, width:] = reach[:, width:] + before[head, :, width:]
-            if not final:
-                mine = fine_low(product, group[head, :, :width], theirs)
-                group_out[head, :, :width] = mine[:, :width]
-                group_out[head, :, width:] = mine[:, width:] + group[head, :, width:]
+            pieces = []
+            for left in lefts:
+                pieces += list(split(left[head, :, :width]))
+            stacked.append(product(jnp.concatenate(pieces, 0), other[head]))
+        for head in range(heads):
+            if final:
+                before_out[head, :, :width] = before[head, :, :width]
+                before_out[head, :, width:] = before[head, :, width:] + (
+                    stacked[head][:width] + stacked[head][width:]
+                )
+                continue
+            for at, (left, out) in enumerate(zip(lefts, (before_out, group_out))):
+                start = 2 * at * width
+                both = stacked[head][start : start + width]
+                both = both + stacked[head][start + width : start + 2 * width]
+                out[head, :, :width] = both[:, :width]
+                out[head, :, width:] = both[:, width:] + left[head, :, width:]
 
     @pl.when(upper[0] == 0)
     def _():
@@ -1003,18 +1041,22 @@
                 group_out[head, :, :width] = mine[:, :width]
                 group_out[head, :, width:] = mine[:, width:] + theirs[:, width:].astype(F32)
 
-    low_out[...] = low(group_out[...]) if not final else low(before_out[...])
-
-
-def join_groups(final, upper, group, other, before):
+    if final:
+        low_out[...] = low(before_out[:, :, width:])
+    else:
+        low_out[...] = low(group_out[:, :, width:] if shift_next else group_out[...])
+
+
+def join_groups(final, shift_next, upper, group, other, before):
     whole = pl.BlockSpec(memory_space=pltpu.VMEM)
     full = jax.ShapeDtypeStruct(group.shape, F32)
+    sent = group.shape[1] if final or shift_next else group.shape[2]
     return pl.pallas_call(
-        functools.partial(join_kernel, final),
+        functools.partial(join_kernel, final, shift_next),
         in_specs=[pl.BlockSpec(memory_space=pltpu.SMEM), whole, whole, whole],
         out_specs=[whole, whole, whole],
-        out_shape=[full, jax.ShapeDtypeStruct(group.shape, BF16), full],
-        compiler_params=pltpu.CompilerParams(vmem_limit_bytes=VMEM_BYTES),
+        out_shape=[full, jax.ShapeDtypeStruct(group.shape[:2] + (sent,), BF16), full],
+        compiler_params=pltpu.CompilerParams(vmem_limit_bytes=8 * 1024 * 1024),
         name="join_groups",
     )(upper, group, other, before)
 
@@ -1038,13 +1080,17 @@
 
     @pl.when(upper[0] == 0)
     def _():
+        stacked = []
         for head in range(heads):
-            theirs = other[head]
-            after_out[head] += fine_low(inner_rows, after_map[head], theirs)
+            pieces = list(split(after_map[head]))
             if not final:
-                group_out[head] = group[head] + fine_low(
-                    inner_rows, group_map[head, :, :width], theirs
-                )
+                pieces += list(split(group_map[head, :, :width]))
+            stacked.append(inner_rows(jnp.concatenate(pieces, 1), other[head]))
+        for head in range(heads):
+            quarter = lambda k: stacked[head][k * width : (k + 1) * width]
+            after_out[head] += quarter(0) + quarter(1)
+            if not final:
+                group_out[head] = group[head] + (quarter(2) + quarter(3))
                 after_map_out[head] = fine_first(
                     product, other_map[head, :, :width], after_map[head]
                 )
@@ -1060,7 +1106,7 @@
         in_specs=[pl.BlockSpec(memory_space=pltpu.SMEM)] + [whole] * 6,
         out_specs=[whole] * 4,
         out_shape=[full, jax.ShapeDtypeStruct(group.shape, BF16), full, full],
-        compiler_params=pltpu.CompilerParams(vmem_limit_bytes=VMEM_BYTES),
+        compiler_params=pltpu.CompilerParams(vmem_limit_bytes=8 * 1024 * 1024),
         name="join_back",
     )(upper, group, other, after, group_map, other_map, after_map)
 
@@ -1078,9 +1124,11 @@
         upper = ((mine // distance) % 2).astype(jnp.int32).reshape(1)
         kept.append((group, other, upper))
         final = 2 * distance >= count
-        group, group_low, before = join_groups(final, upper, group, other, before)
+        group, group_low, before = join_groups(
+            final, 4 * distance >= count, upper, group, other, before
+        )
         distance *= 2
-    return group_low[:, :, group.shape[1] :], kept
+    return group_low, kept
 
 
 def adjoints_after(own, kept, eye):
@@ -1415,7 +1463,7 @@
     state_low, feed_parts = tied(state_low, feed_parts)
     others = swap_all(feed_parts, gather_at(2))
     q_reach, local_out = run_query(
-        raw_query, edge_query, taps_all[:, :query_cols], same, cum_col, cum_row, key_rows, solved,
+        raw_query, edge_query, taps_all, same, cum_col, cum_row, key_rows, solved,
         p_part, s_part, head_count, substeps, width,
     )
     head_gain_row = head_gain.astype(F32)[None]
@@ -1545,11 +1593,7 @@
     zh_other = swap_seq(jnp.concatenate(zh_sends, -1), far[0])
     returned = shift_seq(first_rows, -1)
     same_after = same_docs(token_position[-1] + 1 + jnp.arange(8, dtype=jnp.int32))
-    spread = jnp.zeros_like(tail)
-    for offset in range(1, tap_count):
-        masked = returned * same_after[:, offset : offset + 1] * taps_all[offset]
-        spread = spread + jnp.pad(masked[:offset], ((8 - offset, 0), (0, 0)))
-    d_raw = lax.dynamic_update_slice(d_raw, low(tail + spread), (count - 8, 0))
+    d_raw = mend(d_raw, tail, returned, same_after, taps_all)
     d_beta_low = low(d_beta_logit)
     fifth = -(-conv_cols // (5 * width)) * width
     conv_marks = [0, 2 * fifth, 4 * fifth, conv_cols]
@@ -1560,7 +1604,7 @@
         ],
         at_step(0),
     )
-    d_raw, d_beta_low, sends, keeps = tied(d_raw, d_beta_low, sends, keeps)
+    d_raw, d_beta_low, sends = tied(d_raw, d_beta_low, sends)
     others = swap_all(sends, at_step(0))
     d_extra = jnp.pad(d_beta_low, ((0, 0), (0, extra - beta_cols)))
     d_low, gain_part = run_back_project(

time: 544 us -> 538 us (0.989)
  Pallas kernels: 220 us -> 208 us
  matrix products: 32.9 us -> 27 us
  waiting for transfers between devices: 92.2 us -> 98 us
    pallas_call x4, Pallas kernels: 11 us -> 3.46 us  [join_back(): pl.pallas_call(functools.partial(back_kernel, final), in_specs=[pl.BlockS...]
    ppermute x68, waiting for transfers between devices: 88.5 us -> 95.4 us  [swap_seq(): lax.ppermute(array, 'seq', [(i, i ^ distance) for i in range(lax.axis_siz...]
    unnamed x165, local copies, waits for them, and re-layouts: 10.7 us -> 17.2 us
    dot_general x9, matrix products: 32.9 us -> 27 us  [inner_rows(): lax.dot_general(former, latter, (((0,), (0,)), ((), ())), preferred_eleme...]
  transfers between devices with their start and end apart: 75 -> 75, of which waited for: 28 -> 29; matrix products, arithmetic and copies ran while one was open for 20% -> 19% of each run, Pallas kernels for 31% -> 30%
where the time goes in v5:
time: 538 us; the launch traced here: 527 us
  Pallas kernels  208 us (39%)
  waiting for transfers between devices  98 us (18%)
  starting transfers between devices  77.9 us (14%)
  other arithmetic  64 us (12%)
  local copies, waits for them, and re-layouts  49.5 us (9%)
  matrix products  27 us (5%)
    ppermute x68, waiting for transfers between devices, swap_seq(): lax.ppermute(array, 'seq', [(i, i ^ distance) for i in range(lax.axis_siz...  95.4 us
    ppermute x68, starting transfers between devices, swap_seq(): lax.ppermute(array, 'seq', [(i, i ^ distance) for i in range(lax.axis_siz...  72 us
    pallas_call x3, Pallas kernels, run_backward(): pl.pallas_call(functools.partial(backward_kernel, head_count, substeps, w...  51.5 us
    pallas_call x3, Pallas kernels, run_forward(): pl.pallas_call(functools.partial(forward_kernel, head_count, substeps, wi...  36.8 us
    pallas_call x1, Pallas kernels, run_feed(): pl.pallas_call(functools.partial(feed_kernel, distances, rows), grid=(cou...  29.1 us
    dot_general x9, matrix products, inner_rows(): lax.dot_general(former, latter, (((0,), (0,)), ((), ())), preferred_eleme...  27 us
    unnamed x165, local copies, waits for them, and re-layouts  17.2 us
    pallas_call x1, Pallas kernels, run_back_project(): pl.pallas_call(functools.partial(back_project_kernel, d_extra.shape[1]),...  14 us
  transfers between devices with their start and end apart: 75, of which 29 were waited for; matrix products, arithmetic and copies ran while one was open for 19% of the time, Pallas kernels for 30%

profile of v5, /device:TPU:0, one launch (start us, length us, event | category | flops | bytes accessed | tf_op | source)
XLA Modules:
  0.0 527.4 jit_solution(15469195531790027042)
XLA Ops:
  4.2 4.1 collective-permute-start
  15.8 6.3 %fusion.38 = f32[16,64,4]{2,0,1:T(8,128)S(1)} fusion(f32[16,64,4]{2,0,1:T(8,128)S(1)} %copy.186), kind=kOutput, calls=%fused_computation.211 | output fusion | flops 258048 | bytes 32768 | tf_op jit(solution)/shard_map/jit(cumsum)/reduce_window_sum | solution.py:1408
  43.8 6.7 %collective-permute-done.5 = bf16[2,1,1,2,64,768]{5,4,3,2,1,0:T(8,128)(2,1)S(1)} collective-permute-done((bf16[2,1,1,2,64,768]{5,4,3,2,1,0:T(8,128)(2,1)S(1)}, bf16[2,1,1,2,64,768]{5,4,3,2,1,0:T(8,128)(2,1)S(1)}, u32[]{:S(2)}, u32[]{:S(2)}) %collective-permute-start.5) | collective-permute-done | bytes 393248 | tf_op jit(solution)/shard_map/ppermute | solution.py:987
  52.5 9.1 %collective-permute-done.9 = bf16[2,1,2,2,64,640]{5,4,3,2,1,0:T(8,128)(2,1)S(1)} collective-permute-done((bf16[2,1,2,2,64,640]{5,4,3,2,1,0:T(8,128)(2,1)S(1)}, bf16[2,1,2,2,64,640]{5,4,3,2,1,0:T(8,128)(2,1)S(1)}, u32[]{:S(2)}, u32[]{:S(2)}) %collective-permute-start.9) | collective-permute-done | bytes 655392 | tf_op jit(solution)/shard_map/ppermute | solution.py:987
  74.2 10.5 %project.1 = (bf16[1024,1024]{1,0:T(8,128)(2,1)}, bf16[16,1024]{1,0:T(8,128)(2,1)}, bf16[1024,2048]{1,0:T(8,128)(2,1)}, bf16[16,2048]{1,0:T(8,128)(2,1)}, f32[1024,128]{1,0:T(8,128)}) custom-call(bf16[1024,1024]{1,0:T(8,128)(2,1)} %inputs.5, bf16[16,1024]{1,0:T(8,128)(2,1)} %copy-done.66, f32[1,1024]{1,0:T(1,128)} %copy.184.gain, ...), custom_call_target="tpu_custom_call" | custom-call | tf_op jit(solution)/shard_map/project/pallas_call | solution.py:646
  94.1 9.7 %mixer_forward.3 = (bf16[16,4,128,128]{3,2,1,0:T(8,128)(2,1)}, bf16[16,4,128,128]{3,2,1,0:T(8,128)(2,1)}, bf16[16,4,128,128]{3,2,1,0:T(8,128)(2,1)}, bf16[16,4,1...) custom-call(bf16[1024,2048]{1,0:T(8,128)(2,1)} %get-tuple-element.276.raw.before, ...), custom_call_target="tpu_custom_call" | custom-call | tf_op jit(solution)/shard_map/mixer_forward/pallas_call | solution.py:237
  115.8 4.0 collective-permute-done.22
  121.2 13.7 %mixer_forward.4 = (bf16[16,4,128,128]{3,2,1,0:T(8,128)(2,1)}, bf16[16,4,128,128]{3,2,1,0:T(8,128)(2,1)}, bf16[16,4,128,128]{3,2,1,0:T(8,128)(2,1)}, bf16[16,4,1...) custom-call(bf16[1024,2048]{1,0:T(8,128)(2,1)} %get-tuple-element.27, ...), custom_call_target="tpu_custom_call", output_to_operand_aliasing={{0}: (9, {}), {1}: (10, {}), {2}: (11, {}), {3}: (12, {}), ... | custom-call | tf_op jit(solution)/shard_map/mixer_forward/pallas_call | solution.py:237
  139.9 13.4 %mixer_forward.5 = (bf16[16,4,128,128]{3,2,1,0:T(8,128)(2,1)}, bf16[16,4,128,128]{3,2,1,0:T(8,128)(2,1)}, bf16[16,4,128,128]{3,2,1,0:T(8,128)(2,1)}, bf16[16,4,1...) custom-call(bf16[1024,2048]{1,0:T(8,128)(2,1)} %get-tuple-element.27, ...), custom_call_target="tpu_custom_call", output_to_operand_aliasing={{0}: (9, {}), {1}: (10, {}), {2}: (11, {}), {3}: (12, {}), ... | custom-call | tf_op jit(solution)/shard_map/mixer_forward/pallas_call | solution.py:237
  157.8 3.4 collective-permute-done.28.other.other_map
  167.7 6.4 %project_side.1 = (bf16[1024,512]{1,0:T(8,128)(2,1)}, bf16[16,512]{1,0:T(8,128)(2,1)}, f32[1024,512]{1,0:T(8,128)}) custom-call(bf16[1024,1024]{1,0:T(8,128)(2,1)} %get-tuple-element.274.normed, bf16[16,1024]{1,0:T(8,128)(2,1)} %get-tuple-element.275.edge, bf16[1024,512]{1,0:T(8,128)(2,1)} %bitcast.226, bf16[1024,512]{1,0:T(8,128)(2,1)} %bitcast.224), custom_call_target="tpu_custom_call" | custom-call | tf_op jit(solution)/shard_map/project_side/pallas_call | solution.py:683
  178.9 6.3 %collective-permute-done.30.other.other_map = bf16[4,128,256]{2,1,0:T(8,128)(2,1)S(1)} collective-permute-done((bf16[4,128,256]{2,1,0:T(8,128)(2,1)S(1)}, bf16[4,128,256]{2,1,0:T(8,128)(2,1)S(1)}, u32[]{:S(2)}, u32[]{:S(2)}) %collective-permute-start.30) | collective-permute-done | bytes 262176 | tf_op jit(solution)/shard_map/ppermute | solution.py:987
  190.1 5.0 lay.3
  204.3 11.5 %mixer_query.1 = (bf16[1024,512]{1,0:T(8,128)(2,1)}, f32[1024,512]{1,0:T(8,128)}) custom-call(bf16[1024,512]{1,0:T(8,128)(2,1)} %get-tuple-element.308.raw.before.raw_q.before_q, bf16[1024,512]{1,0:T(8,128)(2,1)} %get-tuple-element.308.raw.before.raw_q.before_q, bf16[16,512]{1,0:T(8,128)(2,1)} %get-tuple-element.309.edge.edge_q, ...), custom_call_target="tpu_custom_call" | custom-call | tf_op jit(solution)/shard_map/mixer_query/pallas_call | solution.py:321
  218.2 7.5 %heads.1 = (f32[1024,512]{1,0:T(8,128)}, bf16[1024,512]{1,0:T(8,128)(2,1)}, f32[1024,1024]{1,0:T(8,128)}, bf16[1024,1024]{1,0:T(8,128)(2,1)}) custom-call(f32[1024,512]{1,0:T(8,128)} %get-tuple-element.327.local, bf16[1024,512]{1,0:T(8,128)(2,1)} %get-tuple-element.328.reach, bf16[4,128,128]{2,1,0:T(8,128)(2,1)} %copy-done.2, ...), custom_call_target="tpu_custom_call" | custom-call | tf_op jit(solution)/shard_map/heads/pallas_call | solution.py:726
  230.3 29.1 %feed.1 = (f32[1024,1024]{1,0:T(8,128)}, bf16[1024,1024]{1,0:T(8,128)(2,1)}, bf16[1024,1408]{1,0:T(8,128)(2,1)}, bf16[1024,1408]{1,0:T(8,128)(2,1)}, bf16[1024,1...) custom-call(s32[1]{0:T(128)} %bitcast.me, ...), custom_call_target="tpu_custom_call" | custom-call | tf_op jit(solution)/shard_map/feed/pallas_call | solution.py:818
  259.6 6.1 %convolution_convert_fusion.2 = bf16[1408,1024]{0,1:T(8,128)(2,1)S(1)} fusion(bf16[1024,1408]{1,0:T(8,128)(2,1)} %get-tuple-element.367, bf16[1024,1024]{1,0:T(8,128)(2,1)} %cotangent.3), kind=kOutput, calls=%fused_computation.7 | convolution fusion | flops 2954231808 | bytes 7864320 | tf_op jit(solution)/shard_map/dot_general | solution.py:29
  269.1 3.7 convolution_convert_fusion
  272.8 5.0 convolution_convert_fusion.1
  279.6 11.9 %turn.1 = (f32[1024,1024]{1,0:T(8,128)}, bf16[1024,1024]{1,0:T(8,128)(2,1)}, bf16[1024,512]{1,0:T(8,128)(2,1)}, bf16[1024,512]{1,0:T(8,128)(2,1)}, f32[4,128,128...) custom-call(f32[1024,1024]{1,0:T(8,128)} %get-tuple-element.363.hidden, f32[1024,1024]{1,0:T(8,128)} %get-tuple-element.365.own, ...), custom_call_target="tpu_custom_call" | custom-call | tf_op jit(solution)/shard_map/turn/pallas_call | solution.py:885
  308.1 6.7 %collective-permute-done.41.other = bf16[4,128,128]{2,1,0:T(8,128)(2,1)S(1)} collective-permute-done((bf16[4,128,128]{2,1,0:T(8,128)(2,1)S(1)}, bf16[4,128,128]{2,1,0:T(8,128)(2,1)S(1)}, u32[]{:S(2)}, u32[]{:S(2)}) %collective-permute-start.41) | collective-permute-done | bytes 131104 | tf_op jit(solution)/shard_map/ppermute | solution.py:987
  318.4 5.4 %collective-permute-done.42.other = bf16[4,128,128]{2,1,0:T(8,128)(2,1)S(1)} collective-permute-done((bf16[4,128,128]{2,1,0:T(8,128)(2,1)S(1)}, bf16[4,128,128]{2,1,0:T(8,128)(2,1)S(1)}, u32[]{:S(2)}, u32[]{:S(2)}) %collective-permute-start.42) | collective-permute-done | bytes 131104 | tf_op jit(solution)/shard_map/ppermute | solution.py:987
  331.8 29.9 %mixer_backward.3 = (bf16[1024,2560]{1,0:T(8,128)(2,1)}, f32[1024,8]{1,0:T(8,128)}, f32[8,2560]{1,0:T(8,128)}, f32[4,128,128]{2,1,0:T(8,128)}, f32[8,2560]{1,0:T(8,128)}, /*index=5*/f32[4,2560]{1,0:T(4,128)}) custom-call(bf16[1024,512]{1,0:T(8,128)(2,1)} %get-tuple-element.308.raw.before.raw_q.before_q, ...), custom_call_target="tpu_custom_call" | custom-call | tf_op jit(solution)/shard_map/mixer_backward/pallas_call | solution.py:551
  362.5 7.0 %halve.2 = (bf16[256,1408]{1,0:T(8,128)(2,1)}, bf16[256,1408]{1,0:T(8,128)(2,1)}, bf16[256,1408]{1,0:T(8,128)(2,1)}, bf16[256,1408]{1,0:T(8,128)(2,1)}, bf16[256...) custom-call(s32[1]{0:T(128)} %bitcast.me, ...), custom_call_target="tpu_custom_call" | custom-call | tf_op jit(solution)/shard_map/halve/pallas_call | solution.py:1219
  376.5 13.7 %mixer_backward.4 = (bf16[1024,2560]{1,0:T(8,128)(2,1)}, f32[1024,8]{1,0:T(8,128)}, f32[8,2560]{1,0:T(8,128)}, f32[4,128,128]{2,1,0:T(8,128)}, f32[8,2560]{1,0:T(8,128)}, /*index=5*/f32[4,2560]{1,0:T(4,128)}) custom-call(bf16[1024,512]{1,0:T(8,128)(2,1)} %get-tuple-element.308.raw.before.raw_q.before_q, ...), custom_call_target="tpu_custom_call", output_to_operand_aliasing={{0}: (20, {}), {1}: (21, {})} | custom-call | tf_op jit(solution)/shard_map/mixer_backward/pallas_call | solution.py:551
  393.8 4.1 halve.3
  405.8 7.8 %mixer_backward.5 = (bf16[1024,2560]{1,0:T(8,128)(2,1)}, f32[1024,8]{1,0:T(8,128)}, f32[8,2560]{1,0:T(8,128)}, f32[4,128,128]{2,1,0:T(8,128)}, f32[8,2560]{1,0:T(8,128)}, /*index=5*/f32[4,2560]{1,0:T(4,128)}) custom-call(bf16[1024,512]{1,0:T(8,128)(2,1)} %get-tuple-element.308.raw.before.raw_q.before_q, ...), custom_call_target="tpu_custom_call", output_to_operand_aliasing={{0}: (20, {}), {1}: (21, {})} | custom-call | tf_op jit(solution)/shard_map/mixer_backward/pallas_call | solution.py:551
  445.3 14.0 %back_project.1 = (bf16[1024,1024]{1,0:T(8,128)(2,1)}, f32[1,1024]{1,0:T(1,128)}) custom-call(bf16[1024,1024]{1,0:T(8,128)(2,1)} %inputs.5, bf16[1024,2560]{1,0:T(8,128)(2,1)} %mend.1.d_raw, bf16[1024,128]{1,0:T(8,128)(2,1)} %pad.9.d_extra, bf16[1024,512]{1,0:T(8,128)(2,1)} %get-tuple-element.394.d_gate, bf16[1024,512]{1,0:T(8,128)(2,1)} %bitcast.227, ...), custom_call_target="tpu_custom_call" | custom-call | tf_op jit(solution)/shard_map/back_project/pallas_call | solution.py:935
  463.7 6.0 %collective-permute-done.61 = bf16[1,1,1,1,64,5248]{5,4,3,2,1,0:T(8,128)(2,1)S(1)} collective-permute-done((bf16[1,1,1,1,64,5248]{5,4,3,2,1,0:T(8,128)(2,1)}, bf16[1,1,1,1,64,5248]{5,4,3,2,1,0:T(8,128)(2,1)S(1)}, u32[]{:S(2)}, u32[]{:S(2)}) %collective-permute-start.61) | collective-permute-done | bytes 671776 | tf_op jit(solution)/shard_map/ppermute | solution.py:987
  488.1 5.4 %collective-permute-done.65 = bf16[2,2,1,1,64,1024]{5,4,3,2,1,0:T(8,128)(2,1)S(1)} collective-permute-done((bf16[2,2,1,1,64,1024]{5,4,3,2,1,0:T(8,128)(2,1)S(1)}, bf16[2,2,1,1,64,1024]{5,4,3,2,1,0:T(8,128)(2,1)S(1)}, u32[]{:S(2)}, u32[]{:S(2)}) %collective-permute-start.65) | collective-permute-done | bytes 524320 | tf_op jit(solution)/shard_map/ppermute | solution.py:987
  505.6 3.6 collective-permute-done.73
  512.3 7.8 %collective-permute-done.74 = f32[168,128]{1,0:T(8,128)S(1)} collective-permute-done((f32[168,128]{1,0:T(8,128)S(1)}, f32[168,128]{1,0:T(8,128)S(1)}, u32[]{:S(2)}, u32[]{:S(2)}) %collective-permute-start.74) | collective-permute-done | bytes 86048 | tf_op jit(solution)/shard_map/ppermute | solution.py:987
  (474 shorter events, 239.2 us)
Async XLA Ops:
  4.2 22.9 %collective-permute-start = (bf16[1,1,1,1,64,2176]{5,4,3,2,1,0:T(8,128)(2,1)S(1)}, bf16[1,1,1,1,64,2176]{5,4,3,2,1,0:T(8,128)(2,1)S(1)}, u32[]{:S(2)}, u32[]{:S(2)}) collective-permute-start(bf16[1,1,1,1,64,2176]{5,4,3,2,1,0:T(8,128)(2,1)S(1)} %bitcast.244), channel_id=1, source_target_pairs={{0,16},{2,18},{4,20},{6,22},{8,24},{10,26},{12,28},{14,30},{16,0},... | collective-permute-start | bytes 835592 | tf_op jit(solution)/shard_map/ppermute | solution.py:987
  9.6 58.5 %collective-permute-start.11 = (bf16[16,1024]{1,0:T(8,128)(2,1)}, bf16[16,1024]{1,0:T(8,128)(2,1)S(1)}, u32[]{:S(2)}, u32[]{:S(2)}) collective-permute-start(bf16[16,1024]{1,0:T(8,128)(2,1)} %slice.136), channel_id=1, source_target_pairs={{0,2},{2,4},{4,6},{6,8},{8,10},{10,12},{12,14},{14,16},{16,18},{18... | collective-permute-start | bytes 98312 | tf_op jit(solution)/shard_map/ppermute | solution.py:981
  43.2 18.4 %collective-permute-start.9 = (bf16[2,1,2,2,64,640]{5,4,3,2,1,0:T(8,128)(2,1)S(1)}, bf16[2,1,2,2,64,640]{5,4,3,2,1,0:T(8,128)(2,1)S(1)}, u32[]{:S(2)}, u32[]{:S(2)}) collective-permute-start(bf16[2,1,2,2,64,640]{5,4,3,2,1,0:T(8,128)(2,1)S(1)} %pad_maximum_fusion.9), channel_id=1, source_target_pairs={{0,8},{2,10},{4,12},{6,14},{8,0},{10,2},{12,4},{14,6},{16,24},{18,... | collective-permute-start | bytes 1966088 | tf_op jit(solution)/shard_map/ppermute | solution.py:987
  68.2 35.6 %collective-permute-start.18 = (bf16[1,1,1,1,64,4224]{5,4,0,3,2,1:T(8,128)(2,1)S(1)}, bf16[1,1,1,1,64,4224]{5,4,0,3,2,1:T(8,128)(2,1)}, u32[]{:S(2)}, u32[]{:S(2)}) collective-permute-start(bf16[1,1,1,1,64,4224]{5,4,0,3,2,1:T(8,128)(2,1)S(1)} %bitcast.230), channel_id=1, source_target_pairs={{0,16},{2,18},{4,20},{6,22},{8,24},{10,26},{12,28},{14,30},{16,0},... | collective-permute-start | bytes 1622024 | tf_op jit(solution)/shard_map/ppermute | solution.py:987
  71.3 16.8 %collective-permute-start.12 = (bf16[2,1,1,1,64,512]{5,4,3,2,1,0:T(8,128)(2,1)S(1)}, bf16[2,1,1,1,64,512]{5,4,3,2,1,0:T(8,128)(2,1)}, u32[]{:S(2)}, u32[]{:S(2)}) collective-permute-start(bf16[2,1,1,1,64,512]{5,4,3,2,1,0:T(8,128)(2,1)S(1)} %get-tuple-element.279), channel_id=1, source_target_pairs={{0,8},{2,10},{4,12},{6,14},{8,0},{10,2},{12,4},{14,6},{16,24},{18,... | collective-permute-start | bytes 393224 | tf_op jit(solution)/shard_map/ppermute | solution.py:987
  111.3 23.6 %collective-permute-start.19 = (bf16[2,2,2,1,64,512]{5,4,3,2,1,0:T(8,128)(2,1)}, bf16[2,2,2,1,64,512]{5,4,3,2,1,0:T(8,128)(2,1)}, u32[]{:S(2)}, u32[]{:S(2)}) collective-permute-start(bf16[2,2,2,1,64,512]{5,4,3,2,1,0:T(8,128)(2,1)} %pad_maximum_fusion.12), channel_id=1, source_target_pairs={{0,2},{2,0},{4,6},{6,4},{8,10},{10,8},{12,14},{14,12},{16,18},{18,... | collective-permute-start | bytes 1572872 | tf_op jit(solution)/shard_map/ppermute | solution.py:987
  111.5 23.4 %collective-permute-start.20 = (bf16[2,2,1,2,64,512]{5,4,3,2,1,0:T(8,128)(2,1)}, bf16[2,2,1,2,64,512]{5,4,3,2,1,0:T(8,128)(2,1)}, u32[]{:S(2)}, u32[]{:S(2)}) collective-permute-start(bf16[2,2,1,2,64,512]{5,4,3,2,1,0:T(8,128)(2,1)} %pad_maximum_fusion.13), channel_id=1, source_target_pairs={{0,4},{2,6},{4,0},{6,2},{8,12},{10,14},{12,8},{14,10},{16,20},{18,... | collective-permute-start | bytes 1572872 | tf_op jit(solution)/shard_map/ppermute | solution.py:987
  113.1 21.8 %collective-permute-start.21 = (bf16[2,1,2,2,64,512]{5,4,3,2,1,0:T(8,128)(2,1)S(1)}, bf16[2,1,2,2,64,512]{5,4,3,2,1,0:T(8,128)(2,1)}, u32[]{:S(2)}, u32[]{:S(2)}) collective-permute-start(bf16[2,1,2,2,64,512]{5,4,3,2,1,0:T(8,128)(2,1)S(1)} %pad_maximum_fusion.14), channel_id=1, source_target_pairs={{0,8},{2,10},{4,12},{6,14},{8,0},{10,2},{12,4},{14,6},{16,24},{18,... | collective-permute-start | bytes 1572872 | tf_op jit(solution)/shard_map/ppermute | solution.py:987
  114.8 20.1 %collective-permute-start.23 = (bf16[2,1,1,1,64,1408]{5,4,0,3,2,1:T(8,128)(2,1)}, bf16[2,1,1,1,64,1408]{5,4,0,3,2,1:T(8,128)(2,1)}, u32[]{:S(2)}, u32[]{:S(2)}) collective-permute-start(bf16[2,1,1,1,64,1408]{5,4,0,3,2,1:T(8,128)(2,1)} %get-tuple-element.304), channel_id=1, source_target_pairs={{0,2},{2,0},{4,6},{6,4},{8,10},{10,8},{12,14},{14,12},{16,18},{18,... | collective-permute-start | bytes 1081352 | tf_op jit(solution)/shard_map/ppermute | solution.py:987
  137.6 17.1 %collective-permute-start.25 = (bf16[2,2,1,1,64,1408]{5,4,1,0,3,2:T(8,128)(2,1)}, bf16[2,2,1,1,64,1408]{5,4,1,0,3,2:T(8,128)(2,1)}, u32[]{:S(2)}, u32[]{:S(2)}) collective-permute-start(bf16[2,2,1,1,64,1408]{5,4,1,0,3,2:T(8,128)(2,1)} %bitcast.248), channel_id=1, source_target_pairs={{0,4},{2,6},{4,0},{6,2},{8,12},{10,14},{12,8},{14,10},{16,20},{18,... | collective-permute-start | bytes 2162696 | tf_op jit(solution)/shard_map/ppermute | solution.py:987
  139.1 15.7 %collective-permute-start.26 = (bf16[2,1,1,2,64,1408]{5,4,3,0,2,1:T(8,128)(2,1)}, bf16[2,1,1,2,64,1408]{5,4,3,0,2,1:T(8,128)(2,1)}, u32[]{:S(2)}, u32[]{:S(2)}) collective-permute-start(bf16[2,1,1,2,64,1408]{5,4,3,0,2,1:T(8,128)(2,1)} %bitcast.250), channel_id=1, source_target_pairs={{0,8},{2,10},{4,12},{6,14},{8,0},{10,2},{12,4},{14,6},{16,24},{18,... | collective-permute-start | bytes 2162696 | tf_op jit(solution)/shard_map/ppermute | solution.py:987
  198.9 26.8 %collective-permute-start.32 = (bf16[2,2,2,1,64,1408]{5,4,2,1,0,3:T(8,128)(2,1)}, bf16[2,2,2,1,64,1408]{5,4,2,1,0,3:T(8,128)(2,1)}, u32[]{:S(2)}, u32[]{:S(2)}) collective-permute-start(bf16[2,2,2,1,64,1408]{5,4,2,1,0,3:T(8,128)(2,1)} %bitcast.238), channel_id=1, source_target_pairs={{0,2},{2,0},{4,6},{6,4},{8,10},{10,8},{12,14},{14,12},{16,18},{18,... | collective-permute-start | bytes 4325384 | tf_op jit(solution)/shard_map/ppermute | solution.py:987
  199.7 26.0 %collective-permute-start.33 = (bf16[2,2,1,2,64,1408]{5,4,3,1,0,2:T(8,128)(2,1)}, bf16[2,2,1,2,64,1408]{5,4,3,1,0,2:T(8,128)(2,1)}, u32[]{:S(2)}, u32[]{:S(2)}) collective-permute-start(bf16[2,2,1,2,64,1408]{5,4,3,1,0,2:T(8,128)(2,1)} %bitcast.240), channel_id=1, source_target_pairs={{0,4},{2,6},{4,0},{6,2},{8,12},{10,14},{12,8},{14,10},{16,20},{18,... | collective-permute-start | bytes 4325384 | tf_op jit(solution)/shard_map/ppermute | solution.py:987
  201.3 24.4 %collective-permute-start.34 = (bf16[2,1,2,2,64,1408]{5,4,3,2,0,1:T(8,128)(2,1)}, bf16[2,1,2,2,64,1408]{5,4,3,2,0,1:T(8,128)(2,1)}, u32[]{:S(2)}, u32[]{:S(2)}) collective-permute-start(bf16[2,1,2,2,64,1408]{5,4,3,2,0,1:T(8,128)(2,1)} %bitcast.242), channel_id=1, source_target_pairs={{0,8},{2,10},{4,12},{6,14},{8,0},{10,2},{12,4},{14,6},{16,24},{18,... | collective-permute-start | bytes 4325384 | tf_op jit(solution)/shard_map/ppermute | solution.py:987
  259.4 18.4 %collective-permute-start.37 = (bf16[1024,1024]{1,0:T(8,128)(2,1)}, bf16[1024,1024]{1,0:T(8,128)(2,1)S(1)}, u32[]{:S(2)}, u32[]{:S(2)}) collective-permute-start(bf16[1024,1024]{1,0:T(8,128)(2,1)} %get-tuple-element.366), channel_id=1, source_target_pairs={{0,1},{1,0},{2,3},{3,2},{4,5},{5,4},{6,7},{7,6},{8,9},{9,8},{10,11... | collective-permute-start | bytes 6291464 | tf_op jit(solution)/shard_map/ppermute | solution.py:991
  277.9 47.8 %collective-permute-start.38 = (bf16[2,1,2,2,64,1408]{5,4,3,2,0,1:T(8,128)(2,1)}, bf16[2,1,2,2,64,1408]{5,4,3,2,0,1:T(8,128)(2,1)}, u32[]{:S(2)}, u32[]{:S(2)}) collective-permute-start(bf16[2,1,2,2,64,1408]{5,4,3,2,0,1:T(8,128)(2,1)} %dynamic-slice_bitcast_fusion.2), channel_id=1, source_target_pairs={{0,8},{2,10},{4,12},{6,14},{8,0},{10,2},{12,4},{14,6},{16,24},{18,... | collective-permute-start | bytes 4325384 | tf_op jit(solution)/shard_map/ppermute | solution.py:987
  325.6 36.1 %collective-permute-start.43 = (bf16[2,2,1,2,64,1408]{5,4,3,1,0,2:T(8,128)(2,1)}, bf16[2,2,1,2,64,1408]{5,4,3,1,0,2:T(8,128)(2,1)}, u32[]{:S(2)}, u32[]{:S(2)}) collective-permute-start(bf16[2,2,1,2,64,1408]{5,4,3,1,0,2:T(8,128)(2,1)} %dynamic-slice_bitcast_fusion.1), channel_id=1, source_target_pairs={{0,4},{2,6},{4,0},{6,2},{8,12},{10,14},{12,8},{14,10},{16,20},{18,... | collective-permute-start | bytes 4325384 | tf_op jit(solution)/shard_map/ppermute | solution.py:987
  326.2 35.5 %collective-permute-start.44 = (bf16[2,2,2,1,64,1408]{5,4,2,1,0,3:T(8,128)(2,1)}, bf16[2,2,2,1,64,1408]{5,4,2,1,0,3:T(8,128)(2,1)}, u32[]{:S(2)}, u32[]{:S(2)}) collective-permute-start(bf16[2,2,2,1,64,1408]{5,4,2,1,0,3:T(8,128)(2,1)} %dynamic-slice_bitcast_fusion), channel_id=1, source_target_pairs={{0,2},{2,0},{4,6},{6,4},{8,10},{10,8},{12,14},{14,12},{16,18},{18,... | collective-permute-start | bytes 4325384 | tf_op jit(solution)/shard_map/ppermute | solution.py:987
  327.3 34.4 %collective-permute-start.45 = (bf16[2,1,2,2,64,512]{5,4,3,2,0,1:T(8,128)(2,1)}, bf16[2,1,2,2,64,512]{5,4,3,2,0,1:T(8,128)(2,1)S(1)}, u32[]{:S(2)}, u32[]{:S(2)}) collective-permute-start(bf16[2,1,2,2,64,512]{5,4,3,2,0,1:T(8,128)(2,1)} %dynamic-slice_bitcast_fusion.4), channel_id=1, source_target_pairs={{0,8},{2,10},{4,12},{6,14},{8,0},{10,2},{12,4},{14,6},{16,24},{18,... | collective-permute-start | bytes 1572872 | tf_op jit(solution)/shard_map/ppermute | solution.py:987
  327.3 34.5 %collective-permute-start.46 = (bf16[2,1,2,2,64,512]{5,4,3,2,0,1:T(8,128)(2,1)}, bf16[2,1,2,2,64,512]{5,4,3,2,0,1:T(8,128)(2,1)}, u32[]{:S(2)}, u32[]{:S(2)}) collective-permute-start(bf16[2,1,2,2,64,512]{5,4,3,2,0,1:T(8,128)(2,1)} %dynamic-slice_bitcast_fusion.3), channel_id=1, source_target_pairs={{0,8},{2,10},{4,12},{6,14},{8,0},{10,2},{12,4},{14,6},{16,24},{18,... | collective-permute-start | bytes 1572872 | tf_op jit(solution)/shard_map/ppermute | solution.py:987
  369.5 23.3 %collective-permute-start.47 = (bf16[256,1408]{1,0:T(8,128)(2,1)}, bf16[256,1408]{1,0:T(8,128)(2,1)S(1)}, u32[]{:S(2)}, u32[]{:S(2)}) collective-permute-start(bf16[256,1408]{1,0:T(8,128)(2,1)} %get-tuple-element.429), channel_id=1, source_target_pairs={{0,8},{2,10},{4,12},{6,14},{8,0},{10,2},{12,4},{14,6},{16,24},{18,... | collective-permute-start | bytes 2162696 | tf_op jit(solution)/shard_map/ppermute | solution.py:987
  369.6 23.2 %collective-permute-start.48 = (bf16[256,1408]{1,0:T(8,128)(2,1)}, bf16[256,1408]{1,0:T(8,128)(2,1)}, u32[]{:S(2)}, u32[]{:S(2)}) collective-permute-start(bf16[256,1408]{1,0:T(8,128)(2,1)} %get-tuple-element.430), channel_id=1, source_target_pairs={{0,4},{2,6},{4,0},{6,2},{8,12},{10,14},{12,8},{14,10},{16,20},{18,... | collective-permute-start | bytes 2162696 | tf_op jit(solution)/shard_map/ppermute | solution.py:987
  370.1 22.7 %collective-permute-start.49 = (bf16[256,1408]{1,0:T(8,128)(2,1)}, bf16[256,1408]{1,0:T(8,128)(2,1)}, u32[]{:S(2)}, u32[]{:S(2)}) collective-permute-start(bf16[256,1408]{1,0:T(8,128)(2,1)} %get-tuple-element.431), channel_id=1, source_target_pairs={{0,2},{2,0},{4,6},{6,4},{8,10},{10,8},{12,14},{14,12},{16,18},{18,... | collective-permute-start | bytes 2162696 | tf_op jit(solution)/shard_map/ppermute | solution.py:987
  372.1 20.7 %collective-permute-start.50 = (bf16[256,512]{1,0:T(8,128)(2,1)}, bf16[256,512]{1,0:T(8,128)(2,1)S(1)}, u32[]{:S(2)}, u32[]{:S(2)}) collective-permute-start(bf16[256,512]{1,0:T(8,128)(2,1)} %get-tuple-element.432), channel_id=1, source_target_pairs={{0,2},{2,0},{4,6},{6,4},{8,10},{10,8},{12,14},{14,12},{16,18},{18,... | collective-permute-start | bytes 786440 | tf_op jit(solution)/shard_map/ppermute | solution.py:987
  372.3 20.6 %collective-permute-start.51 = (bf16[256,512]{1,0:T(8,128)(2,1)}, bf16[256,512]{1,0:T(8,128)(2,1)}, u32[]{:S(2)}, u32[]{:S(2)}) collective-permute-start(bf16[256,512]{1,0:T(8,128)(2,1)} %get-tuple-element.433), channel_id=1, source_target_pairs={{0,4},{2,6},{4,0},{6,2},{8,12},{10,14},{12,8},{14,10},{16,20},{18,... | collective-permute-start | bytes 786440 | tf_op jit(solution)/shard_map/ppermute | solution.py:987
  397.9 16.9 %collective-permute-start.52 = (bf16[128,1408]{1,0:T(8,128)(2,1)}, bf16[128,1408]{1,0:T(8,128)(2,1)}, u32[]{:S(2)}, u32[]{:S(2)}) collective-permute-start(bf16[128,1408]{1,0:T(8,128)(2,1)} %get-tuple-element.463), channel_id=1, source_target_pairs={{0,2},{2,0},{4,6},{6,4},{8,10},{10,8},{12,14},{14,12},{16,18},{18,... | collective-permute-start | bytes 1081352 | tf_op jit(solution)/shard_map/ppermute | solution.py:987
  434.8 34.9 %collective-permute-start.58 = (bf16[2,2,2,1,64,1024]{5,4,3,2,1,0:T(8,128)(2,1)}, bf16[2,2,2,1,64,1024]{5,4,3,2,1,0:T(8,128)(2,1)}, u32[]{:S(2)}, u32[]{:S(2)}) collective-permute-start(bf16[2,2,2,1,64,1024]{5,4,3,2,1,0:T(8,128)(2,1)} %constant_dynamic-slice_fusion.3), channel_id=1, source_target_pairs={{0,2},{2,0},{4,6},{6,4},{8,10},{10,8},{12,14},{14,12},{16,18},{18,... | collective-permute-start | bytes 3145736 | tf_op jit(solution)/shard_map/ppermute | solution.py:987
  437.5 32.2 %collective-permute-start.59 = (bf16[2,2,1,2,64,1024]{5,4,3,2,1,0:T(8,128)(2,1)}, bf16[2,2,1,2,64,1024]{5,4,3,2,1,0:T(8,128)(2,1)}, u32[]{:S(2)}, u32[]{:S(2)}) collective-permute-start(bf16[2,2,1,2,64,1024]{5,4,3,2,1,0:T(8,128)(2,1)} %constant_dynamic-slice_fusion.2), channel_id=1, source_target_pairs={{0,4},{2,6},{4,0},{6,2},{8,12},{10,14},{12,8},{14,10},{16,20},{18,... | collective-permute-start | bytes 3145736 | tf_op jit(solution)/shard_map/ppermute | solution.py:987
  441.9 27.9 %collective-permute-start.61 = (bf16[1,1,1,1,64,5248]{5,4,3,2,1,0:T(8,128)(2,1)}, bf16[1,1,1,1,64,5248]{5,4,3,2,1,0:T(8,128)(2,1)S(1)}, u32[]{:S(2)}, u32[]{:S(2)}) collective-permute-start(bf16[1,1,1,1,64,5248]{5,4,3,2,1,0:T(8,128)(2,1)} %fusion.19), channel_id=1, source_target_pairs={{0,16},{2,18},{4,20},{6,22},{8,24},{10,26},{12,28},{14,30},{16,0},... | collective-permute-start | bytes 2015240 | tf_op jit(solution)/shard_map/ppermute | solution.py:987
  442.4 21.3 %collective-permute-start.60 = (bf16[2,1,2,2,64,512]{5,4,3,2,1,0:T(8,128)(2,1)}, bf16[2,1,2,2,64,512]{5,4,3,2,1,0:T(8,128)(2,1)}, u32[]{:S(2)}, u32[]{:S(2)}) collective-permute-start(bf16[2,1,2,2,64,512]{5,4,3,2,1,0:T(8,128)(2,1)} %constant_dynamic-slice_fusion.1), channel_id=1, source_target_pairs={{0,8},{2,10},{4,12},{6,14},{8,0},{10,2},{12,4},{14,6},{16,24},{18,... | collective-permute-start | bytes 1572872 | tf_op jit(solution)/shard_map/ppermute | solution.py:987
  444.5 32.5 %collective-permute-start.36 = (bf16[1024,512]{1,0:T(8,128)(2,1)}, bf16[1024,512]{1,0:T(8,128)(2,1)}, u32[]{:S(2)}, u32[]{:S(2)}) collective-permute-start(bf16[1024,512]{1,0:T(8,128)(2,1)} %constant_dynamic-slice_fusion.4), channel_id=1, source_target_pairs={{0,1},{1,0},{2,3},{3,2},{4,5},{5,4},{6,7},{7,6},{8,9},{9,8},{10,11... | collective-permute-start | bytes 3145736 | tf_op jit(solution)/shard_map/ppermute | solution.py:991
  509.3 16.3 %collective-permute-start.72 = (bf16[1,1,1,1,64,2560]{5,4,3,2,1,0:T(8,128)(2,1)S(1)}, bf16[1,1,1,1,64,2560]{5,4,3,2,1,0:T(8,128)(2,1)S(1)}, u32[]{:S(2)}, u32[]{:S(2)}) collective-permute-start(bf16[1,1,1,1,64,2560]{5,4,3,2,1,0:T(8,128)(2,1)S(1)} %pad_maximum_fusion.18), channel_id=1, source_target_pairs={{0,16},{2,18},{4,20},{6,22},{8,24},{10,26},{12,28},{14,30},{16,0},... | collective-permute-start | bytes 983048 | tf_op jit(solution)/shard_map/ppermute | solution.py:987
  (123 other events, 988.9 us)

commit v6 on v5

--- a/solution.py
+++ b/solution.py
@@ -14,6 +14,7 @@
 PAIR = 2
 QUERY_CHUNKS = 2
 TILE = 256
+LONG_TILE = 512
 AHEAD_CALLS = 3
 NORM_EPS = 1e-05
 UNIT_EPS = 1e-06
@@ -486,7 +487,8 @@
             at = j * head_count + h
             logits = d_betas[at] * betas[at] * (1.0 - betas[at])
             logit_cols += [logits[n * BLOCK : (n + 1) * BLOCK] for n in range(substeps)]
-        d_logit[rows_at[j], :] = jnp.concatenate(logit_cols, 1)
+        logit_cols.append(jnp.zeros((BLOCK, width - len(logit_cols)), F32))
+        d_logit[rows_at[j], :] = low(jnp.concatenate(logit_cols, 1))
 
     for head in heads:
         mine = [j * head_count + head for j in range(PAIR)]
@@ -574,7 +576,7 @@
         + [anywhere] * len(passed),
         out_specs=[
             tokens(columns),
-            tokens(head_count * substeps),
+            tokens(width),
             whole_spec(8, columns),
             whole_spec(*state),
             whole_spec(8, columns),
@@ -582,7 +584,7 @@
         ],
         out_shape=[
             jax.ShapeDtypeStruct((count, columns), BF16),
-            jax.ShapeDtypeStruct((count, head_count * substeps), F32),
+            jax.ShapeDtypeStruct((count, width), BF16),
             jax.ShapeDtypeStruct((8, columns), F32),
             jax.ShapeDtypeStruct(state, F32),
             jax.ShapeDtypeStruct((8, columns), F32),
@@ -678,7 +680,7 @@
 def run_project_side(normed, edge, query_w, gate_w):
     count, features = normed.shape
     cols = query_w.shape[1]
-    tile = min(TILE, count)
+    tile = min(LONG_TILE, count)
     tokens = lambda cols: pl.BlockSpec((tile, cols), lambda c: (c, 0))
     return pl.pallas_call(
         project_side_kernel,
@@ -721,7 +723,7 @@
 def run_heads(local, reach, state, gate, gain, weight, head_count, width):
     count, cols = local.shape
     features = weight.shape[0]
-    tile = min(TILE, count)
+    tile = min(LONG_TILE, count)
     tokens = lambda cols: pl.BlockSpec((tile, cols), lambda c: (c, 0))
     return pl.pallas_call(
         functools.partial(heads_kernel, head_count, width),
@@ -878,7 +880,7 @@
 ):
     count, features = hidden.shape
     cols = mixer.shape[1]
-    tile = min(TILE, count)
+    tile = min(LONG_TILE, count)
     tokens = lambda cols: pl.BlockSpec((tile, cols), lambda c: (c, 0))
     shape = lambda cols, kind: jax.ShapeDtypeStruct((count, cols), kind)
     state = (head_count, width, width)
@@ -1415,7 +1417,7 @@
     normed, edge_normed, raw_kv, edge_kv, sigmas = run_project(
         activations, input_edge, gain_one, weights_kv, 2 * key_cols, extra
     )
-    beta_gate = sigmas[:, :beta_cols]
+    beta_gate = sigmas
     eye = jnp.broadcast_to(jnp.eye(width, dtype=F32), (head_count, width, width))
     chain = jnp.concatenate([eye, jnp.zeros_like(eye)], 2)
     passed = ()
@@ -1594,7 +1596,7 @@
     returned = shift_seq(first_rows, -1)
     same_after = same_docs(token_position[-1] + 1 + jnp.arange(8, dtype=jnp.int32))
     d_raw = mend(d_raw, tail, returned, same_after, taps_all)
-    d_beta_low = low(d_beta_logit)
+    d_beta_low = d_beta_logit
     fifth = -(-conv_cols // (5 * width)) * width
     conv_marks = [0, 2 * fifth, 4 * fifth, conv_cols]
     keeps, sends = halve_all(
@@ -1606,7 +1608,7 @@
     )
     d_raw, d_beta_low, sends = tied(d_raw, d_beta_low, sends)
     others = swap_all(sends, at_step(0))
-    d_extra = jnp.pad(d_beta_low, ((0, 0), (0, extra - beta_cols)))
+    d_extra = d_beta_low
     d_low, gain_part = run_back_project(
         activations, d_raw, d_extra, d_gate_logit, [weight_query, weight_gate, *weights_kv]
     )
@@ -1623,7 +1625,7 @@
     d_other = swap_head(d_low)
     small = jnp.concatenate(
         [
-            inner_rows(d_beta_low, normed).reshape(-1),
+            inner_rows(d_beta_low, normed)[:beta_cols].reshape(-1),
             both_heads[:features],
             grad_feed_gain,
             tap_grads.reshape(-1),

time: 538 us -> 535 us (level)
    unnamed x165 -> x175, local copies, waits for them, and re-layouts: 17.2 us -> 17 us
  transfers between devices with their start and end apart: 75 -> 75, of which waited for: 29 -> 30; matrix products, arithmetic and copies ran while one was open for 19% -> 19% of each run, Pallas kernels for 30% -> 30%
where the time goes in v6:
time: 535 us; the launch traced here: 525 us
  Pallas kernels  207 us (39%)
  waiting for transfers between devices  98.2 us (18%)
  starting transfers between devices  80.7 us (15%)
  other arithmetic  60.4 us (11%)
  local copies, waits for them, and re-layouts  48.3 us (9%)
  matrix products  27.2 us (5%)
    ppermute x68, waiting for transfers between devices, swap_seq(): lax.ppermute(array, 'seq', [(i, i ^ distance) for i in range(lax.axis_siz...  95.5 us
    ppermute x68, starting transfers between devices, swap_seq(): lax.ppermute(array, 'seq', [(i, i ^ distance) for i in range(lax.axis_siz...  75 us
    pallas_call x3, Pallas kernels, run_backward(): pl.pallas_call(functools.partial(backward_kernel, head_count, substeps, w...  52.2 us
    pallas_call x3, Pallas kernels, run_forward(): pl.pallas_call(functools.partial(forward_kernel, head_count, substeps, wi...  36.7 us
    pallas_call x1, Pallas kernels, run_feed(): pl.pallas_call(functools.partial(feed_kernel, distances, rows), grid=(cou...  29.1 us
    dot_general x9, matrix products, inner_rows(): lax.dot_general(former, latter, (((0,), (0,)), ((), ())), preferred_eleme...  27.2 us
    unnamed x175, local copies, waits for them, and re-layouts  17 us
    pallas_call x1, Pallas kernels, run_back_project(): pl.pallas_call(functools.partial(back_project_kernel, d_extra.shape[1]),...  14.2 us
  transfers between devices with their start and end apart: 75, of which 30 were waited for; matrix products, arithmetic and copies ran while one was open for 19% of the time, Pallas kernels for 30%

profile of v6, /device:TPU:0, one launch (start us, length us, event | category | flops | bytes accessed | tf_op | source)
XLA Modules:
  0.0 525.0 jit_solution(10355574128468522879)
XLA Ops:
  4.2 4.1 collective-permute-start
  9.6 3.4 collective-permute-start.11
  15.8 6.3 %fusion.39 = f32[16,64,4]{2,0,1:T(8,128)S(1)} fusion(f32[16,64,4]{2,0,1:T(8,128)S(1)} %copy.186), kind=kOutput, calls=%fused_computation.212 | output fusion | flops 258048 | bytes 32768 | tf_op jit(solution)/shard_map/jit(cumsum)/reduce_window_sum | solution.py:1410
  43.9 6.7 %collective-permute-done.5 = bf16[2,1,1,2,64,768]{5,4,3,2,1,0:T(8,128)(2,1)S(1)} collective-permute-done((bf16[2,1,1,2,64,768]{5,4,3,2,1,0:T(8,128)(2,1)S(1)}, bf16[2,1,1,2,64,768]{5,4,3,2,1,0:T(8,128)(2,1)S(1)}, u32[]{:S(2)}, u32[]{:S(2)}) %collective-permute-start.5) | collective-permute-done | bytes 393248 | tf_op jit(solution)/shard_map/ppermute | solution.py:989
  52.6 9.1 %collective-permute-done.9 = bf16[2,1,2,2,64,640]{5,4,3,2,1,0:T(8,128)(2,1)S(1)} collective-permute-done((bf16[2,1,2,2,64,640]{5,4,3,2,1,0:T(8,128)(2,1)S(1)}, bf16[2,1,2,2,64,640]{5,4,3,2,1,0:T(8,128)(2,1)S(1)}, u32[]{:S(2)}, u32[]{:S(2)}) %collective-permute-start.9) | collective-permute-done | bytes 655392 | tf_op jit(solution)/shard_map/ppermute | solution.py:989
  74.2 10.5 %project.1 = (bf16[1024,1024]{1,0:T(8,128)(2,1)}, bf16[16,1024]{1,0:T(8,128)(2,1)}, bf16[1024,2048]{1,0:T(8,128)(2,1)}, bf16[16,2048]{1,0:T(8,128)(2,1)}, f32[1024,128]{1,0:T(8,128)}) custom-call(bf16[1024,1024]{1,0:T(8,128)(2,1)} %inputs.5, bf16[16,1024]{1,0:T(8,128)(2,1)} %copy-done.71, f32[1,1024]{1,0:T(1,128)} %copy.184.gain, ...), custom_call_target="tpu_custom_call" | custom-call | tf_op jit(solution)/shard_map/project/pallas_call | solution.py:648
  94.1 9.7 %mixer_forward.3 = (bf16[16,4,128,128]{3,2,1,0:T(8,128)(2,1)}, bf16[16,4,128,128]{3,2,1,0:T(8,128)(2,1)}, bf16[16,4,128,128]{3,2,1,0:T(8,128)(2,1)}, bf16[16,4,1...) custom-call(bf16[1024,2048]{1,0:T(8,128)(2,1)} %get-tuple-element.276.raw.before, ...), custom_call_target="tpu_custom_call" | custom-call | tf_op jit(solution)/shard_map/mixer_forward/pallas_call | solution.py:238
  115.8 4.0 collective-permute-done.22
  121.2 13.6 %mixer_forward.4 = (bf16[16,4,128,128]{3,2,1,0:T(8,128)(2,1)}, bf16[16,4,128,128]{3,2,1,0:T(8,128)(2,1)}, bf16[16,4,128,128]{3,2,1,0:T(8,128)(2,1)}, bf16[16,4,1...) custom-call(bf16[1024,2048]{1,0:T(8,128)(2,1)} %get-tuple-element.27, ...), custom_call_target="tpu_custom_call", output_to_operand_aliasing={{0}: (9, {}), {1}: (10, {}), {2}: (11, {}), {3}: (12, {}), ... | custom-call | tf_op jit(solution)/shard_map/mixer_forward/pallas_call | solution.py:238
  139.9 13.4 %mixer_forward.5 = (bf16[16,4,128,128]{3,2,1,0:T(8,128)(2,1)}, bf16[16,4,128,128]{3,2,1,0:T(8,128)(2,1)}, bf16[16,4,128,128]{3,2,1,0:T(8,128)(2,1)}, bf16[16,4,1...) custom-call(bf16[1024,2048]{1,0:T(8,128)(2,1)} %get-tuple-element.27, ...), custom_call_target="tpu_custom_call", output_to_operand_aliasing={{0}: (9, {}), {1}: (10, {}), {2}: (11, {}), {3}: (12, {}), ... | custom-call | tf_op jit(solution)/shard_map/mixer_forward/pallas_call | solution.py:238
  167.7 5.8 %project_side.1 = (bf16[1024,512]{1,0:T(8,128)(2,1)}, bf16[16,512]{1,0:T(8,128)(2,1)}, f32[1024,512]{1,0:T(8,128)}) custom-call(bf16[1024,1024]{1,0:T(8,128)(2,1)} %get-tuple-element.274.normed, bf16[16,1024]{1,0:T(8,128)(2,1)} %get-tuple-element.275.edge, bf16[1024,512]{1,0:T(8,128)(2,1)} %bitcast.218, bf16[1024,512]{1,0:T(8,128)(2,1)} %bitcast.216), custom_call_target="tpu_custom_call" | custom-call | tf_op jit(solution)/shard_map/project_side/pallas_call | solution.py:685
  178.3 6.3 %collective-permute-done.30.other.other_map = bf16[4,128,256]{2,1,0:T(8,128)(2,1)S(1)} collective-permute-done((bf16[4,128,256]{2,1,0:T(8,128)(2,1)S(1)}, bf16[4,128,256]{2,1,0:T(8,128)(2,1)S(1)}, u32[]{:S(2)}, u32[]{:S(2)}) %collective-permute-start.30) | collective-permute-done | bytes 262176 | tf_op jit(solution)/shard_map/ppermute | solution.py:989
  189.6 5.0 lay.3
  203.8 11.2 %mixer_query.1 = (bf16[1024,512]{1,0:T(8,128)(2,1)}, f32[1024,512]{1,0:T(8,128)}) custom-call(bf16[1024,512]{1,0:T(8,128)(2,1)} %get-tuple-element.308.raw.before.raw_q.before_q, bf16[1024,512]{1,0:T(8,128)(2,1)} %get-tuple-element.308.raw.before.raw_q.before_q, bf16[16,512]{1,0:T(8,128)(2,1)} %get-tuple-element.309.edge.edge_q, ...), custom_call_target="tpu_custom_call" | custom-call | tf_op jit(solution)/shard_map/mixer_query/pallas_call | solution.py:322
  217.3 6.6 %heads.1 = (f32[1024,512]{1,0:T(8,128)}, bf16[1024,512]{1,0:T(8,128)(2,1)}, f32[1024,1024]{1,0:T(8,128)}, bf16[1024,1024]{1,0:T(8,128)(2,1)}) custom-call(f32[1024,512]{1,0:T(8,128)} %get-tuple-element.327.local, bf16[1024,512]{1,0:T(8,128)(2,1)} %get-tuple-element.328.reach, bf16[4,128,128]{2,1,0:T(8,128)(2,1)} %copy-done.2, ...), custom_call_target="tpu_custom_call" | custom-call | tf_op jit(solution)/shard_map/heads/pallas_call | solution.py:728
  229.1 29.1 %feed.1 = (f32[1024,1024]{1,0:T(8,128)}, bf16[1024,1024]{1,0:T(8,128)(2,1)}, bf16[1024,1408]{1,0:T(8,128)(2,1)}, bf16[1024,1408]{1,0:T(8,128)(2,1)}, bf16[1024,1...) custom-call(s32[1]{0:T(128)} %bitcast.me, ...), custom_call_target="tpu_custom_call" | custom-call | tf_op jit(solution)/shard_map/feed/pallas_call | solution.py:820
  258.5 6.1 %convolution_convert_fusion.2 = bf16[1408,1024]{0,1:T(8,128)(2,1)S(1)} fusion(bf16[1024,1408]{1,0:T(8,128)(2,1)} %get-tuple-element.367, bf16[1024,1024]{1,0:T(8,128)(2,1)} %cotangent.3), kind=kOutput, calls=%fused_computation.7 | convolution fusion | flops 2954231808 | bytes 7864320 | tf_op jit(solution)/shard_map/dot_general | solution.py:30
  267.9 3.7 convolution_convert_fusion
  271.7 5.2 convolution_convert_fusion.1
  278.7 11.3 %turn.1 = (f32[1024,1024]{1,0:T(8,128)}, bf16[1024,1024]{1,0:T(8,128)(2,1)}, bf16[1024,512]{1,0:T(8,128)(2,1)}, bf16[1024,512]{1,0:T(8,128)(2,1)}, f32[4,128,128...) custom-call(f32[1024,1024]{1,0:T(8,128)} %get-tuple-element.363.hidden, f32[1024,1024]{1,0:T(8,128)} %get-tuple-element.365.own, ...), custom_call_target="tpu_custom_call" | custom-call | tf_op jit(solution)/shard_map/turn/pallas_call | solution.py:887
  306.5 7.3 %collective-permute-done.41.other = bf16[4,128,128]{2,1,0:T(8,128)(2,1)S(1)} collective-permute-done((bf16[4,128,128]{2,1,0:T(8,128)(2,1)S(1)}, bf16[4,128,128]{2,1,0:T(8,128)(2,1)S(1)}, u32[]{:S(2)}, u32[]{:S(2)}) %collective-permute-start.41) | collective-permute-done | bytes 131104 | tf_op jit(solution)/shard_map/ppermute | solution.py:989
  317.8 4.9 collective-permute-done.42.other
  330.9 30.5 %mixer_backward.3 = (bf16[1024,2560]{1,0:T(8,128)(2,1)}, bf16[1024,128]{1,0:T(8,128)(2,1)}, f32[8,2560]{1,0:T(8,128)}, f32[4,128,128]{2,1,0:T(8,128)}, f32[8,2560]{1,0:T(8,128)}, /*index=5*/f32[4,2560]{1,0:T(4,128)}) custom-call(bf16[1024,512]{1,0:T(8,128)(2,1)} %get-tuple-element.308.raw.before.raw_q.before_q, ...), custom_call_target="tpu_custom_call" | custom-call | tf_op jit(solution)/shard_map/mixer_backward/pallas_call | solution.py:553
  362.2 7.0 %halve.2 = (bf16[256,1408]{1,0:T(8,128)(2,1)}, bf16[256,1408]{1,0:T(8,128)(2,1)}, bf16[256,1408]{1,0:T(8,128)(2,1)}, bf16[256,1408]{1,0:T(8,128)(2,1)}, bf16[256...) custom-call(s32[1]{0:T(128)} %bitcast.me, ...), custom_call_target="tpu_custom_call" | custom-call | tf_op jit(solution)/shard_map/halve/pallas_call | solution.py:1221
  376.0 13.9 %mixer_backward.4 = (bf16[1024,2560]{1,0:T(8,128)(2,1)}, bf16[1024,128]{1,0:T(8,128)(2,1)}, f32[8,2560]{1,0:T(8,128)}, f32[4,128,128]{2,1,0:T(8,128)}, f32[8,2560]{1,0:T(8,128)}, /*index=5*/f32[4,2560]{1,0:T(4,128)}) custom-call(bf16[1024,512]{1,0:T(8,128)(2,1)} %get-tuple-element.308.raw.before.raw_q.before_q, ...), custom_call_target="tpu_custom_call", output_to_operand_aliasing={{0}: (20, {}), {1}: (21, {})} | custom-call | tf_op jit(solution)/shard_map/mixer_backward/pallas_call | solution.py:553
  393.3 4.3 halve.3
  405.5 7.9 %mixer_backward.5 = (bf16[1024,2560]{1,0:T(8,128)(2,1)}, bf16[1024,128]{1,0:T(8,128)(2,1)}, f32[8,2560]{1,0:T(8,128)}, f32[4,128,128]{2,1,0:T(8,128)}, f32[8,2560]{1,0:T(8,128)}, /*index=5*/f32[4,2560]{1,0:T(4,128)}) custom-call(bf16[1024,512]{1,0:T(8,128)(2,1)} %get-tuple-element.308.raw.before.raw_q.before_q, ...), custom_call_target="tpu_custom_call", output_to_operand_aliasing={{0}: (20, {}), {1}: (21, {})} | custom-call | tf_op jit(solution)/shard_map/mixer_backward/pallas_call | solution.py:553
  442.8 14.2 %back_project.1 = (bf16[1024,1024]{1,0:T(8,128)(2,1)}, f32[1,1024]{1,0:T(1,128)}) custom-call(bf16[1024,1024]{1,0:T(8,128)(2,1)} %inputs.5, bf16[1024,2560]{1,0:T(8,128)(2,1)} %mend.1.d_raw, bf16[1024,128]{1,0:T(8,128)(2,1)} %get-tuple-element.471.d_extra, bf16[1024,512]{1,0:T(8,128)(2,1)} %get-tuple-element.394.d_gate, bf16[1024,512]{1,0:T(8,128)(2,1)} %bitcast.219, ...), custom_call_target="tpu_custom_call" | custom-call | tf_op jit(solution)/shard_map/back_project/pallas_call | solution.py:937
  461.1 5.6 %collective-permute-done.61 = bf16[1,1,1,1,64,5248]{5,4,3,2,1,0:T(8,128)(2,1)S(1)} collective-permute-done((bf16[1,1,1,1,64,5248]{5,4,3,2,1,0:T(8,128)(2,1)}, bf16[1,1,1,1,64,5248]{5,4,3,2,1,0:T(8,128)(2,1)S(1)}, u32[]{:S(2)}, u32[]{:S(2)}) %collective-permute-start.61) | collective-permute-done | bytes 671776 | tf_op jit(solution)/shard_map/ppermute | solution.py:989
  484.9 5.5 %collective-permute-done.65 = bf16[2,2,1,1,64,1024]{5,4,3,2,1,0:T(8,128)(2,1)S(1)} collective-permute-done((bf16[2,2,1,1,64,1024]{5,4,3,2,1,0:T(8,128)(2,1)S(1)}, bf16[2,2,1,1,64,1024]{5,4,3,2,1,0:T(8,128)(2,1)S(1)}, u32[]{:S(2)}, u32[]{:S(2)}) %collective-permute-start.65) | collective-permute-done | bytes 524320 | tf_op jit(solution)/shard_map/ppermute | solution.py:989
  502.6 3.5 collective-permute-done.73
  509.2 8.1 %collective-permute-done.74 = f32[168,128]{1,0:T(8,128)S(1)} collective-permute-done((f32[168,128]{1,0:T(8,128)S(1)}, f32[168,128]{1,0:T(8,128)S(1)}, u32[]{:S(2)}, u32[]{:S(2)}) %collective-permute-start.74) | collective-permute-done | bytes 86048 | tf_op jit(solution)/shard_map/ppermute | solution.py:989
  (482 shorter events, 237.5 us)
Async XLA Ops:
  4.2 22.9 %collective-permute-start = (bf16[1,1,1,1,64,2176]{5,4,3,2,1,0:T(8,128)(2,1)S(1)}, bf16[1,1,1,1,64,2176]{5,4,3,2,1,0:T(8,128)(2,1)S(1)}, u32[]{:S(2)}, u32[]{:S(2)}) collective-permute-start(bf16[1,1,1,1,64,2176]{5,4,3,2,1,0:T(8,128)(2,1)S(1)} %bitcast.236), channel_id=1, source_target_pairs={{0,16},{2,18},{4,20},{6,22},{8,24},{10,26},{12,28},{14,30},{16,0},... | collective-permute-start | bytes 835592 | tf_op jit(solution)/shard_map/ppermute | solution.py:989
  9.6 58.6 %collective-permute-start.11 = (bf16[16,1024]{1,0:T(8,128)(2,1)}, bf16[16,1024]{1,0:T(8,128)(2,1)S(1)}, u32[]{:S(2)}, u32[]{:S(2)}) collective-permute-start(bf16[16,1024]{1,0:T(8,128)(2,1)} %slice.136), channel_id=1, source_target_pairs={{0,2},{2,4},{4,6},{6,8},{8,10},{10,12},{12,14},{14,16},{16,18},{18... | collective-permute-start | bytes 98312 | tf_op jit(solution)/shard_map/ppermute | solution.py:983
  43.2 18.4 %collective-permute-start.9 = (bf16[2,1,2,2,64,640]{5,4,3,2,1,0:T(8,128)(2,1)S(1)}, bf16[2,1,2,2,64,640]{5,4,3,2,1,0:T(8,128)(2,1)S(1)}, u32[]{:S(2)}, u32[]{:S(2)}) collective-permute-start(bf16[2,1,2,2,64,640]{5,4,3,2,1,0:T(8,128)(2,1)S(1)} %pad_maximum_fusion.9), channel_id=1, source_target_pairs={{0,8},{2,10},{4,12},{6,14},{8,0},{10,2},{12,4},{14,6},{16,24},{18,... | collective-permute-start | bytes 1966088 | tf_op jit(solution)/shard_map/ppermute | solution.py:989
  68.2 35.6 %collective-permute-start.18 = (bf16[1,1,1,1,64,4224]{5,4,0,3,2,1:T(8,128)(2,1)S(1)}, bf16[1,1,1,1,64,4224]{5,4,0,3,2,1:T(8,128)(2,1)}, u32[]{:S(2)}, u32[]{:S(2)}) collective-permute-start(bf16[1,1,1,1,64,4224]{5,4,0,3,2,1:T(8,128)(2,1)S(1)} %bitcast.222), channel_id=1, source_target_pairs={{0,16},{2,18},{4,20},{6,22},{8,24},{10,26},{12,28},{14,30},{16,0},... | collective-permute-start | bytes 1622024 | tf_op jit(solution)/shard_map/ppermute | solution.py:989
  70.4 15.4 %collective-permute-start.13 = (bf16[2,1,1,1,64,512]{5,4,3,2,1,0:T(8,128)(2,1)}, bf16[2,1,1,1,64,512]{5,4,3,2,1,0:T(8,128)(2,1)}, u32[]{:S(2)}, u32[]{:S(2)}) collective-permute-start(bf16[2,1,1,1,64,512]{5,4,3,2,1,0:T(8,128)(2,1)} %get-tuple-element.280), channel_id=1, source_target_pairs={{0,2},{2,0},{4,6},{6,4},{8,10},{10,8},{12,14},{14,12},{16,18},{18,... | collective-permute-start | bytes 393224 | tf_op jit(solution)/shard_map/ppermute | solution.py:989
  71.4 16.8 %collective-permute-start.12 = (bf16[2,1,1,1,64,512]{5,4,3,2,1,0:T(8,128)(2,1)S(1)}, bf16[2,1,1,1,64,512]{5,4,3,2,1,0:T(8,128)(2,1)}, u32[]{:S(2)}, u32[]{:S(2)}) collective-permute-start(bf16[2,1,1,1,64,512]{5,4,3,2,1,0:T(8,128)(2,1)S(1)} %get-tuple-element.279), channel_id=1, source_target_pairs={{0,8},{2,10},{4,12},{6,14},{8,0},{10,2},{12,4},{14,6},{16,24},{18,... | collective-permute-start | bytes 393224 | tf_op jit(solution)/shard_map/ppermute | solution.py:989
  111.3 23.5 %collective-permute-start.19 = (bf16[2,2,2,1,64,512]{5,4,3,2,1,0:T(8,128)(2,1)}, bf16[2,2,2,1,64,512]{5,4,3,2,1,0:T(8,128)(2,1)}, u32[]{:S(2)}, u32[]{:S(2)}) collective-permute-start(bf16[2,2,2,1,64,512]{5,4,3,2,1,0:T(8,128)(2,1)} %pad_maximum_fusion.12), channel_id=1, source_target_pairs={{0,2},{2,0},{4,6},{6,4},{8,10},{10,8},{12,14},{14,12},{16,18},{18,... | collective-permute-start | bytes 1572872 | tf_op jit(solution)/shard_map/ppermute | solution.py:989
  111.5 23.3 %collective-permute-start.20 = (bf16[2,2,1,2,64,512]{5,4,3,2,1,0:T(8,128)(2,1)}, bf16[2,2,1,2,64,512]{5,4,3,2,1,0:T(8,128)(2,1)}, u32[]{:S(2)}, u32[]{:S(2)}) collective-permute-start(bf16[2,2,1,2,64,512]{5,4,3,2,1,0:T(8,128)(2,1)} %pad_maximum_fusion.13), channel_id=1, source_target_pairs={{0,4},{2,6},{4,0},{6,2},{8,12},{10,14},{12,8},{14,10},{16,20},{18,... | collective-permute-start | bytes 1572872 | tf_op jit(solution)/shard_map/ppermute | solution.py:989
  113.1 21.8 %collective-permute-start.21 = (bf16[2,1,2,2,64,512]{5,4,3,2,1,0:T(8,128)(2,1)S(1)}, bf16[2,1,2,2,64,512]{5,4,3,2,1,0:T(8,128)(2,1)}, u32[]{:S(2)}, u32[]{:S(2)}) collective-permute-start(bf16[2,1,2,2,64,512]{5,4,3,2,1,0:T(8,128)(2,1)S(1)} %pad_maximum_fusion.14), channel_id=1, source_target_pairs={{0,8},{2,10},{4,12},{6,14},{8,0},{10,2},{12,4},{14,6},{16,24},{18,... | collective-permute-start | bytes 1572872 | tf_op jit(solution)/shard_map/ppermute | solution.py:989
  114.8 20.0 %collective-permute-start.23 = (bf16[2,1,1,1,64,1408]{5,4,0,3,2,1:T(8,128)(2,1)}, bf16[2,1,1,1,64,1408]{5,4,0,3,2,1:T(8,128)(2,1)}, u32[]{:S(2)}, u32[]{:S(2)}) collective-permute-start(bf16[2,1,1,1,64,1408]{5,4,0,3,2,1:T(8,128)(2,1)} %get-tuple-element.304), channel_id=1, source_target_pairs={{0,2},{2,0},{4,6},{6,4},{8,10},{10,8},{12,14},{14,12},{16,18},{18,... | collective-permute-start | bytes 1081352 | tf_op jit(solution)/shard_map/ppermute | solution.py:989
  137.6 17.1 %collective-permute-start.25 = (bf16[2,2,1,1,64,1408]{5,4,1,0,3,2:T(8,128)(2,1)}, bf16[2,2,1,1,64,1408]{5,4,1,0,3,2:T(8,128)(2,1)}, u32[]{:S(2)}, u32[]{:S(2)}) collective-permute-start(bf16[2,2,1,1,64,1408]{5,4,1,0,3,2:T(8,128)(2,1)} %bitcast.240), channel_id=1, source_target_pairs={{0,4},{2,6},{4,0},{6,2},{8,12},{10,14},{12,8},{14,10},{16,20},{18,... | collective-permute-start | bytes 2162696 | tf_op jit(solution)/shard_map/ppermute | solution.py:989
  139.1 15.7 %collective-permute-start.26 = (bf16[2,1,1,2,64,1408]{5,4,3,0,2,1:T(8,128)(2,1)}, bf16[2,1,1,2,64,1408]{5,4,3,0,2,1:T(8,128)(2,1)}, u32[]{:S(2)}, u32[]{:S(2)}) collective-permute-start(bf16[2,1,1,2,64,1408]{5,4,3,0,2,1:T(8,128)(2,1)} %bitcast.242), channel_id=1, source_target_pairs={{0,8},{2,10},{4,12},{6,14},{8,0},{10,2},{12,4},{14,6},{16,24},{18,... | collective-permute-start | bytes 2162696 | tf_op jit(solution)/shard_map/ppermute | solution.py:989
  198.4 25.5 %collective-permute-start.32 = (bf16[2,2,2,1,64,1408]{5,4,2,1,0,3:T(8,128)(2,1)}, bf16[2,2,2,1,64,1408]{5,4,2,1,0,3:T(8,128)(2,1)}, u32[]{:S(2)}, u32[]{:S(2)}) collective-permute-start(bf16[2,2,2,1,64,1408]{5,4,2,1,0,3:T(8,128)(2,1)} %bitcast.230), channel_id=1, source_target_pairs={{0,2},{2,0},{4,6},{6,4},{8,10},{10,8},{12,14},{14,12},{16,18},{18,... | collective-permute-start | bytes 4325384 | tf_op jit(solution)/shard_map/ppermute | solution.py:989
  199.2 24.7 %collective-permute-start.33 = (bf16[2,2,1,2,64,1408]{5,4,3,1,0,2:T(8,128)(2,1)}, bf16[2,2,1,2,64,1408]{5,4,3,1,0,2:T(8,128)(2,1)}, u32[]{:S(2)}, u32[]{:S(2)}) collective-permute-start(bf16[2,2,1,2,64,1408]{5,4,3,1,0,2:T(8,128)(2,1)} %bitcast.232), channel_id=1, source_target_pairs={{0,4},{2,6},{4,0},{6,2},{8,12},{10,14},{12,8},{14,10},{16,20},{18,... | collective-permute-start | bytes 4325384 | tf_op jit(solution)/shard_map/ppermute | solution.py:989
  200.7 23.9 %collective-permute-start.34 = (bf16[2,1,2,2,64,1408]{5,4,3,2,0,1:T(8,128)(2,1)}, bf16[2,1,2,2,64,1408]{5,4,3,2,0,1:T(8,128)(2,1)}, u32[]{:S(2)}, u32[]{:S(2)}) collective-permute-start(bf16[2,1,2,2,64,1408]{5,4,3,2,0,1:T(8,128)(2,1)} %bitcast.234), channel_id=1, source_target_pairs={{0,8},{2,10},{4,12},{6,14},{8,0},{10,2},{12,4},{14,6},{16,24},{18,... | collective-permute-start | bytes 4325384 | tf_op jit(solution)/shard_map/ppermute | solution.py:989
  258.3 18.7 %collective-permute-start.37 = (bf16[1024,1024]{1,0:T(8,128)(2,1)}, bf16[1024,1024]{1,0:T(8,128)(2,1)S(1)}, u32[]{:S(2)}, u32[]{:S(2)}) collective-permute-start(bf16[1024,1024]{1,0:T(8,128)(2,1)} %get-tuple-element.366), channel_id=1, source_target_pairs={{0,1},{1,0},{2,3},{3,2},{4,5},{5,4},{6,7},{7,6},{8,9},{9,8},{10,11... | collective-permute-start | bytes 6291464 | tf_op jit(solution)/shard_map/ppermute | solution.py:993
  276.9 47.6 %collective-permute-start.38 = (bf16[2,1,2,2,64,1408]{5,4,3,2,0,1:T(8,128)(2,1)}, bf16[2,1,2,2,64,1408]{5,4,3,2,0,1:T(8,128)(2,1)}, u32[]{:S(2)}, u32[]{:S(2)}) collective-permute-start(bf16[2,1,2,2,64,1408]{5,4,3,2,0,1:T(8,128)(2,1)} %dynamic-slice_bitcast_fusion.2), channel_id=1, source_target_pairs={{0,8},{2,10},{4,12},{6,14},{8,0},{10,2},{12,4},{14,6},{16,24},{18,... | collective-permute-start | bytes 4325384 | tf_op jit(solution)/shard_map/ppermute | solution.py:989
  324.6 36.8 %collective-permute-start.43 = (bf16[2,2,1,2,64,1408]{5,4,3,1,0,2:T(8,128)(2,1)}, bf16[2,2,1,2,64,1408]{5,4,3,1,0,2:T(8,128)(2,1)}, u32[]{:S(2)}, u32[]{:S(2)}) collective-permute-start(bf16[2,2,1,2,64,1408]{5,4,3,1,0,2:T(8,128)(2,1)} %dynamic-slice_bitcast_fusion.1), channel_id=1, source_target_pairs={{0,4},{2,6},{4,0},{6,2},{8,12},{10,14},{12,8},{14,10},{16,20},{18,... | collective-permute-start | bytes 4325384 | tf_op jit(solution)/shard_map/ppermute | solution.py:989
  325.3 36.1 %collective-permute-start.44 = (bf16[2,2,2,1,64,1408]{5,4,2,1,0,3:T(8,128)(2,1)}, bf16[2,2,2,1,64,1408]{5,4,2,1,0,3:T(8,128)(2,1)}, u32[]{:S(2)}, u32[]{:S(2)}) collective-permute-start(bf16[2,2,2,1,64,1408]{5,4,2,1,0,3:T(8,128)(2,1)} %dynamic-slice_bitcast_fusion), channel_id=1, source_target_pairs={{0,2},{2,0},{4,6},{6,4},{8,10},{10,8},{12,14},{14,12},{16,18},{18,... | collective-permute-start | bytes 4325384 | tf_op jit(solution)/shard_map/ppermute | solution.py:989
  326.4 35.0 %collective-permute-start.45 = (bf16[2,1,2,2,64,512]{5,4,3,2,0,1:T(8,128)(2,1)}, bf16[2,1,2,2,64,512]{5,4,3,2,0,1:T(8,128)(2,1)S(1)}, u32[]{:S(2)}, u32[]{:S(2)}) collective-permute-start(bf16[2,1,2,2,64,512]{5,4,3,2,0,1:T(8,128)(2,1)} %dynamic-slice_bitcast_fusion.4), channel_id=1, source_target_pairs={{0,8},{2,10},{4,12},{6,14},{8,0},{10,2},{12,4},{14,6},{16,24},{18,... | collective-permute-start | bytes 1572872 | tf_op jit(solution)/shard_map/ppermute | solution.py:989
  326.4 35.0 %collective-permute-start.46 = (bf16[2,1,2,2,64,512]{5,4,3,2,0,1:T(8,128)(2,1)}, bf16[2,1,2,2,64,512]{5,4,3,2,0,1:T(8,128)(2,1)}, u32[]{:S(2)}, u32[]{:S(2)}) collective-permute-start(bf16[2,1,2,2,64,512]{5,4,3,2,0,1:T(8,128)(2,1)} %dynamic-slice_bitcast_fusion.3), channel_id=1, source_target_pairs={{0,8},{2,10},{4,12},{6,14},{8,0},{10,2},{12,4},{14,6},{16,24},{18,... | collective-permute-start | bytes 1572872 | tf_op jit(solution)/shard_map/ppermute | solution.py:989
  369.2 23.2 %collective-permute-start.47 = (bf16[256,1408]{1,0:T(8,128)(2,1)}, bf16[256,1408]{1,0:T(8,128)(2,1)S(1)}, u32[]{:S(2)}, u32[]{:S(2)}) collective-permute-start(bf16[256,1408]{1,0:T(8,128)(2,1)} %get-tuple-element.429), channel_id=1, source_target_pairs={{0,8},{2,10},{4,12},{6,14},{8,0},{10,2},{12,4},{14,6},{16,24},{18,... | collective-permute-start | bytes 2162696 | tf_op jit(solution)/shard_map/ppermute | solution.py:989
  369.3 23.1 %collective-permute-start.48 = (bf16[256,1408]{1,0:T(8,128)(2,1)}, bf16[256,1408]{1,0:T(8,128)(2,1)}, u32[]{:S(2)}, u32[]{:S(2)}) collective-permute-start(bf16[256,1408]{1,0:T(8,128)(2,1)} %get-tuple-element.430), channel_id=1, source_target_pairs={{0,4},{2,6},{4,0},{6,2},{8,12},{10,14},{12,8},{14,10},{16,20},{18,... | collective-permute-start | bytes 2162696 | tf_op jit(solution)/shard_map/ppermute | solution.py:989
  370.1 22.3 %collective-permute-start.49 = (bf16[256,1408]{1,0:T(8,128)(2,1)}, bf16[256,1408]{1,0:T(8,128)(2,1)}, u32[]{:S(2)}, u32[]{:S(2)}) collective-permute-start(bf16[256,1408]{1,0:T(8,128)(2,1)} %get-tuple-element.431), channel_id=1, source_target_pairs={{0,2},{2,0},{4,6},{6,4},{8,10},{10,8},{12,14},{14,12},{16,18},{18,... | collective-permute-start | bytes 2162696 | tf_op jit(solution)/shard_map/ppermute | solution.py:989
  371.6 20.8 %collective-permute-start.50 = (bf16[256,512]{1,0:T(8,128)(2,1)}, bf16[256,512]{1,0:T(8,128)(2,1)S(1)}, u32[]{:S(2)}, u32[]{:S(2)}) collective-permute-start(bf16[256,512]{1,0:T(8,128)(2,1)} %get-tuple-element.432), channel_id=1, source_target_pairs={{0,2},{2,0},{4,6},{6,4},{8,10},{10,8},{12,14},{14,12},{16,18},{18,... | collective-permute-start | bytes 786440 | tf_op jit(solution)/shard_map/ppermute | solution.py:989
  372.2 20.2 %collective-permute-start.51 = (bf16[256,512]{1,0:T(8,128)(2,1)}, bf16[256,512]{1,0:T(8,128)(2,1)}, u32[]{:S(2)}, u32[]{:S(2)}) collective-permute-start(bf16[256,512]{1,0:T(8,128)(2,1)} %get-tuple-element.433), channel_id=1, source_target_pairs={{0,4},{2,6},{4,0},{6,2},{8,12},{10,14},{12,8},{14,10},{16,20},{18,... | collective-permute-start | bytes 786440 | tf_op jit(solution)/shard_map/ppermute | solution.py:989
  397.6 15.8 %collective-permute-start.52 = (bf16[128,1408]{1,0:T(8,128)(2,1)}, bf16[128,1408]{1,0:T(8,128)(2,1)}, u32[]{:S(2)}, u32[]{:S(2)}) collective-permute-start(bf16[128,1408]{1,0:T(8,128)(2,1)} %get-tuple-element.463), channel_id=1, source_target_pairs={{0,2},{2,0},{4,6},{6,4},{8,10},{10,8},{12,14},{14,12},{16,18},{18,... | collective-permute-start | bytes 1081352 | tf_op jit(solution)/shard_map/ppermute | solution.py:989
  433.5 33.2 %collective-permute-start.58 = (bf16[2,2,2,1,64,1024]{5,4,3,2,1,0:T(8,128)(2,1)}, bf16[2,2,2,1,64,1024]{5,4,3,2,1,0:T(8,128)(2,1)}, u32[]{:S(2)}, u32[]{:S(2)}) collective-permute-start(bf16[2,2,2,1,64,1024]{5,4,3,2,1,0:T(8,128)(2,1)} %constant_dynamic-slice_fusion.3), channel_id=1, source_target_pairs={{0,2},{2,0},{4,6},{6,4},{8,10},{10,8},{12,14},{14,12},{16,18},{18,... | collective-permute-start | bytes 3145736 | tf_op jit(solution)/shard_map/ppermute | solution.py:989
  436.1 30.6 %collective-permute-start.59 = (bf16[2,2,1,2,64,1024]{5,4,3,2,1,0:T(8,128)(2,1)}, bf16[2,2,1,2,64,1024]{5,4,3,2,1,0:T(8,128)(2,1)}, u32[]{:S(2)}, u32[]{:S(2)}) collective-permute-start(bf16[2,2,1,2,64,1024]{5,4,3,2,1,0:T(8,128)(2,1)} %constant_dynamic-slice_fusion.2), channel_id=1, source_target_pairs={{0,4},{2,6},{4,0},{6,2},{8,12},{10,14},{12,8},{14,10},{16,20},{18,... | collective-permute-start | bytes 3145736 | tf_op jit(solution)/shard_map/ppermute | solution.py:989
  438.9 27.8 %collective-permute-start.61 = (bf16[1,1,1,1,64,5248]{5,4,3,2,1,0:T(8,128)(2,1)}, bf16[1,1,1,1,64,5248]{5,4,3,2,1,0:T(8,128)(2,1)S(1)}, u32[]{:S(2)}, u32[]{:S(2)}) collective-permute-start(bf16[1,1,1,1,64,5248]{5,4,3,2,1,0:T(8,128)(2,1)} %fusion.20), channel_id=1, source_target_pairs={{0,16},{2,18},{4,20},{6,22},{8,24},{10,26},{12,28},{14,30},{16,0},... | collective-permute-start | bytes 2015240 | tf_op jit(solution)/shard_map/ppermute | solution.py:989
  440.7 20.4 %collective-permute-start.60 = (bf16[2,1,2,2,64,512]{5,4,3,2,1,0:T(8,128)(2,1)}, bf16[2,1,2,2,64,512]{5,4,3,2,1,0:T(8,128)(2,1)}, u32[]{:S(2)}, u32[]{:S(2)}) collective-permute-start(bf16[2,1,2,2,64,512]{5,4,3,2,1,0:T(8,128)(2,1)} %constant_dynamic-slice_fusion.1), channel_id=1, source_target_pairs={{0,8},{2,10},{4,12},{6,14},{8,0},{10,2},{12,4},{14,6},{16,24},{18,... | collective-permute-start | bytes 1572872 | tf_op jit(solution)/shard_map/ppermute | solution.py:989
  442.8 31.1 %collective-permute-start.36 = (bf16[1024,512]{1,0:T(8,128)(2,1)}, bf16[1024,512]{1,0:T(8,128)(2,1)}, u32[]{:S(2)}, u32[]{:S(2)}) collective-permute-start(bf16[1024,512]{1,0:T(8,128)(2,1)} %constant_dynamic-slice_fusion.4), channel_id=1, source_target_pairs={{0,1},{1,0},{2,3},{3,2},{4,5},{5,4},{6,7},{7,6},{8,9},{9,8},{10,11... | collective-permute-start | bytes 3145736 | tf_op jit(solution)/shard_map/ppermute | solution.py:993
  (128 other events, 1053.8 us)
